TPU v7x, 32 devices: a whole 2x2x4 slice. The times are simulated.
32 devices in a mesh: prow: 4 (over z), pcol: 8 (over y, x, core).
Axes of the slice: x: 2, y: 2, z: 4, core: 2. Of those that a mesh axis runs over, the one named last changes fastest.
Arguments:
- factors: bfloat16 [4, 4096, 512], P(None, ('prow', 'pcol')), may hold values from -0.25 to 0.25
- x_factor: bfloat16 [512, 512], replicated, may hold values from -0.25 to 0.25
- zinv_factor: bfloat16 [512, 512], replicated, may hold values from -0.25 to 0.25
- placement: int32 [4096], replicated, may hold values from 0 to 4095, as said below
Outputs:
- trailing: float32 [4096, 4096], P('prow', 'pcol')
- panels: float32 [4096, 1024], P('prow', 'pcol')
Inputs may be any that keep to these rules, and one draw needn't show every extreme that they name: placement is a permutation of the Schur rows; device d (grid rows slowest) assembles the rows placement[d * 128] to placement[d * 128 + 127]; among one device's rows at most 64 share the same owner grid row (natural row i belongs to grid row (i div 64) mod 4), and some device has exactly 64 such rows.
All inputs are finite; a program needn't handle non-finite values.
Results may differ from a plain program's by a relative error of at most 0.003.
Values may be sent and summed in bfloat16 or wider, within the bound.
No kernel may reach another device: no remote copies, remote signals or barrier semaphores. Data moves between devices by JAX's collectives and lax.ppermute only.
A program may use at most 128 MiB of HBM per device.

v0:
```python
import jax
import jax.numpy as jnp
from jax import lax
from jax.sharding import PartitionSpec as P

RANK = 4
NB = 64
K = 1024


rank_signs = (1.0, 1.0, -1.0, -1.0)


def project(segment, factor_mat):
    span_cols = segment.shape[1]
    flat_rows = segment.reshape(RANK * span_cols, segment.shape[2])
    images = jnp.dot(flat_rows, factor_mat, preferred_element_type=jnp.float32).astype(jnp.bfloat16)
    return images.reshape(RANK, span_cols, factor_mat.shape[1])


def pair_terms(left_x, left_z, right_x, right_z):
    weights = jnp.array(rank_signs, jnp.float32)
    contract = (((1,), (1,)), ((), ()))
    span_rows = left_x.shape[1]
    span_cols = right_x.shape[1]
    width = left_x.shape[2]
    inner_x = lax.dot_general(
        left_x.reshape(RANK * span_rows, width),
        right_x.reshape(RANK * span_cols, width),
        contract,
        preferred_element_type=jnp.float32,
    )
    inner_z = lax.dot_general(
        left_z.reshape(RANK * span_rows, width),
        right_z.reshape(RANK * span_cols, width),
        contract,
        preferred_element_type=jnp.float32,
    )
    product = (inner_x * inner_z).reshape(RANK, span_rows, RANK, span_cols)
    return jnp.einsum("r,riqj,q->ij", weights, product, weights)


def per_device(factors, x_factor, zinv_factor, placement):
    prow_count = lax.axis_size("prow")
    pcol_count = lax.axis_size("pcol")
    total_rows = placement.shape[0]
    local_rows = total_rows // prow_count
    local_cols = total_rows // pcol_count
    prow_id = lax.axis_index("prow")
    pcol_id = lax.axis_index("pcol")
    inverse = (
        jnp.zeros((total_rows,), jnp.int32)
        .at[placement]
        .set(jnp.arange(total_rows, dtype=jnp.int32))
    )
    slot_k = jnp.arange(local_rows)
    natural_k = slot_k // NB * NB * prow_count + prow_id * NB + slot_k % NB
    every = lax.all_gather(factors, ("prow", "pcol"), axis=1, tiled=True)
    slot_j = jnp.arange(local_cols)
    natural_j = slot_j // NB * NB * pcol_count + pcol_id * NB + slot_j % NB
    row_fac = jnp.take(every, inverse[natural_k], axis=1)
    col_fac = jnp.take(every, inverse[natural_j], axis=1)
    schur_local = pair_terms(
        project(row_fac, x_factor),
        project(row_fac, zinv_factor),
        project(col_fac, x_factor),
        project(col_fac, zinv_factor),
    )
    lead_cols = K // pcol_count
    front_cols = schur_local[:, :lead_cols]
    row_panel = lax.all_gather(front_cols, "pcol", axis=1, tiled=True)
    row_panel = (
        row_panel.reshape(local_rows, pcol_count, lead_cols // NB, NB)
        .transpose(0, 2, 1, 3)
        .reshape(local_rows, K)
    )
    lead_rows = K // prow_count
    top_panel, top_cols = (
        lax.all_gather(row_panel[:lead_rows], "prow", axis=0, tiled=True),
        lax.all_gather(schur_local[:lead_rows], "prow", axis=0, tiled=True),
    )

    def natural_rows(stacked):
        return (
            stacked.reshape(prow_count, lead_rows // NB, NB, stacked.shape[1])
            .transpose(1, 0, 2, 3)
            .reshape(K, stacked.shape[1])
        )

    leading = jnp.linalg.cholesky(natural_rows(top_panel))
    panel_rows = lax.linalg.triangular_solve(
        leading, row_panel, left_side=False, lower=True, transpose_a=True
    )
    panel_cols = lax.linalg.triangular_solve(
        leading, natural_rows(top_cols).T, left_side=False, lower=True, transpose_a=True
    )
    trailing = schur_local - jnp.dot(panel_rows, panel_cols.T, precision=lax.Precision.HIGHEST)
    own_panel = lax.dynamic_index_in_dim(
        panel_rows.reshape(local_rows, K // (NB * pcol_count), pcol_count, NB),
        pcol_id,
        2,
        keepdims=False,
    )
    return (trailing, own_panel.reshape(local_rows, K // pcol_count))


def solution(mesh):
    in_specs = (P(None, ("prow", "pcol"), None), P(), P(), P())
    out_specs = (P("prow", "pcol"), P("prow", "pcol"))
    return jax.shard_map(
        per_device, mesh=mesh, in_specs=in_specs, out_specs=out_specs, check_vma=False
    )
```

profile of v0, /device:TPU:0, one launch (start us, length us, event | category | flops | bytes accessed | tf_op | source)
XLA Modules:
  0.0 826.6 jit_solution(14999769741528478548)
XLA Ops:
  10.3 15.5 %scatter_custom_fusion = s32[4096]{0:T(1024)S(1)} fusion(s32[4096]{0:T(1024)S(1)} %compare_select_fusion, s32[4096]{0:T(1024)S(1)} %iota.146, s32[]{:T(128)} %copy.142), kind=kCustom, calls=%fused_computation.226 | custom fusion | bytes 16388 | tf_op jit(solution)/shard_map/scatter | solution.py:54
  29.1 6.2 gather_fusion
  35.5 93.5 %all-gather.5.cloned.1.call-done = bf16[4,4096,512]{2,0,1:T(4,128)(2,1)} async-done(((bf16[4,128,512]{2,0,1:T(4,128)(2,1)}), bf16[4,4096,512]{2,0,1:T(4,128)(2,1)}) %all-gather.5.cloned.1.call-update) | async-done | bytes 16777232 | tf_op jit(solution)/shard_map/all_gather | solution.py:58
  129.0 9.6 %gather_fusion.3 = bf16[512,4,512]{2,1,0:T(4,128)(2,1)} fusion(bf16[4,4096,512]{2,0,1:T(4,128)(2,1)} %all-gather.5.cloned.1.call-done, s32[1024]{0:T(1024)S(1)} %get-tuple-element.115), kind=kCustom, calls=%fused_computation.3 | custom fusion | bytes 4196352 | tf_op jit(solution)/shard_map/jit(_take)/gather | solution.py:62
  140.6 16.5 %gather_fusion.1 = bf16[1024,4,512]{2,1,0:T(4,128)(2,1)} fusion(bf16[4,4096,512]{2,0,1:T(4,128)(2,1)} %all-gather.5.cloned.1.call-done, s32[1024]{0:T(1024)S(1)} %get-tuple-element.116), kind=kCustom, calls=%fused_computation.1 | custom fusion | bytes 8392704 | tf_op jit(solution)/shard_map/jit(_take)/gather | solution.py:61
  168.6 19.2 %fusion.15 = f32[4096,2048]{1,0:T(8,128)} fusion(bf16[2048,512]{1,0:T(8,128)(2,1)} %convolution_convert_fusion.3, bf16[4096,512]{1,0:T(8,128)(2,1)} %bitcast_select_fusion, bf16[512,512]{1,0:T(8,128)(2,1)S(1)} %copy-done), kind=kOutput, calls=%fused_computation.34 | convolution fusion | flops 10739515392 | bytes 40370176 | tf_op jit(solution)/shard_map/dot_general | solution.py:27
  187.8 24.0 %convolution_multiply_fusion = bf16[4096,2048]{1,0:T(8,128)(2,1)} fusion(f32[4096,2048]{1,0:T(8,128)} %fusion.15, bf16[2048,512]{1,0:T(8,128)(2,1)} %convolution_convert_fusion.2, bf16[4096,512]{1,0:T(8,128)(2,1)} %bitcast_select_fusion, bf16[512,512]{1,0:T(8,128)(2,1)S(1)} %copy-done.16), kind=kOutput, calls=%fused_computation.7 | convolution fusion | flops 10756292608 | bytes 57147392 | tf_op jit(solution)/shard_map/dot_general | solution.py:33
  211.8 27.8 %reshape.294 = bf16[4,1024,4,512]{3,2,1,0:T(4,128)(2,1)} reshape(bf16[4096,2048]{1,0:T(8,128)(2,1)} %convolution_multiply_fusion) | data formatting | bytes 33554432 | tf_op jit(solution)/shard_map/reshape | solution.py:39
  239.6 10.5 %fusion.113 = f32[1,1024,512,1]{2,0,1,3:T(1,128)S(1)} fusion(bf16[4,1024,4,512]{3,2,1,0:T(4,128)(2,1)} %reshape.294, bf16[4,4,1,1]{0,2,3,1:T(2,128)(2,1)S(1)} %copy.59), kind=kOutput, calls=%fused_computation.275 | convolution fusion | flops 16777216 | bytes 18874400 | tf_op jit(solution)/shard_map/r,riqj,q->ij/dot_general | solution.py:40
  254.5 33.8 %all-gather.7.cloned.1.call-done = f32[1024,1024]{1,0:T(8,128)} async-done(((f32[1024,128]{1,0:T(8,128)}), f32[1024,1024]{1,0:T(8,128)}) %all-gather.7.cloned.1.call-update) | async-done | bytes 4194320 | tf_op jit(solution)/shard_map/all_gather | solution.py:71
  296.1 39.8 %all-gather.11.cloned.1.call-done = f32[1024,512]{1,0:T(8,128)} async-done(((f32[256,512]{1,0:T(8,128)}), f32[1024,512]{1,0:T(8,128)}) %all-gather.11.cloned.1.call-update) | async-done | bytes 2097168 | tf_op jit(solution)/shard_map/all_gather | solution.py:80
  359.0 57.8 %all-gather.9.cloned.1.call-done = f32[1024,1024]{0,1:T(8,128)} async-done(((f32[256,1024]{0,1:T(8,128)}), f32[1024,1024]{0,1:T(8,128)}) %all-gather.9.cloned.1.call-update) | async-done | bytes 4194320 | tf_op jit(solution)/shard_map/all_gather | solution.py:79
  426.9 5.8 copy.47
  439.1 11.7 %cholesky.223 = f32[128,128]{1,0:T(8,128)S(1)} custom-call(f32[128,128]{1,0:T(8,128)S(1)} %cholesky.580), custom_call_target="Cholesky" | custom-call | tf_op jit(solution)/shard_map/jit(cholesky)/cholesky | solution.py:90
  450.8 9.8 %custom-call.64 = f32[1,128,128]{1,2,0:T(8,128)S(1)} custom-call(f32[1,128,128]{2,1,0:T(8,128)S(1)} %get-tuple-element.104), custom_call_target="InvertDiagBlocksLowerTriangular" | custom-call | tf_op jit(solution)/shard_map/jit(cholesky)/cholesky | solution.py:90
  467.8 11.9 %cholesky.244 = f32[128,128]{1,0:T(8,128)S(1)} custom-call(f32[128,128]{1,0:T(8,128)S(1)} %cholesky.584), custom_call_target="Cholesky" | custom-call | tf_op jit(solution)/shard_map/jit(cholesky)/cholesky | solution.py:90
  481.7 9.8 %custom-call.65 = f32[1,128,128]{1,2,0:T(8,128)S(1)} custom-call(f32[1,128,128]{2,1,0:T(8,128)S(1)} %get-tuple-element.101), custom_call_target="InvertDiagBlocksLowerTriangular" | custom-call | tf_op jit(solution)/shard_map/jit(cholesky)/cholesky | solution.py:90
  495.9 11.7 %cholesky.468 = f32[128,128]{1,0:T(8,128)S(1)} custom-call(f32[128,128]{1,0:T(8,128)S(1)} %cholesky.589), custom_call_target="Cholesky" | custom-call | tf_op jit(solution)/shard_map/jit(cholesky)/cholesky | solution.py:90
  508.8 9.8 %custom-call.66 = f32[1,128,128]{1,2,0:T(8,128)S(1)} custom-call(f32[1,128,128]{2,1,0:T(8,128)S(1)} %get-tuple-element.98), custom_call_target="InvertDiagBlocksLowerTriangular" | custom-call | tf_op jit(solution)/shard_map/jit(cholesky)/cholesky | solution.py:90
  522.2 11.9 %cholesky.487 = f32[128,128]{1,0:T(8,128)S(1)} custom-call(f32[128,128]{1,0:T(8,128)S(1)} %cholesky.594), custom_call_target="Cholesky" | custom-call | tf_op jit(solution)/shard_map/jit(cholesky)/cholesky | solution.py:90
  535.4 9.8 %custom-call.67 = f32[1,128,128]{1,2,0:T(8,128)S(1)} custom-call(f32[1,128,128]{2,1,0:T(8,128)S(1)} %get-tuple-element.95), custom_call_target="InvertDiagBlocksLowerTriangular" | custom-call | tf_op jit(solution)/shard_map/jit(cholesky)/cholesky | solution.py:90
  548.7 11.7 %cholesky.506 = f32[128,128]{1,0:T(8,128)S(1)} custom-call(f32[128,128]{1,0:T(8,128)S(1)} %cholesky.599), custom_call_target="Cholesky" | custom-call | tf_op jit(solution)/shard_map/jit(cholesky)/cholesky | solution.py:90
  561.7 10.2 %custom-call.68 = f32[1,128,128]{1,2,0:T(8,128)S(1)} custom-call(f32[1,128,128]{2,1,0:T(8,128)S(1)} %get-tuple-element.92), custom_call_target="InvertDiagBlocksLowerTriangular" | custom-call | tf_op jit(solution)/shard_map/jit(cholesky)/cholesky | solution.py:90
  575.2 11.7 %cholesky.526 = f32[128,128]{1,0:T(8,128)S(1)} custom-call(f32[128,128]{1,0:T(8,128)S(1)} %cholesky.604), custom_call_target="Cholesky" | custom-call | tf_op jit(solution)/shard_map/jit(cholesky)/cholesky | solution.py:90
  588.2 9.8 %custom-call.69 = f32[1,128,128]{1,2,0:T(8,128)S(1)} custom-call(f32[1,128,128]{2,1,0:T(8,128)S(1)} %get-tuple-element.89), custom_call_target="InvertDiagBlocksLowerTriangular" | custom-call | tf_op jit(solution)/shard_map/jit(cholesky)/cholesky | solution.py:90
  601.0 11.9 %cholesky.546 = f32[128,128]{1,0:T(8,128)S(1)} custom-call(f32[128,128]{1,0:T(8,128)S(1)} %cholesky.609), custom_call_target="Cholesky" | custom-call | tf_op jit(solution)/shard_map/jit(cholesky)/cholesky | solution.py:90
  614.3 9.8 %custom-call.70 = f32[1,128,128]{1,2,0:T(8,128)S(1)} custom-call(f32[1,128,128]{2,1,0:T(8,128)S(1)} %get-tuple-element.86), custom_call_target="InvertDiagBlocksLowerTriangular" | custom-call | tf_op jit(solution)/shard_map/jit(cholesky)/cholesky | solution.py:90
  626.7 11.7 %cholesky.564 = f32[128,128]{1,0:T(8,128)S(1)} custom-call(f32[128,128]{1,0:T(8,128)S(1)} %convolution_subtract_fusion.19), custom_call_target="Cholesky" | custom-call | tf_op jit(solution)/shard_map/jit(cholesky)/cholesky | solution.py:90
  649.6 28.1 %while.1 = (s32[]{:T(128)}, f32[1024,1024]{1,0:T(8,128)}, s32[8,2]{0,1:T(2,128)S(1)}, f32[8,128,128]{2,1,0:T(8,128)}, s32[]{:T(128)}) while((s32[]{:T(128)}, f32[1024,1024]{1,0:T(8,128)}, s32[8,2]{0,1:T(2,128)S(1)}, f32[8,128,128]{2,1,0:T(8,128)}, s32[]{:T(128)}) %tuple.92), condition=%wide.while_cond, body=%wide.while_body.sunk | while | flops 2 | bytes 132705 | solution.py:91
  677.7 80.2 %custom-call.71 = f32[8,128,128]{1,2,0:T(8,128)} custom-call(f32[8,128,128]{2,1,0:T(8,128)} %get-tuple-element.9), custom_call_target="InvertDiagBlocksLowerTriangular" | custom-call | tf_op jit(solution)/shard_map/triangular_solve | solution.py:91
  803.4 6.1 convolution_subtract_fusion.4
  810.2 8.4 %convolution_subtract_fusion = f32[1024,512]{1,0:T(8,128)} fusion(f32[1024,1024]{0,1:T(8,128)S(1)} %convolution_dynamic-update-slice_fusion, f32[512,1024]{0,1:T(8,128)S(1)} %convolution_dynamic-update-slice_fusion.3, f32[1,1024,512,1]{2,0,1,3:T(1,128)S(1)} %fusion.113), kind=kOutput, calls=%fused_computation.33 | convolution fusion | flops 6442975232 | bytes 10485760 | tf_op jit(solution)/shard_map/dot_general | solution.py:97
  (184 shorter events, 188.7 us)
Async XLA Ops:
  7.2 153.6 %copy-start = (bf16[512,512]{1,0:T(8,128)(2,1)S(1)}, bf16[512,512]{1,0:T(8,128)(2,1)}, u32[]{:S(2)}) copy-start(bf16[512,512]{1,0:T(8,128)(2,1)} %param.6) | copy-start | bytes 1572868
  7.2 121.9 %all-gather.5.cloned.1.call-start = ((), (), s32[]{:S(2)}) async-start(), calls=%async_computation | async-start | bytes 17301504 | tf_op jit(solution)/shard_map/all_gather | solution.py:58
  9.5 25.8 %copy-start.15 = (f32[4]{0:T(128)S(1)}, f32[4]{0:T(128)}, u32[]{:S(2)}) copy-start(f32[4]{0:T(128)} %constant.385.clone) | copy-start | bytes 52
  9.5 278.8 %all-gather.7.cloned.1.call-start = ((), (), s32[]{:S(2)}) async-start(), calls=%async_computation.1 | async-start | bytes 4718592 | tf_op jit(solution)/shard_map/all_gather | solution.py:71
  160.8 2.6 copy-start.16
  250.3 1.3 copy-start.6
  252.5 83.3 %all-gather.11.cloned.1.call-start = ((), (), s32[]{:S(2)}) async-start(), calls=%async_computation.3 | async-start | bytes 2621440 | tf_op jit(solution)/shard_map/all_gather | solution.py:80
  254.4 162.3 %all-gather.9.cloned.1.call-start = ((), (), s32[]{:S(2)}) async-start(), calls=%async_computation.2 | async-start | bytes 5242880 | tf_op jit(solution)/shard_map/all_gather | solution.py:79
  344.8 2.8 copy-start.2
  437.1 2.0 copy-start.4
  467.0 0.8 copy-start.13
  758.0 3.6 copy-start.3
  758.0 6.5 copy-start.5
  758.0 7.5 copy-start.12
  772.5 7.5 copy-start.10
  776.4 5.3 copy-start.9
  781.0 3.3 copy-start.11
  784.3 3.5 copy-start.14
  787.8 4.4 copy-start.8
  792.2 5.1 copy-start.7
  810.2 9.4 %copy-start.1 = (bf16[512,512]{1,0:T(8,128)(2,1)S(1)}, bf16[512,512]{1,0:T(8,128)(2,1)}, u32[]{:S(2)}) copy-start(bf16[512,512]{1,0:T(8,128)(2,1)} %param.6) | copy-start | bytes 1572868
Sparse Core Ops, SparseCore 0:
  11.4 117.5 all-gather.4
  252.6 35.6 all-gather.6
  289.9 45.9 all-gather.10
  337.3 79.4 all-gather.8
where the time goes:
time: 838 us; the launch traced here: 827 us
  other arithmetic  267 us (32%)
  waiting for transfers between devices  225 us (27%)
  local copies, waits for them, and re-layouts  172 us (21%)
  matrix products  143 us (17%)
  between operations  20.1 us (2%)
    another operation x31, other arithmetic, per_device(): leading = jnp.linalg.cholesky(natural_rows(top_panel))  173 us
    all_gather x1, waiting for transfers between devices, per_device(): every = lax.all_gather(factors, ('prow', 'pcol'), axis=1, tiled=True)  93.5 us
    another operation x3, other arithmetic, per_device(): lax.linalg.triangular_solve(leading, row_panel, left_side=False, lower=Tr...  85.1 us
    all_gather x1, waiting for transfers between devices, per_device(): lax.all_gather(row_panel[:lead_rows], 'prow', axis=0, tiled=True)  57.8 us
    all_gather x1, waiting for transfers between devices, per_device(): lax.all_gather(schur_local[:lead_rows], 'prow', axis=0, tiled=True)  39.8 us
    all_gather x1, waiting for transfers between devices, per_device(): row_panel = lax.all_gather(front_cols, 'pcol', axis=1, tiled=True)  33.8 us
    another operation x15, matrix products, per_device(): lax.linalg.triangular_solve(leading, row_panel, left_side=False, lower=Tr...  31.9 us
    another operation x24, local copies, waits for them, and re-layouts  28.1 us
  transfers between devices with their start and end apart: 4, of which 4 were waited for; matrix products, arithmetic and copies ran while one was open for 7% of the time, Pallas kernels for 0%

commit v1 on v0

v1 whole, which is shorter than its diff:
```python
import functools

import jax
import jax.numpy as jnp
from jax import lax
from jax.experimental import pallas as pl
from jax.experimental.pallas import tpu as pltpu
from jax.sharding import PartitionSpec as P

RANK = 4
NB = 64
K = 1024
SUB = 8
BLK = 128
MIB = 2**20

rank_signs = (1.0, 1.0, -1.0, -1.0)
NT = ((1,), (1,))
NN = ((1,), (0,))
VMEM = pl.BlockSpec(memory_space=pltpu.VMEM)
SMEM = pl.BlockSpec(memory_space=pltpu.SMEM)


def split(x):
    hi = x.astype(jnp.bfloat16)
    lo = (x - hi.astype(jnp.float32)).astype(jnp.bfloat16)
    return hi, lo


def dot_bf16(a, b, dims):
    return lax.dot_general(a, b, (dims, ((), ())), preferred_element_type=jnp.float32)


def dot3(a, b, dims):
    return dot_bf16(a[0], b[0], dims) + (dot_bf16(a[0], b[1], dims) + dot_bf16(a[1], b[0], dims))


def project_kernel(wanted_ref, placement_ref, factors_ref, x_ref, z_ref, yx_ref, yz_ref, *, chunk):
    slots = factors_ref.shape[0]
    width = x_ref.shape[0]
    rows = wanted_ref.shape[0]
    wanted = wanted_ref[...]
    total = jnp.zeros((rows, RANK * width), jnp.float32)
    for first in range(0, slots, chunk):
        here = placement_ref[:, first:first + chunk]
        pick = jnp.where(wanted == here, 1.0, 0.0).astype(jnp.bfloat16)
        total = total + dot_bf16(pick, factors_ref[first:first + chunk, :], NN)
    picked = total.astype(jnp.bfloat16)
    for r in range(RANK):
        mine = picked[:, r * width:(r + 1) * width]
        yx_ref[r] = dot_bf16(mine, x_ref[...], NN).astype(jnp.bfloat16)
        yz_ref[r] = dot_bf16(mine, z_ref[...], NN).astype(jnp.bfloat16)


def project(wanted, placement, factors, x_factor, z_factor):
    rows = wanted.shape[0]
    slots, wide = factors.shape
    width = x_factor.shape[0]
    tile = min(256, rows)
    whole = lambda *shape: pl.BlockSpec(shape, lambda i: (0,) * len(shape))
    out = pl.BlockSpec((RANK, tile, width), lambda i: (0, i, 0))
    return pl.pallas_call(
        functools.partial(project_kernel, chunk=512),
        grid=(rows // tile,),
        out_shape=(jax.ShapeDtypeStruct((RANK, rows, width), jnp.bfloat16),) * 2,
        in_specs=[pl.BlockSpec((tile, 1), lambda i: (i, 0)), whole(1, slots), whole(slots, wide), whole(width, width), whole(width, width)],
        out_specs=(out, out),
        compiler_params=pltpu.CompilerParams(vmem_limit_bytes=56 * MIB),
        cost_estimate=pl.CostEstimate(flops=2 * rows * wide * (slots + 2 * width), bytes_accessed=2 * slots * wide + 4 * rows * wide, transcendentals=0),
    )(wanted.reshape(rows, 1), placement.reshape(1, slots), factors, x_factor, z_factor)


def gram_kernel(lx_ref, lz_ref, rx_ref, rz_ref, out_ref):
    total = jnp.zeros(out_ref.shape, jnp.float32)
    for q in range(RANK):
        for r in range(RANK):
            gx = dot_bf16(lx_ref[r], rx_ref[q], NT)
            gz = dot_bf16(lz_ref[r], rz_ref[q], NT)
            if rank_signs[q] * rank_signs[r] > 0:
                total = total + gx * gz
            else:
                total = total - gx * gz
    out_ref[...] = total


def gram(lx, lz, rx, rz):
    _, rows, width = lx.shape
    cols = rx.shape[1]
    row_tile, col_tile = min(512, rows), min(256, cols)
    left = pl.BlockSpec((RANK, row_tile, width), lambda i, j: (0, i, 0))
    right = pl.BlockSpec((RANK, col_tile, width), lambda i, j: (0, j, 0))
    return pl.pallas_call(
        gram_kernel,
        grid=(rows // row_tile, cols // col_tile),
        out_shape=jax.ShapeDtypeStruct((rows, cols), jnp.float32),
        in_specs=[left, left, right, right],
        out_specs=pl.BlockSpec((row_tile, col_tile), lambda i, j: (i, j)),
        compiler_params=pltpu.CompilerParams(vmem_limit_bytes=56 * MIB),
        cost_estimate=pl.CostEstimate(flops=4 * RANK * RANK * rows * cols * width, bytes_accessed=4 * RANK * (rows + cols) * width + 4 * rows * cols, transcendentals=0),
    )(lx, lz, rx, rz)


def factor_block(block, u_ref, v_ref):
    count = BLK // SUB
    sub_iota = lax.broadcasted_iota(jnp.int32, (SUB, BLK), 0)
    lane_iota = lax.broadcasted_iota(jnp.int32, (SUB, BLK), 1)
    rows_a = [block[SUB * i:SUB * (i + 1), :] for i in range(count)]
    rows_v = [(lane_iota == sub_iota + SUB * i).astype(jnp.float32) for i in range(count)]

    def spread_lane(x, lane):
        return jnp.broadcast_to(x[:, lane:lane + 1], (SUB, BLK))

    def spread_row(x, row):
        return jnp.broadcast_to(x[row:row + 1, :], (SUB, BLK))

    for m in range(count):
        head_a, head_v = rows_a[m], rows_v[m]
        cols = [spread_lane(head_a, SUB * m + k) for k in range(SUB)]
        below = [[spread_lane(rows_a[i], SUB * m + k) for k in range(SUB)] for i in range(m + 1, count)]
        scale = jnp.zeros((SUB, BLK), jnp.float32)
        for j in range(SUB):
            pivot = spread_row(cols[j], j)
            root = lax.rsqrt(pivot)
            scale = jnp.where(sub_iota == j, root, scale)
            mult = jnp.where(sub_iota > j, cols[j] * root, 0.0)
            row_a = spread_row(head_a, j) * root
            row_v = spread_row(head_v, j) * root
            lead = [spread_row(cols[k], j) * root if k > j else None for k in range(SUB)]
            if j + 1 < SUB:
                head_a = head_a - mult * row_a
                head_v = head_v - mult * row_v
                for k in range(j + 1, SUB):
                    cols[k] = cols[k] - mult * lead[k]
            for n, i in enumerate(range(m + 1, count)):
                mult_i = below[n][j] * root
                rows_a[i] = rows_a[i] - mult_i * row_a
                rows_v[i] = rows_v[i] - mult_i * row_v
                for k in range(j + 1, SUB):
                    below[n][k] = below[n][k] - mult_i * lead[k]
        u = jnp.where(lane_iota >= sub_iota + SUB * m, head_a * scale, 0.0)
        v = jnp.where(lane_iota <= sub_iota + SUB * m, head_v * scale, 0.0)
        u_ref[SUB * m:SUB * (m + 1), :] = u
        v_ref[SUB * m:SUB * (m + 1), :] = v


def natural_tile(pieces, row_block, col_pair):
    prow, pcol = pieces.shape[:2]
    rows = pl.ds(row_block // prow * NB, NB)
    halves = []
    for block in (2 * col_pair, 2 * col_pair + 1):
        halves.append(pieces[row_block % prow, block % pcol, rows, pl.ds(block // pcol * NB, NB)])
    return jnp.concatenate(halves, axis=1)


def factor_kernel(pieces_ref, l_ref, d_ref, w_ref, u_ref, v_ref):
    order = l_ref.shape[0]
    steps = order // BLK
    for i in range(order // NB):
        for j in range(steps):
            w_ref[i * NB:(i + 1) * NB, j * BLK:(j + 1) * BLK] = natural_tile(pieces_ref, i, j)
    l_ref[...] = jnp.zeros_like(l_ref)

    def step(b, carry):
        at = pl.ds(pl.multiple_of(b * BLK, BLK), BLK)
        factor_block(w_ref[at, at], u_ref, v_ref)
        l_ref[at, at] = u_ref[...].T
        d_ref[at, :] = v_ref[...]
        for k in range(steps - 1):
            @pl.when(b == k)
            def _():
                first = (k + 1) * BLK
                inv = split(v_ref[...])
                def panel(t, c):
                    rows = pl.ds(pl.multiple_of(first + t * BLK, BLK), BLK)
                    l_ref[rows, k * BLK:first] = dot3(split(w_ref[rows, k * BLK:first]), inv, NT)
                    return c
                lax.fori_loop(0, steps - 1 - k, panel, 0)
                right = split(l_ref[first:, k * BLK:first])
                def update(t, c):
                    rows = pl.ds(pl.multiple_of(first + t * BLK, BLK), BLK)
                    left = split(l_ref[rows, k * BLK:first])
                    w_ref[rows, first:] = w_ref[rows, first:] - dot3(left, right, NT)
                    return c
                lax.fori_loop(0, steps - 1 - k, update, 0)
        return carry
    lax.fori_loop(0, steps, step, 0)


def factor(pieces):
    return pl.pallas_call(
        factor_kernel,
        out_shape=(jax.ShapeDtypeStruct((K, K), jnp.float32), jax.ShapeDtypeStruct((K, BLK), jnp.float32)),
        in_specs=[VMEM],
        out_specs=(VMEM, VMEM),
        scratch_shapes=[pltpu.VMEM((K, K), jnp.float32), pltpu.VMEM((BLK, BLK), jnp.float32), pltpu.VMEM((BLK, BLK), jnp.float32)],
        compiler_params=pltpu.CompilerParams(vmem_limit_bytes=48 * MIB),
        cost_estimate=pl.CostEstimate(flops=40 * 10**9, bytes_accessed=12 * MIB, transcendentals=0),
    )(pieces)


def solve_kernel(column_ref, l_ref, d_ref, pieces_ref, tops_ref, schur_ref, rest_ref, panel_ref, lh, ll, xh, xl, zh, zl):
    rows = schur_ref.shape[0]
    pcol = pieces_ref.shape[0]
    prow = tops_ref.shape[0]
    column = column_ref[0]
    low = l_ref[...]
    lh[...], ll[...] = split(low)
    for b in range(K // BLK):
        at = slice(b * BLK, (b + 1) * BLK)
        inverse = split(d_ref[at, :])
        halves = []
        for block in (2 * b, 2 * b + 1):
            halves.append(pieces_ref[block % pcol, :, block // pcol * NB:(block // pcol + 1) * NB])
        value = jnp.concatenate(halves, axis=1)
        lower = []
        for block in (2 * b, 2 * b + 1):
            lower.append(tops_ref[block % prow, block // prow * NB:(block // prow + 1) * NB, :])
        top = jnp.concatenate(lower, axis=0)
        if b > 0:
            done = slice(0, b * BLK)
            left = (lh[at, done], ll[at, done])
            value = value - dot3((xh[:, done], xl[:, done]), left, NT)
            top = top - dot3(left, (zh[done, :], zl[done, :]), NN)
        value = dot3(split(value), inverse, NT)
        top = dot3(inverse, split(top), NN)
        xh[:, at], xl[:, at] = split(value)
        zh[at, :], zl[at, :] = split(top)
        for half, block in enumerate((2 * b, 2 * b + 1)):
            @pl.when(column == block % pcol)
            def _():
                panel_ref[:, block // pcol * NB:(block // pcol + 1) * NB] = value[:, half * NB:(half + 1) * NB]
    rest_ref[...] = schur_ref[...] - dot3((xh[...], xl[...]), (zh[...], zl[...]), NN)


def solve(column, low, inverses, pieces, tops, schur):
    rows, cols = schur.shape
    lead = K // pieces.shape[0]
    bf16 = jnp.bfloat16
    return pl.pallas_call(
        solve_kernel,
        out_shape=(jax.ShapeDtypeStruct((rows, cols), jnp.float32), jax.ShapeDtypeStruct((rows, lead), jnp.float32)),
        in_specs=[SMEM] + [VMEM] * 5,
        out_specs=(VMEM, VMEM),
        scratch_shapes=[pltpu.VMEM((K, K), bf16)] * 2 + [pltpu.VMEM((rows, K), bf16)] * 2 + [pltpu.VMEM((K, cols), bf16)] * 2,
        compiler_params=pltpu.CompilerParams(vmem_limit_bytes=56 * MIB),
        cost_estimate=pl.CostEstimate(flops=12 * 10**9, bytes_accessed=24 * MIB, transcendentals=0),
    )(column, low, inverses, pieces, tops, schur)


def per_device(factors, x_factor, zinv_factor, placement):
    prow_count = lax.axis_size("prow")
    pcol_count = lax.axis_size("pcol")
    total_rows = placement.shape[0]
    local_rows = total_rows // prow_count
    local_cols = total_rows // pcol_count
    prow_id = lax.axis_index("prow")
    pcol_id = lax.axis_index("pcol")
    _, own, width = factors.shape
    every = lax.all_gather(factors.transpose(1, 0, 2).reshape(own, RANK * width), ("prow", "pcol"), axis=0, tiled=True)
    slot_k = jnp.arange(local_rows)
    natural_k = slot_k // NB * NB * prow_count + prow_id * NB + slot_k % NB
    slot_j = jnp.arange(local_cols)
    natural_j = slot_j // NB * NB * pcol_count + pcol_id * NB + slot_j % NB
    wanted = jnp.concatenate([natural_k, natural_j]).astype(jnp.int32)
    yx, yz = project(wanted, placement, every, x_factor, zinv_factor)
    schur_local = gram(yx[:, :local_rows], yz[:, :local_rows], yx[:, local_rows:], yz[:, local_rows:])
    lead_rows, lead_cols = K // prow_count, K // pcol_count
    front = schur_local[:, :lead_cols]
    lead = lax.all_gather(front[:lead_rows], ("prow", "pcol"), axis=0, tiled=False)
    lead = lead.reshape(prow_count, pcol_count, lead_rows, lead_cols)
    pieces = lax.all_gather(front, "pcol", axis=0, tiled=False)
    tops = lax.all_gather(schur_local[:lead_rows], "prow", axis=0, tiled=False)
    low, inverses = factor(lead)
    return solve(pcol_id.astype(jnp.int32).reshape(1), low, inverses, pieces, tops, schur_local)


def solution(mesh):
    in_specs = (P(None, ("prow", "pcol"), None), P(), P(), P())
    out_specs = (P("prow", "pcol"), P("prow", "pcol"))
    return jax.shard_map(
        per_device, mesh=mesh, in_specs=in_specs, out_specs=out_specs, check_vma=False
    )
```

time: 838 us -> 383 us (0.46); the launches traced: 827 us -> 383 us
  other arithmetic: 267 us -> 0.02 us
  local copies, waits for them, and re-layouts: 172 us -> 22.7 us
  matrix products: 143 us -> 0 us
  Pallas kernels: 0 us -> 140 us
  waiting for transfers between devices: 225 us -> 206 us
    another operation x34 -> x0, other arithmetic: 258 us -> none  [the longest x31 173 us: per_device(): leading = jnp.linalg.cholesky(natural_rows(top_panel))]
    pallas_call x0 -> x4, Pallas kernels: none -> 140 us  [the longest x1 50.9 us: factor(): pl.pallas_call(factor_kernel, out_shape=(jax.ShapeDtypeStruct((K, K), jnp...]
    another operation x44 -> x0, matrix products: 75.9 us -> none  [the longest x15 31.9 us: per_device(): lax.linalg.triangular_solve(leading, row_panel, left_side=False, lower=Tr...]
    dot_general x6 -> x0, matrix products: 67.2 us -> none  [the longest x1 24 us: pair_terms(): lax.dot_general(left_z.reshape(RANK * span_rows, width), right_z.reshape(...]
    gather x6 -> x0, local copies, waits for them, and re-layouts: 40.4 us -> none  [the longest x3 25.7 us: per_device(): row_fac = jnp.take(every, inverse[natural_k], axis=1)]
    reshape x4 -> x2, local copies, waits for them, and re-layouts: 39.6 us -> 3.04 us  [the longest x1 1.89 us: per_device(): factors.transpose(1, 0, 2).reshape(own, RANK * width)]
    another operation x34 -> x0, local copies, waits for them, and re-layouts: 32.3 us -> none
    all_gather x4, waiting for transfers between devices: 225 us -> 206 us  [the longest x1 119 us: per_device(): lax.all_gather(factors.transpose(1, 0, 2).reshape(own, RANK * width), ('p...]
  transfers between devices with their start and end apart: 4 -> 4, of which waited for: 4 -> 3; matrix products, arithmetic and copies ran while one was open for 7% -> 1% of each run, Pallas kernels for 0% -> 13%
where the time goes in v1:
time: 383 us
  waiting for transfers between devices  206 us (54%)
  Pallas kernels  140 us (37%)
  local copies, waits for them, and re-layouts  22.7 us (6%)
  between operations  13.8 us (4%)
    all_gather x1, waiting for transfers between devices, per_device(): lax.all_gather(factors.transpose(1, 0, 2).reshape(own, RANK * width), ('p...  119 us
    all_gather x1, waiting for transfers between devices, per_device(): lax.all_gather(front[:lead_rows], ('prow', 'pcol'), axis=0, tiled=False)  56.3 us
    pallas_call x1, Pallas kernels, factor(): pl.pallas_call(factor_kernel, out_shape=(jax.ShapeDtypeStruct((K, K), jnp...  50.9 us
    pallas_call x1, Pallas kernels, project(): pl.pallas_call(functools.partial(project_kernel, chunk=512), grid=(rows /...  41.3 us
    all_gather x1, waiting for transfers between devices, per_device(): pieces = lax.all_gather(front, 'pcol', axis=0, tiled=False)  30.7 us
    pallas_call x1, Pallas kernels, solve(): pl.pallas_call(solve_kernel, out_shape=(jax.ShapeDtypeStruct((rows, cols)...  26.3 us
    pallas_call x1, Pallas kernels, gram(): pl.pallas_call(gram_kernel, grid=(rows // row_tile, cols // col_tile), ou...  22 us
  transfers between devices with their start and end apart: 4, of which 3 were waited for; matrix products, arithmetic and copies ran while one was open for 1% of the time, Pallas kernels for 13%

profile of v1, /device:TPU:0, one launch (start us, length us, event | category | flops | bytes accessed | tf_op | source)
XLA Modules:
  0.0 383.1 jit_solution(8194113697656966115)
XLA Ops:
  7.2 0.0 all-gather.8.cloned.1.call-start
  7.2 1.9 copy.9
  9.1 0.0 all-gather.8.cloned.1.call-update
  9.1 0.0 all-gather.10.cloned.1.call-start
  9.2 1.1 reshape.28.wanted_ref
  10.4 118.6 %all-gather.8.cloned.1.call-done.factors_ref = bf16[4096,2048]{1,0:T(8,128)(2,1)} async-done(((bf16[128,2048]{1,0:T(8,128)(2,1)}), bf16[4096,2048]{1,0:T(8,128)(2,1)}) %all-gather.8.cloned.1.call-update) | async-done | bytes 16777232 | tf_op jit(solution)/shard_map/all_gather | solution.py:259
  129.0 41.3 %shard_map.59 = (bf16[4,1536,512]{2,1,0:T(8,128)(2,1)}, bf16[4,1536,512]{2,1,0:T(8,128)(2,1)}) custom-call(s32[1536,1]{1,0:T(8,128)} %reshape.28.wanted_ref, s32[1,4096]{1,0:T(1,128)} %bitcast.15, bf16[4096,2048]{1,0:T(8,128)(2,1)} %all-gather.8.cloned.1.call-done.factors_ref, bf16[512,512]{1,0:T(8,128)(2,1)} %x_ref.1, bf16[512,512]{1,0:T(8,128)(2,1)} %z_ref.1), custom_call_target="tpu_custom_call" | custom-call | flops 32212254720 | bytes 29360128 | tf_op jit(solution)/shard_map/pallas_call | solution.py:62
  170.3 0.0 slice-start
  170.3 3.2 slice.24.rx_ref
  173.5 0.0 slice-start.1
  173.5 4.6 %slice.22.lx_ref = bf16[4,1024,512]{2,1,0:T(8,128)(2,1)} slice(bf16[4,1536,512]{2,1,0:T(8,128)(2,1)} %get-tuple-element.6), slice={[0:4], [0:1024], [0:512]} | slice | bytes 8388608 | tf_op jit(solution)/shard_map/slice | solution.py:266
  178.1 0.0 slice-done
  178.1 0.0 slice-done.1
  178.1 1.5 slice.25.rz_ref
  179.6 2.3 slice.23.lz_ref
  181.8 22.0 %shard_map.60.schur_ref = f32[1024,512]{1,0:T(8,128)} custom-call(bf16[4,1024,512]{2,1,0:T(8,128)(2,1)} %slice.22.lx_ref, bf16[4,1024,512]{2,1,0:T(8,128)(2,1)} %slice.23.lz_ref, bf16[4,512,512]{2,1,0:T(8,128)(2,1)} %slice.24.rx_ref, bf16[4,512,512]{2,1,0:T(8,128)(2,1)} %slice.25.rz_ref), custom_call_target="tpu_custom_call" | custom-call | flops 17179869184 | bytes 14680064 | tf_op jit(solution)/shard_map/pallas_call | solution.py:92
  203.9 1.6 slice.29
  205.4 0.0 all-gather.10.cloned.1.call-update
  205.5 0.0 all-gather.14.cloned.1.call-start
  205.5 1.9 slice.31
  207.4 0.0 all-gather.14.cloned.1.call-update
  207.4 0.2 all-gather.12.cloned.1.call-start
  207.6 1.9 slice.30
  209.5 0.0 all-gather.12.cloned.1.call-update
  209.5 56.3 %all-gather.10.cloned.1.call-done = f32[8192,128]{1,0:T(8,128)} async-done(((f32[256,128]{1,0:T(8,128)}), f32[8192,128]{1,0:T(8,128)}) %all-gather.10.cloned.1.call-update) | async-done | bytes 4194320 | tf_op jit(solution)/shard_map/all_gather | solution.py:269
  265.8 50.9 %shard_map.61 = (f32[1024,1024]{1,0:T(8,128)S(1)}, f32[1024,128]{1,0:T(8,128)S(1)}) custom-call(f32[4,8,256,128]{3,2,1,0:T(8,128)} %bitcast.12), custom_call_target="tpu_custom_call" | custom-call | flops 40000000000 | bytes 12582912 | tf_op jit(solution)/shard_map/pallas_call | solution.py:190
  316.7 0.0 copy-start
  316.7 2.0 copy-done
  318.7 0.8 copy-done.1
  319.6 0.0 all-gather.14.cloned.1.call-done
  319.6 30.7 %all-gather.12.cloned.1.call-done = f32[8192,128]{1,0:T(8,128)} async-done(((f32[1024,128]{1,0:T(8,128)}), f32[8192,128]{1,0:T(8,128)}) %all-gather.12.cloned.1.call-update) | async-done | bytes 4194320 | tf_op jit(solution)/shard_map/all_gather | solution.py:271
  350.3 26.3 %shard_map.62 = (f32[1024,512]{1,0:T(8,128)}, f32[1024,128]{1,0:T(8,128)}) custom-call(s32[1]{0:T(128)} %bitcast.column_ref, f32[1024,1024]{1,0:T(8,128)} %copy-done, f32[1024,128]{1,0:T(8,128)} %copy-done.1, f32[8,1024,128]{2,1,0:T(8,128)} %bitcast.13, f32[4,256,512]{2,1,0:T(8,128)} %bitcast.14, f32[1024,512]{1,0:T(8,128)} %shard_map.60.schur_ref), custom_call_target="tpu_custom_call" | custom-call | flops 12000000000 | bytes 25165824 | tf_op jit(solution)/shard_map/pallas_call | solution.py:239
  (5 shorter events, 0.0 us)
Async XLA Ops:
  7.2 121.9 %all-gather.8.cloned.1.call-start = ((), (), s32[]{:S(2)}) async-start(), calls=%async_computation | async-start | bytes 17301504 | tf_op jit(solution)/shard_map/all_gather | solution.py:259
  9.1 256.7 %all-gather.10.cloned.1.call-start = ((), (), s32[]{:S(2)}) async-start(), calls=%async_computation.1 | async-start | bytes 4325376 | tf_op jit(solution)/shard_map/all_gather | solution.py:269
  170.3 7.8 %slice-start = ((s8[6291456]{0:T(1024)(128)(4,1)}), s8[4194304]{0:T(1024)(128)(4,1)S(1)}, s32[]{:S(2)}) async-start(s8[6291456]{0:T(1024)(128)(4,1)} %bitcast.8), calls=%async_computation.4 | async-start | bytes 8388608
  173.5 4.6 %slice-start.1 = ((s8[6291456]{0:T(1024)(128)(4,1)}), s8[2097152]{0:T(1024)(128)(4,1)S(1)}, s32[]{:S(2)}) async-start(s8[6291456]{0:T(1024)(128)(4,1)} %bitcast.8), calls=%async_computation.5 | async-start | bytes 4194304
  205.5 114.1 %all-gather.14.cloned.1.call-start = ((), (), s32[]{:S(2)}) async-start(), calls=%async_computation.3 | async-start | bytes 2621440 | tf_op jit(solution)/shard_map/all_gather | solution.py:272
  207.4 142.9 %all-gather.12.cloned.1.call-start = ((), (), s32[]{:S(2)}) async-start(), calls=%async_computation.2 | async-start | bytes 4718592 | tf_op jit(solution)/shard_map/all_gather | solution.py:271
  316.7 2.0 copy-start
  318.7 0.8 copy-start.1
Sparse Core Ops, SparseCore 0:
  11.4 117.5 all-gather.7
  205.6 60.1 all-gather.9
  268.0 44.7 all-gather.13
  315.0 35.1 all-gather.11

commit v2 on v1

v2 whole, which is shorter than its diff:
```python
import functools

import jax
import jax.numpy as jnp
from jax import lax
from jax.experimental import pallas as pl
from jax.experimental.pallas import tpu as pltpu
from jax.sharding import PartitionSpec as P

RANK = 4
NB = 64
K = 1024
SUB = 8
BLK = 128
MIB = 2**20

rank_signs = (1.0, 1.0, -1.0, -1.0)
NT = ((1,), (1,))
NN = ((1,), (0,))
VMEM = pl.BlockSpec(memory_space=pltpu.VMEM)
SMEM = pl.BlockSpec(memory_space=pltpu.SMEM)


def split(x):
    hi = x.astype(jnp.bfloat16)
    lo = (x - hi.astype(jnp.float32)).astype(jnp.bfloat16)
    return hi, lo


def dot_bf16(a, b, dims):
    return lax.dot_general(a, b, (dims, ((), ())), preferred_element_type=jnp.float32)


def dot3(a, b, dims):
    return dot_bf16(a[0], b[0], dims) + (dot_bf16(a[0], b[1], dims) + dot_bf16(a[1], b[0], dims))


def assemble_kernel(slots_ref, own_ref, other_ref, x_ref, z_ref, lead_x_ref, lead_z_ref, schur_ref, front_ref, top_ref,
                    every_ref, picked_ref, yx_ref, yz_ref, sem_ref, *, lead_tiles, pick_tiles, row_tiles, col_tiles, rows):
    step = pl.program_id(0)
    half = own_ref.shape[0]
    tile, parts, lanes = picked_ref.shape
    width = x_ref.shape[0]
    per_rank = width // lanes

    @pl.when(step == 0)
    def _():
        first = pltpu.make_async_copy(own_ref, every_ref.at[pl.ds(0, half)], sem_ref.at[0])
        second = pltpu.make_async_copy(other_ref, every_ref.at[pl.ds(half, half)], sem_ref.at[1])
        first.start()
        second.start()
        first.wait()
        second.wait()

    @pl.when(step < pick_tiles)
    def _():
        def pick(group, carry):
            for k in range(16):
                i = group * 16 + k
                picked_ref[i] = every_ref[slots_ref[step * tile + i]]
            return carry
        lax.fori_loop(0, tile // 16, pick, 0)
        by_part = jnp.swapaxes(picked_ref[...], 0, 1)
        images = []
        for r in range(RANK):
            mine = jnp.concatenate([by_part[r * per_rank + k] for k in range(per_rank)], axis=1)
            images.append((dot_bf16(mine, x_ref[...], NN).astype(jnp.bfloat16), dot_bf16(mine, z_ref[...], NN).astype(jnp.bfloat16)))

        @pl.when(step < lead_tiles)
        def _():
            for r in range(RANK):
                lead_x_ref[r], lead_z_ref[r] = images[r]

        @pl.when(step >= lead_tiles)
        def _():
            at = pl.ds(pl.multiple_of((step - lead_tiles) * tile, tile), tile)
            for r in range(RANK):
                yx_ref[r, at, :], yz_ref[r, at, :] = images[r]

    @pl.when(step >= pick_tiles)
    def _():
        high, wide = schur_ref.shape
        i, j = (step - pick_tiles) // col_tiles, (step - pick_tiles) % col_tiles
        left = pl.ds(pl.multiple_of(i * high, high), high)
        right = pl.ds(pl.multiple_of(rows + j * wide, wide), wide)
        value = gram_tile(yx_ref, yz_ref, left, right)
        schur_ref[...] = value

        @pl.when(j == 0)
        def _():
            front_ref[...] = value[:, :front_ref.shape[1]]

        @pl.when(i == 0)
        def _():
            top_ref[...] = value[:top_ref.shape[0], :]


def gram_tile(yx_ref, yz_ref, left, right):
    total = None
    for q in range(RANK):
        for r in range(RANK):
            gx = dot_bf16(yx_ref[r, left, :], yx_ref[q, right, :], NT)
            gz = dot_bf16(yz_ref[r, left, :], yz_ref[q, right, :], NT)
            if total is None:
                total = gx * gz
            elif rank_signs[q] * rank_signs[r] > 0:
                total = total + gx * gz
            else:
                total = total - gx * gz
    return total


def assemble(slots, own, other, x_factor, z_factor, rows, cols, lead_rows, lead_cols):
    half, parts, lanes = own.shape
    width = x_factor.shape[0]
    tile = 256
    high, wide = min(512, rows), min(256, cols)
    lead_tiles, pick_tiles = K // tile, slots.shape[0] // tile
    row_tiles, col_tiles = rows // high, cols // wide
    whole = pl.BlockSpec((width, width), lambda s: (0, 0), pipeline_mode=pl.Buffered(1))
    lead = pl.BlockSpec((RANK, tile, width), lambda s: (0, jnp.minimum(s, lead_tiles - 1), 0))
    after = lambda s: jnp.maximum(s - pick_tiles, 0)
    bf16 = jnp.bfloat16
    any_space = pl.BlockSpec(memory_space=pl.ANY)
    body = functools.partial(assemble_kernel, lead_tiles=lead_tiles, pick_tiles=pick_tiles, row_tiles=row_tiles, col_tiles=col_tiles, rows=rows)
    return pl.pallas_call(
        body,
        grid=(pick_tiles + row_tiles * col_tiles,),
        out_shape=(jax.ShapeDtypeStruct((RANK, K, width), bf16),) * 2 + (
            jax.ShapeDtypeStruct((rows, cols), jnp.float32),
            jax.ShapeDtypeStruct((rows, lead_cols), jnp.float32),
            jax.ShapeDtypeStruct((lead_rows, cols), jnp.float32)),
        in_specs=[SMEM, any_space, any_space, whole, whole],
        out_specs=(lead, lead,
                   pl.BlockSpec((high, wide), lambda s: (after(s) // col_tiles, after(s) % col_tiles)),
                   pl.BlockSpec((high, lead_cols), lambda s: (after(s) // col_tiles, 0)),
                   pl.BlockSpec((lead_rows, wide), lambda s: (0, jnp.minimum(after(s), col_tiles - 1)))),
        scratch_shapes=[pltpu.VMEM((2 * half, parts, lanes), bf16), pltpu.VMEM((tile, parts, lanes), bf16)]
        + [pltpu.VMEM((RANK, rows + cols, width), bf16)] * 2 + [pltpu.SemaphoreType.DMA((2,))],
        compiler_params=pltpu.CompilerParams(vmem_limit_bytes=58 * MIB),
        cost_estimate=pl.CostEstimate(flops=28 * 10**9, bytes_accessed=30 * MIB, transcendentals=0),
    )(slots, own, other, x_factor, z_factor)


def factor_block(block, u_ref, v_ref):
    count = BLK // SUB
    sub_iota = lax.broadcasted_iota(jnp.int32, (SUB, BLK), 0)
    lane_iota = lax.broadcasted_iota(jnp.int32, (SUB, BLK), 1)
    rows_a = [block[SUB * i:SUB * (i + 1), :] for i in range(count)]
    rows_v = [(lane_iota == sub_iota + SUB * i).astype(jnp.float32) for i in range(count)]

    def spread_lane(x, lane):
        return jnp.broadcast_to(x[:, lane:lane + 1], (SUB, BLK))

    def spread_row(x, row):
        return jnp.broadcast_to(x[row:row + 1, :], (SUB, BLK))

    for m in range(count):
        head_a, head_v = rows_a[m], rows_v[m]
        cols = [spread_lane(head_a, SUB * m + k) for k in range(SUB)]
        below = [[spread_lane(rows_a[i], SUB * m + k) for k in range(SUB)] for i in range(m + 1, count)]
        scale = jnp.zeros((SUB, BLK), jnp.float32)
        for j in range(SUB):
            pivot = spread_row(cols[j], j)
            root = lax.rsqrt(pivot)
            scale = jnp.where(sub_iota == j, root, scale)
            mult = jnp.where(sub_iota > j, cols[j] * root, 0.0)
            row_a = spread_row(head_a, j) * root
            row_v = spread_row(head_v, j) * root
            lead = [spread_row(cols[k], j) * root if k > j else None for k in range(SUB)]
            if j + 1 < SUB:
                head_a = head_a - mult * row_a
                head_v = head_v - mult * row_v
                for k in range(j + 1, SUB):
                    cols[k] = cols[k] - mult * lead[k]
            for n, i in enumerate(range(m + 1, count)):
                mult_i = below[n][j] * root
                rows_a[i] = rows_a[i] - mult_i * row_a
                rows_v[i] = rows_v[i] - mult_i * row_v
                for k in range(j + 1, SUB):
                    below[n][k] = below[n][k] - mult_i * lead[k]
        u = jnp.where(lane_iota >= sub_iota + SUB * m, head_a * scale, 0.0)
        v = jnp.where(lane_iota <= sub_iota + SUB * m, head_v * scale, 0.0)
        u_ref[SUB * m:SUB * (m + 1), :] = u
        v_ref[SUB * m:SUB * (m + 1), :] = v


def factor_kernel(yx_ref, yz_ref, l_ref, d_ref, w_ref, u_ref, v_ref):
    order = l_ref.shape[0]
    steps = order // BLK
    tile = 256
    l_ref[...] = jnp.zeros_like(l_ref)
    w_ref[...] = jnp.zeros_like(w_ref)

    def columns(j, carry):
        right = pl.ds(pl.multiple_of(j * tile, tile), tile)

        def rows(i, carry):
            left = pl.ds(pl.multiple_of(i * tile, tile), tile)
            w_ref[left, right] = gram_tile(yx_ref, yz_ref, left, right)
            return carry
        return lax.fori_loop(j, order // tile, rows, carry)
    lax.fori_loop(0, order // tile, columns, 0)

    def step(b, carry):
        at = pl.ds(pl.multiple_of(b * BLK, BLK), BLK)
        factor_block(w_ref[at, at], u_ref, v_ref)
        l_ref[at, at] = u_ref[...].T
        d_ref[at, :] = v_ref[...]
        for k in range(steps - 1):
            @pl.when(b == k)
            def _():
                first = (k + 1) * BLK
                inv = split(v_ref[...])
                def panel(t, c):
                    rows = pl.ds(pl.multiple_of(first + t * BLK, BLK), BLK)
                    l_ref[rows, k * BLK:first] = dot3(split(w_ref[rows, k * BLK:first]), inv, NT)
                    return c
                lax.fori_loop(0, steps - 1 - k, panel, 0)
                right = split(l_ref[first:, k * BLK:first])
                def update(t, c):
                    rows = pl.ds(pl.multiple_of(first + t * BLK, BLK), BLK)
                    left = split(l_ref[rows, k * BLK:first])
                    w_ref[rows, first:] = w_ref[rows, first:] - dot3(left, right, NT)
                    return c
                lax.fori_loop(0, steps - 1 - k, update, 0)
        return carry
    lax.fori_loop(0, steps, step, 0)


def factor(yx, yz):
    return pl.pallas_call(
        factor_kernel,
        out_shape=(jax.ShapeDtypeStruct((K, K), jnp.float32), jax.ShapeDtypeStruct((K, BLK), jnp.float32)),
        in_specs=[VMEM] * 2,
        out_specs=(VMEM, VMEM),
        scratch_shapes=[pltpu.VMEM((K, K), jnp.float32), pltpu.VMEM((BLK, BLK), jnp.float32), pltpu.VMEM((BLK, BLK), jnp.float32)],
        compiler_params=pltpu.CompilerParams(vmem_limit_bytes=48 * MIB),
        cost_estimate=pl.CostEstimate(flops=40 * 10**9, bytes_accessed=12 * MIB, transcendentals=0),
    )(yx, yz)


def solve_kernel(column_ref, l_ref, d_ref, pieces_ref, tops_ref, schur_ref, rest_ref, panel_ref, lh, ll, xh, xl, zh, zl):
    pcol = pieces_ref.shape[0]
    prow = tops_ref.shape[0]
    column = column_ref[0]
    lh[...], ll[...] = split(l_ref[...])
    wide = 2 * BLK
    for b in range(K // wide):
        at = slice(b * wide, (b + 1) * wide)
        upper, lower = slice(b * wide, b * wide + BLK), slice(b * wide + BLK, (b + 1) * wide)
        first, second = split(d_ref[upper, :]), split(d_ref[lower, :])
        between = dot3((lh[lower, upper], ll[lower, upper]), first, NN)
        corner = -dot3(second, split(between), NN)
        inverse = split(jnp.concatenate([
            jnp.concatenate([d_ref[upper, :], jnp.zeros((BLK, BLK), jnp.float32)], axis=1),
            jnp.concatenate([corner, d_ref[lower, :]], axis=1)], axis=0))
        blocks = range(wide // NB * b, wide // NB * (b + 1))
        value = jnp.concatenate([pieces_ref[n % pcol, :, n // pcol * NB:(n // pcol + 1) * NB] for n in blocks], axis=1)
        top = jnp.concatenate([tops_ref[n % prow, n // prow * NB:(n // prow + 1) * NB, :] for n in blocks], axis=0)
        if b > 0:
            done = slice(0, b * wide)
            left = (lh[at, done], ll[at, done])
            value = value - dot3((xh[:, done], xl[:, done]), left, NT)
            top = top - dot3(left, (zh[done, :], zl[done, :]), NN)
        value = dot3(split(value), inverse, NT)
        top = dot3(inverse, split(top), NN)
        xh[:, at], xl[:, at] = split(value)
        zh[at, :], zl[at, :] = split(top)
        for place, block in enumerate(blocks):
            @pl.when(column == block % pcol)
            def _():
                panel_ref[:, block // pcol * NB:(block // pcol + 1) * NB] = value[:, place * NB:(place + 1) * NB]
    rest_ref[...] = schur_ref[...] - dot3((xh[...], xl[...]), (zh[...], zl[...]), NN)


def solve(column, low, inverses, pieces, tops, schur):
    rows, cols = schur.shape
    lead = K // pieces.shape[0]
    bf16 = jnp.bfloat16
    return pl.pallas_call(
        solve_kernel,
        out_shape=(jax.ShapeDtypeStruct((rows, cols), jnp.float32), jax.ShapeDtypeStruct((rows, lead), jnp.float32)),
        in_specs=[SMEM] + [VMEM] * 5,
        out_specs=(VMEM, VMEM),
        scratch_shapes=[pltpu.VMEM((K, K), bf16)] * 2 + [pltpu.VMEM((rows, K), bf16)] * 2 + [pltpu.VMEM((K, cols), bf16)] * 2,
        compiler_params=pltpu.CompilerParams(vmem_limit_bytes=56 * MIB),
        cost_estimate=pl.CostEstimate(flops=12 * 10**9, bytes_accessed=24 * MIB, transcendentals=0),
    )(column, low, inverses, pieces, tops, schur)


def per_device(factors, x_factor, zinv_factor, placement):
    prow_count = lax.axis_size("prow")
    pcol_count = lax.axis_size("pcol")
    total_rows = placement.shape[0]
    local_rows = total_rows // prow_count
    local_cols = total_rows // pcol_count
    prow_id = lax.axis_index("prow")
    pcol_id = lax.axis_index("pcol")
    _, own, width = factors.shape
    count = prow_count * pcol_count
    lanes = BLK
    mine = factors.transpose(1, 0, 2).reshape(own, RANK * width // lanes, lanes)
    alike = [[d for d in range(count) if d % 2 == parity] for parity in range(2)]
    near = lax.all_gather(mine, ("prow", "pcol"), axis=0, tiled=True, axis_index_groups=alike)
    far = lax.ppermute(near, "pcol", [(c, c ^ 1) for c in range(pcol_count)])
    slot_k = jnp.arange(local_rows)
    natural_k = slot_k // NB * NB * prow_count + prow_id * NB + slot_k % NB
    slot_j = jnp.arange(local_cols)
    natural_j = slot_j // NB * NB * pcol_count + pcol_id * NB + slot_j % NB
    inverse = jnp.zeros((total_rows,), jnp.int32).at[placement].set(jnp.arange(total_rows, dtype=jnp.int32))
    wanted = jnp.concatenate([jnp.arange(K), natural_k, natural_j]).astype(jnp.int32)
    slots = inverse[wanted]
    holder = slots // own
    places = holder // 2 * own + slots % own + jnp.where(holder % 2 == pcol_id % 2, 0, total_rows // 2)
    lead_rows, lead_cols = K // prow_count, K // pcol_count
    lead_x, lead_z, schur_local, front, top = assemble(
        places.astype(jnp.int32), near, far, x_factor, zinv_factor, local_rows, local_cols, lead_rows, lead_cols)
    pieces = lax.all_gather(front, "pcol", axis=0, tiled=False)
    tops = lax.all_gather(top, "prow", axis=0, tiled=False)
    low, inverses = factor(lead_x, lead_z)
    return solve(pcol_id.astype(jnp.int32).reshape(1), low, inverses, pieces, tops, schur_local)


def solution(mesh):
    in_specs = (P(None, ("prow", "pcol"), None), P(), P(), P())
    out_specs = (P("prow", "pcol"), P("prow", "pcol"))
    return jax.shard_map(
        per_device, mesh=mesh, in_specs=in_specs, out_specs=out_specs, check_vma=False
    )
```

time: 383 us -> 314 us (0.82)
  waiting for transfers between devices: 206 us -> 121 us
  local copies, waits for them, and re-layouts: 22.7 us -> 34.4 us
    all_gather x3 -> x2, waiting for transfers between devices: 175 us -> 117 us  [the longest x1 117 us: per_device(): lax.all_gather(mine, ('prow', 'pcol'), axis=0, tiled=True, axis_index_gro...]
    all_gather x1, waiting for transfers between devices: 30.7 us -> 3.71 us  [per_device(): pieces = lax.all_gather(front, 'pcol', axis=0, tiled=False)]
    pallas_call x1, Pallas kernels: 50.9 us -> 75.2 us  [factor(): pl.pallas_call(factor_kernel, out_shape=(jax.ShapeDtypeStruct((K, K), jnp...]
    slice x7 -> x0, local copies, waits for them, and re-layouts: 16.8 us -> none  [the longest x1 4.56 us: per_device(): yx[:, :local_rows]]
    pallas_call x2 -> x1, Pallas kernels: 63.4 us -> 47.3 us  [assemble(): pl.pallas_call(body, grid=(pick_tiles + row_tiles * col_tiles,), out_shap...]
    scatter x0 -> x1, local copies, waits for them, and re-layouts: none -> 15.5 us  [per_device(): jnp.zeros((total_rows,), jnp.int32).at[placement]]
    gather x0 -> x1, local copies, waits for them, and re-layouts: none -> 13.6 us  [per_device(): slots = inverse[wanted]]
    pallas_call x1, Pallas kernels: 26.3 us -> 20.3 us  [solve(): pl.pallas_call(solve_kernel, out_shape=(jax.ShapeDtypeStruct((rows, cols)...]
  transfers between devices with their start and end apart: 4 -> 4, of which waited for: 3 -> 2; matrix products, arithmetic and copies ran while one was open for 1% -> 10% of each run, Pallas kernels for 13% -> 24%
where the time goes in v2:
time: 314 us
  Pallas kernels  143 us (46%)
  waiting for transfers between devices  121 us (39%)
  local copies, waits for them, and re-layouts  34.4 us (11%)
  between operations  13.8 us (4%)
    all_gather x1, waiting for transfers between devices, per_device(): lax.all_gather(mine, ('prow', 'pcol'), axis=0, tiled=True, axis_index_gro...  117 us
    pallas_call x1, Pallas kernels, factor(): pl.pallas_call(factor_kernel, out_shape=(jax.ShapeDtypeStruct((K, K), jnp...  75.2 us
    pallas_call x1, Pallas kernels, assemble(): pl.pallas_call(body, grid=(pick_tiles + row_tiles * col_tiles,), out_shap...  47.3 us
    pallas_call x1, Pallas kernels, solve(): pl.pallas_call(solve_kernel, out_shape=(jax.ShapeDtypeStruct((rows, cols)...  20.3 us
    scatter x1, local copies, waits for them, and re-layouts, per_device(): jnp.zeros((total_rows,), jnp.int32).at[placement]  15.5 us
    gather x1, local copies, waits for them, and re-layouts, per_device(): slots = inverse[wanted]  13.6 us
  transfers between devices with their start and end apart: 4, of which 2 were waited for; matrix products, arithmetic and copies ran while one was open for 10% of the time, Pallas kernels for 24%

profile of v2, /device:TPU:0, one launch (start us, length us, event | category | flops | bytes accessed | tf_op | source)
XLA Modules:
  0.0 314.1 jit_solution(4097524532263695589)
XLA Ops:
  7.2 0.0 all-gather.6.cloned.1.call-start
  7.2 1.4 copy.8
  8.7 1.0 reshape.83
  9.7 0.0 all-gather.6.cloned.1.call-update
  9.7 0.0 all-gather.10.cloned.1.call-start
  9.7 117.2 %all-gather.6.cloned.1.call-done.own_ref = bf16[2048,16,128]{2,1,0:T(8,128)(2,1)} async-done(((bf16[128,16,128]{2,1,0:T(8,128)(2,1)}), bf16[2048,16,128]{2,1,0:T(8,128)(2,1)}) %all-gather.6.cloned.1.call-update) | async-done | bytes 8388624 | tf_op jit(solution)/shard_map/all_gather | solution.py:305
  126.9 0.0 collective-permute-start
  126.9 0.7 compare_select_fusion.1
  127.6 15.5 %scatter_custom_fusion = s32[4096]{0:T(1024)S(1)} fusion(s32[4096]{0:T(1024)S(1)} %compare_select_fusion.1, s32[4096]{0:T(1024)S(1)} %iota.35, s32[]{:T(128)} %constant.110.clone.1), kind=kCustom, calls=%fused_computation.33 | custom fusion | bytes 16388 | tf_op jit(solution)/shard_map/scatter | solution.py:311
  143.3 13.6 %gather_fusion = s32[2560]{0:T(1024)S(1)} fusion(s32[4096]{0:T(1024)S(1)} %scatter_custom_fusion, s32[3072]{0:T(1024)S(1)} %pad_clamp_fusion), kind=kCustom, calls=%fused_computation | custom fusion | bytes 30720 | tf_op jit(solution)/shard_map/gather | solution.py:313
  156.9 0.6 fusion.2.slots_ref
  157.5 0.0 collective-permute-done.other_ref
  157.5 47.3 %shard_map.59 = (bf16[4,1024,512]{2,1,0:T(8,128)(2,1)}, bf16[4,1024,512]{2,1,0:T(8,128)(2,1)}, f32[1024,512]{1,0:T(8,128)}, f32[1024,128]{1,0:T(8,128)}, f32[256,512]{1,0:T(8,128)}) custom-call(s32[2560]{0:T(1024)} %fusion.2.slots_ref, bf16[2048,16,128]{2,1,0:T(8,128)(2,1)} %all-gather.6.cloned.1.call-done.own_ref, ...), custom_call_target="tpu_custom_call" | custom-call | flops 28000000000 | bytes 31457280 | tf_op jit(solution)/shard_map/pallas_call | solution.py:126
  204.8 0.0 all-gather.10.cloned.1.call-update
  204.8 0.2 all-gather.8.cloned.1.call-start
  205.0 0.5 all-gather.8.cloned.1.call-update
  205.6 75.2 %shard_map.60 = (f32[1024,1024]{1,0:T(8,128)S(1)}, f32[1024,128]{1,0:T(8,128)S(1)}) custom-call(bf16[4,1024,512]{2,1,0:T(8,128)(2,1)} %get-tuple-element.9.yx_ref, bf16[4,1024,512]{2,1,0:T(8,128)(2,1)} %get-tuple-element.10.yz_ref), custom_call_target="tpu_custom_call" | custom-call | flops 40000000000 | bytes 12582912 | tf_op jit(solution)/shard_map/pallas_call | solution.py:232
  280.7 0.0 copy-start
  280.7 2.0 copy-done
  282.7 0.0 copy-start.1
  282.7 0.8 copy-done.1
  283.5 0.0 all-gather.10.cloned.1.call-done
  283.5 3.7 %all-gather.8.cloned.1.call-done = f32[8192,128]{1,0:T(8,128)} async-done(((f32[1024,128]{1,0:T(8,128)}), f32[8192,128]{1,0:T(8,128)}) %all-gather.8.cloned.1.call-update) | async-done | bytes 4194320 | tf_op jit(solution)/shard_map/all_gather | solution.py:319
  287.2 20.3 %shard_map.61 = (f32[1024,512]{1,0:T(8,128)}, f32[1024,128]{1,0:T(8,128)}) custom-call(s32[1]{0:T(128)} %bitcast.column_ref, f32[1024,1024]{1,0:T(8,128)} %copy-done, f32[1024,128]{1,0:T(8,128)} %copy-done.1, f32[8,1024,128]{2,1,0:T(8,128)} %bitcast.10, f32[4,256,512]{2,1,0:T(8,128)} %bitcast.11, f32[1024,512]{1,0:T(8,128)} %get-tuple-element.15.schur_ref), custom_call_target="tpu_custom_call" | custom-call | flops 12000000000 | bytes 25165824 | tf_op jit(solution)/shard_map/pallas_call | solution.py:281
  (6 shorter events, 0.1 us)
Async XLA Ops:
  7.2 119.7 %all-gather.6.cloned.1.call-start = ((), (), s32[]{:S(2)}) async-start(), calls=%async_computation | async-start | bytes 8912896 | tf_op jit(solution)/shard_map/all_gather | solution.py:305
  9.7 273.9 %all-gather.10.cloned.1.call-start = ((), (), s32[]{:S(2)}) async-start(), calls=%async_computation.2 | async-start | bytes 2621440 | tf_op jit(solution)/shard_map/all_gather | solution.py:320
  126.9 30.6 %collective-permute-start = (bf16[2048,16,128]{2,1,0:T(8,128)(2,1)}, bf16[2048,16,128]{2,1,0:T(8,128)(2,1)}, u32[]{:S(2)}, u32[]{:S(2)}) collective-permute-start(bf16[2048,16,128]{2,1,0:T(8,128)(2,1)} %all-gather.6.cloned.1.call-done.own_ref), channel_id=1, source_target_pairs={{0,1},{1,0},{2,3},{3,2},{4,5},{5,4},{6,7},{7,6},{8,9},{9,8},{10,11... | collective-permute-start | bytes 25165832 | tf_op jit(solution)/shard_map/ppermute | solution.py:306
  204.8 82.4 %all-gather.8.cloned.1.call-start = ((), (), s32[]{:S(2)}) async-start(), calls=%async_computation.1 | async-start | bytes 4718592 | tf_op jit(solution)/shard_map/all_gather | solution.py:319
  280.7 2.0 copy-start
  282.7 0.8 copy-start.1
Sparse Core Ops, SparseCore 0:
  11.3 115.5 all-gather.5
  204.9 44.2 all-gather.9
  251.7 35.4 all-gather.7

commit v3 on v2

--- a/solution.py
+++ b/solution.py
@@ -35,22 +35,22 @@
     return dot_bf16(a[0], b[0], dims) + (dot_bf16(a[0], b[1], dims) + dot_bf16(a[1], b[0], dims))
 
 
-def assemble_kernel(slots_ref, own_ref, other_ref, x_ref, z_ref, lead_x_ref, lead_z_ref, schur_ref, front_ref, top_ref,
-                    every_ref, picked_ref, yx_ref, yz_ref, sem_ref, *, lead_tiles, pick_tiles, row_tiles, col_tiles, rows):
+def assemble_kernel(slots_ref, x_ref, z_ref, *refs, sources, lead_tiles, pick_tiles, col_tiles, rows):
+    source_refs, refs = refs[:sources], refs[sources:]
+    lead_x_ref, lead_z_ref, schur_ref, front_ref, top_ref, every_ref, picked_ref, yx_ref, yz_ref, sem_ref = refs
     step = pl.program_id(0)
-    half = own_ref.shape[0]
+    share = every_ref.shape[0] // sources
     tile, parts, lanes = picked_ref.shape
     width = x_ref.shape[0]
     per_rank = width // lanes
 
     @pl.when(step == 0)
     def _():
-        first = pltpu.make_async_copy(own_ref, every_ref.at[pl.ds(0, half)], sem_ref.at[0])
-        second = pltpu.make_async_copy(other_ref, every_ref.at[pl.ds(half, half)], sem_ref.at[1])
-        first.start()
-        second.start()
-        first.wait()
-        second.wait()
+        copies = [pltpu.make_async_copy(ref, every_ref.at[pl.ds(n * share, share)], sem_ref.at[n]) for n, ref in enumerate(source_refs)]
+        for copy in copies:
+            copy.start()
+        for copy in copies:
+            copy.wait()
 
     @pl.when(step < pick_tiles)
     def _():
@@ -110,8 +110,8 @@
     return total
 
 
-def assemble(slots, own, other, x_factor, z_factor, rows, cols, lead_rows, lead_cols):
-    half, parts, lanes = own.shape
+def assemble(slots, sources, x_factor, z_factor, rows, cols, lead_rows, lead_cols):
+    share, parts, lanes = sources[0].shape
     width = x_factor.shape[0]
     tile = 256
     high, wide = min(512, rows), min(256, cols)
@@ -122,7 +122,7 @@
     after = lambda s: jnp.maximum(s - pick_tiles, 0)
     bf16 = jnp.bfloat16
     any_space = pl.BlockSpec(memory_space=pl.ANY)
-    body = functools.partial(assemble_kernel, lead_tiles=lead_tiles, pick_tiles=pick_tiles, row_tiles=row_tiles, col_tiles=col_tiles, rows=rows)
+    body = functools.partial(assemble_kernel, sources=len(sources), lead_tiles=lead_tiles, pick_tiles=pick_tiles, col_tiles=col_tiles, rows=rows)
     return pl.pallas_call(
         body,
         grid=(pick_tiles + row_tiles * col_tiles,),
@@ -130,16 +130,16 @@
             jax.ShapeDtypeStruct((rows, cols), jnp.float32),
             jax.ShapeDtypeStruct((rows, lead_cols), jnp.float32),
             jax.ShapeDtypeStruct((lead_rows, cols), jnp.float32)),
-        in_specs=[SMEM, any_space, any_space, whole, whole],
+        in_specs=[SMEM, whole, whole] + [any_space] * len(sources),
         out_specs=(lead, lead,
                    pl.BlockSpec((high, wide), lambda s: (after(s) // col_tiles, after(s) % col_tiles)),
                    pl.BlockSpec((high, lead_cols), lambda s: (after(s) // col_tiles, 0)),
                    pl.BlockSpec((lead_rows, wide), lambda s: (0, jnp.minimum(after(s), col_tiles - 1)))),
-        scratch_shapes=[pltpu.VMEM((2 * half, parts, lanes), bf16), pltpu.VMEM((tile, parts, lanes), bf16)]
-        + [pltpu.VMEM((RANK, rows + cols, width), bf16)] * 2 + [pltpu.SemaphoreType.DMA((2,))],
+        scratch_shapes=[pltpu.VMEM((len(sources) * share, parts, lanes), bf16), pltpu.VMEM((tile, parts, lanes), bf16)]
+        + [pltpu.VMEM((RANK, rows + cols, width), bf16)] * 2 + [pltpu.SemaphoreType.DMA((len(sources),))],
         compiler_params=pltpu.CompilerParams(vmem_limit_bytes=58 * MIB),
         cost_estimate=pl.CostEstimate(flops=28 * 10**9, bytes_accessed=30 * MIB, transcendentals=0),
-    )(slots, own, other, x_factor, z_factor)
+    )(slots, x_factor, z_factor, *sources)
 
 
 def factor_block(block, u_ref, v_ref):
@@ -289,6 +289,33 @@
     )(column, low, inverses, pieces, tops, schur)
 
 
+def gather_factors(mine, prow_count, pcol_count):
+    own = mine.shape[0]
+    half = own // 2
+
+    def swap(axis, count, turn, value):
+        return lax.ppermute(value, axis, [(n, n ^ turn) for n in range(count)])
+
+    items = {0: mine}
+    for turn in range(1, prow_count, 2):
+        items[turn] = swap("prow", prow_count, turn, mine)
+    for turn in range(2, prow_count, 2):
+        items[turn] = swap("prow", prow_count, 1, items[turn + 1])
+    near, far = {}, {}
+    for turn in [0] + list(range(1, prow_count, 2)) + list(range(2, prow_count, 2)):
+        held = {0: items[turn]}
+        for j in range(1, pcol_count // 2):
+            low = j & -j
+            high = 1 << (j.bit_length() - 1)
+            if low == high:
+                held[j] = swap("pcol", pcol_count, 2 * j, items[turn])
+            else:
+                held[j] = jnp.concatenate([swap("pcol", pcol_count, 2 * high, held[j ^ high][:half]), swap("pcol", pcol_count, 2 * low, held[j ^ low][half:])])
+        near[turn] = jnp.concatenate([held[j] for j in range(pcol_count // 2)])
+        far[turn] = swap("pcol", pcol_count, 1, near[turn])
+    return [near[m] for m in range(prow_count)] + [far[m] for m in range(prow_count)]
+
+
 def per_device(factors, x_factor, zinv_factor, placement):
     prow_count = lax.axis_size("prow")
     pcol_count = lax.axis_size("pcol")
@@ -301,9 +328,7 @@
     count = prow_count * pcol_count
     lanes = BLK
     mine = factors.transpose(1, 0, 2).reshape(own, RANK * width // lanes, lanes)
-    alike = [[d for d in range(count) if d % 2 == parity] for parity in range(2)]
-    near = lax.all_gather(mine, ("prow", "pcol"), axis=0, tiled=True, axis_index_groups=alike)
-    far = lax.ppermute(near, "pcol", [(c, c ^ 1) for c in range(pcol_count)])
+    sources = gather_factors(mine, prow_count, pcol_count)
     slot_k = jnp.arange(local_rows)
     natural_k = slot_k // NB * NB * prow_count + prow_id * NB + slot_k % NB
     slot_j = jnp.arange(local_cols)
@@ -312,10 +337,11 @@
     wanted = jnp.concatenate([jnp.arange(K), natural_k, natural_j]).astype(jnp.int32)
     slots = inverse[wanted]
     holder = slots // own
-    places = holder // 2 * own + slots % own + jnp.where(holder % 2 == pcol_id % 2, 0, total_rows // 2)
+    row_turn, col_turn = (holder // pcol_count) ^ prow_id, (holder % pcol_count) ^ pcol_id
+    places = (((col_turn % 2) * prow_count + row_turn) * (pcol_count // 2) + col_turn // 2) * own + slots % own
     lead_rows, lead_cols = K // prow_count, K // pcol_count
     lead_x, lead_z, schur_local, front, top = assemble(
-        places.astype(jnp.int32), near, far, x_factor, zinv_factor, local_rows, local_cols, lead_rows, lead_cols)
+        places.astype(jnp.int32), sources, x_factor, zinv_factor, local_rows, local_cols, lead_rows, lead_cols)
     pieces = lax.all_gather(front, "pcol", axis=0, tiled=False)
     tops = lax.all_gather(top, "prow", axis=0, tiled=False)
     low, inverses = factor(lead_x, lead_z)

time: 314 us -> 298 us (0.949)
  waiting for transfers between devices: 121 us -> 65.7 us
  starting transfers between devices: 0.31 us -> 27.8 us
  local copies, waits for them, and re-layouts: 34.4 us -> 45.9 us
    all_gather x1 -> x0, waiting for transfers between devices: 117 us -> none  [per_device(): lax.all_gather(mine, ('prow', 'pcol'), axis=0, tiled=True, axis_index_gro...]
    ppermute x1 -> x23, waiting for transfers between devices: 0.01 us -> 53.2 us  [swap(): return lax.ppermute(value, axis, [(n, n ^ turn) for n in range(count)])]
    ppermute x1 -> x23, starting transfers between devices: 0.01 us -> 27.6 us  [swap(): return lax.ppermute(value, axis, [(n, n ^ turn) for n in range(count)])]
    unnamed x4 -> x24, local copies, waits for them, and re-layouts: 2.78 us -> 12.7 us
    all_gather x1, waiting for transfers between devices: 3.71 us -> 12 us  [per_device(): pieces = lax.all_gather(front, 'pcol', axis=0, tiled=False)]
  transfers between devices with their start and end apart: 4 -> 25, of which waited for: 2 -> 11; matrix products, arithmetic and copies ran while one was open for 10% -> 14% of each run, Pallas kernels for 24% -> 25%
where the time goes in v3:
time: 298 us
  Pallas kernels  143 us (48%)
  waiting for transfers between devices  65.7 us (22%)
  local copies, waits for them, and re-layouts  45.9 us (15%)
  starting transfers between devices  27.8 us (9%)
  between operations  14.3 us (5%)
    pallas_call x1, Pallas kernels, factor(): pl.pallas_call(factor_kernel, out_shape=(jax.ShapeDtypeStruct((K, K), jnp...  75.2 us
    ppermute x23, waiting for transfers between devices, swap(): return lax.ppermute(value, axis, [(n, n ^ turn) for n in range(count)])  53.2 us
    pallas_call x1, Pallas kernels, assemble(): pl.pallas_call(body, grid=(pick_tiles + row_tiles * col_tiles,), out_shap...  47.7 us
    ppermute x23, starting transfers between devices, swap(): return lax.ppermute(value, axis, [(n, n ^ turn) for n in range(count)])  27.6 us
    pallas_call x1, Pallas kernels, solve(): pl.pallas_call(solve_kernel, out_shape=(jax.ShapeDtypeStruct((rows, cols)...  20.3 us
    scatter x1, local copies, waits for them, and re-layouts, per_device(): jnp.zeros((total_rows,), jnp.int32).at[placement]  15.5 us
    gather x1, local copies, waits for them, and re-layouts, per_device(): slots = inverse[wanted]  13.6 us
    unnamed x24, local copies, waits for them, and re-layouts  12.7 us
  transfers between devices with their start and end apart: 25, of which 11 were waited for; matrix products, arithmetic and copies ran while one was open for 14% of the time, Pallas kernels for 25%

profile of v3, /device:TPU:0, one launch (start us, length us, event | category | flops | bytes accessed | tf_op | source)
XLA Modules:
  0.0 297.5 jit_solution(6504305441735979245)
XLA Ops:
  7.2 1.4 copy.7
  8.9 3.0 %collective-permute-start = (bf16[128,16,128]{2,1,0:T(8,128)(2,1)S(1)}, bf16[128,16,128]{2,1,0:T(8,128)(2,1)S(1)}, u32[]{:S(2)}, u32[]{:S(2)}) collective-permute-start(bf16[128,16,128]{2,1,0:T(8,128)(2,1)S(1)} %reshape.83), channel_id=1, source_target_pairs={{0,2},{1,3},{2,0},{3,1},{4,6},{5,7},{6,4},{7,5},{8,10},{9,11},{10,... | collective-permute-start | bytes 1572872 | tf_op jit(solution)/shard_map/ppermute | solution.py:297
  11.9 3.6 %collective-permute-start.9 = (bf16[128,16,128]{2,1,0:T(8,128)(2,1)S(1)}, bf16[128,16,128]{2,1,0:T(8,128)(2,1)S(1)}, u32[]{:S(2)}, u32[]{:S(2)}) collective-permute-start(bf16[128,16,128]{2,1,0:T(8,128)(2,1)S(1)} %reshape.83), channel_id=1, source_target_pairs={{0,24},{8,16},{16,8},{24,0},{1,25},{9,17},{17,9},{25,1},{2,26},{10... | collective-permute-start | bytes 1572872 | tf_op jit(solution)/shard_map/ppermute | solution.py:297
  15.5 1.5 collective-permute-start.1
  17.0 6.8 %collective-permute-done = bf16[128,16,128]{2,1,0:T(8,128)(2,1)S(1)} collective-permute-done((bf16[128,16,128]{2,1,0:T(8,128)(2,1)S(1)}, bf16[128,16,128]{2,1,0:T(8,128)(2,1)S(1)}, u32[]{:S(2)}, u32[]{:S(2)}) %collective-permute-start) | collective-permute-done | bytes 524320 | tf_op jit(solution)/shard_map/ppermute | solution.py:297
  23.8 1.8 collective-permute-start.2
  26.5 2.1 collective-permute-done.9
  28.6 1.5 collective-permute-start.16
  30.6 7.8 %collective-permute-done.4 = bf16[128,16,128]{2,1,0:T(8,128)(2,1)S(1)} collective-permute-done((bf16[128,16,128]{2,1,0:T(8,128)(2,1)S(1)}, bf16[128,16,128]{2,1,0:T(8,128)(2,1)S(1)}, u32[]{:S(2)}, u32[]{:S(2)}) %collective-permute-start.4) | collective-permute-done | bytes 524320 | tf_op jit(solution)/shard_map/ppermute | solution.py:297
  38.5 1.7 collective-permute-start.10
  41.0 1.5 collective-permute-start.5
  46.4 12.5 %collective-permute-done.3 = bf16[64,16,128]{2,1,0:T(8,128)(2,1)S(1)} collective-permute-done((bf16[64,16,128]{2,1,0:T(8,128)(2,1)S(1)}, bf16[64,16,128]{2,1,0:T(8,128)(2,1)S(1)}, u32[]{:S(2)}, u32[]{:S(2)}) %collective-permute-start.3) | collective-permute-done | bytes 262176 | tf_op jit(solution)/shard_map/ppermute | solution.py:297
  58.8 1.5 collective-permute-start.6
  61.7 1.4 collective-permute-start.17
  63.9 1.5 collective-permute-start.11
  68.0 5.7 %collective-permute-done.6 = bf16[128,16,128]{2,1,0:T(8,128)(2,1)S(1)} collective-permute-done((bf16[128,16,128]{2,1,0:T(8,128)(2,1)S(1)}, bf16[128,16,128]{2,1,0:T(8,128)(2,1)S(1)}, u32[]{:S(2)}, u32[]{:S(2)}) %collective-permute-start.6) | collective-permute-done | bytes 524320 | tf_op jit(solution)/shard_map/ppermute | solution.py:297
  73.7 1.5 collective-permute-start.12
  76.1 3.2 %collective-permute-done.17 = bf16[64,16,128]{2,1,0:T(8,128)(2,1)S(1)} collective-permute-done((bf16[64,16,128]{2,1,0:T(8,128)(2,1)S(1)}, bf16[64,16,128]{2,1,0:T(8,128)(2,1)S(1)}, u32[]{:S(2)}, u32[]{:S(2)}) %collective-permute-start.17) | collective-permute-done | bytes 262176 | tf_op jit(solution)/shard_map/ppermute | solution.py:297
  79.3 1.3 collective-permute-start.8
  82.1 2.8 collective-permute-done.7
  85.7 1.6 collective-permute-start.13
  88.3 7.2 %collective-permute-done.12 = bf16[128,16,128]{2,1,0:T(8,128)(2,1)S(1)} collective-permute-done((bf16[128,16,128]{2,1,0:T(8,128)(2,1)S(1)}, bf16[128,16,128]{2,1,0:T(8,128)(2,1)S(1)}, u32[]{:S(2)}, u32[]{:S(2)}) %collective-permute-start.12) | collective-permute-done | bytes 524320 | tf_op jit(solution)/shard_map/ppermute | solution.py:297
  95.5 1.3 collective-permute-start.14
  96.9 1.4 collective-permute-done.13
  98.3 3.6 %collective-permute-done.14 = bf16[64,16,128]{2,1,0:T(8,128)(2,1)S(1)} collective-permute-done((bf16[64,16,128]{2,1,0:T(8,128)(2,1)S(1)}, bf16[64,16,128]{2,1,0:T(8,128)(2,1)S(1)}, u32[]{:S(2)}, u32[]{:S(2)}) %collective-permute-start.14) | collective-permute-done | bytes 262176 | tf_op jit(solution)/shard_map/ppermute | solution.py:297
  102.1 15.5 %scatter_custom_fusion = s32[4096]{0:T(1024)S(1)} fusion(s32[4096]{0:T(1024)S(1)} %compare_select_fusion.1, s32[4096]{0:T(1024)S(1)} %iota.35, s32[]{:T(128)} %constant.120.clone.1), kind=kCustom, calls=%fused_computation.66 | custom fusion | bytes 16388 | tf_op jit(solution)/shard_map/scatter | solution.py:336
  117.7 13.6 %gather_fusion = s32[2560]{0:T(1024)S(1)} fusion(s32[4096]{0:T(1024)S(1)} %scatter_custom_fusion, s32[3072]{0:T(1024)S(1)} %pad_clamp_fusion), kind=kCustom, calls=%fused_computation | custom fusion | bytes 30720 | tf_op jit(solution)/shard_map/gather | solution.py:338
  132.0 47.7 %shard_map.59 = (bf16[4,1024,512]{2,1,0:T(8,128)(2,1)}, bf16[4,1024,512]{2,1,0:T(8,128)(2,1)}, f32[1024,512]{1,0:T(8,128)}, f32[1024,128]{1,0:T(8,128)}, f32[256,512]{1,0:T(8,128)}) custom-call(s32[2560]{0:T(1024)} %fusion.6.slots_ref, bf16[512,512]{1,0:T(8,128)(2,1)} %x_ref.1, bf16[512,512]{1,0:T(8,128)(2,1)} %z_ref.1, ...), custom_call_target="tpu_custom_call" | custom-call | flops 28000000000 | bytes 31457280 | tf_op jit(solution)/shard_map/pallas_call | solution.py:126
  180.5 75.2 %shard_map.60 = (f32[1024,1024]{1,0:T(8,128)S(1)}, f32[1024,128]{1,0:T(8,128)S(1)}) custom-call(bf16[4,1024,512]{2,1,0:T(8,128)(2,1)} %get-tuple-element.9.yx_ref, bf16[4,1024,512]{2,1,0:T(8,128)(2,1)} %get-tuple-element.10.yz_ref), custom_call_target="tpu_custom_call" | custom-call | flops 40000000000 | bytes 12582912 | tf_op jit(solution)/shard_map/pallas_call | solution.py:232
  255.7 1.9 copy-done
  258.4 12.0 %all-gather.5.cloned.1.call-done = f32[8192,128]{1,0:T(8,128)} async-done(((f32[1024,128]{1,0:T(8,128)}), f32[8192,128]{1,0:T(8,128)}) %all-gather.5.cloned.1.call-update) | async-done | bytes 4194320 | tf_op jit(solution)/shard_map/all_gather | solution.py:345
  270.4 20.3 %shard_map.61 = (f32[1024,512]{1,0:T(8,128)}, f32[1024,128]{1,0:T(8,128)}) custom-call(s32[1]{0:T(128)} %bitcast.column_ref, f32[1024,1024]{1,0:T(8,128)} %copy-done, f32[1024,128]{1,0:T(8,128)} %copy-done.1, f32[8,1024,128]{2,1,0:T(8,128)} %bitcast.10, f32[4,256,512]{2,1,0:T(8,128)} %bitcast.11, f32[1024,512]{1,0:T(8,128)} %get-tuple-element.15.schur_ref), custom_call_target="tpu_custom_call" | custom-call | flops 12000000000 | bytes 25165824 | tf_op jit(solution)/shard_map/pallas_call | solution.py:281
  (71 shorter events, 17.7 us)
Async XLA Ops:
  7.2 251.3 %all-gather.7.cloned.1.call-start = ((), (), s32[]{:S(2)}) async-start(), calls=%async_computation.1 | async-start | bytes 2621440 | tf_op jit(solution)/shard_map/all_gather | solution.py:346
  8.9 14.9 %collective-permute-start = (bf16[128,16,128]{2,1,0:T(8,128)(2,1)S(1)}, bf16[128,16,128]{2,1,0:T(8,128)(2,1)S(1)}, u32[]{:S(2)}, u32[]{:S(2)}) collective-permute-start(bf16[128,16,128]{2,1,0:T(8,128)(2,1)S(1)} %reshape.83), channel_id=1, source_target_pairs={{0,2},{1,3},{2,0},{3,1},{4,6},{5,7},{6,4},{7,5},{8,10},{9,11},{10,... | collective-permute-start | bytes 1572872 | tf_op jit(solution)/shard_map/ppermute | solution.py:297
  11.9 16.7 %collective-permute-start.9 = (bf16[128,16,128]{2,1,0:T(8,128)(2,1)S(1)}, bf16[128,16,128]{2,1,0:T(8,128)(2,1)S(1)}, u32[]{:S(2)}, u32[]{:S(2)}) collective-permute-start(bf16[128,16,128]{2,1,0:T(8,128)(2,1)S(1)} %reshape.83), channel_id=1, source_target_pairs={{0,24},{8,16},{16,8},{24,0},{1,25},{9,17},{17,9},{25,1},{2,26},{10... | collective-permute-start | bytes 1572872 | tf_op jit(solution)/shard_map/ppermute | solution.py:297
  15.5 23.0 %collective-permute-start.4 = (bf16[128,16,128]{2,1,0:T(8,128)(2,1)S(1)}, bf16[128,16,128]{2,1,0:T(8,128)(2,1)S(1)}, u32[]{:S(2)}, u32[]{:S(2)}) collective-permute-start(bf16[128,16,128]{2,1,0:T(8,128)(2,1)S(1)} %reshape.83), channel_id=1, source_target_pairs={{0,8},{8,0},{16,24},{24,16},{1,9},{9,1},{17,25},{25,17},{2,10},{10... | collective-permute-start | bytes 1572872 | tf_op jit(solution)/shard_map/ppermute | solution.py:297
  15.5 25.5 %collective-permute-start.1 = (bf16[128,16,128]{2,1,0:T(8,128)(2,1)S(1)}, bf16[128,16,128]{2,1,0:T(8,128)(2,1)S(1)}, u32[]{:S(2)}, u32[]{:S(2)}) collective-permute-start(bf16[128,16,128]{2,1,0:T(8,128)(2,1)S(1)} %reshape.83), channel_id=1, source_target_pairs={{0,4},{1,5},{2,6},{3,7},{4,0},{5,1},{6,2},{7,3},{8,12},{9,13},{10,... | collective-permute-start | bytes 1572872 | tf_op jit(solution)/shard_map/ppermute | solution.py:297
  23.8 19.5 %collective-permute-start.2 = (bf16[64,16,128]{2,1,0:T(8,128)(2,1)S(1)}, bf16[64,16,128]{2,1,0:T(8,128)(2,1)S(1)}, u32[]{:S(2)}, u32[]{:S(2)}) collective-permute-start(bf16[64,16,128]{2,1,0:T(8,128)(2,1)S(1)} %slice.34), channel_id=1, source_target_pairs={{0,4},{1,5},{2,6},{3,7},{4,0},{5,1},{6,2},{7,3},{8,12},{9,13},{10,... | collective-permute-start | bytes 786440 | tf_op jit(solution)/shard_map/ppermute | solution.py:297
  28.6 32.5 %collective-permute-start.16 = (bf16[128,16,128]{2,1,0:T(8,128)(2,1)S(1)}, bf16[128,16,128]{2,1,0:T(8,128)(2,1)S(1)}, u32[]{:S(2)}, u32[]{:S(2)}) collective-permute-start(bf16[128,16,128]{2,1,0:T(8,128)(2,1)S(1)} %collective-permute-done.9), channel_id=1, source_target_pairs={{0,4},{1,5},{2,6},{3,7},{4,0},{5,1},{6,2},{7,3},{8,12},{9,13},{10,... | collective-permute-start | bytes 1572872 | tf_op jit(solution)/shard_map/ppermute | solution.py:297
  30.1 31.6 %collective-permute-start.15 = (bf16[128,16,128]{2,1,0:T(8,128)(2,1)S(1)}, bf16[128,16,128]{2,1,0:T(8,128)(2,1)S(1)}, u32[]{:S(2)}, u32[]{:S(2)}) collective-permute-start(bf16[128,16,128]{2,1,0:T(8,128)(2,1)S(1)} %collective-permute-done.9), channel_id=1, source_target_pairs={{0,2},{1,3},{2,0},{3,1},{4,6},{5,7},{6,4},{7,5},{8,10},{9,11},{10,... | collective-permute-start | bytes 1572872 | tf_op jit(solution)/shard_map/ppermute | solution.py:297
  38.5 25.5 %collective-permute-start.10 = (bf16[128,16,128]{2,1,0:T(8,128)(2,1)S(1)}, bf16[128,16,128]{2,1,0:T(8,128)(2,1)S(1)}, u32[]{:S(2)}, u32[]{:S(2)}) collective-permute-start(bf16[128,16,128]{2,1,0:T(8,128)(2,1)S(1)} %collective-permute-done.9), channel_id=1, source_target_pairs={{0,8},{8,0},{16,24},{24,16},{1,9},{9,1},{17,25},{25,17},{2,10},{10... | collective-permute-start | bytes 1572872 | tf_op jit(solution)/shard_map/ppermute | solution.py:297
  41.0 22.1 %collective-permute-start.5 = (bf16[128,16,128]{2,1,0:T(8,128)(2,1)S(1)}, bf16[128,16,128]{2,1,0:T(8,128)(2,1)S(1)}, u32[]{:S(2)}, u32[]{:S(2)}) collective-permute-start(bf16[128,16,128]{2,1,0:T(8,128)(2,1)S(1)} %collective-permute-done.4), channel_id=1, source_target_pairs={{0,2},{1,3},{2,0},{3,1},{4,6},{5,7},{6,4},{7,5},{8,10},{9,11},{10,... | collective-permute-start | bytes 1572872 | tf_op jit(solution)/shard_map/ppermute | solution.py:297
  43.4 15.5 %collective-permute-start.3 = (bf16[64,16,128]{2,1,0:T(8,128)(2,1)S(1)}, bf16[64,16,128]{2,1,0:T(8,128)(2,1)S(1)}, u32[]{:S(2)}, u32[]{:S(2)}) collective-permute-start(bf16[64,16,128]{2,1,0:T(8,128)(2,1)S(1)} %slice.35), channel_id=1, source_target_pairs={{0,2},{1,3},{2,0},{3,1},{4,6},{5,7},{6,4},{7,5},{8,10},{9,11},{10,... | collective-permute-start | bytes 786440 | tf_op jit(solution)/shard_map/ppermute | solution.py:297
  58.8 14.9 %collective-permute-start.6 = (bf16[128,16,128]{2,1,0:T(8,128)(2,1)S(1)}, bf16[128,16,128]{2,1,0:T(8,128)(2,1)S(1)}, u32[]{:S(2)}, u32[]{:S(2)}) collective-permute-start(bf16[128,16,128]{2,1,0:T(8,128)(2,1)S(1)} %collective-permute-done.4), channel_id=1, source_target_pairs={{0,4},{1,5},{2,6},{3,7},{4,0},{5,1},{6,2},{7,3},{8,12},{9,13},{10,... | collective-permute-start | bytes 1572872 | tf_op jit(solution)/shard_map/ppermute | solution.py:297
  61.1 20.3 %collective-permute-start.18 = (bf16[64,16,128]{2,1,0:T(8,128)(2,1)S(1)}, bf16[64,16,128]{2,1,0:T(8,128)(2,1)S(1)}, u32[]{:S(2)}, u32[]{:S(2)}) collective-permute-start(bf16[64,16,128]{2,1,0:T(8,128)(2,1)S(1)} %slice.41), channel_id=1, source_target_pairs={{0,2},{1,3},{2,0},{3,1},{4,6},{5,7},{6,4},{7,5},{8,10},{9,11},{10,... | collective-permute-start | bytes 786440 | tf_op jit(solution)/shard_map/ppermute | solution.py:297
  61.7 17.6 %collective-permute-start.17 = (bf16[64,16,128]{2,1,0:T(8,128)(2,1)S(1)}, bf16[64,16,128]{2,1,0:T(8,128)(2,1)S(1)}, u32[]{:S(2)}, u32[]{:S(2)}) collective-permute-start(bf16[64,16,128]{2,1,0:T(8,128)(2,1)S(1)} %slice.40), channel_id=1, source_target_pairs={{0,4},{1,5},{2,6},{3,7},{4,0},{5,1},{6,2},{7,3},{8,12},{9,13},{10,... | collective-permute-start | bytes 786440 | tf_op jit(solution)/shard_map/ppermute | solution.py:297
  63.1 21.8 %collective-permute-start.7 = (bf16[64,16,128]{2,1,0:T(8,128)(2,1)S(1)}, bf16[64,16,128]{2,1,0:T(8,128)(2,1)S(1)}, u32[]{:S(2)}, u32[]{:S(2)}) collective-permute-start(bf16[64,16,128]{2,1,0:T(8,128)(2,1)S(1)} %slice.36), channel_id=1, source_target_pairs={{0,4},{1,5},{2,6},{3,7},{4,0},{5,1},{6,2},{7,3},{8,12},{9,13},{10,... | collective-permute-start | bytes 786440 | tf_op jit(solution)/shard_map/ppermute | solution.py:297
  63.9 21.8 %collective-permute-start.11 = (bf16[128,16,128]{2,1,0:T(8,128)(2,1)S(1)}, bf16[128,16,128]{2,1,0:T(8,128)(2,1)S(1)}, u32[]{:S(2)}, u32[]{:S(2)}) collective-permute-start(bf16[128,16,128]{2,1,0:T(8,128)(2,1)S(1)} %collective-permute-done.10), channel_id=1, source_target_pairs={{0,2},{1,3},{2,0},{3,1},{4,6},{5,7},{6,4},{7,5},{8,10},{9,11},{10,... | collective-permute-start | bytes 1572872 | tf_op jit(solution)/shard_map/ppermute | solution.py:297
  73.7 21.7 %collective-permute-start.12 = (bf16[128,16,128]{2,1,0:T(8,128)(2,1)S(1)}, bf16[128,16,128]{2,1,0:T(8,128)(2,1)S(1)}, u32[]{:S(2)}, u32[]{:S(2)}) collective-permute-start(bf16[128,16,128]{2,1,0:T(8,128)(2,1)S(1)} %collective-permute-done.10), channel_id=1, source_target_pairs={{0,4},{1,5},{2,6},{3,7},{4,0},{5,1},{6,2},{7,3},{8,12},{9,13},{10,... | collective-permute-start | bytes 1572872 | tf_op jit(solution)/shard_map/ppermute | solution.py:297
  79.3 8.0 %collective-permute-start.8 = (bf16[64,16,128]{2,1,0:T(8,128)(2,1)S(1)}, bf16[64,16,128]{2,1,0:T(8,128)(2,1)S(1)}, u32[]{:S(2)}, u32[]{:S(2)}) collective-permute-start(bf16[64,16,128]{2,1,0:T(8,128)(2,1)S(1)} %slice.37), channel_id=1, source_target_pairs={{0,2},{1,3},{2,0},{3,1},{4,6},{5,7},{6,4},{7,5},{8,10},{9,11},{10,... | collective-permute-start | bytes 786440 | tf_op jit(solution)/shard_map/ppermute | solution.py:297
  81.4 50.6 %collective-permute-start.19 = (bf16[512,16,128]{2,1,0:T(8,128)(2,1)}, bf16[512,16,128]{2,1,0:T(8,128)(2,1)}, u32[]{:S(2)}, u32[]{:S(2)}) collective-permute-start(bf16[512,16,128]{2,1,0:T(8,128)(2,1)} %constant_dynamic-update-slice_fusion.refs_0_), channel_id=1, source_target_pairs={{0,1},{1,0},{2,3},{3,2},{4,5},{5,4},{6,7},{7,6},{8,9},{9,8},{10,11... | collective-permute-start | bytes 6291464 | tf_op jit(solution)/shard_map/ppermute | solution.py:297
  84.9 47.1 %collective-permute-start.22 = (bf16[512,16,128]{2,1,0:T(8,128)(2,1)}, bf16[512,16,128]{2,1,0:T(8,128)(2,1)}, u32[]{:S(2)}, u32[]{:S(2)}) collective-permute-start(bf16[512,16,128]{2,1,0:T(8,128)(2,1)} %constant_dynamic-update-slice_fusion.15.refs_3_), channel_id=1, source_target_pairs={{0,1},{1,0},{2,3},{3,2},{4,5},{5,4},{6,7},{7,6},{8,9},{9,8},{10,11... | collective-permute-start | bytes 6291464 | tf_op jit(solution)/shard_map/ppermute | solution.py:297
  85.7 16.3 %copy-start.3 = (s32[4096]{0:T(1024)S(1)}, s32[4096]{0:T(1024)}, u32[]{:S(2)}) copy-start(s32[4096]{0:T(1024)} %param.7) | copy-start | bytes 49156
  85.7 12.5 %collective-permute-start.13 = (bf16[64,16,128]{2,1,0:T(8,128)(2,1)S(1)}, bf16[64,16,128]{2,1,0:T(8,128)(2,1)S(1)}, u32[]{:S(2)}, u32[]{:S(2)}) collective-permute-start(bf16[64,16,128]{2,1,0:T(8,128)(2,1)S(1)} %slice.38), channel_id=1, source_target_pairs={{0,4},{1,5},{2,6},{3,7},{4,0},{5,1},{6,2},{7,3},{8,12},{9,13},{10,... | collective-permute-start | bytes 786440 | tf_op jit(solution)/shard_map/ppermute | solution.py:297
  88.0 44.0 %collective-permute-start.20 = (bf16[512,16,128]{2,1,0:T(8,128)(2,1)}, bf16[512,16,128]{2,1,0:T(8,128)(2,1)}, u32[]{:S(2)}, u32[]{:S(2)}) collective-permute-start(bf16[512,16,128]{2,1,0:T(8,128)(2,1)} %constant_dynamic-update-slice_fusion.5.refs_1_), channel_id=1, source_target_pairs={{0,1},{1,0},{2,3},{3,2},{4,5},{5,4},{6,7},{7,6},{8,9},{9,8},{10,11... | collective-permute-start | bytes 6291464 | tf_op jit(solution)/shard_map/ppermute | solution.py:297
  95.5 6.4 %collective-permute-start.14 = (bf16[64,16,128]{2,1,0:T(8,128)(2,1)S(1)}, bf16[64,16,128]{2,1,0:T(8,128)(2,1)S(1)}, u32[]{:S(2)}, u32[]{:S(2)}) collective-permute-start(bf16[64,16,128]{2,1,0:T(8,128)(2,1)S(1)} %slice.39), channel_id=1, source_target_pairs={{0,2},{1,3},{2,0},{3,1},{4,6},{5,7},{6,4},{7,5},{8,10},{9,11},{10,... | collective-permute-start | bytes 786440 | tf_op jit(solution)/shard_map/ppermute | solution.py:297
  101.9 29.4 %copy-start.2 = (bf16[512,16,128]{2,1,0:T(8,128)(2,1)}, bf16[512,16,128]{2,1,0:T(8,128)(2,1)S(1)}, u32[]{:S(2)}) copy-start(bf16[512,16,128]{2,1,0:T(8,128)(2,1)S(1)} %constant_dynamic-update-slice_fusion.10.refs_2_) | copy-start | bytes 6291460
  102.0 30.1 %collective-permute-start.21 = (bf16[512,16,128]{2,1,0:T(8,128)(2,1)S(1)}, bf16[512,16,128]{2,1,0:T(8,128)(2,1)}, u32[]{:S(2)}, u32[]{:S(2)}) collective-permute-start(bf16[512,16,128]{2,1,0:T(8,128)(2,1)S(1)} %constant_dynamic-update-slice_fusion.10.refs_2_), channel_id=1, source_target_pairs={{0,1},{1,0},{2,3},{3,2},{4,5},{5,4},{6,7},{7,6},{8,9},{9,8},{10,11... | collective-permute-start | bytes 6291464 | tf_op jit(solution)/shard_map/ppermute | solution.py:297
  179.7 90.7 %all-gather.5.cloned.1.call-start = ((), (), s32[]{:S(2)}) async-start(), calls=%async_computation | async-start | bytes 4718592 | tf_op jit(solution)/shard_map/all_gather | solution.py:345
  255.6 2.0 copy-start
  257.6 0.8 copy-start.1
Sparse Core Ops, SparseCore 0:
  179.8 52.5 all-gather.6
  234.9 35.4 all-gather.4

commit v4 on v3

--- a/solution.py
+++ b/solution.py
@@ -39,14 +39,16 @@
     source_refs, refs = refs[:sources], refs[sources:]
     lead_x_ref, lead_z_ref, schur_ref, front_ref, top_ref, every_ref, picked_ref, yx_ref, yz_ref, sem_ref = refs
     step = pl.program_id(0)
-    share = every_ref.shape[0] // sources
     tile, parts, lanes = picked_ref.shape
     width = x_ref.shape[0]
     per_rank = width // lanes
 
     @pl.when(step == 0)
     def _():
-        copies = [pltpu.make_async_copy(ref, every_ref.at[pl.ds(n * share, share)], sem_ref.at[n]) for n, ref in enumerate(source_refs)]
+        copies, first = [], 0
+        for n, ref in enumerate(source_refs):
+            copies.append(pltpu.make_async_copy(ref, every_ref.at[pl.ds(first, ref.shape[0])], sem_ref.at[n]))
+            first += ref.shape[0]
         for copy in copies:
             copy.start()
         for copy in copies:
@@ -111,7 +113,8 @@
 
 
 def assemble(slots, sources, x_factor, z_factor, rows, cols, lead_rows, lead_cols):
-    share, parts, lanes = sources[0].shape
+    _, parts, lanes = sources[0].shape
+    slots_held = sum(source.shape[0] for source in sources)
     width = x_factor.shape[0]
     tile = 256
     high, wide = min(512, rows), min(256, cols)
@@ -135,14 +138,14 @@
                    pl.BlockSpec((high, wide), lambda s: (after(s) // col_tiles, after(s) % col_tiles)),
                    pl.BlockSpec((high, lead_cols), lambda s: (after(s) // col_tiles, 0)),
                    pl.BlockSpec((lead_rows, wide), lambda s: (0, jnp.minimum(after(s), col_tiles - 1)))),
-        scratch_shapes=[pltpu.VMEM((len(sources) * share, parts, lanes), bf16), pltpu.VMEM((tile, parts, lanes), bf16)]
+        scratch_shapes=[pltpu.VMEM((slots_held, parts, lanes), bf16), pltpu.VMEM((tile, parts, lanes), bf16)]
         + [pltpu.VMEM((RANK, rows + cols, width), bf16)] * 2 + [pltpu.SemaphoreType.DMA((len(sources),))],
         compiler_params=pltpu.CompilerParams(vmem_limit_bytes=58 * MIB),
         cost_estimate=pl.CostEstimate(flops=28 * 10**9, bytes_accessed=30 * MIB, transcendentals=0),
     )(slots, x_factor, z_factor, *sources)
 
 
-def factor_block(block, u_ref, v_ref):
+def factor_block(block, u_ref, v_ref, beside):
     count = BLK // SUB
     sub_iota = lax.broadcasted_iota(jnp.int32, (SUB, BLK), 0)
     lane_iota = lax.broadcasted_iota(jnp.int32, (SUB, BLK), 1)
@@ -156,6 +159,7 @@
         return jnp.broadcast_to(x[row:row + 1, :], (SUB, BLK))
 
     for m in range(count):
+        beside(m)
         head_a, head_v = rows_a[m], rows_v[m]
         cols = [spread_lane(head_a, SUB * m + k) for k in range(SUB)]
         below = [[spread_lane(rows_a[i], SUB * m + k) for k in range(SUB)] for i in range(m + 1, count)]
@@ -185,26 +189,37 @@
         v_ref[SUB * m:SUB * (m + 1), :] = v
 
 
-def factor_kernel(yx_ref, yz_ref, l_ref, d_ref, w_ref, u_ref, v_ref):
+def factor_kernel(yx_ref, yz_ref, l_ref, d_ref, w_ref, g_ref, u_ref, v_ref):
     order = l_ref.shape[0]
     steps = order // BLK
-    tile = 256
+    tile = 2 * BLK
+    window = 3 * BLK
     l_ref[...] = jnp.zeros_like(l_ref)
     w_ref[...] = jnp.zeros_like(w_ref)
 
-    def columns(j, carry):
-        right = pl.ds(pl.multiple_of(j * tile, tile), tile)
-
-        def rows(i, carry):
-            left = pl.ds(pl.multiple_of(i * tile, tile), tile)
-            w_ref[left, right] = gram_tile(yx_ref, yz_ref, left, right)
-            return carry
-        return lax.fori_loop(j, order // tile, rows, carry)
-    lax.fori_loop(0, order // tile, columns, 0)
+    def rows_of(i, carry):
+        left = pl.ds(pl.multiple_of(i * 2 * tile, 2 * tile), 2 * tile)
+        w_ref[left, :tile] = gram_tile(yx_ref, yz_ref, left, pl.ds(0, tile))
+        return carry
+    lax.fori_loop(0, order // (2 * tile), rows_of, 0)
 
     def step(b, carry):
         at = pl.ds(pl.multiple_of(b * BLK, BLK), BLK)
-        factor_block(w_ref[at, at], u_ref, v_ref)
+        ahead = jnp.minimum(b // 2 + 1, order // tile - 1)
+        left = pl.ds(pl.multiple_of(jnp.minimum(ahead * tile + (b % 2) * window, order - window), BLK), window)
+        right = pl.ds(pl.multiple_of(ahead * tile, tile), tile)
+
+        def beside(m):
+            q, r = m // RANK, m % RANK
+            term = dot_bf16(yx_ref[r, left, :], yx_ref[q, right, :], NT) * dot_bf16(yz_ref[r, left, :], yz_ref[q, right, :], NT)
+            if m == 0:
+                g_ref[left, :] = term
+            elif rank_signs[q] * rank_signs[r] > 0:
+                g_ref[left, :] = g_ref[left, :] + term
+            else:
+                g_ref[left, :] = g_ref[left, :] - term
+
+        factor_block(w_ref[at, at], u_ref, v_ref, beside)
         l_ref[at, at] = u_ref[...].T
         d_ref[at, :] = v_ref[...]
         for k in range(steps - 1):
@@ -224,6 +239,8 @@
                     w_ref[rows, first:] = w_ref[rows, first:] - dot3(left, right, NT)
                     return c
                 lax.fori_loop(0, steps - 1 - k, update, 0)
+                if k % 2 == 1:
+                    w_ref[first:, first:first + tile] = w_ref[first:, first:first + tile] + g_ref[first:, :]
         return carry
     lax.fori_loop(0, steps, step, 0)
 
@@ -234,16 +251,16 @@
         out_shape=(jax.ShapeDtypeStruct((K, K), jnp.float32), jax.ShapeDtypeStruct((K, BLK), jnp.float32)),
         in_specs=[VMEM] * 2,
         out_specs=(VMEM, VMEM),
-        scratch_shapes=[pltpu.VMEM((K, K), jnp.float32), pltpu.VMEM((BLK, BLK), jnp.float32), pltpu.VMEM((BLK, BLK), jnp.float32)],
+        scratch_shapes=[pltpu.VMEM((K, K), jnp.float32), pltpu.VMEM((K, 2 * BLK), jnp.float32), pltpu.VMEM((BLK, BLK), jnp.float32), pltpu.VMEM((BLK, BLK), jnp.float32)],
         compiler_params=pltpu.CompilerParams(vmem_limit_bytes=48 * MIB),
         cost_estimate=pl.CostEstimate(flops=40 * 10**9, bytes_accessed=12 * MIB, transcendentals=0),
     )(yx, yz)
 
 
-def solve_kernel(column_ref, l_ref, d_ref, pieces_ref, tops_ref, schur_ref, rest_ref, panel_ref, lh, ll, xh, xl, zh, zl):
+def solve_kernel(place_ref, l_ref, d_ref, pieces_ref, tops_ref, schur_ref, rest_ref, panel_ref, lh, ll, xh, xl, zh, zl):
     pcol = pieces_ref.shape[0]
     prow = tops_ref.shape[0]
-    column = column_ref[0]
+    row, column = place_ref[0], place_ref[1]
     lh[...], ll[...] = split(l_ref[...])
     wide = 2 * BLK
     for b in range(K // wide):
@@ -257,7 +274,7 @@
             jnp.concatenate([corner, d_ref[lower, :]], axis=1)], axis=0))
         blocks = range(wide // NB * b, wide // NB * (b + 1))
         value = jnp.concatenate([pieces_ref[n % pcol, :, n // pcol * NB:(n // pcol + 1) * NB] for n in blocks], axis=1)
-        top = jnp.concatenate([tops_ref[n % prow, n // prow * NB:(n // prow + 1) * NB, :] for n in blocks], axis=0)
+        top = jnp.concatenate([tops_ref[(n % prow) ^ row, n // prow * NB:(n // prow + 1) * NB, :] for n in blocks], axis=0)
         if b > 0:
             done = slice(0, b * wide)
             left = (lh[at, done], ll[at, done])
@@ -274,7 +291,7 @@
     rest_ref[...] = schur_ref[...] - dot3((xh[...], xl[...]), (zh[...], zl[...]), NN)
 
 
-def solve(column, low, inverses, pieces, tops, schur):
+def solve(place, low, inverses, pieces, tops, schur):
     rows, cols = schur.shape
     lead = K // pieces.shape[0]
     bf16 = jnp.bfloat16
@@ -286,7 +303,7 @@
         scratch_shapes=[pltpu.VMEM((K, K), bf16)] * 2 + [pltpu.VMEM((rows, K), bf16)] * 2 + [pltpu.VMEM((K, cols), bf16)] * 2,
         compiler_params=pltpu.CompilerParams(vmem_limit_bytes=56 * MIB),
         cost_estimate=pl.CostEstimate(flops=12 * 10**9, bytes_accessed=24 * MIB, transcendentals=0),
-    )(column, low, inverses, pieces, tops, schur)
+    )(place, low, inverses, pieces, tops, schur)
 
 
 def gather_factors(mine, prow_count, pcol_count):
@@ -301,19 +318,46 @@
         items[turn] = swap("prow", prow_count, turn, mine)
     for turn in range(2, prow_count, 2):
         items[turn] = swap("prow", prow_count, 1, items[turn + 1])
-    near, far = {}, {}
-    for turn in [0] + list(range(1, prow_count, 2)) + list(range(2, prow_count, 2)):
-        held = {0: items[turn]}
+    near, far, near_order, far_order = [], [], [], []
+    groups = [[0], [1], [m ^ 1 for m in range(2, prow_count)]]
+    for n, group in enumerate(groups):
+        value = jnp.concatenate([items[m] for m in group]) if len(group) > 1 else items[group[0]]
+        middle = len(group) * half
+        held = {0: value}
         for j in range(1, pcol_count // 2):
             low = j & -j
             high = 1 << (j.bit_length() - 1)
             if low == high:
-                held[j] = swap("pcol", pcol_count, 2 * j, items[turn])
+                held[j] = swap("pcol", pcol_count, 2 * j, value)
             else:
-                held[j] = jnp.concatenate([swap("pcol", pcol_count, 2 * high, held[j ^ high][:half]), swap("pcol", pcol_count, 2 * low, held[j ^ low][half:])])
-        near[turn] = jnp.concatenate([held[j] for j in range(pcol_count // 2)])
-        far[turn] = swap("pcol", pcol_count, 1, near[turn])
-    return [near[m] for m in range(prow_count)] + [far[m] for m in range(prow_count)]
+                held[j] = jnp.concatenate([swap("pcol", pcol_count, 2 * high, held[j ^ high][:middle]), swap("pcol", pcol_count, 2 * low, held[j ^ low][middle:])])
+        direct = [j for j in held if j & (j - 1) == 0]
+        relayed = [j for j in held if j & (j - 1) != 0]
+        for part in [direct, relayed] if n == len(groups) - 1 else [direct + relayed]:
+            whole = jnp.concatenate([held[j] for j in part]) if len(part) > 1 else held[part[0]]
+            near.append(whole)
+            near_order += [(m, 2 * j) for j in part for m in group]
+            far.append(swap("pcol", pcol_count, 1, whole))
+            far_order += [(m, 2 * j + 1) for j in part for m in group]
+    return near + far, near_order + far_order
+
+
+def places_of(placement, order, prow_id, pcol_id, pcol_count):
+    total = placement.shape[0]
+    own = total // len(order)
+    unit_of = [0] * len(order)
+    for unit, (row_turn, col_turn) in enumerate(order):
+        unit_of[row_turn * pcol_count + col_turn] = unit
+    holder = jnp.arange(len(order))
+    turn = ((holder // pcol_count) ^ prow_id) * pcol_count + ((holder % pcol_count) ^ pcol_id)
+    units = jnp.sum(jnp.where(turn[:, None] == jnp.arange(len(order))[None, :], jnp.array(unit_of)[None, :], 0), axis=1)
+    place = (units[:, None] * own + jnp.arange(own)[None, :]).reshape(1, total)
+    blocks = total // NB
+    in_block = jnp.arange(blocks)[:, None] == placement[None, :] // NB
+    digits = jnp.concatenate([jnp.where(in_block, place // NB, 0), jnp.where(in_block, place % NB, 0)]).astype(jnp.bfloat16)
+    at_row = (jnp.arange(NB)[:, None] == placement[None, :] % NB).astype(jnp.bfloat16)
+    found = dot_bf16(digits, at_row, NT).astype(jnp.int32)
+    return found[:blocks] * NB + found[blocks:]
 
 
 def per_device(factors, x_factor, zinv_factor, placement):
@@ -328,24 +372,19 @@
     count = prow_count * pcol_count
     lanes = BLK
     mine = factors.transpose(1, 0, 2).reshape(own, RANK * width // lanes, lanes)
-    sources = gather_factors(mine, prow_count, pcol_count)
-    slot_k = jnp.arange(local_rows)
-    natural_k = slot_k // NB * NB * prow_count + prow_id * NB + slot_k % NB
-    slot_j = jnp.arange(local_cols)
-    natural_j = slot_j // NB * NB * pcol_count + pcol_id * NB + slot_j % NB
-    inverse = jnp.zeros((total_rows,), jnp.int32).at[placement].set(jnp.arange(total_rows, dtype=jnp.int32))
-    wanted = jnp.concatenate([jnp.arange(K), natural_k, natural_j]).astype(jnp.int32)
-    slots = inverse[wanted]
-    holder = slots // own
-    row_turn, col_turn = (holder // pcol_count) ^ prow_id, (holder % pcol_count) ^ pcol_id
-    places = (((col_turn % 2) * prow_count + row_turn) * (pcol_count // 2) + col_turn // 2) * own + slots % own
+    sources, order = gather_factors(mine, prow_count, pcol_count)
+    found = places_of(placement, order, prow_id, pcol_id, pcol_count)
+    by_row = lax.dynamic_index_in_dim(found.reshape(local_rows // NB, prow_count, NB), prow_id, 1, keepdims=False)
+    by_col = lax.dynamic_index_in_dim(found.reshape(local_cols // NB, pcol_count, NB), pcol_id, 1, keepdims=False)
+    places = jnp.concatenate([found[:K // NB], by_row, by_col]).reshape(-1)
     lead_rows, lead_cols = K // prow_count, K // pcol_count
     lead_x, lead_z, schur_local, front, top = assemble(
         places.astype(jnp.int32), sources, x_factor, zinv_factor, local_rows, local_cols, lead_rows, lead_cols)
     pieces = lax.all_gather(front, "pcol", axis=0, tiled=False)
-    tops = lax.all_gather(top, "prow", axis=0, tiled=False)
+    turned = [lax.ppermute(top, "prow", [(n, n ^ turn) for n in range(prow_count)]) for turn in range(1, prow_count)]
+    tops = jnp.stack([top] + turned)
     low, inverses = factor(lead_x, lead_z)
-    return solve(pcol_id.astype(jnp.int32).reshape(1), low, inverses, pieces, tops, schur_local)
+    return solve(jnp.stack([prow_id, pcol_id]).astype(jnp.int32), low, inverses, pieces, tops, schur_local)
 
 
 def solution(mesh):

time: 298 us -> 277 us (0.930)
  local copies, waits for them, and re-layouts: 45.9 us -> 21.3 us
  Pallas kernels: 143 us -> 132 us
  starting transfers between devices: 27.8 us -> 36 us
  waiting for transfers between devices: 65.7 us -> 70 us
    ppermute x23 -> x19, waiting for transfers between devices: 53.2 us -> 69.9 us  [swap(): return lax.ppermute(value, axis, [(n, n ^ turn) for n in range(count)])]
    scatter x1 -> x0, local copies, waits for them, and re-layouts: 15.5 us -> none  [per_device(): jnp.zeros((total_rows,), jnp.int32).at[placement]]
    gather x1 -> x0, local copies, waits for them, and re-layouts: 13.6 us -> none  [per_device(): slots = inverse[wanted]]
    all_gather x1, waiting for transfers between devices: 12 us -> 0.01 us  [per_device(): pieces = lax.all_gather(front, 'pcol', axis=0, tiled=False)]
    pallas_call x1, Pallas kernels: 75.2 us -> 63.9 us  [factor(): pl.pallas_call(factor_kernel, out_shape=(jax.ShapeDtypeStruct((K, K), jnp...]
    ppermute x0 -> x3, starting transfers between devices: none -> 4.39 us  [per_device(): lax.ppermute(top, 'prow', [(n, n ^ turn) for n in range(prow_count)])]
    ppermute x23 -> x19, starting transfers between devices: 27.6 us -> 31.6 us  [swap(): return lax.ppermute(value, axis, [(n, n ^ turn) for n in range(count)])]
    unnamed x24 -> x23, local copies, waits for them, and re-layouts: 12.7 us -> 13.7 us
  transfers between devices with their start and end apart: 25 -> 23, of which waited for: 11 -> 8; matrix products, arithmetic and copies ran while one was open for 14% -> 7% of each run, Pallas kernels for 25% -> 23%
where the time goes in v4:
time: 277 us
  Pallas kernels  132 us (48%)
  waiting for transfers between devices  70 us (25%)
  starting transfers between devices  36 us (13%)
  local copies, waits for them, and re-layouts  21.3 us (8%)
  between operations  14.2 us (5%)
  other arithmetic  2.81 us (1%)
    ppermute x19, waiting for transfers between devices, swap(): return lax.ppermute(value, axis, [(n, n ^ turn) for n in range(count)])  69.9 us
    pallas_call x1, Pallas kernels, factor(): pl.pallas_call(factor_kernel, out_shape=(jax.ShapeDtypeStruct((K, K), jnp...  63.9 us
    pallas_call x1, Pallas kernels, assemble(): pl.pallas_call(body, grid=(pick_tiles + row_tiles * col_tiles,), out_shap...  47.7 us
    ppermute x19, starting transfers between devices, swap(): return lax.ppermute(value, axis, [(n, n ^ turn) for n in range(count)])  31.6 us
    pallas_call x1, Pallas kernels, solve(): pl.pallas_call(solve_kernel, out_shape=(jax.ShapeDtypeStruct((rows, cols)...  20.3 us
    unnamed x23, local copies, waits for them, and re-layouts  13.7 us
  transfers between devices with their start and end apart: 23, of which 8 were waited for; matrix products, arithmetic and copies ran while one was open for 7% of the time, Pallas kernels for 23%

profile of v4, /device:TPU:0, one launch (start us, length us, event | category | flops | bytes accessed | tf_op | source)
XLA Modules:
  0.0 276.7 jit_solution(16022796597326371090)
XLA Ops:
  7.2 1.4 copy.19
  8.9 5.1 %collective-permute-start.9 = (bf16[128,16,128]{2,1,0:T(8,128)(2,1)S(1)}, bf16[128,16,128]{2,1,0:T(8,128)(2,1)S(1)}, u32[]{:S(2)}, u32[]{:S(2)}) collective-permute-start(bf16[128,16,128]{2,1,0:T(8,128)(2,1)S(1)} %reshape.177), channel_id=1, source_target_pairs={{0,24},{8,16},{16,8},{24,0},{1,25},{9,17},{17,9},{25,1},{2,26},{10... | collective-permute-start | bytes 1572872 | tf_op jit(solution)/shard_map/ppermute | solution.py:314
  14.0 12.0 %collective-permute-done.9 = bf16[128,16,128]{2,1,0:T(8,128)(2,1)S(1)} collective-permute-done((bf16[128,16,128]{2,1,0:T(8,128)(2,1)S(1)}, bf16[128,16,128]{2,1,0:T(8,128)(2,1)S(1)}, u32[]{:S(2)}, u32[]{:S(2)}) %collective-permute-start.9) | collective-permute-done | bytes 524320 | tf_op jit(solution)/shard_map/ppermute | solution.py:314
  26.0 10.8 %collective-permute-start.10 = (bf16[128,16,128]{2,1,0:T(8,128)(2,1)S(1)}, bf16[128,16,128]{2,1,0:T(8,128)(2,1)S(1)}, u32[]{:S(2)}, u32[]{:S(2)}) collective-permute-start(bf16[128,16,128]{2,1,0:T(8,128)(2,1)S(1)} %collective-permute-done.9), channel_id=1, source_target_pairs={{0,8},{8,0},{16,24},{24,16},{1,9},{9,1},{17,25},{25,17},{2,10},{10... | collective-permute-start | bytes 1572872 | tf_op jit(solution)/shard_map/ppermute | solution.py:314
  36.9 1.1 constant_dynamic-update-slice_fusion.11
  38.0 10.1 %collective-permute-done.10 = bf16[128,16,128]{2,1,0:T(8,128)(2,1)S(1)} collective-permute-done((bf16[128,16,128]{2,1,0:T(8,128)(2,1)S(1)}, bf16[128,16,128]{2,1,0:T(8,128)(2,1)S(1)}, u32[]{:S(2)}, u32[]{:S(2)}) %collective-permute-start.10) | collective-permute-done | bytes 524320 | tf_op jit(solution)/shard_map/ppermute | solution.py:314
  48.1 1.1 constant_dynamic-update-slice_fusion.10
  49.2 1.5 collective-permute-start.11
  50.7 1.5 collective-permute-start.12
  52.2 1.7 collective-permute-start.4
  56.0 29.4 %collective-permute-done.1 = bf16[128,16,128]{2,1,0:T(8,128)(2,1)S(1)} collective-permute-done((bf16[128,16,128]{2,1,0:T(8,128)(2,1)S(1)}, bf16[128,16,128]{2,1,0:T(8,128)(2,1)S(1)}, u32[]{:S(2)}, u32[]{:S(2)}) %collective-permute-start.1) | collective-permute-done | bytes 524320 | tf_op jit(solution)/shard_map/ppermute | solution.py:314
  86.1 1.0 slice.39
  87.0 1.6 collective-permute-start.2
  89.1 1.9 constant_dynamic-update-slice_fusion.9
  91.1 1.5 collective-permute-start.5
  92.6 1.2 constant_dynamic-update-slice_fusion.13
  93.8 1.2 constant_dynamic-update-slice_fusion.12.refs_2_
  94.9 1.9 constant_dynamic-update-slice_fusion.3
  98.3 4.8 %collective-permute-done.5 = bf16[128,16,128]{2,1,0:T(8,128)(2,1)S(1)} collective-permute-done((bf16[128,16,128]{2,1,0:T(8,128)(2,1)}, bf16[128,16,128]{2,1,0:T(8,128)(2,1)S(1)}, u32[]{:S(2)}, u32[]{:S(2)}) %collective-permute-start.5) | collective-permute-done | bytes 524320 | tf_op jit(solution)/shard_map/ppermute | solution.py:314
  103.2 1.6 collective-permute-start.7
  105.5 2.3 collective-permute-start.8
  108.7 1.6 collective-permute-start.13
  112.0 2.9 %collective-permute-done.8 = bf16[64,16,128]{2,1,0:T(8,128)(2,1)S(1)} collective-permute-done((bf16[64,16,128]{2,1,0:T(8,128)(2,1)S(1)}, bf16[64,16,128]{2,1,0:T(8,128)(2,1)S(1)}, u32[]{:S(2)}, u32[]{:S(2)}) %collective-permute-start.8) | collective-permute-done | bytes 262176 | tf_op jit(solution)/shard_map/ppermute | solution.py:314
  115.7 5.4 %collective-permute-done.13 = bf16[128,16,128]{2,1,0:T(8,128)(2,1)S(1)} collective-permute-done((bf16[128,16,128]{2,1,0:T(8,128)(2,1)S(1)}, bf16[128,16,128]{2,1,0:T(8,128)(2,1)S(1)}, u32[]{:S(2)}, u32[]{:S(2)}) %collective-permute-start.13) | collective-permute-done | bytes 524320 | tf_op jit(solution)/shard_map/ppermute | solution.py:314
  121.2 4.4 %collective-permute-done.14 = bf16[128,16,128]{2,1,0:T(8,128)(2,1)S(1)} collective-permute-done((bf16[128,16,128]{2,1,0:T(8,128)(2,1)S(1)}, bf16[128,16,128]{2,1,0:T(8,128)(2,1)S(1)}, u32[]{:S(2)}, u32[]{:S(2)}) %collective-permute-start.14) | collective-permute-done | bytes 524320 | tf_op jit(solution)/shard_map/ppermute | solution.py:314
  128.5 47.7 %shard_map.68 = (bf16[4,1024,512]{2,1,0:T(8,128)(2,1)}, bf16[4,1024,512]{2,1,0:T(8,128)(2,1)}, f32[1024,512]{1,0:T(8,128)}, f32[1024,128]{1,0:T(8,128)}, f32[256,512]{1,0:T(8,128)}) custom-call(s32[2560]{0:T(1024)} %reshape.176.slots_ref, bf16[512,512]{1,0:T(8,128)(2,1)} %x_ref.1, bf16[512,512]{1,0:T(8,128)(2,1)} %z_ref.1, ...), custom_call_target="tpu_custom_call" | custom-call | flops 28000000000 | bytes 31457280 | tf_op jit(solution)/shard_map/pallas_call | solution.py:129
  176.9 2.1 collective-permute-start.21
  179.8 1.4 collective-permute-start.19
  181.3 63.9 %shard_map.69 = (f32[1024,1024]{1,0:T(8,128)S(1)}, f32[1024,128]{1,0:T(8,128)S(1)}) custom-call(bf16[4,1024,512]{2,1,0:T(8,128)(2,1)} %get-tuple-element.9.yx_ref, bf16[4,1024,512]{2,1,0:T(8,128)(2,1)} %get-tuple-element.10.yz_ref), custom_call_target="tpu_custom_call" | custom-call | flops 40000000000 | bytes 12582912 | tf_op jit(solution)/shard_map/pallas_call | solution.py:249
  245.1 1.9 copy-done
  247.9 1.5 pad_maximum_fusion.tops_ref
  249.5 20.3 %shard_map.70 = (f32[1024,512]{1,0:T(8,128)}, f32[1024,128]{1,0:T(8,128)}) custom-call(s32[2]{0:T(128)} %pad_add_fusion.1.place_ref, f32[1024,1024]{1,0:T(8,128)} %copy-done, f32[1024,128]{1,0:T(8,128)} %copy-done.1, f32[8,1024,128]{2,1,0:T(8,128)} %bitcast.59, f32[4,256,512]{2,1,0:T(8,128)} %pad_maximum_fusion.tops_ref, f32[1024,512]{1,0:T(8,128)} %get-tuple-element.15.schur_ref), custom_call_target="tpu_custom_call" | custom-call | flops 12000000000 | bytes 25165824 | tf_op jit(solution)/shard_map/pallas_call | solution.py:298
  (71 shorter events, 14.4 us)
Async XLA Ops:
  7.2 242.3 %all-gather.3.cloned.1.call-start = ((), (), s32[]{:S(2)}) async-start(), calls=%async_computation | async-start | bytes 4718592 | tf_op jit(solution)/shard_map/all_gather | solution.py:383
  8.7 46.4 %copy-start.5 = (s32[32]{0:T(128)S(1)}, s32[32]{0:T(128)}, u32[]{:S(2)}) copy-start(s32[32]{0:T(128)} %constant.92.clone) | copy-start | bytes 388
  8.9 17.1 %collective-permute-start.9 = (bf16[128,16,128]{2,1,0:T(8,128)(2,1)S(1)}, bf16[128,16,128]{2,1,0:T(8,128)(2,1)S(1)}, u32[]{:S(2)}, u32[]{:S(2)}) collective-permute-start(bf16[128,16,128]{2,1,0:T(8,128)(2,1)S(1)} %reshape.177), channel_id=1, source_target_pairs={{0,24},{8,16},{16,8},{24,0},{1,25},{9,17},{17,9},{25,1},{2,26},{10... | collective-permute-start | bytes 1572872 | tf_op jit(solution)/shard_map/ppermute | solution.py:314
  26.0 22.1 %collective-permute-start.10 = (bf16[128,16,128]{2,1,0:T(8,128)(2,1)S(1)}, bf16[128,16,128]{2,1,0:T(8,128)(2,1)S(1)}, u32[]{:S(2)}, u32[]{:S(2)}) collective-permute-start(bf16[128,16,128]{2,1,0:T(8,128)(2,1)S(1)} %collective-permute-done.9), channel_id=1, source_target_pairs={{0,8},{8,0},{16,24},{24,16},{1,9},{9,1},{17,25},{25,17},{2,10},{10... | collective-permute-start | bytes 1572872 | tf_op jit(solution)/shard_map/ppermute | solution.py:314
  49.2 41.9 %collective-permute-start.11 = (bf16[256,16,128]{2,1,0:T(8,128)(2,1)}, bf16[256,16,128]{2,1,0:T(8,128)(2,1)S(1)}, u32[]{:S(2)}, u32[]{:S(2)}) collective-permute-start(bf16[256,16,128]{2,1,0:T(8,128)(2,1)} %get-tuple-element.16), channel_id=1, source_target_pairs={{0,2},{1,3},{2,0},{3,1},{4,6},{5,7},{6,4},{7,5},{8,10},{9,11},{10,... | collective-permute-start | bytes 3145736 | tf_op jit(solution)/shard_map/ppermute | solution.py:314
  50.7 43.0 %collective-permute-start.12 = (bf16[256,16,128]{2,1,0:T(8,128)(2,1)}, bf16[256,16,128]{2,1,0:T(8,128)(2,1)S(1)}, u32[]{:S(2)}, u32[]{:S(2)}) collective-permute-start(bf16[256,16,128]{2,1,0:T(8,128)(2,1)} %get-tuple-element.16), channel_id=1, source_target_pairs={{0,4},{1,5},{2,6},{3,7},{4,0},{5,1},{6,2},{7,3},{8,12},{9,13},{10,... | collective-permute-start | bytes 3145736 | tf_op jit(solution)/shard_map/ppermute | solution.py:314
  52.2 36.4 %collective-permute-start.4 = (bf16[128,16,128]{2,1,0:T(8,128)(2,1)S(1)}, bf16[128,16,128]{2,1,0:T(8,128)(2,1)}, u32[]{:S(2)}, u32[]{:S(2)}) collective-permute-start(bf16[128,16,128]{2,1,0:T(8,128)(2,1)S(1)} %reshape.177), channel_id=1, source_target_pairs={{0,8},{8,0},{16,24},{24,16},{1,9},{9,1},{17,25},{25,17},{2,10},{10... | collective-permute-start | bytes 1572872 | tf_op jit(solution)/shard_map/ppermute | solution.py:314
  54.0 31.5 %collective-permute-start.1 = (bf16[128,16,128]{2,1,0:T(8,128)(2,1)S(1)}, bf16[128,16,128]{2,1,0:T(8,128)(2,1)S(1)}, u32[]{:S(2)}, u32[]{:S(2)}) collective-permute-start(bf16[128,16,128]{2,1,0:T(8,128)(2,1)S(1)} %reshape.177), channel_id=1, source_target_pairs={{0,4},{1,5},{2,6},{3,7},{4,0},{5,1},{6,2},{7,3},{8,12},{9,13},{10,... | collective-permute-start | bytes 1572872 | tf_op jit(solution)/shard_map/ppermute | solution.py:314
  54.5 31.6 %collective-permute-start = (bf16[128,16,128]{2,1,0:T(8,128)(2,1)S(1)}, bf16[128,16,128]{2,1,0:T(8,128)(2,1)}, u32[]{:S(2)}, u32[]{:S(2)}) collective-permute-start(bf16[128,16,128]{2,1,0:T(8,128)(2,1)S(1)} %reshape.177), channel_id=1, source_target_pairs={{0,2},{1,3},{2,0},{3,1},{4,6},{5,7},{6,4},{7,5},{8,10},{9,11},{10,... | collective-permute-start | bytes 1572872 | tf_op jit(solution)/shard_map/ppermute | solution.py:314
  85.5 19.3 %collective-permute-start.3 = (bf16[64,16,128]{2,1,0:T(8,128)(2,1)S(1)}, bf16[64,16,128]{2,1,0:T(8,128)(2,1)S(1)}, u32[]{:S(2)}, u32[]{:S(2)}) collective-permute-start(bf16[64,16,128]{2,1,0:T(8,128)(2,1)S(1)} %slice.40), channel_id=1, source_target_pairs={{0,2},{1,3},{2,0},{3,1},{4,6},{5,7},{6,4},{7,5},{8,10},{9,11},{10,... | collective-permute-start | bytes 786440 | tf_op jit(solution)/shard_map/ppermute | solution.py:314
  87.0 10.6 %collective-permute-start.2 = (bf16[64,16,128]{2,1,0:T(8,128)(2,1)S(1)}, bf16[64,16,128]{2,1,0:T(8,128)(2,1)S(1)}, u32[]{:S(2)}, u32[]{:S(2)}) collective-permute-start(bf16[64,16,128]{2,1,0:T(8,128)(2,1)S(1)} %slice.39), channel_id=1, source_target_pairs={{0,4},{1,5},{2,6},{3,7},{4,0},{5,1},{6,2},{7,3},{8,12},{9,13},{10,... | collective-permute-start | bytes 786440 | tf_op jit(solution)/shard_map/ppermute | solution.py:314
  88.6 16.8 %collective-permute-start.6 = (bf16[128,16,128]{2,1,0:T(8,128)(2,1)}, bf16[128,16,128]{2,1,0:T(8,128)(2,1)S(1)}, u32[]{:S(2)}, u32[]{:S(2)}) collective-permute-start(bf16[128,16,128]{2,1,0:T(8,128)(2,1)} %collective-permute-done.4), channel_id=1, source_target_pairs={{0,4},{1,5},{2,6},{3,7},{4,0},{5,1},{6,2},{7,3},{8,12},{9,13},{10,... | collective-permute-start | bytes 1572872 | tf_op jit(solution)/shard_map/ppermute | solution.py:314
  91.1 12.1 %collective-permute-start.5 = (bf16[128,16,128]{2,1,0:T(8,128)(2,1)}, bf16[128,16,128]{2,1,0:T(8,128)(2,1)S(1)}, u32[]{:S(2)}, u32[]{:S(2)}) collective-permute-start(bf16[128,16,128]{2,1,0:T(8,128)(2,1)} %collective-permute-done.4), channel_id=1, source_target_pairs={{0,2},{1,3},{2,0},{3,1},{4,6},{5,7},{6,4},{7,5},{8,10},{9,11},{10,... | collective-permute-start | bytes 1572872 | tf_op jit(solution)/shard_map/ppermute | solution.py:314
  94.9 33.6 %collective-permute-start.17 = (bf16[768,16,128]{2,1,0:T(8,128)(2,1)}, bf16[768,16,128]{2,1,0:T(8,128)(2,1)}, u32[]{:S(2)}, u32[]{:S(2)}) collective-permute-start(bf16[768,16,128]{2,1,0:T(8,128)(2,1)} %constant_dynamic-update-slice_fusion.12.refs_2_), channel_id=1, source_target_pairs={{0,1},{1,0},{2,3},{3,2},{4,5},{5,4},{6,7},{7,6},{8,9},{9,8},{10,11... | collective-permute-start | bytes 9437192 | tf_op jit(solution)/shard_map/ppermute | solution.py:314
  103.2 8.0 %collective-permute-start.7 = (bf16[64,16,128]{2,1,0:T(8,128)(2,1)S(1)}, bf16[64,16,128]{2,1,0:T(8,128)(2,1)S(1)}, u32[]{:S(2)}, u32[]{:S(2)}) collective-permute-start(bf16[64,16,128]{2,1,0:T(8,128)(2,1)S(1)} %slice.41), channel_id=1, source_target_pairs={{0,4},{1,5},{2,6},{3,7},{4,0},{5,1},{6,2},{7,3},{8,12},{9,13},{10,... | collective-permute-start | bytes 786440 | tf_op jit(solution)/shard_map/ppermute | solution.py:314
  105.5 22.1 %collective-permute-start.15 = (bf16[512,16,128]{2,1,0:T(8,128)(2,1)}, bf16[512,16,128]{2,1,0:T(8,128)(2,1)}, u32[]{:S(2)}, u32[]{:S(2)}) collective-permute-start(bf16[512,16,128]{2,1,0:T(8,128)(2,1)} %constant_dynamic-update-slice_fusion.refs_0_), channel_id=1, source_target_pairs={{0,1},{1,0},{2,3},{3,2},{4,5},{5,4},{6,7},{7,6},{8,9},{9,8},{10,11... | collective-permute-start | bytes 6291464 | tf_op jit(solution)/shard_map/ppermute | solution.py:314
  105.5 9.4 %collective-permute-start.8 = (bf16[64,16,128]{2,1,0:T(8,128)(2,1)S(1)}, bf16[64,16,128]{2,1,0:T(8,128)(2,1)S(1)}, u32[]{:S(2)}, u32[]{:S(2)}) collective-permute-start(bf16[64,16,128]{2,1,0:T(8,128)(2,1)S(1)} %slice.42), channel_id=1, source_target_pairs={{0,2},{1,3},{2,0},{3,1},{4,6},{5,7},{6,4},{7,5},{8,10},{9,11},{10,... | collective-permute-start | bytes 786440 | tf_op jit(solution)/shard_map/ppermute | solution.py:314
  108.7 7.0 %copy-start.4 = (s32[4096]{0:T(1024)S(1)}, s32[4096]{0:T(1024)}, u32[]{:S(2)}) copy-start(s32[4096]{0:T(1024)} %param.8) | copy-start | bytes 49156
  108.7 12.4 %collective-permute-start.13 = (bf16[128,16,128]{2,1,0:T(8,128)(2,1)S(1)}, bf16[128,16,128]{2,1,0:T(8,128)(2,1)S(1)}, u32[]{:S(2)}, u32[]{:S(2)}) collective-permute-start(bf16[128,16,128]{2,1,0:T(8,128)(2,1)S(1)} %slice.43), channel_id=1, source_target_pairs={{0,4},{1,5},{2,6},{3,7},{4,0},{5,1},{6,2},{7,3},{8,12},{9,13},{10,... | collective-permute-start | bytes 1572872 | tf_op jit(solution)/shard_map/ppermute | solution.py:314
  111.2 14.3 %collective-permute-start.14 = (bf16[128,16,128]{2,1,0:T(8,128)(2,1)S(1)}, bf16[128,16,128]{2,1,0:T(8,128)(2,1)S(1)}, u32[]{:S(2)}, u32[]{:S(2)}) collective-permute-start(bf16[128,16,128]{2,1,0:T(8,128)(2,1)S(1)} %slice.44), channel_id=1, source_target_pairs={{0,2},{1,3},{2,0},{3,1},{4,6},{5,7},{6,4},{7,5},{8,10},{9,11},{10,... | collective-permute-start | bytes 1572872 | tf_op jit(solution)/shard_map/ppermute | solution.py:314
  115.6 11.9 %collective-permute-start.16 = (bf16[512,16,128]{2,1,0:T(8,128)(2,1)}, bf16[512,16,128]{2,1,0:T(8,128)(2,1)}, u32[]{:S(2)}, u32[]{:S(2)}) collective-permute-start(bf16[512,16,128]{2,1,0:T(8,128)(2,1)} %constant_dynamic-update-slice_fusion.5.refs_1_), channel_id=1, source_target_pairs={{0,1},{1,0},{2,3},{3,2},{4,5},{5,4},{6,7},{7,6},{8,9},{9,8},{10,11... | collective-permute-start | bytes 6291464 | tf_op jit(solution)/shard_map/ppermute | solution.py:314
  125.6 2.9 %copy-start.3 = (bf16[256,16,128]{2,1,0:T(8,128)(2,1)}, bf16[256,16,128]{2,1,0:T(8,128)(2,1)S(1)}, u32[]{:S(2)}) copy-start(bf16[256,16,128]{2,1,0:T(8,128)(2,1)S(1)} %constant_dynamic-update-slice_fusion.16.refs_3_) | copy-start | bytes 3145732
  125.6 2.9 %collective-permute-start.18 = (bf16[256,16,128]{2,1,0:T(8,128)(2,1)S(1)}, bf16[256,16,128]{2,1,0:T(8,128)(2,1)}, u32[]{:S(2)}, u32[]{:S(2)}) collective-permute-start(bf16[256,16,128]{2,1,0:T(8,128)(2,1)S(1)} %constant_dynamic-update-slice_fusion.16.refs_3_), channel_id=1, source_target_pairs={{0,1},{1,0},{2,3},{3,2},{4,5},{5,4},{6,7},{7,6},{8,9},{9,8},{10,11... | collective-permute-start | bytes 3145736 | tf_op jit(solution)/shard_map/ppermute | solution.py:314
  176.9 71.0 %collective-permute-start.21 = (f32[256,512]{1,0:T(8,128)}, f32[256,512]{1,0:T(8,128)S(1)}, u32[]{:S(2)}, u32[]{:S(2)}) collective-permute-start(f32[256,512]{1,0:T(8,128)} %get-tuple-element.14), channel_id=1, source_target_pairs={{0,24},{8,16},{16,8},{24,0},{1,25},{9,17},{17,9},{25,1},{2,26},{10... | collective-permute-start | bytes 1572872 | tf_op jit(solution)/shard_map/ppermute | solution.py:384
  179.0 68.9 %collective-permute-start.20 = (f32[256,512]{1,0:T(8,128)}, f32[256,512]{1,0:T(8,128)S(1)}, u32[]{:S(2)}, u32[]{:S(2)}) collective-permute-start(f32[256,512]{1,0:T(8,128)} %get-tuple-element.14), channel_id=1, source_target_pairs={{0,16},{8,24},{16,0},{24,8},{1,17},{9,25},{17,1},{25,9},{2,18},{10... | collective-permute-start | bytes 1572872 | tf_op jit(solution)/shard_map/ppermute | solution.py:384
  179.8 68.1 %collective-permute-start.19 = (f32[256,512]{1,0:T(8,128)}, f32[256,512]{1,0:T(8,128)S(1)}, u32[]{:S(2)}, u32[]{:S(2)}) collective-permute-start(f32[256,512]{1,0:T(8,128)} %get-tuple-element.14), channel_id=1, source_target_pairs={{0,8},{8,0},{16,24},{24,16},{1,9},{9,1},{17,25},{25,17},{2,10},{10... | collective-permute-start | bytes 1572872 | tf_op jit(solution)/shard_map/ppermute | solution.py:384
  181.3 66.7 %copy-start.2 = (f32[256,512]{1,0:T(8,128)S(1)}, f32[256,512]{1,0:T(8,128)}, u32[]{:S(2)}) copy-start(f32[256,512]{1,0:T(8,128)} %get-tuple-element.14) | copy-start | bytes 1572868
  245.1 2.0 copy-start
  247.1 0.8 copy-start.1
Sparse Core Ops, SparseCore 0:
  176.3 34.6 all-gather.2

commit v5 on v4

--- a/solution.py
+++ b/solution.py
@@ -63,21 +63,19 @@
             return carry
         lax.fori_loop(0, tile // 16, pick, 0)
         by_part = jnp.swapaxes(picked_ref[...], 0, 1)
-        images = []
-        for r in range(RANK):
-            mine = jnp.concatenate([by_part[r * per_rank + k] for k in range(per_rank)], axis=1)
-            images.append((dot_bf16(mine, x_ref[...], NN).astype(jnp.bfloat16), dot_bf16(mine, z_ref[...], NN).astype(jnp.bfloat16)))
+        mine = jnp.concatenate([
+            jnp.concatenate([by_part[r * per_rank + k] for k in range(per_rank)], axis=1) for r in range(RANK)], axis=0)
+        images_x = dot_bf16(mine, x_ref[...], NN).astype(jnp.bfloat16).reshape(RANK, tile, width)
+        images_z = dot_bf16(mine, z_ref[...], NN).astype(jnp.bfloat16).reshape(RANK, tile, width)
 
         @pl.when(step < lead_tiles)
         def _():
-            for r in range(RANK):
-                lead_x_ref[r], lead_z_ref[r] = images[r]
+            lead_x_ref[...], lead_z_ref[...] = images_x, images_z
 
         @pl.when(step >= lead_tiles)
         def _():
             at = pl.ds(pl.multiple_of((step - lead_tiles) * tile, tile), tile)
-            for r in range(RANK):
-                yx_ref[r, at, :], yz_ref[r, at, :] = images[r]
+            yx_ref[:, at, :], yz_ref[:, at, :] = images_x, images_z
 
     @pl.when(step >= pick_tiles)
     def _():
@@ -98,17 +96,21 @@
 
 
 def gram_tile(yx_ref, yz_ref, left, right):
+    left_x, left_z = yx_ref[:, left, :], yz_ref[:, left, :]
+    _, high, width = left_x.shape
+    left_x, left_z = left_x.reshape(RANK * high, width), left_z.reshape(RANK * high, width)
     total = None
     for q in range(RANK):
+        gx = dot_bf16(left_x, yx_ref[q, right, :], NT)
+        gz = dot_bf16(left_z, yz_ref[q, right, :], NT)
         for r in range(RANK):
-            gx = dot_bf16(yx_ref[r, left, :], yx_ref[q, right, :], NT)
-            gz = dot_bf16(yz_ref[r, left, :], yz_ref[q, right, :], NT)
+            term = gx[r * high:(r + 1) * high] * gz[r * high:(r + 1) * high]
             if total is None:
-                total = gx * gz
+                total = term
             elif rank_signs[q] * rank_signs[r] > 0:
-                total = total + gx * gz
+                total = total + term
             else:
-                total = total - gx * gz
+                total = total - term
     return total
 
 
@@ -301,7 +303,7 @@
         in_specs=[SMEM] + [VMEM] * 5,
         out_specs=(VMEM, VMEM),
         scratch_shapes=[pltpu.VMEM((K, K), bf16)] * 2 + [pltpu.VMEM((rows, K), bf16)] * 2 + [pltpu.VMEM((K, cols), bf16)] * 2,
-        compiler_params=pltpu.CompilerParams(vmem_limit_bytes=56 * MIB),
+        compiler_params=pltpu.CompilerParams(vmem_limit_bytes=40 * MIB),
         cost_estimate=pl.CostEstimate(flops=12 * 10**9, bytes_accessed=24 * MIB, transcendentals=0),
     )(place, low, inverses, pieces, tops, schur)
 
@@ -319,7 +321,7 @@
     for turn in range(2, prow_count, 2):
         items[turn] = swap("prow", prow_count, 1, items[turn + 1])
     near, far, near_order, far_order = [], [], [], []
-    groups = [[0], [1], [m ^ 1 for m in range(2, prow_count)]]
+    groups = [[0]] + [[m] for m in range(1, prow_count, 2)] + [[m] for m in range(2, prow_count, 2)]
     for n, group in enumerate(groups):
         value = jnp.concatenate([items[m] for m in group]) if len(group) > 1 else items[group[0]]
         middle = len(group) * half

time: 277 us -> 251 us (0.906)
  waiting for transfers between devices: 70 us -> 44.7 us
  Pallas kernels: 132 us -> 127 us
  local copies, waits for them, and re-layouts: 21.3 us -> 26 us
    ppermute x19 -> x24, waiting for transfers between devices: 69.9 us -> 44.6 us  [swap(): return lax.ppermute(value, axis, [(n, n ^ turn) for n in range(count)])]
    unnamed x23 -> x33, local copies, waits for them, and re-layouts: 13.7 us -> 20.1 us
    pallas_call x1, Pallas kernels: 20.3 us -> 16.2 us  [solve(): pl.pallas_call(solve_kernel, out_shape=(jax.ShapeDtypeStruct((rows, cols)...]
    ppermute x19 -> x24, starting transfers between devices: 31.6 us -> 32.7 us  [swap(): return lax.ppermute(value, axis, [(n, n ^ turn) for n in range(count)])]
  transfers between devices with their start and end apart: 23 -> 28, of which waited for: 8 -> 9; matrix products, arithmetic and copies ran while one was open for 7% -> 7% of each run, Pallas kernels for 23% -> 25%
where the time goes in v5:
time: 251 us
  Pallas kernels  127 us (51%)
  waiting for transfers between devices  44.7 us (18%)
  starting transfers between devices  37.1 us (15%)
  local copies, waits for them, and re-layouts  26 us (10%)
  between operations  14.3 us (6%)
    pallas_call x1, Pallas kernels, factor(): pl.pallas_call(factor_kernel, out_shape=(jax.ShapeDtypeStruct((K, K), jnp...  63.7 us
    pallas_call x1, Pallas kernels, assemble(): pl.pallas_call(body, grid=(pick_tiles + row_tiles * col_tiles,), out_shap...  47.4 us
    ppermute x24, waiting for transfers between devices, swap(): return lax.ppermute(value, axis, [(n, n ^ turn) for n in range(count)])  44.6 us
    ppermute x24, starting transfers between devices, swap(): return lax.ppermute(value, axis, [(n, n ^ turn) for n in range(count)])  32.7 us
    unnamed x33, local copies, waits for them, and re-layouts  20.1 us
    pallas_call x1, Pallas kernels, solve(): pl.pallas_call(solve_kernel, out_shape=(jax.ShapeDtypeStruct((rows, cols)...  16.2 us
  transfers between devices with their start and end apart: 28, of which 9 were waited for; matrix products, arithmetic and copies ran while one was open for 7% of the time, Pallas kernels for 25%

profile of v5, /device:TPU:0, one launch (start us, length us, event | category | flops | bytes accessed | tf_op | source)
XLA Modules:
  0.0 250.7 jit_solution(13775917339515943060)
XLA Ops:
  7.2 1.4 copy.19
  8.9 3.0 %collective-permute-start.1 = (bf16[128,16,128]{2,1,0:T(8,128)(2,1)S(1)}, bf16[128,16,128]{2,1,0:T(8,128)(2,1)S(1)}, u32[]{:S(2)}, u32[]{:S(2)}) collective-permute-start(bf16[128,16,128]{2,1,0:T(8,128)(2,1)S(1)} %reshape.177), channel_id=1, source_target_pairs={{0,4},{1,5},{2,6},{3,7},{4,0},{5,1},{6,2},{7,3},{8,12},{9,13},{10,... | collective-permute-start | bytes 1572872 | tf_op jit(solution)/shard_map/ppermute | solution.py:316
  11.9 1.5 collective-permute-start
  13.4 3.6 %collective-permute-start.9 = (bf16[128,16,128]{2,1,0:T(8,128)(2,1)S(1)}, bf16[128,16,128]{2,1,0:T(8,128)(2,1)S(1)}, u32[]{:S(2)}, u32[]{:S(2)}) collective-permute-start(bf16[128,16,128]{2,1,0:T(8,128)(2,1)S(1)} %reshape.177), channel_id=1, source_target_pairs={{0,24},{8,16},{16,8},{24,0},{1,25},{9,17},{17,9},{25,1},{2,26},{10... | collective-permute-start | bytes 1572872 | tf_op jit(solution)/shard_map/ppermute | solution.py:316
  17.2 6.6 %collective-permute-done.1 = bf16[128,16,128]{2,1,0:T(8,128)(2,1)S(1)} collective-permute-done((bf16[128,16,128]{2,1,0:T(8,128)(2,1)S(1)}, bf16[128,16,128]{2,1,0:T(8,128)(2,1)S(1)}, u32[]{:S(2)}, u32[]{:S(2)}) %collective-permute-start.1) | collective-permute-done | bytes 524320 | tf_op jit(solution)/shard_map/ppermute | solution.py:316
  23.9 1.8 collective-permute-start.3
  25.7 1.6 collective-permute-start.2
  28.2 1.9 collective-permute-done.9
  30.1 9.2 %collective-permute-start.14 = (bf16[128,16,128]{2,1,0:T(8,128)(2,1)S(1)}, bf16[128,16,128]{2,1,0:T(8,128)(2,1)S(1)}, u32[]{:S(2)}, u32[]{:S(2)}) collective-permute-start(bf16[128,16,128]{2,1,0:T(8,128)(2,1)S(1)} %collective-permute-done.9), channel_id=1, source_target_pairs={{0,8},{8,0},{16,24},{24,16},{1,9},{9,1},{17,25},{25,17},{2,10},{10... | collective-permute-start | bytes 1572872 | tf_op jit(solution)/shard_map/ppermute | solution.py:316
  40.4 0.8 constant_dynamic-update-slice_fusion.9
  41.2 1.5 collective-permute-start.6
  42.7 1.5 collective-permute-start.5
  48.2 6.0 %collective-permute-done.11 = bf16[128,16,128]{2,1,0:T(8,128)(2,1)S(1)} collective-permute-done((bf16[128,16,128]{2,1,0:T(8,128)(2,1)S(1)}, bf16[128,16,128]{2,1,0:T(8,128)(2,1)S(1)}, u32[]{:S(2)}, u32[]{:S(2)}) %collective-permute-start.11) | collective-permute-done | bytes 524320 | tf_op jit(solution)/shard_map/ppermute | solution.py:316
  54.8 1.5 collective-permute-start.12
  56.3 9.1 %collective-permute-done.6 = bf16[128,16,128]{2,1,0:T(8,128)(2,1)S(1)} collective-permute-done((bf16[128,16,128]{2,1,0:T(8,128)(2,1)S(1)}, bf16[128,16,128]{2,1,0:T(8,128)(2,1)S(1)}, u32[]{:S(2)}, u32[]{:S(2)}) %collective-permute-start.6) | collective-permute-done | bytes 524320 | tf_op jit(solution)/shard_map/ppermute | solution.py:316
  66.1 1.5 collective-permute-start.7
  68.1 0.8 constant_dynamic-update-slice_fusion.17
  70.6 0.8 constant_dynamic-update-slice_fusion.13
  72.3 1.5 collective-permute-start.16
  75.3 1.4 collective-permute-done.7
  78.6 8.6 %collective-permute-done.15 = bf16[128,16,128]{2,1,0:T(8,128)(2,1)S(1)} collective-permute-done((bf16[128,16,128]{2,1,0:T(8,128)(2,1)S(1)}, bf16[128,16,128]{2,1,0:T(8,128)(2,1)S(1)}, u32[]{:S(2)}, u32[]{:S(2)}) %collective-permute-start.15) | collective-permute-done | bytes 524320 | tf_op jit(solution)/shard_map/ppermute | solution.py:316
  87.9 0.9 constant_dynamic-update-slice_fusion.16
  89.8 4.8 %collective-permute-done.17 = bf16[64,16,128]{2,1,0:T(8,128)(2,1)S(1)} collective-permute-done((bf16[64,16,128]{2,1,0:T(8,128)(2,1)S(1)}, bf16[64,16,128]{2,1,0:T(8,128)(2,1)S(1)}, u32[]{:S(2)}, u32[]{:S(2)}) %collective-permute-start.17) | collective-permute-done | bytes 262176 | tf_op jit(solution)/shard_map/ppermute | solution.py:316
  95.6 5.3 %collective-permute-done.18 = bf16[64,16,128]{2,1,0:T(8,128)(2,1)S(1)} collective-permute-done((bf16[64,16,128]{2,1,0:T(8,128)(2,1)S(1)}, bf16[64,16,128]{2,1,0:T(8,128)(2,1)S(1)}, u32[]{:S(2)}, u32[]{:S(2)}) %collective-permute-start.18) | collective-permute-done | bytes 262176 | tf_op jit(solution)/shard_map/ppermute | solution.py:316
  103.8 47.4 %shard_map.68 = (bf16[4,1024,512]{2,1,0:T(8,128)(2,1)}, bf16[4,1024,512]{2,1,0:T(8,128)(2,1)}, f32[1024,512]{1,0:T(8,128)}, f32[1024,128]{1,0:T(8,128)}, f32[256,512]{1,0:T(8,128)}) custom-call(s32[2560]{0:T(1024)} %reshape.176.slots_ref, bf16[512,512]{1,0:T(8,128)(2,1)} %x_ref.1, bf16[512,512]{1,0:T(8,128)(2,1)} %z_ref.1, ...), custom_call_target="tpu_custom_call" | custom-call | flops 28000000000 | bytes 31457280 | tf_op jit(solution)/shard_map/pallas_call | solution.py:131
  152.0 3.7 %collective-permute-start.24 = (f32[256,512]{1,0:T(8,128)}, f32[256,512]{1,0:T(8,128)S(1)}, u32[]{:S(2)}, u32[]{:S(2)}) collective-permute-start(f32[256,512]{1,0:T(8,128)} %get-tuple-element.14), channel_id=1, source_target_pairs={{0,8},{8,0},{16,24},{24,16},{1,9},{9,1},{17,25},{25,17},{2,10},{10... | collective-permute-start | bytes 1572872 | tf_op jit(solution)/shard_map/ppermute | solution.py:386
  155.7 63.7 %shard_map.69 = (f32[1024,1024]{1,0:T(8,128)S(1)}, f32[1024,128]{1,0:T(8,128)S(1)}) custom-call(bf16[4,1024,512]{2,1,0:T(8,128)(2,1)} %get-tuple-element.9.yx_ref, bf16[4,1024,512]{2,1,0:T(8,128)(2,1)} %get-tuple-element.10.yz_ref), custom_call_target="tpu_custom_call" | custom-call | flops 40000000000 | bytes 12582912 | tf_op jit(solution)/shard_map/pallas_call | solution.py:251
  219.5 2.0 copy-done.1
  221.7 2.2 copy-done
  223.9 2.2 copy-done.2
  226.1 1.6 copy-done.3
  227.7 16.2 %shard_map.70 = (f32[1024,512]{1,0:T(8,128)}, f32[1024,128]{1,0:T(8,128)}) custom-call(s32[2]{0:T(128)S(1)} %pad_add_fusion.1.place_ref, f32[1024,1024]{1,0:T(8,128)S(1)} %copy-done.2, f32[1024,128]{1,0:T(8,128)S(1)} %get-tuple-element.12.d_ref, f32[8,1024,128]{2,1,0:T(8,128)S(1)} %bitcast.49, f32[4,256,512]{2,1,0:T(8,128)S(1)} %pad_maximum_fusion.tops_ref, ...), custom_call_target="tpu_custom_call" | custom-call | flops 12000000000 | bytes 25165824 | tf_op jit(solution)/shard_map/pallas_call | solution.py:300
  (93 shorter events, 20.6 us)
Async XLA Ops:
  7.2 9.9 %copy-start.8 = (s32[32]{0:T(128)S(1)}, s32[32]{0:T(128)}, u32[]{:S(2)}) copy-start(s32[32]{0:T(128)} %constant.92.clone) | copy-start | bytes 388
  7.2 20.1 %copy-start.6 = (s32[4096]{0:T(1024)S(1)}, s32[4096]{0:T(1024)}, u32[]{:S(2)}) copy-start(s32[4096]{0:T(1024)} %param.8) | copy-start | bytes 49156
  7.2 214.5 %all-gather.3.cloned.1.call-start = ((), (), s32[]{:S(2)}) async-start(), calls=%async_computation | async-start | bytes 4718592 | tf_op jit(solution)/shard_map/all_gather | solution.py:385
  8.9 15.0 %collective-permute-start.1 = (bf16[128,16,128]{2,1,0:T(8,128)(2,1)S(1)}, bf16[128,16,128]{2,1,0:T(8,128)(2,1)S(1)}, u32[]{:S(2)}, u32[]{:S(2)}) collective-permute-start(bf16[128,16,128]{2,1,0:T(8,128)(2,1)S(1)} %reshape.177), channel_id=1, source_target_pairs={{0,4},{1,5},{2,6},{3,7},{4,0},{5,1},{6,2},{7,3},{8,12},{9,13},{10,... | collective-permute-start | bytes 1572872 | tf_op jit(solution)/shard_map/ppermute | solution.py:316
  11.9 13.7 %collective-permute-start = (bf16[128,16,128]{2,1,0:T(8,128)(2,1)S(1)}, bf16[128,16,128]{2,1,0:T(8,128)(2,1)S(1)}, u32[]{:S(2)}, u32[]{:S(2)}) collective-permute-start(bf16[128,16,128]{2,1,0:T(8,128)(2,1)S(1)} %reshape.177), channel_id=1, source_target_pairs={{0,2},{1,3},{2,0},{3,1},{4,6},{5,7},{6,4},{7,5},{8,10},{9,11},{10,... | collective-permute-start | bytes 1572872 | tf_op jit(solution)/shard_map/ppermute | solution.py:316
  13.4 16.7 %collective-permute-start.9 = (bf16[128,16,128]{2,1,0:T(8,128)(2,1)S(1)}, bf16[128,16,128]{2,1,0:T(8,128)(2,1)S(1)}, u32[]{:S(2)}, u32[]{:S(2)}) collective-permute-start(bf16[128,16,128]{2,1,0:T(8,128)(2,1)S(1)} %reshape.177), channel_id=1, source_target_pairs={{0,24},{8,16},{16,8},{24,0},{1,25},{9,17},{17,9},{25,1},{2,26},{10... | collective-permute-start | bytes 1572872 | tf_op jit(solution)/shard_map/ppermute | solution.py:316
  17.0 22.8 %collective-permute-start.4 = (bf16[128,16,128]{2,1,0:T(8,128)(2,1)S(1)}, bf16[128,16,128]{2,1,0:T(8,128)(2,1)S(1)}, u32[]{:S(2)}, u32[]{:S(2)}) collective-permute-start(bf16[128,16,128]{2,1,0:T(8,128)(2,1)S(1)} %reshape.177), channel_id=1, source_target_pairs={{0,8},{8,0},{16,24},{24,16},{1,9},{9,1},{17,25},{25,17},{2,10},{10... | collective-permute-start | bytes 1572872 | tf_op jit(solution)/shard_map/ppermute | solution.py:316
  23.9 17.4 %collective-permute-start.3 = (bf16[64,16,128]{2,1,0:T(8,128)(2,1)S(1)}, bf16[64,16,128]{2,1,0:T(8,128)(2,1)S(1)}, u32[]{:S(2)}, u32[]{:S(2)}) collective-permute-start(bf16[64,16,128]{2,1,0:T(8,128)(2,1)S(1)} %slice.48), channel_id=1, source_target_pairs={{0,2},{1,3},{2,0},{3,1},{4,6},{5,7},{6,4},{7,5},{8,10},{9,11},{10,... | collective-permute-start | bytes 786440 | tf_op jit(solution)/shard_map/ppermute | solution.py:316
  25.7 17.1 %collective-permute-start.2 = (bf16[64,16,128]{2,1,0:T(8,128)(2,1)S(1)}, bf16[64,16,128]{2,1,0:T(8,128)(2,1)S(1)}, u32[]{:S(2)}, u32[]{:S(2)}) collective-permute-start(bf16[64,16,128]{2,1,0:T(8,128)(2,1)S(1)} %slice.47), channel_id=1, source_target_pairs={{0,4},{1,5},{2,6},{3,7},{4,0},{5,1},{6,2},{7,3},{8,12},{9,13},{10,... | collective-permute-start | bytes 786440 | tf_op jit(solution)/shard_map/ppermute | solution.py:316
  30.1 37.4 %collective-permute-start.14 = (bf16[128,16,128]{2,1,0:T(8,128)(2,1)S(1)}, bf16[128,16,128]{2,1,0:T(8,128)(2,1)S(1)}, u32[]{:S(2)}, u32[]{:S(2)}) collective-permute-start(bf16[128,16,128]{2,1,0:T(8,128)(2,1)S(1)} %collective-permute-done.9), channel_id=1, source_target_pairs={{0,8},{8,0},{16,24},{24,16},{1,9},{9,1},{17,25},{25,17},{2,10},{10... | collective-permute-start | bytes 1572872 | tf_op jit(solution)/shard_map/ppermute | solution.py:316
  39.3 14.9 %collective-permute-start.11 = (bf16[128,16,128]{2,1,0:T(8,128)(2,1)S(1)}, bf16[128,16,128]{2,1,0:T(8,128)(2,1)S(1)}, u32[]{:S(2)}, u32[]{:S(2)}) collective-permute-start(bf16[128,16,128]{2,1,0:T(8,128)(2,1)S(1)} %collective-permute-done.9), channel_id=1, source_target_pairs={{0,4},{1,5},{2,6},{3,7},{4,0},{5,1},{6,2},{7,3},{8,12},{9,13},{10,... | collective-permute-start | bytes 1572872 | tf_op jit(solution)/shard_map/ppermute | solution.py:316
  39.8 15.0 %collective-permute-start.10 = (bf16[128,16,128]{2,1,0:T(8,128)(2,1)S(1)}, bf16[128,16,128]{2,1,0:T(8,128)(2,1)S(1)}, u32[]{:S(2)}, u32[]{:S(2)}) collective-permute-start(bf16[128,16,128]{2,1,0:T(8,128)(2,1)S(1)} %collective-permute-done.9), channel_id=1, source_target_pairs={{0,2},{1,3},{2,0},{3,1},{4,6},{5,7},{6,4},{7,5},{8,10},{9,11},{10,... | collective-permute-start | bytes 1572872 | tf_op jit(solution)/shard_map/ppermute | solution.py:316
  41.2 24.2 %collective-permute-start.6 = (bf16[128,16,128]{2,1,0:T(8,128)(2,1)S(1)}, bf16[128,16,128]{2,1,0:T(8,128)(2,1)S(1)}, u32[]{:S(2)}, u32[]{:S(2)}) collective-permute-start(bf16[128,16,128]{2,1,0:T(8,128)(2,1)S(1)} %collective-permute-done.4), channel_id=1, source_target_pairs={{0,4},{1,5},{2,6},{3,7},{4,0},{5,1},{6,2},{7,3},{8,12},{9,13},{10,... | collective-permute-start | bytes 1572872 | tf_op jit(solution)/shard_map/ppermute | solution.py:316
  42.7 23.3 %collective-permute-start.5 = (bf16[128,16,128]{2,1,0:T(8,128)(2,1)S(1)}, bf16[128,16,128]{2,1,0:T(8,128)(2,1)S(1)}, u32[]{:S(2)}, u32[]{:S(2)}) collective-permute-start(bf16[128,16,128]{2,1,0:T(8,128)(2,1)S(1)} %collective-permute-done.4), channel_id=1, source_target_pairs={{0,2},{1,3},{2,0},{3,1},{4,6},{5,7},{6,4},{7,5},{8,10},{9,11},{10,... | collective-permute-start | bytes 1572872 | tf_op jit(solution)/shard_map/ppermute | solution.py:316
  54.2 20.3 %collective-permute-start.13 = (bf16[64,16,128]{2,1,0:T(8,128)(2,1)S(1)}, bf16[64,16,128]{2,1,0:T(8,128)(2,1)S(1)}, u32[]{:S(2)}, u32[]{:S(2)}) collective-permute-start(bf16[64,16,128]{2,1,0:T(8,128)(2,1)S(1)} %slice.52), channel_id=1, source_target_pairs={{0,2},{1,3},{2,0},{3,1},{4,6},{5,7},{6,4},{7,5},{8,10},{9,11},{10,... | collective-permute-start | bytes 786440 | tf_op jit(solution)/shard_map/ppermute | solution.py:316
  54.8 17.5 %collective-permute-start.12 = (bf16[64,16,128]{2,1,0:T(8,128)(2,1)S(1)}, bf16[64,16,128]{2,1,0:T(8,128)(2,1)S(1)}, u32[]{:S(2)}, u32[]{:S(2)}) collective-permute-start(bf16[64,16,128]{2,1,0:T(8,128)(2,1)S(1)} %slice.51), channel_id=1, source_target_pairs={{0,4},{1,5},{2,6},{3,7},{4,0},{5,1},{6,2},{7,3},{8,12},{9,13},{10,... | collective-permute-start | bytes 786440 | tf_op jit(solution)/shard_map/ppermute | solution.py:316
  65.4 11.9 %collective-permute-start.8 = (bf16[64,16,128]{2,1,0:T(8,128)(2,1)S(1)}, bf16[64,16,128]{2,1,0:T(8,128)(2,1)S(1)}, u32[]{:S(2)}, u32[]{:S(2)}) collective-permute-start(bf16[64,16,128]{2,1,0:T(8,128)(2,1)S(1)} %slice.50), channel_id=1, source_target_pairs={{0,2},{1,3},{2,0},{3,1},{4,6},{5,7},{6,4},{7,5},{8,10},{9,11},{10,... | collective-permute-start | bytes 786440 | tf_op jit(solution)/shard_map/ppermute | solution.py:316
  66.1 10.6 %collective-permute-start.7 = (bf16[64,16,128]{2,1,0:T(8,128)(2,1)S(1)}, bf16[64,16,128]{2,1,0:T(8,128)(2,1)S(1)}, u32[]{:S(2)}, u32[]{:S(2)}) collective-permute-start(bf16[64,16,128]{2,1,0:T(8,128)(2,1)S(1)} %slice.49), channel_id=1, source_target_pairs={{0,4},{1,5},{2,6},{3,7},{4,0},{5,1},{6,2},{7,3},{8,12},{9,13},{10,... | collective-permute-start | bytes 786440 | tf_op jit(solution)/shard_map/ppermute | solution.py:316
  67.5 19.7 %collective-permute-start.15 = (bf16[128,16,128]{2,1,0:T(8,128)(2,1)S(1)}, bf16[128,16,128]{2,1,0:T(8,128)(2,1)S(1)}, u32[]{:S(2)}, u32[]{:S(2)}) collective-permute-start(bf16[128,16,128]{2,1,0:T(8,128)(2,1)S(1)} %collective-permute-done.14), channel_id=1, source_target_pairs={{0,2},{1,3},{2,0},{3,1},{4,6},{5,7},{6,4},{7,5},{8,10},{9,11},{10,... | collective-permute-start | bytes 1572872 | tf_op jit(solution)/shard_map/ppermute | solution.py:316
  72.3 16.4 %collective-permute-start.16 = (bf16[128,16,128]{2,1,0:T(8,128)(2,1)S(1)}, bf16[128,16,128]{2,1,0:T(8,128)(2,1)S(1)}, u32[]{:S(2)}, u32[]{:S(2)}) collective-permute-start(bf16[128,16,128]{2,1,0:T(8,128)(2,1)S(1)} %collective-permute-done.14), channel_id=1, source_target_pairs={{0,4},{1,5},{2,6},{3,7},{4,0},{5,1},{6,2},{7,3},{8,12},{9,13},{10,... | collective-permute-start | bytes 1572872 | tf_op jit(solution)/shard_map/ppermute | solution.py:316
  74.6 28.4 %collective-permute-start.19 = (bf16[512,16,128]{2,1,0:T(8,128)(2,1)}, bf16[512,16,128]{2,1,0:T(8,128)(2,1)}, u32[]{:S(2)}, u32[]{:S(2)}) collective-permute-start(bf16[512,16,128]{2,1,0:T(8,128)(2,1)} %constant_dynamic-update-slice_fusion.refs_0_), channel_id=1, source_target_pairs={{0,1},{1,0},{2,3},{3,2},{4,5},{5,4},{6,7},{7,6},{8,9},{9,8},{10,11... | collective-permute-start | bytes 6291464 | tf_op jit(solution)/shard_map/ppermute | solution.py:316
  76.7 26.3 %collective-permute-start.21 = (bf16[512,16,128]{2,1,0:T(8,128)(2,1)}, bf16[512,16,128]{2,1,0:T(8,128)(2,1)}, u32[]{:S(2)}, u32[]{:S(2)}) collective-permute-start(bf16[512,16,128]{2,1,0:T(8,128)(2,1)} %constant_dynamic-update-slice_fusion.10.refs_2_), channel_id=1, source_target_pairs={{0,1},{1,0},{2,3},{3,2},{4,5},{5,4},{6,7},{7,6},{8,9},{9,8},{10,11... | collective-permute-start | bytes 6291464 | tf_op jit(solution)/shard_map/ppermute | solution.py:316
  78.1 24.9 %collective-permute-start.20 = (bf16[512,16,128]{2,1,0:T(8,128)(2,1)}, bf16[512,16,128]{2,1,0:T(8,128)(2,1)}, u32[]{:S(2)}, u32[]{:S(2)}) collective-permute-start(bf16[512,16,128]{2,1,0:T(8,128)(2,1)} %constant_dynamic-update-slice_fusion.5.refs_1_), channel_id=1, source_target_pairs={{0,1},{1,0},{2,3},{3,2},{4,5},{5,4},{6,7},{7,6},{8,9},{9,8},{10,11... | collective-permute-start | bytes 6291464 | tf_op jit(solution)/shard_map/ppermute | solution.py:316
  87.3 7.3 %collective-permute-start.17 = (bf16[64,16,128]{2,1,0:T(8,128)(2,1)S(1)}, bf16[64,16,128]{2,1,0:T(8,128)(2,1)S(1)}, u32[]{:S(2)}, u32[]{:S(2)}) collective-permute-start(bf16[64,16,128]{2,1,0:T(8,128)(2,1)S(1)} %slice.53), channel_id=1, source_target_pairs={{0,4},{1,5},{2,6},{3,7},{4,0},{5,1},{6,2},{7,3},{8,12},{9,13},{10,... | collective-permute-start | bytes 786440 | tf_op jit(solution)/shard_map/ppermute | solution.py:316
  89.5 13.5 %collective-permute-start.22 = (bf16[384,16,128]{2,1,0:T(8,128)(2,1)}, bf16[384,16,128]{2,1,0:T(8,128)(2,1)}, u32[]{:S(2)}, u32[]{:S(2)}) collective-permute-start(bf16[384,16,128]{2,1,0:T(8,128)(2,1)} %constant_dynamic-update-slice_fusion.15.refs_3_), channel_id=1, source_target_pairs={{0,1},{1,0},{2,3},{3,2},{4,5},{5,4},{6,7},{7,6},{8,9},{9,8},{10,11... | collective-permute-start | bytes 4718600 | tf_op jit(solution)/shard_map/ppermute | solution.py:316
  94.6 6.4 %collective-permute-start.18 = (bf16[64,16,128]{2,1,0:T(8,128)(2,1)S(1)}, bf16[64,16,128]{2,1,0:T(8,128)(2,1)S(1)}, u32[]{:S(2)}, u32[]{:S(2)}) collective-permute-start(bf16[64,16,128]{2,1,0:T(8,128)(2,1)S(1)} %slice.54), channel_id=1, source_target_pairs={{0,2},{1,3},{2,0},{3,1},{4,6},{5,7},{6,4},{7,5},{8,10},{9,11},{10,... | collective-permute-start | bytes 786440 | tf_op jit(solution)/shard_map/ppermute | solution.py:316
  101.0 2.0 collective-permute-start.23
  151.4 70.1 %collective-permute-start.26 = (f32[256,512]{1,0:T(8,128)}, f32[256,512]{1,0:T(8,128)S(1)}, u32[]{:S(2)}, u32[]{:S(2)}) collective-permute-start(f32[256,512]{1,0:T(8,128)} %get-tuple-element.14), channel_id=1, source_target_pairs={{0,24},{8,16},{16,8},{24,0},{1,25},{9,17},{17,9},{25,1},{2,26},{10... | collective-permute-start | bytes 1572872 | tf_op jit(solution)/shard_map/ppermute | solution.py:386
  151.4 70.1 %collective-permute-start.25 = (f32[256,512]{1,0:T(8,128)}, f32[256,512]{1,0:T(8,128)S(1)}, u32[]{:S(2)}, u32[]{:S(2)}) collective-permute-start(f32[256,512]{1,0:T(8,128)} %get-tuple-element.14), channel_id=1, source_target_pairs={{0,16},{8,24},{16,0},{24,8},{1,17},{9,25},{17,1},{25,9},{2,18},{10... | collective-permute-start | bytes 1572872 | tf_op jit(solution)/shard_map/ppermute | solution.py:386
  152.0 69.4 %collective-permute-start.24 = (f32[256,512]{1,0:T(8,128)}, f32[256,512]{1,0:T(8,128)S(1)}, u32[]{:S(2)}, u32[]{:S(2)}) collective-permute-start(f32[256,512]{1,0:T(8,128)} %get-tuple-element.14), channel_id=1, source_target_pairs={{0,8},{8,0},{16,24},{24,16},{1,9},{9,1},{17,25},{25,17},{2,10},{10... | collective-permute-start | bytes 1572872 | tf_op jit(solution)/shard_map/ppermute | solution.py:386
  155.7 65.7 %copy-start.4 = (f32[256,512]{1,0:T(8,128)S(1)}, f32[256,512]{1,0:T(8,128)}, u32[]{:S(2)}) copy-start(f32[256,512]{1,0:T(8,128)} %get-tuple-element.14) | copy-start | bytes 1572868
  221.7 2.2 copy-start
  (5 other events, 8.6 us)
Sparse Core Ops, SparseCore 0:
  151.4 33.0 all-gather.2

commit v6 on v5

--- a/solution.py
+++ b/solution.py
@@ -37,7 +37,7 @@
 
 def assemble_kernel(slots_ref, x_ref, z_ref, *refs, sources, lead_tiles, pick_tiles, col_tiles, rows):
     source_refs, refs = refs[:sources], refs[sources:]
-    lead_x_ref, lead_z_ref, schur_ref, front_ref, top_ref, every_ref, picked_ref, yx_ref, yz_ref, sem_ref = refs
+    lead_x_ref, lead_z_ref, schur_ref, front_ref, top_ref, every_ref, picked_ref, yx_ref, yz_ref, gx_ref, gz_ref, sem_ref = refs
     step = pl.program_id(0)
     tile, parts, lanes = picked_ref.shape
     width = x_ref.shape[0]
@@ -83,35 +83,45 @@
         i, j = (step - pick_tiles) // col_tiles, (step - pick_tiles) % col_tiles
         left = pl.ds(pl.multiple_of(i * high, high), high)
         right = pl.ds(pl.multiple_of(rows + j * wide, wide), wide)
-        value = gram_tile(yx_ref, yz_ref, left, right)
-        schur_ref[...] = value
+        gram_tile(yx_ref, yz_ref, left, right, schur_ref, gx_ref, gz_ref)
 
         @pl.when(j == 0)
         def _():
-            front_ref[...] = value[:, :front_ref.shape[1]]
+            front_ref[...] = schur_ref[:, :front_ref.shape[1]]
 
         @pl.when(i == 0)
         def _():
-            top_ref[...] = value[:top_ref.shape[0], :]
-
-
-def gram_tile(yx_ref, yz_ref, left, right):
+            top_ref[...] = schur_ref[:top_ref.shape[0], :]
+
+
+CHUNK = 32
+
+
+def gram_tile(yx_ref, yz_ref, left, right, out_ref, gx_ref, gz_ref):
     left_x, left_z = yx_ref[:, left, :], yz_ref[:, left, :]
     _, high, width = left_x.shape
     left_x, left_z = left_x.reshape(RANK * high, width), left_z.reshape(RANK * high, width)
-    total = None
+
+    def products(q):
+        gx_ref[q % 2] = dot_bf16(left_x, yx_ref[q, right, :], NT)
+        gz_ref[q % 2] = dot_bf16(left_z, yz_ref[q, right, :], NT)
+
+    products(0)
     for q in range(RANK):
-        gx = dot_bf16(left_x, yx_ref[q, right, :], NT)
-        gz = dot_bf16(left_z, yz_ref[q, right, :], NT)
-        for r in range(RANK):
-            term = gx[r * high:(r + 1) * high] * gz[r * high:(r + 1) * high]
-            if total is None:
-                total = term
-            elif rank_signs[q] * rank_signs[r] > 0:
-                total = total + term
-            else:
-                total = total - term
-    return total
+        if q + 1 < RANK:
+            products(q + 1)
+        for first in range(0, high, CHUNK):
+            total = out_ref[first:first + CHUNK, :] if q > 0 else None
+            for r in range(RANK):
+                at = slice(r * high + first, r * high + first + CHUNK)
+                total = signed(total, gx_ref[q % 2, at, :] * gz_ref[q % 2, at, :], q, r)
+            out_ref[first:first + CHUNK, :] = total
+
+
+def signed(total, term, q, r):
+    if total is None:
+        return term
+    return total + term if rank_signs[q] * rank_signs[r] > 0 else total - term
 
 
 def assemble(slots, sources, x_factor, z_factor, rows, cols, lead_rows, lead_cols):
@@ -141,7 +151,7 @@
                    pl.BlockSpec((high, lead_cols), lambda s: (after(s) // col_tiles, 0)),
                    pl.BlockSpec((lead_rows, wide), lambda s: (0, jnp.minimum(after(s), col_tiles - 1)))),
         scratch_shapes=[pltpu.VMEM((slots_held, parts, lanes), bf16), pltpu.VMEM((tile, parts, lanes), bf16)]
-        + [pltpu.VMEM((RANK, rows + cols, width), bf16)] * 2 + [pltpu.SemaphoreType.DMA((len(sources),))],
+        + [pltpu.VMEM((RANK, rows + cols, width), bf16)] * 2 + [pltpu.VMEM((2, RANK * high, wide), jnp.float32)] * 2 + [pltpu.SemaphoreType.DMA((len(sources),))],
         compiler_params=pltpu.CompilerParams(vmem_limit_bytes=58 * MIB),
         cost_estimate=pl.CostEstimate(flops=28 * 10**9, bytes_accessed=30 * MIB, transcendentals=0),
     )(slots, x_factor, z_factor, *sources)
@@ -160,84 +170,104 @@
     def spread_row(x, row):
         return jnp.broadcast_to(x[row:row + 1, :], (SUB, BLK))
 
+    cols = [spread_lane(rows_a[0], k) for k in range(SUB)]
     for m in range(count):
         beside(m)
         head_a, head_v = rows_a[m], rows_v[m]
-        cols = [spread_lane(head_a, SUB * m + k) for k in range(SUB)]
         below = [[spread_lane(rows_a[i], SUB * m + k) for k in range(SUB)] for i in range(m + 1, count)]
+        ahead, coming = [], []
+        if m + 1 < count:
+            ahead = [spread_lane(head_a, SUB * (m + 1) + k) for k in range(SUB)]
+            coming = [spread_lane(rows_a[m + 1], SUB * (m + 1) + k) for k in range(SUB)]
         scale = jnp.zeros((SUB, BLK), jnp.float32)
         for j in range(SUB):
             pivot = spread_row(cols[j], j)
             root = lax.rsqrt(pivot)
             scale = jnp.where(sub_iota == j, root, scale)
             mult = jnp.where(sub_iota > j, cols[j] * root, 0.0)
+            lead = [spread_row(cols[k], j) * root if k > j else None for k in range(SUB)]
             row_a = spread_row(head_a, j) * root
             row_v = spread_row(head_v, j) * root
-            lead = [spread_row(cols[k], j) * root if k > j else None for k in range(SUB)]
+            row_ahead = [spread_row(value, j) * root for value in ahead]
             if j + 1 < SUB:
+                for k in range(j + 1, SUB):
+                    cols[k] = cols[k] - mult * lead[k]
                 head_a = head_a - mult * row_a
                 head_v = head_v - mult * row_v
-                for k in range(j + 1, SUB):
-                    cols[k] = cols[k] - mult * lead[k]
+                ahead = [value - mult * row for value, row in zip(ahead, row_ahead)]
             for n, i in enumerate(range(m + 1, count)):
                 mult_i = below[n][j] * root
+                for k in range(j + 1, SUB):
+                    below[n][k] = below[n][k] - mult_i * lead[k]
+                if n == 0:
+                    coming = [value - mult_i * row for value, row in zip(coming, row_ahead)]
                 rows_a[i] = rows_a[i] - mult_i * row_a
                 rows_v[i] = rows_v[i] - mult_i * row_v
-                for k in range(j + 1, SUB):
-                    below[n][k] = below[n][k] - mult_i * lead[k]
-        u = jnp.where(lane_iota >= sub_iota + SUB * m, head_a * scale, 0.0)
-        v = jnp.where(lane_iota <= sub_iota + SUB * m, head_v * scale, 0.0)
-        u_ref[SUB * m:SUB * (m + 1), :] = u
-        v_ref[SUB * m:SUB * (m + 1), :] = v
-
-
-def factor_kernel(yx_ref, yz_ref, l_ref, d_ref, w_ref, g_ref, u_ref, v_ref):
-    order = l_ref.shape[0]
+        u_ref[SUB * m:SUB * (m + 1), :] = jnp.where(lane_iota >= sub_iota + SUB * m, head_a * scale, 0.0)
+        v_ref[SUB * m:SUB * (m + 1), :] = jnp.where(lane_iota <= sub_iota + SUB * m, head_v * scale, 0.0)
+        cols = coming
+
+
+def factor_kernel(yx_ref, yz_ref, lh_ref, ll_ref, d_ref, w_ref, g_ref, u_ref, v_ref, gx_ref, gz_ref, px_ref, pz_ref):
+    order = lh_ref.shape[0]
     steps = order // BLK
     tile = 2 * BLK
     window = 3 * BLK
-    l_ref[...] = jnp.zeros_like(l_ref)
-    w_ref[...] = jnp.zeros_like(w_ref)
+    lh_ref[...] = jnp.zeros_like(lh_ref)
+    ll_ref[...] = jnp.zeros_like(ll_ref)
+    w_ref[:, tile:] = jnp.zeros((order, order - tile), jnp.float32)
 
     def rows_of(i, carry):
-        left = pl.ds(pl.multiple_of(i * 2 * tile, 2 * tile), 2 * tile)
-        w_ref[left, :tile] = gram_tile(yx_ref, yz_ref, left, pl.ds(0, tile))
+        left = pl.ds(pl.multiple_of(i * tile, tile), tile)
+        gram_tile(yx_ref, yz_ref, left, pl.ds(0, tile), w_ref.at[left, pl.ds(0, tile)], gx_ref, gz_ref)
         return carry
-    lax.fori_loop(0, order // (2 * tile), rows_of, 0)
+    lax.fori_loop(0, order // tile, rows_of, 0)
 
     def step(b, carry):
         at = pl.ds(pl.multiple_of(b * BLK, BLK), BLK)
-        ahead = jnp.minimum(b // 2 + 1, order // tile - 1)
-        left = pl.ds(pl.multiple_of(jnp.minimum(ahead * tile + (b % 2) * window, order - window), BLK), window)
-        right = pl.ds(pl.multiple_of(ahead * tile, tile), tile)
+        after = jnp.minimum(b // 2 + 1, order // tile - 1)
+        top = pl.multiple_of(jnp.minimum(after * tile + (b % 2) * window, order - window), BLK)
+        left = pl.ds(top, window)
+        right = pl.ds(pl.multiple_of(after * tile, tile), tile)
+        pairs = RANK * RANK
+
+        def products(m):
+            q, r = m // RANK, m % RANK
+            px_ref[m % 2] = dot_bf16(yx_ref[r, left, :], yx_ref[q, right, :], NT)
+            pz_ref[m % 2] = dot_bf16(yz_ref[r, left, :], yz_ref[q, right, :], NT)
+
+        def add_up(m):
+            for first in range(0, window, CHUNK):
+                rows = pl.ds(pl.multiple_of(top + first, CHUNK), CHUNK)
+                total = g_ref[rows, :] if m > 0 else None
+                g_ref[rows, :] = signed(total, px_ref[m % 2, first:first + CHUNK, :] * pz_ref[m % 2, first:first + CHUNK, :], m // RANK, m % RANK)
 
         def beside(m):
-            q, r = m // RANK, m % RANK
-            term = dot_bf16(yx_ref[r, left, :], yx_ref[q, right, :], NT) * dot_bf16(yz_ref[r, left, :], yz_ref[q, right, :], NT)
-            if m == 0:
-                g_ref[left, :] = term
-            elif rank_signs[q] * rank_signs[r] > 0:
-                g_ref[left, :] = g_ref[left, :] + term
-            else:
-                g_ref[left, :] = g_ref[left, :] - term
+            if m < pairs:
+                products(m)
+            if 0 < m <= pairs:
+                add_up(m - 1)
 
         factor_block(w_ref[at, at], u_ref, v_ref, beside)
-        l_ref[at, at] = u_ref[...].T
+        add_up(pairs - 1)
+        lh_ref[at, at], ll_ref[at, at] = split(u_ref[...].T)
         d_ref[at, :] = v_ref[...]
         for k in range(steps - 1):
             @pl.when(b == k)
             def _():
                 first = (k + 1) * BLK
                 inv = split(v_ref[...])
+
                 def panel(t, c):
                     rows = pl.ds(pl.multiple_of(first + t * BLK, BLK), BLK)
-                    l_ref[rows, k * BLK:first] = dot3(split(w_ref[rows, k * BLK:first]), inv, NT)
+                    lh_ref[rows, k * BLK:first], ll_ref[rows, k * BLK:first] = split(dot3(split(w_ref[rows, k * BLK:first]), inv, NT))
                     return c
                 lax.fori_loop(0, steps - 1 - k, panel, 0)
-                right = split(l_ref[first:, k * BLK:first])
+                right = (lh_ref[first:, k * BLK:first], ll_ref[first:, k * BLK:first])
+
                 def update(t, c):
                     rows = pl.ds(pl.multiple_of(first + t * BLK, BLK), BLK)
-                    left = split(l_ref[rows, k * BLK:first])
+                    left = (lh_ref[rows, k * BLK:first], ll_ref[rows, k * BLK:first])
                     w_ref[rows, first:] = w_ref[rows, first:] - dot3(left, right, NT)
                     return c
                 lax.fori_loop(0, steps - 1 - k, update, 0)
@@ -248,64 +278,83 @@
 
 
 def factor(yx, yz):
+    tile, window = 2 * BLK, 3 * BLK
+    f32 = jnp.float32
     return pl.pallas_call(
         factor_kernel,
-        out_shape=(jax.ShapeDtypeStruct((K, K), jnp.float32), jax.ShapeDtypeStruct((K, BLK), jnp.float32)),
+        out_shape=(jax.ShapeDtypeStruct((K, K), jnp.bfloat16),) * 2 + (jax.ShapeDtypeStruct((K, BLK), f32),),
         in_specs=[VMEM] * 2,
-        out_specs=(VMEM, VMEM),
-        scratch_shapes=[pltpu.VMEM((K, K), jnp.float32), pltpu.VMEM((K, 2 * BLK), jnp.float32), pltpu.VMEM((BLK, BLK), jnp.float32), pltpu.VMEM((BLK, BLK), jnp.float32)],
+        out_specs=(VMEM,) * 3,
+        scratch_shapes=[pltpu.VMEM((K, K), f32), pltpu.VMEM((K, tile), f32), pltpu.VMEM((BLK, BLK), f32), pltpu.VMEM((BLK, BLK), f32)]
+        + [pltpu.VMEM((2, RANK * tile, tile), f32)] * 2 + [pltpu.VMEM((2, window, tile), f32)] * 2,
         compiler_params=pltpu.CompilerParams(vmem_limit_bytes=48 * MIB),
         cost_estimate=pl.CostEstimate(flops=40 * 10**9, bytes_accessed=12 * MIB, transcendentals=0),
     )(yx, yz)
 
 
-def solve_kernel(place_ref, l_ref, d_ref, pieces_ref, tops_ref, schur_ref, rest_ref, panel_ref, lh, ll, xh, xl, zh, zl):
+def solve_kernel(place_ref, lh, ll, d_ref, pieces_any, schur_any, *refs, prow):
+    top_refs, refs = refs[:prow], refs[prow:]
+    rest_ref, panel_ref, pieces_ref, tops_ref, schur_ref, xh, xl, zh, zl, sem_ref = refs
     pcol = pieces_ref.shape[0]
-    prow = tops_ref.shape[0]
     row, column = place_ref[0], place_ref[1]
-    lh[...], ll[...] = split(l_ref[...])
+    tops = [pltpu.make_async_copy(ref, tops_ref.at[turn ^ row], sem_ref.at[turn]) for turn, ref in enumerate(top_refs)]
+    pieces = pltpu.make_async_copy(pieces_any, pieces_ref, sem_ref.at[prow])
+    schur = pltpu.make_async_copy(schur_any, schur_ref, sem_ref.at[prow + 1])
+    for copy in tops:
+        copy.start()
+    pieces.start()
+    schur.start()
     wide = 2 * BLK
+    inverses = []
     for b in range(K // wide):
-        at = slice(b * wide, (b + 1) * wide)
         upper, lower = slice(b * wide, b * wide + BLK), slice(b * wide + BLK, (b + 1) * wide)
         first, second = split(d_ref[upper, :]), split(d_ref[lower, :])
         between = dot3((lh[lower, upper], ll[lower, upper]), first, NN)
         corner = -dot3(second, split(between), NN)
-        inverse = split(jnp.concatenate([
+        inverses.append(split(jnp.concatenate([
             jnp.concatenate([d_ref[upper, :], jnp.zeros((BLK, BLK), jnp.float32)], axis=1),
-            jnp.concatenate([corner, d_ref[lower, :]], axis=1)], axis=0))
+            jnp.concatenate([corner, d_ref[lower, :]], axis=1)], axis=0)))
+    for copy in tops:
+        copy.wait()
+    for b in range(K // wide):
+        at, done = slice(b * wide, (b + 1) * wide), slice(0, b * wide)
+        blocks = range(wide // NB * b, wide // NB * (b + 1))
+        top = jnp.concatenate([tops_ref[n % prow, n // prow * NB:(n // prow + 1) * NB, :] for n in blocks], axis=0)
+        if b > 0:
+            top = top - dot3((lh[at, done], ll[at, done]), (zh[done, :], zl[done, :]), NN)
+        zh[at, :], zl[at, :] = split(dot3(inverses[b], split(top), NN))
+    pieces.wait()
+    for b in range(K // wide):
+        at, done = slice(b * wide, (b + 1) * wide), slice(0, b * wide)
         blocks = range(wide // NB * b, wide // NB * (b + 1))
         value = jnp.concatenate([pieces_ref[n % pcol, :, n // pcol * NB:(n // pcol + 1) * NB] for n in blocks], axis=1)
-        top = jnp.concatenate([tops_ref[(n % prow) ^ row, n // prow * NB:(n // prow + 1) * NB, :] for n in blocks], axis=0)
         if b > 0:
-            done = slice(0, b * wide)
-            left = (lh[at, done], ll[at, done])
-            value = value - dot3((xh[:, done], xl[:, done]), left, NT)
-            top = top - dot3(left, (zh[done, :], zl[done, :]), NN)
-        value = dot3(split(value), inverse, NT)
-        top = dot3(inverse, split(top), NN)
+            value = value - dot3((xh[:, done], xl[:, done]), (lh[at, done], ll[at, done]), NT)
+        value = dot3(split(value), inverses[b], NT)
         xh[:, at], xl[:, at] = split(value)
-        zh[at, :], zl[at, :] = split(top)
         for place, block in enumerate(blocks):
             @pl.when(column == block % pcol)
             def _():
                 panel_ref[:, block // pcol * NB:(block // pcol + 1) * NB] = value[:, place * NB:(place + 1) * NB]
+    schur.wait()
     rest_ref[...] = schur_ref[...] - dot3((xh[...], xl[...]), (zh[...], zl[...]), NN)
 
 
-def solve(place, low, inverses, pieces, tops, schur):
+def solve(place, high, low, inverses, pieces, schur, tops):
     rows, cols = schur.shape
     lead = K // pieces.shape[0]
-    bf16 = jnp.bfloat16
+    bf16, f32 = jnp.bfloat16, jnp.float32
+    any_space = pl.BlockSpec(memory_space=pl.ANY)
     return pl.pallas_call(
-        solve_kernel,
-        out_shape=(jax.ShapeDtypeStruct((rows, cols), jnp.float32), jax.ShapeDtypeStruct((rows, lead), jnp.float32)),
-        in_specs=[SMEM] + [VMEM] * 5,
+        functools.partial(solve_kernel, prow=len(tops)),
+        out_shape=(jax.ShapeDtypeStruct((rows, cols), f32), jax.ShapeDtypeStruct((rows, lead), f32)),
+        in_specs=[SMEM] + [VMEM] * 3 + [any_space] * (2 + len(tops)),
         out_specs=(VMEM, VMEM),
-        scratch_shapes=[pltpu.VMEM((K, K), bf16)] * 2 + [pltpu.VMEM((rows, K), bf16)] * 2 + [pltpu.VMEM((K, cols), bf16)] * 2,
-        compiler_params=pltpu.CompilerParams(vmem_limit_bytes=40 * MIB),
+        scratch_shapes=[pltpu.VMEM(pieces.shape, f32), pltpu.VMEM((len(tops),) + tops[0].shape, f32), pltpu.VMEM(schur.shape, f32)]
+        + [pltpu.VMEM((rows, K), bf16)] * 2 + [pltpu.VMEM((K, cols), bf16)] * 2 + [pltpu.SemaphoreType.DMA((len(tops) + 2,))],
+        compiler_params=pltpu.CompilerParams(vmem_limit_bytes=44 * MIB),
         cost_estimate=pl.CostEstimate(flops=12 * 10**9, bytes_accessed=24 * MIB, transcendentals=0),
-    )(place, low, inverses, pieces, tops, schur)
+    )(place, high, low, inverses, pieces, schur, *tops)
 
 
 def gather_factors(mine, prow_count, pcol_count):
@@ -383,10 +432,9 @@
     lead_x, lead_z, schur_local, front, top = assemble(
         places.astype(jnp.int32), sources, x_factor, zinv_factor, local_rows, local_cols, lead_rows, lead_cols)
     pieces = lax.all_gather(front, "pcol", axis=0, tiled=False)
-    turned = [lax.ppermute(top, "prow", [(n, n ^ turn) for n in range(prow_count)]) for turn in range(1, prow_count)]
-    tops = jnp.stack([top] + turned)
-    low, inverses = factor(lead_x, lead_z)
-    return solve(jnp.stack([prow_id, pcol_id]).astype(jnp.int32), low, inverses, pieces, tops, schur_local)
+    tops = [top] + [lax.ppermute(top, "prow", [(n, n ^ turn) for n in range(prow_count)]) for turn in range(1, prow_count)]
+    high, low, inverses = factor(lead_x, lead_z)
+    return solve(jnp.stack([prow_id, pcol_id]).astype(jnp.int32), high, low, inverses, pieces, schur_local, tops)
 
 
 def solution(mesh):

time: 251 us -> 263 us (1.048)
  Pallas kernels: 127 us -> 140 us
    pallas_call x1, Pallas kernels: 63.7 us -> 71.2 us  [factor(): pl.pallas_call(factor_kernel, out_shape=(jax.ShapeDtypeStruct((K, K), jnp...]
    pallas_call x1, Pallas kernels: 16.2 us -> 21.4 us  [solve(): pl.pallas_call(functools.partial(solve_kernel, prow=len(tops)), out_shape...]
    unnamed x33 -> x35, local copies, waits for them, and re-layouts: 20.1 us -> 19.5 us
  transfers between devices with their start and end apart: 28 -> 28, of which waited for: 9 -> 9; matrix products, arithmetic and copies ran while one was open for 7% -> 6% of each run, Pallas kernels for 25% -> 27%
where the time goes in v6:
time: 263 us
  Pallas kernels  140 us (53%)
  waiting for transfers between devices  44.7 us (17%)
  starting transfers between devices  37.1 us (14%)
  local copies, waits for them, and re-layouts  25.4 us (10%)
  between operations  14.3 us (5%)
    pallas_call x1, Pallas kernels, factor(): pl.pallas_call(factor_kernel, out_shape=(jax.ShapeDtypeStruct((K, K), jnp...  71.2 us
    pallas_call x1, Pallas kernels, assemble(): pl.pallas_call(body, grid=(pick_tiles + row_tiles * col_tiles,), out_shap...  47.4 us
    ppermute x24, waiting for transfers between devices, swap(): return lax.ppermute(value, axis, [(n, n ^ turn) for n in range(count)])  44.7 us
    ppermute x24, starting transfers between devices, swap(): return lax.ppermute(value, axis, [(n, n ^ turn) for n in range(count)])  32.7 us
    pallas_call x1, Pallas kernels, solve(): pl.pallas_call(functools.partial(solve_kernel, prow=len(tops)), out_shape...  21.4 us
    unnamed x35, local copies, waits for them, and re-layouts  19.5 us
  transfers between devices with their start and end apart: 28, of which 9 were waited for; matrix products, arithmetic and copies ran while one was open for 6% of the time, Pallas kernels for 27%

profile of v6, /device:TPU:0, one launch (start us, length us, event | category | flops | bytes accessed | tf_op | source)
XLA Modules:
  0.0 262.7 jit_solution(11190216713418683651)
XLA Ops:
  7.2 1.4 copy.19
  8.9 3.0 %collective-permute-start.1 = (bf16[128,16,128]{2,1,0:T(8,128)(2,1)S(1)}, bf16[128,16,128]{2,1,0:T(8,128)(2,1)S(1)}, u32[]{:S(2)}, u32[]{:S(2)}) collective-permute-start(bf16[128,16,128]{2,1,0:T(8,128)(2,1)S(1)} %reshape.177), channel_id=1, source_target_pairs={{0,4},{1,5},{2,6},{3,7},{4,0},{5,1},{6,2},{7,3},{8,12},{9,13},{10,... | collective-permute-start | bytes 1572872 | tf_op jit(solution)/shard_map/ppermute | solution.py:365
  11.9 1.5 collective-permute-start
  13.4 3.6 %collective-permute-start.9 = (bf16[128,16,128]{2,1,0:T(8,128)(2,1)S(1)}, bf16[128,16,128]{2,1,0:T(8,128)(2,1)S(1)}, u32[]{:S(2)}, u32[]{:S(2)}) collective-permute-start(bf16[128,16,128]{2,1,0:T(8,128)(2,1)S(1)} %reshape.177), channel_id=1, source_target_pairs={{0,24},{8,16},{16,8},{24,0},{1,25},{9,17},{17,9},{25,1},{2,26},{10... | collective-permute-start | bytes 1572872 | tf_op jit(solution)/shard_map/ppermute | solution.py:365
  17.2 6.6 %collective-permute-done.1 = bf16[128,16,128]{2,1,0:T(8,128)(2,1)S(1)} collective-permute-done((bf16[128,16,128]{2,1,0:T(8,128)(2,1)S(1)}, bf16[128,16,128]{2,1,0:T(8,128)(2,1)S(1)}, u32[]{:S(2)}, u32[]{:S(2)}) %collective-permute-start.1) | collective-permute-done | bytes 524320 | tf_op jit(solution)/shard_map/ppermute | solution.py:365
  23.9 1.8 collective-permute-start.3
  25.7 1.6 collective-permute-start.2
  28.2 1.9 collective-permute-done.9
  30.1 9.2 %collective-permute-start.14 = (bf16[128,16,128]{2,1,0:T(8,128)(2,1)S(1)}, bf16[128,16,128]{2,1,0:T(8,128)(2,1)S(1)}, u32[]{:S(2)}, u32[]{:S(2)}) collective-permute-start(bf16[128,16,128]{2,1,0:T(8,128)(2,1)S(1)} %collective-permute-done.9), channel_id=1, source_target_pairs={{0,8},{8,0},{16,24},{24,16},{1,9},{9,1},{17,25},{25,17},{2,10},{10... | collective-permute-start | bytes 1572872 | tf_op jit(solution)/shard_map/ppermute | solution.py:365
  41.2 1.5 collective-permute-start.6
  42.7 1.5 collective-permute-start.5
  48.1 6.0 %collective-permute-done.11 = bf16[128,16,128]{2,1,0:T(8,128)(2,1)S(1)} collective-permute-done((bf16[128,16,128]{2,1,0:T(8,128)(2,1)S(1)}, bf16[128,16,128]{2,1,0:T(8,128)(2,1)S(1)}, u32[]{:S(2)}, u32[]{:S(2)}) %collective-permute-start.11) | collective-permute-done | bytes 524320 | tf_op jit(solution)/shard_map/ppermute | solution.py:365
  54.8 1.5 collective-permute-start.12
  56.3 9.1 %collective-permute-done.6 = bf16[128,16,128]{2,1,0:T(8,128)(2,1)S(1)} collective-permute-done((bf16[128,16,128]{2,1,0:T(8,128)(2,1)S(1)}, bf16[128,16,128]{2,1,0:T(8,128)(2,1)S(1)}, u32[]{:S(2)}, u32[]{:S(2)}) %collective-permute-start.6) | collective-permute-done | bytes 524320 | tf_op jit(solution)/shard_map/ppermute | solution.py:365
  66.1 1.5 collective-permute-start.7
  68.1 0.8 constant_dynamic-update-slice_fusion.17
  70.6 0.9 constant_dynamic-update-slice_fusion.13
  72.3 1.5 collective-permute-start.16
  75.3 1.4 collective-permute-done.7
  78.6 8.6 %collective-permute-done.15 = bf16[128,16,128]{2,1,0:T(8,128)(2,1)S(1)} collective-permute-done((bf16[128,16,128]{2,1,0:T(8,128)(2,1)S(1)}, bf16[128,16,128]{2,1,0:T(8,128)(2,1)S(1)}, u32[]{:S(2)}, u32[]{:S(2)}) %collective-permute-start.15) | collective-permute-done | bytes 524320 | tf_op jit(solution)/shard_map/ppermute | solution.py:365
  87.9 0.9 constant_dynamic-update-slice_fusion.16
  89.8 4.8 %collective-permute-done.17 = bf16[64,16,128]{2,1,0:T(8,128)(2,1)S(1)} collective-permute-done((bf16[64,16,128]{2,1,0:T(8,128)(2,1)S(1)}, bf16[64,16,128]{2,1,0:T(8,128)(2,1)S(1)}, u32[]{:S(2)}, u32[]{:S(2)}) %collective-permute-start.17) | collective-permute-done | bytes 262176 | tf_op jit(solution)/shard_map/ppermute | solution.py:365
  95.6 5.3 %collective-permute-done.18 = bf16[64,16,128]{2,1,0:T(8,128)(2,1)S(1)} collective-permute-done((bf16[64,16,128]{2,1,0:T(8,128)(2,1)S(1)}, bf16[64,16,128]{2,1,0:T(8,128)(2,1)S(1)}, u32[]{:S(2)}, u32[]{:S(2)}) %collective-permute-start.18) | collective-permute-done | bytes 262176 | tf_op jit(solution)/shard_map/ppermute | solution.py:365
  103.8 47.4 %shard_map.68 = (bf16[4,1024,512]{2,1,0:T(8,128)(2,1)}, bf16[4,1024,512]{2,1,0:T(8,128)(2,1)}, f32[1024,512]{1,0:T(8,128)}, f32[1024,128]{1,0:T(8,128)}, f32[256,512]{1,0:T(8,128)}) custom-call(s32[2560]{0:T(1024)} %reshape.176.slots_ref, bf16[512,512]{1,0:T(8,128)(2,1)} %x_ref.1, bf16[512,512]{1,0:T(8,128)(2,1)} %z_ref.1, ...), custom_call_target="tpu_custom_call" | custom-call | flops 28000000000 | bytes 31457280 | tf_op jit(solution)/shard_map/pallas_call | solution.py:141
  152.0 3.7 %collective-permute-start.24 = (f32[256,512]{1,0:T(8,128)}, f32[256,512]{1,0:T(8,128)S(1)}, u32[]{:S(2)}, u32[]{:S(2)}) collective-permute-start(f32[256,512]{1,0:T(8,128)} %get-tuple-element.17.refs_0_), channel_id=1, source_target_pairs={{0,8},{8,0},{16,24},{24,16},{1,9},{9,1},{17,25},{25,17},{2,10},{10... | collective-permute-start | bytes 1572872 | tf_op jit(solution)/shard_map/ppermute | solution.py:435
  155.7 71.2 %shard_map.69 = (bf16[1024,1024]{1,0:T(8,128)(2,1)S(1)}, bf16[1024,1024]{1,0:T(8,128)(2,1)S(1)}, f32[1024,128]{1,0:T(8,128)S(1)}) custom-call(bf16[4,1024,512]{2,1,0:T(8,128)(2,1)} %get-tuple-element.10.yx_ref, bf16[4,1024,512]{2,1,0:T(8,128)(2,1)} %get-tuple-element.11.yz_ref), custom_call_target="tpu_custom_call" | custom-call | flops 40000000000 | bytes 12582912 | tf_op jit(solution)/shard_map/pallas_call | solution.py:283
  227.0 1.3 copy-done.2
  228.3 1.4 copy-done.4
  229.7 1.6 copy-done.1
  231.3 1.6 copy-done.3
  232.9 1.6 copy-done.5
  234.4 21.4 %shard_map.70 = (f32[1024,512]{1,0:T(8,128)}, f32[1024,128]{1,0:T(8,128)}) custom-call(s32[2]{0:T(128)S(1)} %pad_add_fusion.1.place_ref, bf16[1024,1024]{1,0:T(8,128)(2,1)S(1)} %copy-done.3, bf16[1024,1024]{1,0:T(8,128)(2,1)S(1)} %copy-done.5, f32[1024,128]{1,0:T(8,128)S(1)} %get-tuple-element.14.d_ref, f32[8,1024,128]{2,1,0:T(8,128)} %bitcast.51, ...), custom_call_target="tpu_custom_call" | custom-call | flops 12000000000 | bytes 25165824 | tf_op jit(solution)/shard_map/pallas_call | solution.py:348
  (94 shorter events, 21.1 us)
Async XLA Ops:
  7.2 9.9 %copy-start.9 = (s32[32]{0:T(128)S(1)}, s32[32]{0:T(128)}, u32[]{:S(2)}) copy-start(s32[32]{0:T(128)} %constant.92.clone) | copy-start | bytes 388
  7.2 20.1 %copy-start.7 = (s32[4096]{0:T(1024)S(1)}, s32[4096]{0:T(1024)}, u32[]{:S(2)}) copy-start(s32[4096]{0:T(1024)} %param.8) | copy-start | bytes 49156
  7.2 222.5 %all-gather.3.cloned.1.call-start = ((), (), s32[]{:S(2)}) async-start(), calls=%async_computation | async-start | bytes 4718592 | tf_op jit(solution)/shard_map/all_gather | solution.py:434
  8.9 15.0 %collective-permute-start.1 = (bf16[128,16,128]{2,1,0:T(8,128)(2,1)S(1)}, bf16[128,16,128]{2,1,0:T(8,128)(2,1)S(1)}, u32[]{:S(2)}, u32[]{:S(2)}) collective-permute-start(bf16[128,16,128]{2,1,0:T(8,128)(2,1)S(1)} %reshape.177), channel_id=1, source_target_pairs={{0,4},{1,5},{2,6},{3,7},{4,0},{5,1},{6,2},{7,3},{8,12},{9,13},{10,... | collective-permute-start | bytes 1572872 | tf_op jit(solution)/shard_map/ppermute | solution.py:365
  11.9 13.7 %collective-permute-start = (bf16[128,16,128]{2,1,0:T(8,128)(2,1)S(1)}, bf16[128,16,128]{2,1,0:T(8,128)(2,1)S(1)}, u32[]{:S(2)}, u32[]{:S(2)}) collective-permute-start(bf16[128,16,128]{2,1,0:T(8,128)(2,1)S(1)} %reshape.177), channel_id=1, source_target_pairs={{0,2},{1,3},{2,0},{3,1},{4,6},{5,7},{6,4},{7,5},{8,10},{9,11},{10,... | collective-permute-start | bytes 1572872 | tf_op jit(solution)/shard_map/ppermute | solution.py:365
  13.4 16.7 %collective-permute-start.9 = (bf16[128,16,128]{2,1,0:T(8,128)(2,1)S(1)}, bf16[128,16,128]{2,1,0:T(8,128)(2,1)S(1)}, u32[]{:S(2)}, u32[]{:S(2)}) collective-permute-start(bf16[128,16,128]{2,1,0:T(8,128)(2,1)S(1)} %reshape.177), channel_id=1, source_target_pairs={{0,24},{8,16},{16,8},{24,0},{1,25},{9,17},{17,9},{25,1},{2,26},{10... | collective-permute-start | bytes 1572872 | tf_op jit(solution)/shard_map/ppermute | solution.py:365
  17.0 22.8 %collective-permute-start.4 = (bf16[128,16,128]{2,1,0:T(8,128)(2,1)S(1)}, bf16[128,16,128]{2,1,0:T(8,128)(2,1)S(1)}, u32[]{:S(2)}, u32[]{:S(2)}) collective-permute-start(bf16[128,16,128]{2,1,0:T(8,128)(2,1)S(1)} %reshape.177), channel_id=1, source_target_pairs={{0,8},{8,0},{16,24},{24,16},{1,9},{9,1},{17,25},{25,17},{2,10},{10... | collective-permute-start | bytes 1572872 | tf_op jit(solution)/shard_map/ppermute | solution.py:365
  23.9 17.3 %collective-permute-start.3 = (bf16[64,16,128]{2,1,0:T(8,128)(2,1)S(1)}, bf16[64,16,128]{2,1,0:T(8,128)(2,1)S(1)}, u32[]{:S(2)}, u32[]{:S(2)}) collective-permute-start(bf16[64,16,128]{2,1,0:T(8,128)(2,1)S(1)} %slice.48), channel_id=1, source_target_pairs={{0,2},{1,3},{2,0},{3,1},{4,6},{5,7},{6,4},{7,5},{8,10},{9,11},{10,... | collective-permute-start | bytes 786440 | tf_op jit(solution)/shard_map/ppermute | solution.py:365
  25.7 17.1 %collective-permute-start.2 = (bf16[64,16,128]{2,1,0:T(8,128)(2,1)S(1)}, bf16[64,16,128]{2,1,0:T(8,128)(2,1)S(1)}, u32[]{:S(2)}, u32[]{:S(2)}) collective-permute-start(bf16[64,16,128]{2,1,0:T(8,128)(2,1)S(1)} %slice.47), channel_id=1, source_target_pairs={{0,4},{1,5},{2,6},{3,7},{4,0},{5,1},{6,2},{7,3},{8,12},{9,13},{10,... | collective-permute-start | bytes 786440 | tf_op jit(solution)/shard_map/ppermute | solution.py:365
  30.1 37.4 %collective-permute-start.14 = (bf16[128,16,128]{2,1,0:T(8,128)(2,1)S(1)}, bf16[128,16,128]{2,1,0:T(8,128)(2,1)S(1)}, u32[]{:S(2)}, u32[]{:S(2)}) collective-permute-start(bf16[128,16,128]{2,1,0:T(8,128)(2,1)S(1)} %collective-permute-done.9), channel_id=1, source_target_pairs={{0,8},{8,0},{16,24},{24,16},{1,9},{9,1},{17,25},{25,17},{2,10},{10... | collective-permute-start | bytes 1572872 | tf_op jit(solution)/shard_map/ppermute | solution.py:365
  39.3 14.9 %collective-permute-start.11 = (bf16[128,16,128]{2,1,0:T(8,128)(2,1)S(1)}, bf16[128,16,128]{2,1,0:T(8,128)(2,1)S(1)}, u32[]{:S(2)}, u32[]{:S(2)}) collective-permute-start(bf16[128,16,128]{2,1,0:T(8,128)(2,1)S(1)} %collective-permute-done.9), channel_id=1, source_target_pairs={{0,4},{1,5},{2,6},{3,7},{4,0},{5,1},{6,2},{7,3},{8,12},{9,13},{10,... | collective-permute-start | bytes 1572872 | tf_op jit(solution)/shard_map/ppermute | solution.py:365
  39.8 15.0 %collective-permute-start.10 = (bf16[128,16,128]{2,1,0:T(8,128)(2,1)S(1)}, bf16[128,16,128]{2,1,0:T(8,128)(2,1)S(1)}, u32[]{:S(2)}, u32[]{:S(2)}) collective-permute-start(bf16[128,16,128]{2,1,0:T(8,128)(2,1)S(1)} %collective-permute-done.9), channel_id=1, source_target_pairs={{0,2},{1,3},{2,0},{3,1},{4,6},{5,7},{6,4},{7,5},{8,10},{9,11},{10,... | collective-permute-start | bytes 1572872 | tf_op jit(solution)/shard_map/ppermute | solution.py:365
  41.2 24.2 %collective-permute-start.6 = (bf16[128,16,128]{2,1,0:T(8,128)(2,1)S(1)}, bf16[128,16,128]{2,1,0:T(8,128)(2,1)S(1)}, u32[]{:S(2)}, u32[]{:S(2)}) collective-permute-start(bf16[128,16,128]{2,1,0:T(8,128)(2,1)S(1)} %collective-permute-done.4), channel_id=1, source_target_pairs={{0,4},{1,5},{2,6},{3,7},{4,0},{5,1},{6,2},{7,3},{8,12},{9,13},{10,... | collective-permute-start | bytes 1572872 | tf_op jit(solution)/shard_map/ppermute | solution.py:365
  42.7 23.3 %collective-permute-start.5 = (bf16[128,16,128]{2,1,0:T(8,128)(2,1)S(1)}, bf16[128,16,128]{2,1,0:T(8,128)(2,1)S(1)}, u32[]{:S(2)}, u32[]{:S(2)}) collective-permute-start(bf16[128,16,128]{2,1,0:T(8,128)(2,1)S(1)} %collective-permute-done.4), channel_id=1, source_target_pairs={{0,2},{1,3},{2,0},{3,1},{4,6},{5,7},{6,4},{7,5},{8,10},{9,11},{10,... | collective-permute-start | bytes 1572872 | tf_op jit(solution)/shard_map/ppermute | solution.py:365
  54.2 20.3 %collective-permute-start.13 = (bf16[64,16,128]{2,1,0:T(8,128)(2,1)S(1)}, bf16[64,16,128]{2,1,0:T(8,128)(2,1)S(1)}, u32[]{:S(2)}, u32[]{:S(2)}) collective-permute-start(bf16[64,16,128]{2,1,0:T(8,128)(2,1)S(1)} %slice.52), channel_id=1, source_target_pairs={{0,2},{1,3},{2,0},{3,1},{4,6},{5,7},{6,4},{7,5},{8,10},{9,11},{10,... | collective-permute-start | bytes 786440 | tf_op jit(solution)/shard_map/ppermute | solution.py:365
  54.8 17.5 %collective-permute-start.12 = (bf16[64,16,128]{2,1,0:T(8,128)(2,1)S(1)}, bf16[64,16,128]{2,1,0:T(8,128)(2,1)S(1)}, u32[]{:S(2)}, u32[]{:S(2)}) collective-permute-start(bf16[64,16,128]{2,1,0:T(8,128)(2,1)S(1)} %slice.51), channel_id=1, source_target_pairs={{0,4},{1,5},{2,6},{3,7},{4,0},{5,1},{6,2},{7,3},{8,12},{9,13},{10,... | collective-permute-start | bytes 786440 | tf_op jit(solution)/shard_map/ppermute | solution.py:365
  65.4 11.9 %collective-permute-start.8 = (bf16[64,16,128]{2,1,0:T(8,128)(2,1)S(1)}, bf16[64,16,128]{2,1,0:T(8,128)(2,1)S(1)}, u32[]{:S(2)}, u32[]{:S(2)}) collective-permute-start(bf16[64,16,128]{2,1,0:T(8,128)(2,1)S(1)} %slice.50), channel_id=1, source_target_pairs={{0,2},{1,3},{2,0},{3,1},{4,6},{5,7},{6,4},{7,5},{8,10},{9,11},{10,... | collective-permute-start | bytes 786440 | tf_op jit(solution)/shard_map/ppermute | solution.py:365
  66.1 10.6 %collective-permute-start.7 = (bf16[64,16,128]{2,1,0:T(8,128)(2,1)S(1)}, bf16[64,16,128]{2,1,0:T(8,128)(2,1)S(1)}, u32[]{:S(2)}, u32[]{:S(2)}) collective-permute-start(bf16[64,16,128]{2,1,0:T(8,128)(2,1)S(1)} %slice.49), channel_id=1, source_target_pairs={{0,4},{1,5},{2,6},{3,7},{4,0},{5,1},{6,2},{7,3},{8,12},{9,13},{10,... | collective-permute-start | bytes 786440 | tf_op jit(solution)/shard_map/ppermute | solution.py:365
  67.5 19.7 %collective-permute-start.15 = (bf16[128,16,128]{2,1,0:T(8,128)(2,1)S(1)}, bf16[128,16,128]{2,1,0:T(8,128)(2,1)S(1)}, u32[]{:S(2)}, u32[]{:S(2)}) collective-permute-start(bf16[128,16,128]{2,1,0:T(8,128)(2,1)S(1)} %collective-permute-done.14), channel_id=1, source_target_pairs={{0,2},{1,3},{2,0},{3,1},{4,6},{5,7},{6,4},{7,5},{8,10},{9,11},{10,... | collective-permute-start | bytes 1572872 | tf_op jit(solution)/shard_map/ppermute | solution.py:365
  72.3 16.4 %collective-permute-start.16 = (bf16[128,16,128]{2,1,0:T(8,128)(2,1)S(1)}, bf16[128,16,128]{2,1,0:T(8,128)(2,1)S(1)}, u32[]{:S(2)}, u32[]{:S(2)}) collective-permute-start(bf16[128,16,128]{2,1,0:T(8,128)(2,1)S(1)} %collective-permute-done.14), channel_id=1, source_target_pairs={{0,4},{1,5},{2,6},{3,7},{4,0},{5,1},{6,2},{7,3},{8,12},{9,13},{10,... | collective-permute-start | bytes 1572872 | tf_op jit(solution)/shard_map/ppermute | solution.py:365
  74.5 28.5 %collective-permute-start.19 = (bf16[512,16,128]{2,1,0:T(8,128)(2,1)}, bf16[512,16,128]{2,1,0:T(8,128)(2,1)}, u32[]{:S(2)}, u32[]{:S(2)}) collective-permute-start(bf16[512,16,128]{2,1,0:T(8,128)(2,1)} %constant_dynamic-update-slice_fusion.refs_0_), channel_id=1, source_target_pairs={{0,1},{1,0},{2,3},{3,2},{4,5},{5,4},{6,7},{7,6},{8,9},{9,8},{10,11... | collective-permute-start | bytes 6291464 | tf_op jit(solution)/shard_map/ppermute | solution.py:365
  76.7 26.3 %collective-permute-start.21 = (bf16[512,16,128]{2,1,0:T(8,128)(2,1)}, bf16[512,16,128]{2,1,0:T(8,128)(2,1)}, u32[]{:S(2)}, u32[]{:S(2)}) collective-permute-start(bf16[512,16,128]{2,1,0:T(8,128)(2,1)} %constant_dynamic-update-slice_fusion.10.refs_2_), channel_id=1, source_target_pairs={{0,1},{1,0},{2,3},{3,2},{4,5},{5,4},{6,7},{7,6},{8,9},{9,8},{10,11... | collective-permute-start | bytes 6291464 | tf_op jit(solution)/shard_map/ppermute | solution.py:365
  78.1 24.9 %collective-permute-start.20 = (bf16[512,16,128]{2,1,0:T(8,128)(2,1)}, bf16[512,16,128]{2,1,0:T(8,128)(2,1)}, u32[]{:S(2)}, u32[]{:S(2)}) collective-permute-start(bf16[512,16,128]{2,1,0:T(8,128)(2,1)} %constant_dynamic-update-slice_fusion.5.refs_1_), channel_id=1, source_target_pairs={{0,1},{1,0},{2,3},{3,2},{4,5},{5,4},{6,7},{7,6},{8,9},{9,8},{10,11... | collective-permute-start | bytes 6291464 | tf_op jit(solution)/shard_map/ppermute | solution.py:365
  87.3 7.3 %collective-permute-start.17 = (bf16[64,16,128]{2,1,0:T(8,128)(2,1)S(1)}, bf16[64,16,128]{2,1,0:T(8,128)(2,1)S(1)}, u32[]{:S(2)}, u32[]{:S(2)}) collective-permute-start(bf16[64,16,128]{2,1,0:T(8,128)(2,1)S(1)} %slice.53), channel_id=1, source_target_pairs={{0,4},{1,5},{2,6},{3,7},{4,0},{5,1},{6,2},{7,3},{8,12},{9,13},{10,... | collective-permute-start | bytes 786440 | tf_op jit(solution)/shard_map/ppermute | solution.py:365
  89.5 13.5 %collective-permute-start.22 = (bf16[384,16,128]{2,1,0:T(8,128)(2,1)}, bf16[384,16,128]{2,1,0:T(8,128)(2,1)}, u32[]{:S(2)}, u32[]{:S(2)}) collective-permute-start(bf16[384,16,128]{2,1,0:T(8,128)(2,1)} %constant_dynamic-update-slice_fusion.15.refs_3_), channel_id=1, source_target_pairs={{0,1},{1,0},{2,3},{3,2},{4,5},{5,4},{6,7},{7,6},{8,9},{9,8},{10,11... | collective-permute-start | bytes 4718600 | tf_op jit(solution)/shard_map/ppermute | solution.py:365
  94.6 6.4 %collective-permute-start.18 = (bf16[64,16,128]{2,1,0:T(8,128)(2,1)S(1)}, bf16[64,16,128]{2,1,0:T(8,128)(2,1)S(1)}, u32[]{:S(2)}, u32[]{:S(2)}) collective-permute-start(bf16[64,16,128]{2,1,0:T(8,128)(2,1)S(1)} %slice.54), channel_id=1, source_target_pairs={{0,2},{1,3},{2,0},{3,1},{4,6},{5,7},{6,4},{7,5},{8,10},{9,11},{10,... | collective-permute-start | bytes 786440 | tf_op jit(solution)/shard_map/ppermute | solution.py:365
  101.0 2.0 copy-start.6
  101.0 2.0 collective-permute-start.23
  151.3 78.3 %collective-permute-start.26 = (f32[256,512]{1,0:T(8,128)}, f32[256,512]{1,0:T(8,128)S(1)}, u32[]{:S(2)}, u32[]{:S(2)}) collective-permute-start(f32[256,512]{1,0:T(8,128)} %get-tuple-element.17.refs_0_), channel_id=1, source_target_pairs={{0,24},{8,16},{16,8},{24,0},{1,25},{9,17},{17,9},{25,1},{2,26},{10... | collective-permute-start | bytes 1572872 | tf_op jit(solution)/shard_map/ppermute | solution.py:435
  151.3 78.3 %collective-permute-start.25 = (f32[256,512]{1,0:T(8,128)}, f32[256,512]{1,0:T(8,128)S(1)}, u32[]{:S(2)}, u32[]{:S(2)}) collective-permute-start(f32[256,512]{1,0:T(8,128)} %get-tuple-element.17.refs_0_), channel_id=1, source_target_pairs={{0,16},{8,24},{16,0},{24,8},{1,17},{9,25},{17,1},{25,9},{2,18},{10... | collective-permute-start | bytes 1572872 | tf_op jit(solution)/shard_map/ppermute | solution.py:435
  152.0 77.6 %collective-permute-start.24 = (f32[256,512]{1,0:T(8,128)}, f32[256,512]{1,0:T(8,128)S(1)}, u32[]{:S(2)}, u32[]{:S(2)}) collective-permute-start(f32[256,512]{1,0:T(8,128)} %get-tuple-element.17.refs_0_), channel_id=1, source_target_pairs={{0,8},{8,0},{16,24},{24,16},{1,9},{9,1},{17,25},{25,17},{2,10},{10... | collective-permute-start | bytes 1572872 | tf_op jit(solution)/shard_map/ppermute | solution.py:435
  155.7 74.0 %copy-start = (f32[256,512]{1,0:T(8,128)S(1)}, f32[256,512]{1,0:T(8,128)}, u32[]{:S(2)}) copy-start(f32[256,512]{1,0:T(8,128)} %get-tuple-element.17.refs_0_) | copy-start | bytes 1572868
  (6 other events, 8.3 us)
Sparse Core Ops, SparseCore 0:
  151.4 33.0 all-gather.2

commit v7 on v6

--- a/solution.py
+++ b/solution.py
@@ -17,6 +17,7 @@
 rank_signs = (1.0, 1.0, -1.0, -1.0)
 NT = ((1,), (1,))
 NN = ((1,), (0,))
+TN = ((0,), (0,))
 VMEM = pl.BlockSpec(memory_space=pltpu.VMEM)
 SMEM = pl.BlockSpec(memory_space=pltpu.SMEM)
 
@@ -174,11 +175,13 @@
     for m in range(count):
         beside(m)
         head_a, head_v = rows_a[m], rows_v[m]
-        below = [[spread_lane(rows_a[i], SUB * m + k) for k in range(SUB)] for i in range(m + 1, count)]
-        ahead, coming = [], []
-        if m + 1 < count:
+        more = m + 1 < count
+        below, ahead, coming = [], [], []
+        if more:
+            next_a, next_v = rows_a[m + 1], rows_v[m + 1]
+            below = [spread_lane(next_a, SUB * m + k) for k in range(SUB)]
             ahead = [spread_lane(head_a, SUB * (m + 1) + k) for k in range(SUB)]
-            coming = [spread_lane(rows_a[m + 1], SUB * (m + 1) + k) for k in range(SUB)]
+            coming = [spread_lane(next_a, SUB * (m + 1) + k) for k in range(SUB)]
         scale = jnp.zeros((SUB, BLK), jnp.float32)
         for j in range(SUB):
             pivot = spread_row(cols[j], j)
@@ -195,20 +198,34 @@
                 head_a = head_a - mult * row_a
                 head_v = head_v - mult * row_v
                 ahead = [value - mult * row for value, row in zip(ahead, row_ahead)]
-            for n, i in enumerate(range(m + 1, count)):
-                mult_i = below[n][j] * root
+            if more:
+                mult_next = below[j] * root
                 for k in range(j + 1, SUB):
-                    below[n][k] = below[n][k] - mult_i * lead[k]
-                if n == 0:
-                    coming = [value - mult_i * row for value, row in zip(coming, row_ahead)]
-                rows_a[i] = rows_a[i] - mult_i * row_a
-                rows_v[i] = rows_v[i] - mult_i * row_v
-        u_ref[SUB * m:SUB * (m + 1), :] = jnp.where(lane_iota >= sub_iota + SUB * m, head_a * scale, 0.0)
-        v_ref[SUB * m:SUB * (m + 1), :] = jnp.where(lane_iota <= sub_iota + SUB * m, head_v * scale, 0.0)
+                    below[k] = below[k] - mult_next * lead[k]
+                coming = [value - mult_next * row for value, row in zip(coming, row_ahead)]
+                next_a = next_a - mult_next * row_a
+                next_v = next_v - mult_next * row_v
+        u = jnp.where(lane_iota >= sub_iota + SUB * m, head_a * scale, 0.0)
+        v = jnp.where(lane_iota <= sub_iota + SUB * m, head_v * scale, 0.0)
+        u_ref[SUB * m:SUB * (m + 1), :] = u
+        v_ref[SUB * m:SUB * (m + 1), :] = v
+        if more:
+            rows_a[m + 1], rows_v[m + 1] = next_a, next_v
+        if m + 2 < count:
+            both = jnp.concatenate([u, v], axis=1)
+            u_hi, both_hi = u.astype(jnp.bfloat16).astype(jnp.float32), both.astype(jnp.bfloat16).astype(jnp.float32)
+            u_lo, both_lo = u - u_hi, both - both_hi
+            left = jnp.concatenate([u_hi, u_hi, u_lo, u_lo], axis=0).astype(jnp.bfloat16)
+            right = jnp.concatenate([both_hi, both_lo, both_hi, both_lo], axis=0).astype(jnp.bfloat16)
+            change = dot_bf16(left, right, TN)
+            for i in range(m + 2, count):
+                at = slice(SUB * i, SUB * (i + 1))
+                rows_a[i] = rows_a[i] - change[at, :BLK]
+                rows_v[i] = rows_v[i] - change[at, BLK:]
         cols = coming
 
 
-def factor_kernel(yx_ref, yz_ref, lh_ref, ll_ref, d_ref, w_ref, g_ref, u_ref, v_ref, gx_ref, gz_ref, px_ref, pz_ref):
+def factor_kernel(yx_ref, yz_ref, lh_ref, ll_ref, d_ref, w_ref, g_ref, u_ref, v_ref, gx_ref, gz_ref):
     order = lh_ref.shape[0]
     steps = order // BLK
     tile = 2 * BLK
@@ -229,27 +246,13 @@
         top = pl.multiple_of(jnp.minimum(after * tile + (b % 2) * window, order - window), BLK)
         left = pl.ds(top, window)
         right = pl.ds(pl.multiple_of(after * tile, tile), tile)
-        pairs = RANK * RANK
-
-        def products(m):
+
+        def beside(m):
             q, r = m // RANK, m % RANK
-            px_ref[m % 2] = dot_bf16(yx_ref[r, left, :], yx_ref[q, right, :], NT)
-            pz_ref[m % 2] = dot_bf16(yz_ref[r, left, :], yz_ref[q, right, :], NT)
-
-        def add_up(m):
-            for first in range(0, window, CHUNK):
-                rows = pl.ds(pl.multiple_of(top + first, CHUNK), CHUNK)
-                total = g_ref[rows, :] if m > 0 else None
-                g_ref[rows, :] = signed(total, px_ref[m % 2, first:first + CHUNK, :] * pz_ref[m % 2, first:first + CHUNK, :], m // RANK, m % RANK)
-
-        def beside(m):
-            if m < pairs:
-                products(m)
-            if 0 < m <= pairs:
-                add_up(m - 1)
+            term = dot_bf16(yx_ref[r, left, :], yx_ref[q, right, :], NT) * dot_bf16(yz_ref[r, left, :], yz_ref[q, right, :], NT)
+            g_ref[left, :] = signed(g_ref[left, :] if m > 0 else None, term, q, r)
 
         factor_block(w_ref[at, at], u_ref, v_ref, beside)
-        add_up(pairs - 1)
         lh_ref[at, at], ll_ref[at, at] = split(u_ref[...].T)
         d_ref[at, :] = v_ref[...]
         for k in range(steps - 1):
@@ -278,7 +281,7 @@
 
 
 def factor(yx, yz):
-    tile, window = 2 * BLK, 3 * BLK
+    tile = 2 * BLK
     f32 = jnp.float32
     return pl.pallas_call(
         factor_kernel,
@@ -286,24 +289,25 @@
         in_specs=[VMEM] * 2,
         out_specs=(VMEM,) * 3,
         scratch_shapes=[pltpu.VMEM((K, K), f32), pltpu.VMEM((K, tile), f32), pltpu.VMEM((BLK, BLK), f32), pltpu.VMEM((BLK, BLK), f32)]
-        + [pltpu.VMEM((2, RANK * tile, tile), f32)] * 2 + [pltpu.VMEM((2, window, tile), f32)] * 2,
-        compiler_params=pltpu.CompilerParams(vmem_limit_bytes=48 * MIB),
+        + [pltpu.VMEM((2, RANK * tile, tile), f32)] * 2,
+        compiler_params=pltpu.CompilerParams(vmem_limit_bytes=58 * MIB),
         cost_estimate=pl.CostEstimate(flops=40 * 10**9, bytes_accessed=12 * MIB, transcendentals=0),
     )(yx, yz)
 
 
-def solve_kernel(place_ref, lh, ll, d_ref, pieces_any, schur_any, *refs, prow):
+def solve_kernel(place_ref, lh_any, ll_any, d_any, pieces_any, schur_any, *refs, prow):
     top_refs, refs = refs[:prow], refs[prow:]
-    rest_ref, panel_ref, pieces_ref, tops_ref, schur_ref, xh, xl, zh, zl, sem_ref = refs
+    rest_ref, panel_ref, lh, ll, d_ref, pieces_ref, tops_ref, schur_ref, xh, xl, zh, zl, sem_ref = refs
     pcol = pieces_ref.shape[0]
     row, column = place_ref[0], place_ref[1]
-    tops = [pltpu.make_async_copy(ref, tops_ref.at[turn ^ row], sem_ref.at[turn]) for turn, ref in enumerate(top_refs)]
-    pieces = pltpu.make_async_copy(pieces_any, pieces_ref, sem_ref.at[prow])
-    schur = pltpu.make_async_copy(schur_any, schur_ref, sem_ref.at[prow + 1])
-    for copy in tops:
+    pairs = [(d_any, d_ref), (lh_any, lh), (ll_any, ll)]
+    pairs += [(ref, tops_ref.at[turn ^ row]) for turn, ref in enumerate(top_refs)]
+    pairs += [(pieces_any, pieces_ref), (schur_any, schur_ref)]
+    copies = [pltpu.make_async_copy(here, there, sem_ref.at[n]) for n, (here, there) in enumerate(pairs)]
+    for copy in copies:
         copy.start()
-    pieces.start()
-    schur.start()
+    for copy in copies[:3]:
+        copy.wait()
     wide = 2 * BLK
     inverses = []
     for b in range(K // wide):
@@ -314,29 +318,26 @@
         inverses.append(split(jnp.concatenate([
             jnp.concatenate([d_ref[upper, :], jnp.zeros((BLK, BLK), jnp.float32)], axis=1),
             jnp.concatenate([corner, d_ref[lower, :]], axis=1)], axis=0)))
-    for copy in tops:
+    for copy in copies[3:-1]:
         copy.wait()
     for b in range(K // wide):
         at, done = slice(b * wide, (b + 1) * wide), slice(0, b * wide)
         blocks = range(wide // NB * b, wide // NB * (b + 1))
+        value = jnp.concatenate([pieces_ref[n % pcol, :, n // pcol * NB:(n // pcol + 1) * NB] for n in blocks], axis=1)
         top = jnp.concatenate([tops_ref[n % prow, n // prow * NB:(n // prow + 1) * NB, :] for n in blocks], axis=0)
         if b > 0:
-            top = top - dot3((lh[at, done], ll[at, done]), (zh[done, :], zl[done, :]), NN)
-        zh[at, :], zl[at, :] = split(dot3(inverses[b], split(top), NN))
-    pieces.wait()
-    for b in range(K // wide):
-        at, done = slice(b * wide, (b + 1) * wide), slice(0, b * wide)
-        blocks = range(wide // NB * b, wide // NB * (b + 1))
-        value = jnp.concatenate([pieces_ref[n % pcol, :, n // pcol * NB:(n // pcol + 1) * NB] for n in blocks], axis=1)
-        if b > 0:
-            value = value - dot3((xh[:, done], xl[:, done]), (lh[at, done], ll[at, done]), NT)
+            left = (lh[at, done], ll[at, done])
+            value = value - dot3((xh[:, done], xl[:, done]), left, NT)
+            top = top - dot3(left, (zh[done, :], zl[done, :]), NN)
         value = dot3(split(value), inverses[b], NT)
+        top = dot3(inverses[b], split(top), NN)
         xh[:, at], xl[:, at] = split(value)
+        zh[at, :], zl[at, :] = split(top)
         for place, block in enumerate(blocks):
             @pl.when(column == block % pcol)
             def _():
                 panel_ref[:, block // pcol * NB:(block // pcol + 1) * NB] = value[:, place * NB:(place + 1) * NB]
-    schur.wait()
+    copies[-1].wait()
     rest_ref[...] = schur_ref[...] - dot3((xh[...], xl[...]), (zh[...], zl[...]), NN)
 
 
@@ -348,11 +349,12 @@
     return pl.pallas_call(
         functools.partial(solve_kernel, prow=len(tops)),
         out_shape=(jax.ShapeDtypeStruct((rows, cols), f32), jax.ShapeDtypeStruct((rows, lead), f32)),
-        in_specs=[SMEM] + [VMEM] * 3 + [any_space] * (2 + len(tops)),
+        in_specs=[SMEM] + [any_space] * (5 + len(tops)),
         out_specs=(VMEM, VMEM),
-        scratch_shapes=[pltpu.VMEM(pieces.shape, f32), pltpu.VMEM((len(tops),) + tops[0].shape, f32), pltpu.VMEM(schur.shape, f32)]
-        + [pltpu.VMEM((rows, K), bf16)] * 2 + [pltpu.VMEM((K, cols), bf16)] * 2 + [pltpu.SemaphoreType.DMA((len(tops) + 2,))],
-        compiler_params=pltpu.CompilerParams(vmem_limit_bytes=44 * MIB),
+        scratch_shapes=[pltpu.VMEM((K, K), bf16)] * 2 + [pltpu.VMEM((K, BLK), f32), pltpu.VMEM(pieces.shape, f32)]
+        + [pltpu.VMEM((len(tops),) + tops[0].shape, f32), pltpu.VMEM(schur.shape, f32)]
+        + [pltpu.VMEM((rows, K), bf16)] * 2 + [pltpu.VMEM((K, cols), bf16)] * 2 + [pltpu.SemaphoreType.DMA((len(tops) + 5,))],
+        compiler_params=pltpu.CompilerParams(vmem_limit_bytes=58 * MIB),
         cost_estimate=pl.CostEstimate(flops=12 * 10**9, bytes_accessed=24 * MIB, transcendentals=0),
     )(place, high, low, inverses, pieces, schur, *tops)
 
@@ -364,32 +366,34 @@
     def swap(axis, count, turn, value):
         return lax.ppermute(value, axis, [(n, n ^ turn) for n in range(count)])
 
+    def after(value, *others):
+        return lax.optimization_barrier((value, *others))[0]
+
+    span = pcol_count // 2
     items = {0: mine}
+    order = [0] + list(range(1, prow_count, 2)) + list(range(2, prow_count, 2))
     for turn in range(1, prow_count, 2):
         items[turn] = swap("prow", prow_count, turn, mine)
-    for turn in range(2, prow_count, 2):
-        items[turn] = swap("prow", prow_count, 1, items[turn + 1])
-    near, far, near_order, far_order = [], [], [], []
-    groups = [[0]] + [[m] for m in range(1, prow_count, 2)] + [[m] for m in range(2, prow_count, 2)]
-    for n, group in enumerate(groups):
-        value = jnp.concatenate([items[m] for m in group]) if len(group) > 1 else items[group[0]]
-        middle = len(group) * half
+    near, far, near_order, far_order, begun = [], [], [], [], []
+    for turn in order:
+        if turn not in items:
+            items[turn] = swap("prow", prow_count, 1, after(items[turn + 1], *begun[1]))
+        value, last = items[turn], turn == order[-1]
         held = {0: value}
-        for j in range(1, pcol_count // 2):
+        for j in range(1, span):
             low = j & -j
             high = 1 << (j.bit_length() - 1)
-            if low == high:
+            if low == high or last:
                 held[j] = swap("pcol", pcol_count, 2 * j, value)
             else:
-                held[j] = jnp.concatenate([swap("pcol", pcol_count, 2 * high, held[j ^ high][:middle]), swap("pcol", pcol_count, 2 * low, held[j ^ low][middle:])])
-        direct = [j for j in held if j & (j - 1) == 0]
-        relayed = [j for j in held if j & (j - 1) != 0]
-        for part in [direct, relayed] if n == len(groups) - 1 else [direct + relayed]:
+                held[j] = jnp.concatenate([swap("pcol", pcol_count, 2 * high, held[j ^ high][:half]), swap("pcol", pcol_count, 2 * low, held[j ^ low][half:])])
+        begun.append([held[j] for j in range(1, span) if j & (j - 1) == 0])
+        for part in [[j] for j in held] if last else [list(held)]:
             whole = jnp.concatenate([held[j] for j in part]) if len(part) > 1 else held[part[0]]
             near.append(whole)
-            near_order += [(m, 2 * j) for j in part for m in group]
+            near_order += [(turn, 2 * j) for j in part]
             far.append(swap("pcol", pcol_count, 1, whole))
-            far_order += [(m, 2 * j + 1) for j in part for m in group]
+            far_order += [(turn, 2 * j + 1) for j in part]
     return near + far, near_order + far_order
 
 

time: 263 us -> 258 us (0.981)
  waiting for transfers between devices: 44.7 us -> 58.1 us
  local copies, waits for them, and re-layouts: 25.4 us -> 17.1 us
  starting transfers between devices: 37.1 us -> 31.5 us
  Pallas kernels: 140 us -> 135 us
    ppermute x24 -> x25, waiting for transfers between devices: 44.7 us -> 58.1 us  [swap(): return lax.ppermute(value, axis, [(n, n ^ turn) for n in range(count)])]
    ppermute x24 -> x25, starting transfers between devices: 32.7 us -> 24 us  [swap(): return lax.ppermute(value, axis, [(n, n ^ turn) for n in range(count)])]
    unnamed x35 -> x30, local copies, waits for them, and re-layouts: 19.5 us -> 12.2 us
    ppermute x3, starting transfers between devices: 4.39 us -> 7.53 us  [per_device(): lax.ppermute(top, 'prow', [(n, n ^ turn) for n in range(prow_count)])]
    pallas_call x1, Pallas kernels: 71.2 us -> 68.2 us  [factor(): pl.pallas_call(factor_kernel, out_shape=(jax.ShapeDtypeStruct((K, K), jnp...]
  transfers between devices with their start and end apart: 28 -> 29, of which waited for: 9 -> 13; matrix products, arithmetic and copies ran while one was open for 6% -> 6% of each run, Pallas kernels for 27% -> 26%
where the time goes in v7:
time: 258 us
  Pallas kernels  135 us (52%)
  waiting for transfers between devices  58.1 us (23%)
  starting transfers between devices  31.5 us (12%)
  local copies, waits for them, and re-layouts  17.1 us (7%)
  between operations  14.3 us (6%)
    pallas_call x1, Pallas kernels, factor(): pl.pallas_call(factor_kernel, out_shape=(jax.ShapeDtypeStruct((K, K), jnp...  68.2 us
    ppermute x25, waiting for transfers between devices, swap(): return lax.ppermute(value, axis, [(n, n ^ turn) for n in range(count)])  58.1 us
    pallas_call x1, Pallas kernels, assemble(): pl.pallas_call(body, grid=(pick_tiles + row_tiles * col_tiles,), out_shap...  47.5 us
    ppermute x25, starting transfers between devices, swap(): return lax.ppermute(value, axis, [(n, n ^ turn) for n in range(count)])  24 us
    pallas_call x1, Pallas kernels, solve(): pl.pallas_call(functools.partial(solve_kernel, prow=len(tops)), out_shape...  19.2 us
    unnamed x30, local copies, waits for them, and re-layouts  12.2 us
    ppermute x3, starting transfers between devices, per_device(): lax.ppermute(top, 'prow', [(n, n ^ turn) for n in range(prow_count)])  7.53 us
  transfers between devices with their start and end apart: 29, of which 13 were waited for; matrix products, arithmetic and copies ran while one was open for 6% of the time, Pallas kernels for 26%

profile of v7, /device:TPU:0, one launch (start us, length us, event | category | flops | bytes accessed | tf_op | source)
XLA Modules:
  0.0 257.7 jit_solution(42231500931896006)
XLA Ops:
  7.2 1.4 copy.19
  8.9 3.1 %collective-permute-start.4 = (bf16[128,16,128]{2,1,0:T(8,128)(2,1)S(1)}, bf16[128,16,128]{2,1,0:T(8,128)(2,1)S(1)}, u32[]{:S(2)}, u32[]{:S(2)}) collective-permute-start(bf16[128,16,128]{2,1,0:T(8,128)(2,1)S(1)} %reshape.177), channel_id=1, source_target_pairs={{0,8},{8,0},{16,24},{24,16},{1,9},{9,1},{17,25},{25,17},{2,10},{10... | collective-permute-start | bytes 1572872 | tf_op jit(solution)/shard_map/ppermute | solution.py:367
  12.0 1.5 collective-permute-start
  13.5 2.5 collective-permute-start.9
  15.9 1.5 collective-permute-start.1
  17.5 6.8 %collective-permute-done.4 = bf16[128,16,128]{2,1,0:T(8,128)(2,1)S(1)} collective-permute-done((bf16[128,16,128]{2,1,0:T(8,128)(2,1)S(1)}, bf16[128,16,128]{2,1,0:T(8,128)(2,1)S(1)}, u32[]{:S(2)}, u32[]{:S(2)}) %collective-permute-start.4) | collective-permute-done | bytes 524320 | tf_op jit(solution)/shard_map/ppermute | solution.py:367
  24.3 1.5 collective-permute-start.6
  25.8 0.8 constant_dynamic-update-slice_fusion.4
  26.7 1.5 collective-permute-start.5
  28.9 8.5 %collective-permute-done.9 = bf16[128,16,128]{2,1,0:T(8,128)(2,1)S(1)} collective-permute-done((bf16[128,16,128]{2,1,0:T(8,128)(2,1)S(1)}, bf16[128,16,128]{2,1,0:T(8,128)(2,1)S(1)}, u32[]{:S(2)}, u32[]{:S(2)}) %collective-permute-start.9) | collective-permute-done | bytes 524320 | tf_op jit(solution)/shard_map/ppermute | solution.py:367
  37.4 1.5 collective-permute-start.11
  38.9 0.8 constant_dynamic-update-slice_fusion.9
  39.8 1.5 collective-permute-start.10
  42.7 0.8 constant_dynamic-update-slice_fusion.3
  43.5 0.8 constant_dynamic-update-slice_fusion.2
  44.4 1.8 collective-permute-start.14
  46.2 1.5 collective-permute-done.2
  48.4 9.5 %collective-permute-done.3 = bf16[64,16,128]{2,1,0:T(8,128)(2,1)S(1)} collective-permute-done((bf16[64,16,128]{2,1,0:T(8,128)(2,1)S(1)}, bf16[64,16,128]{2,1,0:T(8,128)(2,1)S(1)}, u32[]{:S(2)}, u32[]{:S(2)}) %collective-permute-start.3) | collective-permute-done | bytes 262176 | tf_op jit(solution)/shard_map/ppermute | solution.py:367
  58.6 1.6 collective-permute-start.13
  60.8 1.6 collective-permute-start.7
  62.4 0.8 constant_dynamic-update-slice_fusion.8
  63.2 0.8 constant_dynamic-update-slice_fusion.7
  64.0 0.9 constant_dynamic-update-slice_fusion.13
  65.7 3.7 %collective-permute-done.12 = bf16[64,16,128]{2,1,0:T(8,128)(2,1)S(1)} collective-permute-done((bf16[64,16,128]{2,1,0:T(8,128)(2,1)S(1)}, bf16[64,16,128]{2,1,0:T(8,128)(2,1)S(1)}, u32[]{:S(2)}, u32[]{:S(2)}) %collective-permute-start.12) | collective-permute-done | bytes 262176 | tf_op jit(solution)/shard_map/ppermute | solution.py:367
  71.4 2.9 %collective-permute-done.7 = bf16[64,16,128]{2,1,0:T(8,128)(2,1)S(1)} collective-permute-done((bf16[64,16,128]{2,1,0:T(8,128)(2,1)S(1)}, bf16[64,16,128]{2,1,0:T(8,128)(2,1)S(1)}, u32[]{:S(2)}, u32[]{:S(2)}) %collective-permute-start.7) | collective-permute-done | bytes 262176 | tf_op jit(solution)/shard_map/ppermute | solution.py:367
  77.9 11.7 %collective-permute-done.17.refs_6_ = bf16[128,16,128]{2,1,0:T(8,128)(2,1)} collective-permute-done((bf16[128,16,128]{2,1,0:T(8,128)(2,1)}, bf16[128,16,128]{2,1,0:T(8,128)(2,1)}, u32[]{:S(2)}, u32[]{:S(2)}) %collective-permute-start.17) | collective-permute-done | bytes 524320 | tf_op jit(solution)/shard_map/ppermute | solution.py:367
  90.1 9.9 %collective-permute-done.16.refs_5_ = bf16[128,16,128]{2,1,0:T(8,128)(2,1)} collective-permute-done((bf16[128,16,128]{2,1,0:T(8,128)(2,1)}, bf16[128,16,128]{2,1,0:T(8,128)(2,1)}, u32[]{:S(2)}, u32[]{:S(2)}) %collective-permute-start.16) | collective-permute-done | bytes 524320 | tf_op jit(solution)/shard_map/ppermute | solution.py:367
  100.7 1.5 collective-permute-done.15.refs_4_
  106.6 47.5 %shard_map.68 = (bf16[4,1024,512]{2,1,0:T(8,128)(2,1)}, bf16[4,1024,512]{2,1,0:T(8,128)(2,1)}, f32[1024,512]{1,0:T(8,128)}, f32[1024,128]{1,0:T(8,128)}, f32[256,512]{1,0:T(8,128)}) custom-call(s32[2560]{0:T(1024)} %reshape.176.slots_ref, bf16[512,512]{1,0:T(8,128)(2,1)} %x_ref.1, bf16[512,512]{1,0:T(8,128)(2,1)} %z_ref.1, ...), custom_call_target="tpu_custom_call" | custom-call | flops 28000000000 | bytes 31457280 | tf_op jit(solution)/shard_map/pallas_call | solution.py:142
  154.7 7.0 %collective-permute-start.27 = (f32[256,512]{1,0:T(8,128)}, f32[256,512]{1,0:T(8,128)S(1)}, u32[]{:S(2)}, u32[]{:S(2)}) collective-permute-start(f32[256,512]{1,0:T(8,128)} %get-tuple-element.19.refs_0_), channel_id=1, source_target_pairs={{0,24},{8,16},{16,8},{24,0},{1,25},{9,17},{17,9},{25,1},{2,26},{10... | collective-permute-start | bytes 1572872 | tf_op jit(solution)/shard_map/ppermute | solution.py:439
  162.3 68.2 %shard_map.69 = (bf16[1024,1024]{1,0:T(8,128)(2,1)}, bf16[1024,1024]{1,0:T(8,128)(2,1)}, f32[1024,128]{1,0:T(8,128)}) custom-call(bf16[4,1024,512]{2,1,0:T(8,128)(2,1)} %get-tuple-element.12.yx_ref, bf16[4,1024,512]{2,1,0:T(8,128)(2,1)} %get-tuple-element.13.yz_ref), custom_call_target="tpu_custom_call" | custom-call | flops 40000000000 | bytes 12582912 | tf_op jit(solution)/shard_map/pallas_call | solution.py:286
  231.6 19.2 %shard_map.70 = (f32[1024,512]{1,0:T(8,128)}, f32[1024,128]{1,0:T(8,128)}) custom-call(s32[2]{0:T(128)} %pad_add_fusion.1.place_ref, bf16[1024,1024]{1,0:T(8,128)(2,1)} %get-tuple-element.14.lh_any, bf16[1024,1024]{1,0:T(8,128)(2,1)} %get-tuple-element.15.ll_any, f32[1024,128]{1,0:T(8,128)} %get-tuple-element.16.d_any, f32[8,1024,128]{2,1,0:T(8,128)} %bitcast.51, ...), custom_call_target="tpu_custom_call" | custom-call | flops 12000000000 | bytes 25165824 | tf_op jit(solution)/shard_map/pallas_call | solution.py:349
  (87 shorter events, 18.7 us)
Async XLA Ops:
  7.2 21.0 %copy-start.8 = (s32[32]{0:T(128)S(1)}, s32[32]{0:T(128)}, u32[]{:S(2)}) copy-start(s32[32]{0:T(128)} %constant.92.clone) | copy-start | bytes 388
  7.2 223.4 %all-gather.3.cloned.1.call-start = ((), (), s32[]{:S(2)}) async-start(), calls=%async_computation | async-start | bytes 4718592 | tf_op jit(solution)/shard_map/all_gather | solution.py:438
  8.9 15.4 %collective-permute-start.4 = (bf16[128,16,128]{2,1,0:T(8,128)(2,1)S(1)}, bf16[128,16,128]{2,1,0:T(8,128)(2,1)S(1)}, u32[]{:S(2)}, u32[]{:S(2)}) collective-permute-start(bf16[128,16,128]{2,1,0:T(8,128)(2,1)S(1)} %reshape.177), channel_id=1, source_target_pairs={{0,8},{8,0},{16,24},{24,16},{1,9},{9,1},{17,25},{25,17},{2,10},{10... | collective-permute-start | bytes 1572872 | tf_op jit(solution)/shard_map/ppermute | solution.py:367
  12.0 16.4 %collective-permute-start = (bf16[128,16,128]{2,1,0:T(8,128)(2,1)S(1)}, bf16[128,16,128]{2,1,0:T(8,128)(2,1)S(1)}, u32[]{:S(2)}, u32[]{:S(2)}) collective-permute-start(bf16[128,16,128]{2,1,0:T(8,128)(2,1)S(1)} %reshape.177), channel_id=1, source_target_pairs={{0,2},{1,3},{2,0},{3,1},{4,6},{5,7},{6,4},{7,5},{8,10},{9,11},{10,... | collective-permute-start | bytes 1572872 | tf_op jit(solution)/shard_map/ppermute | solution.py:367
  13.5 24.0 %collective-permute-start.9 = (bf16[128,16,128]{2,1,0:T(8,128)(2,1)S(1)}, bf16[128,16,128]{2,1,0:T(8,128)(2,1)S(1)}, u32[]{:S(2)}, u32[]{:S(2)}) collective-permute-start(bf16[128,16,128]{2,1,0:T(8,128)(2,1)S(1)} %reshape.177), channel_id=1, source_target_pairs={{0,24},{8,16},{16,8},{24,0},{1,25},{9,17},{17,9},{25,1},{2,26},{10... | collective-permute-start | bytes 1572872 | tf_op jit(solution)/shard_map/ppermute | solution.py:367
  15.9 23.8 %collective-permute-start.1 = (bf16[128,16,128]{2,1,0:T(8,128)(2,1)S(1)}, bf16[128,16,128]{2,1,0:T(8,128)(2,1)S(1)}, u32[]{:S(2)}, u32[]{:S(2)}) collective-permute-start(bf16[128,16,128]{2,1,0:T(8,128)(2,1)S(1)} %reshape.177), channel_id=1, source_target_pairs={{0,4},{1,5},{2,6},{3,7},{4,0},{5,1},{6,2},{7,3},{8,12},{9,13},{10,... | collective-permute-start | bytes 1572872 | tf_op jit(solution)/shard_map/ppermute | solution.py:367
  24.3 17.8 %collective-permute-start.6 = (bf16[128,16,128]{2,1,0:T(8,128)(2,1)S(1)}, bf16[128,16,128]{2,1,0:T(8,128)(2,1)S(1)}, u32[]{:S(2)}, u32[]{:S(2)}) collective-permute-start(bf16[128,16,128]{2,1,0:T(8,128)(2,1)S(1)} %collective-permute-done.4), channel_id=1, source_target_pairs={{0,4},{1,5},{2,6},{3,7},{4,0},{5,1},{6,2},{7,3},{8,12},{9,13},{10,... | collective-permute-start | bytes 1572872 | tf_op jit(solution)/shard_map/ppermute | solution.py:367
  26.7 17.7 %collective-permute-start.5 = (bf16[128,16,128]{2,1,0:T(8,128)(2,1)S(1)}, bf16[128,16,128]{2,1,0:T(8,128)(2,1)S(1)}, u32[]{:S(2)}, u32[]{:S(2)}) collective-permute-start(bf16[128,16,128]{2,1,0:T(8,128)(2,1)S(1)} %collective-permute-done.4), channel_id=1, source_target_pairs={{0,2},{1,3},{2,0},{3,1},{4,6},{5,7},{6,4},{7,5},{8,10},{9,11},{10,... | collective-permute-start | bytes 1572872 | tf_op jit(solution)/shard_map/ppermute | solution.py:367
  28.4 19.3 %collective-permute-start.2 = (bf16[64,16,128]{2,1,0:T(8,128)(2,1)S(1)}, bf16[64,16,128]{2,1,0:T(8,128)(2,1)S(1)}, u32[]{:S(2)}, u32[]{:S(2)}) collective-permute-start(bf16[64,16,128]{2,1,0:T(8,128)(2,1)S(1)} %slice.39), channel_id=1, source_target_pairs={{0,4},{1,5},{2,6},{3,7},{4,0},{5,1},{6,2},{7,3},{8,12},{9,13},{10,... | collective-permute-start | bytes 786440 | tf_op jit(solution)/shard_map/ppermute | solution.py:367
  37.4 21.2 %collective-permute-start.11 = (bf16[128,16,128]{2,1,0:T(8,128)(2,1)S(1)}, bf16[128,16,128]{2,1,0:T(8,128)(2,1)S(1)}, u32[]{:S(2)}, u32[]{:S(2)}) collective-permute-start(bf16[128,16,128]{2,1,0:T(8,128)(2,1)S(1)} %collective-permute-done.9), channel_id=1, source_target_pairs={{0,4},{1,5},{2,6},{3,7},{4,0},{5,1},{6,2},{7,3},{8,12},{9,13},{10,... | collective-permute-start | bytes 1572872 | tf_op jit(solution)/shard_map/ppermute | solution.py:367
  39.8 20.4 %collective-permute-start.10 = (bf16[128,16,128]{2,1,0:T(8,128)(2,1)S(1)}, bf16[128,16,128]{2,1,0:T(8,128)(2,1)S(1)}, u32[]{:S(2)}, u32[]{:S(2)}) collective-permute-start(bf16[128,16,128]{2,1,0:T(8,128)(2,1)S(1)} %collective-permute-done.9), channel_id=1, source_target_pairs={{0,2},{1,3},{2,0},{3,1},{4,6},{5,7},{6,4},{7,5},{8,10},{9,11},{10,... | collective-permute-start | bytes 1572872 | tf_op jit(solution)/shard_map/ppermute | solution.py:367
  42.1 15.7 %collective-permute-start.3 = (bf16[64,16,128]{2,1,0:T(8,128)(2,1)S(1)}, bf16[64,16,128]{2,1,0:T(8,128)(2,1)S(1)}, u32[]{:S(2)}, u32[]{:S(2)}) collective-permute-start(bf16[64,16,128]{2,1,0:T(8,128)(2,1)S(1)} %slice.40), channel_id=1, source_target_pairs={{0,2},{1,3},{2,0},{3,1},{4,6},{5,7},{6,4},{7,5},{8,10},{9,11},{10,... | collective-permute-start | bytes 786440 | tf_op jit(solution)/shard_map/ppermute | solution.py:367
  44.4 20.5 %collective-permute-start.14 = (bf16[128,16,128]{2,1,0:T(8,128)(2,1)S(1)}, bf16[128,16,128]{2,1,0:T(8,128)(2,1)}, u32[]{:S(2)}, u32[]{:S(2)}) collective-permute-start(bf16[128,16,128]{2,1,0:T(8,128)(2,1)S(1)} %collective-permute-done.9), channel_id=1, source_target_pairs={{0,8},{8,0},{16,24},{24,16},{1,9},{9,1},{17,25},{25,17},{2,10},{10... | collective-permute-start | bytes 1572872 | tf_op jit(solution)/shard_map/ppermute | solution.py:367
  58.6 46.5 %collective-permute-start.18 = (bf16[512,16,128]{2,1,0:T(8,128)(2,1)}, bf16[512,16,128]{2,1,0:T(8,128)(2,1)}, u32[]{:S(2)}, u32[]{:S(2)}) collective-permute-start(bf16[512,16,128]{2,1,0:T(8,128)(2,1)} %constant_dynamic-update-slice_fusion.refs_0_), channel_id=1, source_target_pairs={{0,1},{1,0},{2,3},{3,2},{4,5},{5,4},{6,7},{7,6},{8,9},{9,8},{10,11... | collective-permute-start | bytes 6291464 | tf_op jit(solution)/shard_map/ppermute | solution.py:367
  58.6 12.0 %collective-permute-start.13 = (bf16[64,16,128]{2,1,0:T(8,128)(2,1)S(1)}, bf16[64,16,128]{2,1,0:T(8,128)(2,1)S(1)}, u32[]{:S(2)}, u32[]{:S(2)}) collective-permute-start(bf16[64,16,128]{2,1,0:T(8,128)(2,1)S(1)} %slice.44), channel_id=1, source_target_pairs={{0,2},{1,3},{2,0},{3,1},{4,6},{5,7},{6,4},{7,5},{8,10},{9,11},{10,... | collective-permute-start | bytes 786440 | tf_op jit(solution)/shard_map/ppermute | solution.py:367
  60.2 9.2 %collective-permute-start.12 = (bf16[64,16,128]{2,1,0:T(8,128)(2,1)S(1)}, bf16[64,16,128]{2,1,0:T(8,128)(2,1)S(1)}, u32[]{:S(2)}, u32[]{:S(2)}) collective-permute-start(bf16[64,16,128]{2,1,0:T(8,128)(2,1)S(1)} %slice.43), channel_id=1, source_target_pairs={{0,4},{1,5},{2,6},{3,7},{4,0},{5,1},{6,2},{7,3},{8,12},{9,13},{10,... | collective-permute-start | bytes 786440 | tf_op jit(solution)/shard_map/ppermute | solution.py:367
  60.8 13.5 %collective-permute-start.7 = (bf16[64,16,128]{2,1,0:T(8,128)(2,1)S(1)}, bf16[64,16,128]{2,1,0:T(8,128)(2,1)S(1)}, u32[]{:S(2)}, u32[]{:S(2)}) collective-permute-start(bf16[64,16,128]{2,1,0:T(8,128)(2,1)S(1)} %slice.41), channel_id=1, source_target_pairs={{0,4},{1,5},{2,6},{3,7},{4,0},{5,1},{6,2},{7,3},{8,12},{9,13},{10,... | collective-permute-start | bytes 786440 | tf_op jit(solution)/shard_map/ppermute | solution.py:367
  64.9 12.9 %copy-start = (s32[4096]{0:T(1024)S(1)}, s32[4096]{0:T(1024)}, u32[]{:S(2)}) copy-start(s32[4096]{0:T(1024)} %param.8) | copy-start | bytes 49156
  64.9 12.9 %collective-permute-start.21 = (bf16[128,16,128]{2,1,0:T(8,128)(2,1)}, bf16[128,16,128]{2,1,0:T(8,128)(2,1)S(1)}, u32[]{:S(2)}, u32[]{:S(2)}) collective-permute-start(bf16[128,16,128]{2,1,0:T(8,128)(2,1)} %collective-permute-done.14.refs_3_), channel_id=1, source_target_pairs={{0,1},{1,0},{2,3},{3,2},{4,5},{5,4},{6,7},{7,6},{8,9},{9,8},{10,11... | collective-permute-start | bytes 1572872 | tf_op jit(solution)/shard_map/ppermute | solution.py:367
  69.4 6.9 %collective-permute-start.8 = (bf16[64,16,128]{2,1,0:T(8,128)(2,1)S(1)}, bf16[64,16,128]{2,1,0:T(8,128)(2,1)S(1)}, u32[]{:S(2)}, u32[]{:S(2)}) collective-permute-start(bf16[64,16,128]{2,1,0:T(8,128)(2,1)S(1)} %slice.42), channel_id=1, source_target_pairs={{0,2},{1,3},{2,0},{3,1},{4,6},{5,7},{6,4},{7,5},{8,10},{9,11},{10,... | collective-permute-start | bytes 786440 | tf_op jit(solution)/shard_map/ppermute | solution.py:367
  71.4 33.7 %collective-permute-start.20 = (bf16[512,16,128]{2,1,0:T(8,128)(2,1)}, bf16[512,16,128]{2,1,0:T(8,128)(2,1)S(1)}, u32[]{:S(2)}, u32[]{:S(2)}) collective-permute-start(bf16[512,16,128]{2,1,0:T(8,128)(2,1)} %constant_dynamic-update-slice_fusion.10.refs_2_), channel_id=1, source_target_pairs={{0,1},{1,0},{2,3},{3,2},{4,5},{5,4},{6,7},{7,6},{8,9},{9,8},{10,11... | collective-permute-start | bytes 6291464 | tf_op jit(solution)/shard_map/ppermute | solution.py:367
  75.0 14.6 %collective-permute-start.17 = (bf16[128,16,128]{2,1,0:T(8,128)(2,1)}, bf16[128,16,128]{2,1,0:T(8,128)(2,1)}, u32[]{:S(2)}, u32[]{:S(2)}) collective-permute-start(bf16[128,16,128]{2,1,0:T(8,128)(2,1)} %collective-permute-done.14.refs_3_), channel_id=1, source_target_pairs={{0,6},{1,7},{2,4},{3,5},{4,2},{5,3},{6,0},{7,1},{8,14},{9,15},{10,... | collective-permute-start | bytes 1572872 | tf_op jit(solution)/shard_map/ppermute | solution.py:367
  76.3 23.7 %collective-permute-start.16 = (bf16[128,16,128]{2,1,0:T(8,128)(2,1)}, bf16[128,16,128]{2,1,0:T(8,128)(2,1)}, u32[]{:S(2)}, u32[]{:S(2)}) collective-permute-start(bf16[128,16,128]{2,1,0:T(8,128)(2,1)} %collective-permute-done.14.refs_3_), channel_id=1, source_target_pairs={{0,4},{1,5},{2,6},{3,7},{4,0},{5,1},{6,2},{7,3},{8,12},{9,13},{10,... | collective-permute-start | bytes 1572872 | tf_op jit(solution)/shard_map/ppermute | solution.py:367
  77.8 22.3 %copy-start.2 = (bf16[128,16,128]{2,1,0:T(8,128)(2,1)}, bf16[128,16,128]{2,1,0:T(8,128)(2,1)S(1)}, u32[]{:S(2)}) copy-start(bf16[128,16,128]{2,1,0:T(8,128)(2,1)S(1)} %collective-permute-done.21.refs_10_) | copy-start | bytes 1572868
  77.8 27.3 %collective-permute-start.19 = (bf16[512,16,128]{2,1,0:T(8,128)(2,1)}, bf16[512,16,128]{2,1,0:T(8,128)(2,1)}, u32[]{:S(2)}, u32[]{:S(2)}) collective-permute-start(bf16[512,16,128]{2,1,0:T(8,128)(2,1)} %constant_dynamic-update-slice_fusion.5.refs_1_), channel_id=1, source_target_pairs={{0,1},{1,0},{2,3},{3,2},{4,5},{5,4},{6,7},{7,6},{8,9},{9,8},{10,11... | collective-permute-start | bytes 6291464 | tf_op jit(solution)/shard_map/ppermute | solution.py:367
  89.6 12.6 %collective-permute-start.15 = (bf16[128,16,128]{2,1,0:T(8,128)(2,1)}, bf16[128,16,128]{2,1,0:T(8,128)(2,1)}, u32[]{:S(2)}, u32[]{:S(2)}) collective-permute-start(bf16[128,16,128]{2,1,0:T(8,128)(2,1)} %collective-permute-done.14.refs_3_), channel_id=1, source_target_pairs={{0,2},{1,3},{2,0},{3,1},{4,6},{5,7},{6,4},{7,5},{8,10},{9,11},{10,... | collective-permute-start | bytes 1572872 | tf_op jit(solution)/shard_map/ppermute | solution.py:367
  100.0 2.3 collective-permute-start.24
  102.2 2.1 collective-permute-start.23
  102.3 2.8 %collective-permute-start.22 = (bf16[128,16,128]{2,1,0:T(8,128)(2,1)}, bf16[128,16,128]{2,1,0:T(8,128)(2,1)S(1)}, u32[]{:S(2)}, u32[]{:S(2)}) collective-permute-start(bf16[128,16,128]{2,1,0:T(8,128)(2,1)} %collective-permute-done.15.refs_4_), channel_id=1, source_target_pairs={{0,1},{1,0},{2,3},{3,2},{4,5},{5,4},{6,7},{7,6},{8,9},{9,8},{10,11... | collective-permute-start | bytes 1572872 | tf_op jit(solution)/shard_map/ppermute | solution.py:367
  154.7 75.7 %collective-permute-start.27 = (f32[256,512]{1,0:T(8,128)}, f32[256,512]{1,0:T(8,128)S(1)}, u32[]{:S(2)}, u32[]{:S(2)}) collective-permute-start(f32[256,512]{1,0:T(8,128)} %get-tuple-element.19.refs_0_), channel_id=1, source_target_pairs={{0,24},{8,16},{16,8},{24,0},{1,25},{9,17},{17,9},{25,1},{2,26},{10... | collective-permute-start | bytes 1572872 | tf_op jit(solution)/shard_map/ppermute | solution.py:439
  161.7 68.8 %collective-permute-start.26 = (f32[256,512]{1,0:T(8,128)}, f32[256,512]{1,0:T(8,128)S(1)}, u32[]{:S(2)}, u32[]{:S(2)}) collective-permute-start(f32[256,512]{1,0:T(8,128)} %get-tuple-element.19.refs_0_), channel_id=1, source_target_pairs={{0,16},{8,24},{16,0},{24,8},{1,17},{9,25},{17,1},{25,9},{2,18},{10... | collective-permute-start | bytes 1572872 | tf_op jit(solution)/shard_map/ppermute | solution.py:439
  161.7 68.8 %collective-permute-start.25 = (f32[256,512]{1,0:T(8,128)}, f32[256,512]{1,0:T(8,128)S(1)}, u32[]{:S(2)}, u32[]{:S(2)}) collective-permute-start(f32[256,512]{1,0:T(8,128)} %get-tuple-element.19.refs_0_), channel_id=1, source_target_pairs={{0,8},{8,0},{16,24},{24,16},{1,9},{9,1},{17,25},{25,17},{2,10},{10... | collective-permute-start | bytes 1572872 | tf_op jit(solution)/shard_map/ppermute | solution.py:439
  (6 other events, 6.1 us)
Sparse Core Ops, SparseCore 0:
  154.2 39.4 all-gather.2

commit v8 on v7

--- a/solution.py
+++ b/solution.py
@@ -17,7 +17,6 @@
 rank_signs = (1.0, 1.0, -1.0, -1.0)
 NT = ((1,), (1,))
 NN = ((1,), (0,))
-TN = ((0,), (0,))
 VMEM = pl.BlockSpec(memory_space=pltpu.VMEM)
 SMEM = pl.BlockSpec(memory_space=pltpu.SMEM)
 
@@ -38,7 +37,7 @@
 
 def assemble_kernel(slots_ref, x_ref, z_ref, *refs, sources, lead_tiles, pick_tiles, col_tiles, rows):
     source_refs, refs = refs[:sources], refs[sources:]
-    lead_x_ref, lead_z_ref, schur_ref, front_ref, top_ref, every_ref, picked_ref, yx_ref, yz_ref, gx_ref, gz_ref, sem_ref = refs
+    lead_x_ref, lead_z_ref, schur_ref, front_ref, top_ref, every_ref, picked_ref, yx_ref, yz_ref, sem_ref = refs
     step = pl.program_id(0)
     tile, parts, lanes = picked_ref.shape
     width = x_ref.shape[0]
@@ -84,7 +83,7 @@
         i, j = (step - pick_tiles) // col_tiles, (step - pick_tiles) % col_tiles
         left = pl.ds(pl.multiple_of(i * high, high), high)
         right = pl.ds(pl.multiple_of(rows + j * wide, wide), wide)
-        gram_tile(yx_ref, yz_ref, left, right, schur_ref, gx_ref, gz_ref)
+        schur_ref[...] = gram_tile(yx_ref, yz_ref, left, right)
 
         @pl.when(j == 0)
         def _():
@@ -95,28 +94,18 @@
             top_ref[...] = schur_ref[:top_ref.shape[0], :]
 
 
-CHUNK = 32
-
-
-def gram_tile(yx_ref, yz_ref, left, right, out_ref, gx_ref, gz_ref):
+def gram_tile(yx_ref, yz_ref, left, right):
     left_x, left_z = yx_ref[:, left, :], yz_ref[:, left, :]
     _, high, width = left_x.shape
     left_x, left_z = left_x.reshape(RANK * high, width), left_z.reshape(RANK * high, width)
-
-    def products(q):
-        gx_ref[q % 2] = dot_bf16(left_x, yx_ref[q, right, :], NT)
-        gz_ref[q % 2] = dot_bf16(left_z, yz_ref[q, right, :], NT)
-
-    products(0)
+    total = None
     for q in range(RANK):
-        if q + 1 < RANK:
-            products(q + 1)
-        for first in range(0, high, CHUNK):
-            total = out_ref[first:first + CHUNK, :] if q > 0 else None
-            for r in range(RANK):
-                at = slice(r * high + first, r * high + first + CHUNK)
-                total = signed(total, gx_ref[q % 2, at, :] * gz_ref[q % 2, at, :], q, r)
-            out_ref[first:first + CHUNK, :] = total
+        gx = dot_bf16(left_x, yx_ref[q, right, :], NT)
+        gz = dot_bf16(left_z, yz_ref[q, right, :], NT)
+        for r in range(RANK):
+            term = gx[r * high:(r + 1) * high] * gz[r * high:(r + 1) * high]
+            total = signed(total, term, q, r)
+    return total
 
 
 def signed(total, term, q, r):
@@ -152,7 +141,7 @@
                    pl.BlockSpec((high, lead_cols), lambda s: (after(s) // col_tiles, 0)),
                    pl.BlockSpec((lead_rows, wide), lambda s: (0, jnp.minimum(after(s), col_tiles - 1)))),
         scratch_shapes=[pltpu.VMEM((slots_held, parts, lanes), bf16), pltpu.VMEM((tile, parts, lanes), bf16)]
-        + [pltpu.VMEM((RANK, rows + cols, width), bf16)] * 2 + [pltpu.VMEM((2, RANK * high, wide), jnp.float32)] * 2 + [pltpu.SemaphoreType.DMA((len(sources),))],
+        + [pltpu.VMEM((RANK, rows + cols, width), bf16)] * 2 + [pltpu.SemaphoreType.DMA((len(sources),))],
         compiler_params=pltpu.CompilerParams(vmem_limit_bytes=58 * MIB),
         cost_estimate=pl.CostEstimate(flops=28 * 10**9, bytes_accessed=30 * MIB, transcendentals=0),
     )(slots, x_factor, z_factor, *sources)
@@ -171,61 +160,38 @@
     def spread_row(x, row):
         return jnp.broadcast_to(x[row:row + 1, :], (SUB, BLK))
 
-    cols = [spread_lane(rows_a[0], k) for k in range(SUB)]
     for m in range(count):
         beside(m)
         head_a, head_v = rows_a[m], rows_v[m]
-        more = m + 1 < count
-        below, ahead, coming = [], [], []
-        if more:
-            next_a, next_v = rows_a[m + 1], rows_v[m + 1]
-            below = [spread_lane(next_a, SUB * m + k) for k in range(SUB)]
-            ahead = [spread_lane(head_a, SUB * (m + 1) + k) for k in range(SUB)]
-            coming = [spread_lane(next_a, SUB * (m + 1) + k) for k in range(SUB)]
+        cols = [spread_lane(head_a, SUB * m + k) for k in range(SUB)]
+        below = [[spread_lane(rows_a[i], SUB * m + k) for k in range(SUB)] for i in range(m + 1, count)]
         scale = jnp.zeros((SUB, BLK), jnp.float32)
         for j in range(SUB):
             pivot = spread_row(cols[j], j)
             root = lax.rsqrt(pivot)
             scale = jnp.where(sub_iota == j, root, scale)
-            mult = jnp.where(sub_iota > j, cols[j] * root, 0.0)
-            lead = [spread_row(cols[k], j) * root if k > j else None for k in range(SUB)]
+            mult = jnp.where(sub_iota > j, cols[j], 0.0) * root
             row_a = spread_row(head_a, j) * root
             row_v = spread_row(head_v, j) * root
-            row_ahead = [spread_row(value, j) * root for value in ahead]
+            lead = [spread_row(cols[k], j) * root if k > j else None for k in range(SUB)]
             if j + 1 < SUB:
+                head_a = head_a - mult * row_a
+                head_v = head_v - mult * row_v
                 for k in range(j + 1, SUB):
                     cols[k] = cols[k] - mult * lead[k]
-                head_a = head_a - mult * row_a
-                head_v = head_v - mult * row_v
-                ahead = [value - mult * row for value, row in zip(ahead, row_ahead)]
-            if more:
-                mult_next = below[j] * root
+            for n, i in enumerate(range(m + 1, count)):
+                mult_i = below[n][j] * root
+                rows_a[i] = rows_a[i] - mult_i * row_a
+                rows_v[i] = rows_v[i] - mult_i * row_v
                 for k in range(j + 1, SUB):
-                    below[k] = below[k] - mult_next * lead[k]
-                coming = [value - mult_next * row for value, row in zip(coming, row_ahead)]
-                next_a = next_a - mult_next * row_a
-                next_v = next_v - mult_next * row_v
+                    below[n][k] = below[n][k] - mult_i * lead[k]
         u = jnp.where(lane_iota >= sub_iota + SUB * m, head_a * scale, 0.0)
         v = jnp.where(lane_iota <= sub_iota + SUB * m, head_v * scale, 0.0)
         u_ref[SUB * m:SUB * (m + 1), :] = u
         v_ref[SUB * m:SUB * (m + 1), :] = v
-        if more:
-            rows_a[m + 1], rows_v[m + 1] = next_a, next_v
-        if m + 2 < count:
-            both = jnp.concatenate([u, v], axis=1)
-            u_hi, both_hi = u.astype(jnp.bfloat16).astype(jnp.float32), both.astype(jnp.bfloat16).astype(jnp.float32)
-            u_lo, both_lo = u - u_hi, both - both_hi
-            left = jnp.concatenate([u_hi, u_hi, u_lo, u_lo], axis=0).astype(jnp.bfloat16)
-            right = jnp.concatenate([both_hi, both_lo, both_hi, both_lo], axis=0).astype(jnp.bfloat16)
-            change = dot_bf16(left, right, TN)
-            for i in range(m + 2, count):
-                at = slice(SUB * i, SUB * (i + 1))
-                rows_a[i] = rows_a[i] - change[at, :BLK]
-                rows_v[i] = rows_v[i] - change[at, BLK:]
-        cols = coming
-
-
-def factor_kernel(yx_ref, yz_ref, lh_ref, ll_ref, d_ref, w_ref, g_ref, u_ref, v_ref, gx_ref, gz_ref):
+
+
+def factor_kernel(yx_ref, yz_ref, lh_ref, ll_ref, d_ref, w_ref, g_ref, u_ref, v_ref):
     order = lh_ref.shape[0]
     steps = order // BLK
     tile = 2 * BLK
@@ -235,10 +201,10 @@
     w_ref[:, tile:] = jnp.zeros((order, order - tile), jnp.float32)
 
     def rows_of(i, carry):
-        left = pl.ds(pl.multiple_of(i * tile, tile), tile)
-        gram_tile(yx_ref, yz_ref, left, pl.ds(0, tile), w_ref.at[left, pl.ds(0, tile)], gx_ref, gz_ref)
+        left = pl.ds(pl.multiple_of(i * 2 * tile, 2 * tile), 2 * tile)
+        w_ref[left, :tile] = gram_tile(yx_ref, yz_ref, left, pl.ds(0, tile))
         return carry
-    lax.fori_loop(0, order // tile, rows_of, 0)
+    lax.fori_loop(0, order // (2 * tile), rows_of, 0)
 
     def step(b, carry):
         at = pl.ds(pl.multiple_of(b * BLK, BLK), BLK)
@@ -288,8 +254,7 @@
         out_shape=(jax.ShapeDtypeStruct((K, K), jnp.bfloat16),) * 2 + (jax.ShapeDtypeStruct((K, BLK), f32),),
         in_specs=[VMEM] * 2,
         out_specs=(VMEM,) * 3,
-        scratch_shapes=[pltpu.VMEM((K, K), f32), pltpu.VMEM((K, tile), f32), pltpu.VMEM((BLK, BLK), f32), pltpu.VMEM((BLK, BLK), f32)]
-        + [pltpu.VMEM((2, RANK * tile, tile), f32)] * 2,
+        scratch_shapes=[pltpu.VMEM((K, K), f32), pltpu.VMEM((K, tile), f32), pltpu.VMEM((BLK, BLK), f32), pltpu.VMEM((BLK, BLK), f32)],
         compiler_params=pltpu.CompilerParams(vmem_limit_bytes=58 * MIB),
         cost_estimate=pl.CostEstimate(flops=40 * 10**9, bytes_accessed=12 * MIB, transcendentals=0),
     )(yx, yz)
@@ -366,35 +331,61 @@
     def swap(axis, count, turn, value):
         return lax.ppermute(value, axis, [(n, n ^ turn) for n in range(count)])
 
-    def after(value, *others):
-        return lax.optimization_barrier((value, *others))[0]
-
     span = pcol_count // 2
+    level_of = {j: bin(j).count("1") for j in range(1, span)}
+    levels = max(level_of.values(), default=0)
+    order = [0] + list(range(1, prow_count, 2)) + list(range(2, prow_count, 2))
     items = {0: mine}
-    order = [0] + list(range(1, prow_count, 2)) + list(range(2, prow_count, 2))
     for turn in range(1, prow_count, 2):
         items[turn] = swap("prow", prow_count, turn, mine)
-    near, far, near_order, far_order, begun = [], [], [], [], []
-    for turn in order:
-        if turn not in items:
-            items[turn] = swap("prow", prow_count, 1, after(items[turn + 1], *begun[1]))
-        value, last = items[turn], turn == order[-1]
-        held = {0: value}
-        for j in range(1, span):
-            low = j & -j
-            high = 1 << (j.bit_length() - 1)
-            if low == high or last:
-                held[j] = swap("pcol", pcol_count, 2 * j, value)
+    held = {turn: {} for turn in order}
+    parts = []
+
+    def spread(turn, j):
+        low, high = j & -j, 1 << (j.bit_length() - 1)
+        if low == high:
+            return [swap("pcol", pcol_count, 2 * j, held[turn][0])]
+        return [swap("pcol", pcol_count, 2 * high, held[turn][j ^ high][:half]), swap("pcol", pcol_count, 2 * low, held[turn][j ^ low][half:])]
+
+    def take(turn, which):
+        whole = jnp.concatenate([held[turn][j] for j in which]) if len(which) > 1 else held[turn][which[0]]
+        parts.append((turn, which, whole, swap("pcol", pcol_count, 1, whole)))
+
+    for phase in range(len(order) + levels - 1):
+        moved = {}
+        if phase < len(order):
+            turn = order[phase]
+            held[turn][0] = items[turn]
+            if turn % 2 == 1 and turn > 1:
+                moved["z", turn - 1] = [swap("prow", prow_count, 1, items[turn])]
+        for level in range(1, levels + 1):
+            if 0 <= phase - level + 1 < len(order):
+                turn = order[phase - level + 1]
+                for j in range(1, span):
+                    if level_of[j] == level:
+                        moved[turn, j] = spread(turn, j)
+        if phase + 1 < len(order) and order[phase + 1] in items:
+            moved["z", order[phase + 1]] = [items[order[phase + 1]]]
+        results = iter(lax.optimization_barrier([value for values in moved.values() for value in values]))
+        for (turn, j), values in moved.items():
+            arrived = [next(results) for _ in values]
+            if turn == "z":
+                items[j] = arrived[0]
             else:
-                held[j] = jnp.concatenate([swap("pcol", pcol_count, 2 * high, held[j ^ high][:half]), swap("pcol", pcol_count, 2 * low, held[j ^ low][half:])])
-        begun.append([held[j] for j in range(1, span) if j & (j - 1) == 0])
-        for part in [[j] for j in held] if last else [list(held)]:
-            whole = jnp.concatenate([held[j] for j in part]) if len(part) > 1 else held[part[0]]
-            near.append(whole)
-            near_order += [(turn, 2 * j) for j in part]
-            far.append(swap("pcol", pcol_count, 1, whole))
-            far_order += [(turn, 2 * j + 1) for j in part]
-    return near + far, near_order + far_order
+                held[turn][j] = arrived[0] if len(arrived) == 1 else jnp.concatenate(arrived)
+        if 0 <= phase - levels + 1 < len(order) - 1:
+            take(order[phase - levels + 1], list(held[order[phase - levels + 1]]))
+        if phase == len(order) + levels - 3:
+            early = [j for j in held[order[-1]] if j == 0 or level_of[j] < levels]
+            if len(early) == span or levels < 2:
+                early = []
+            else:
+                take(order[-1], early)
+    take(order[-1], [j for j in range(span) if j not in early])
+    near = [whole for _, _, whole, _ in parts]
+    far = [swapped for _, _, _, swapped in parts]
+    places = [(turn, 2 * j) for turn, which, _, _ in parts for j in which]
+    return near + far, places + [(turn, col + 1) for turn, col in places]
 
 
 def places_of(placement, order, prow_id, pcol_id, pcol_count):

time: 258 us -> 248 us (0.961)
  waiting for transfers between devices: 58.1 us -> 45.3 us
  starting transfers between devices: 31.5 us -> 37.1 us
    ppermute x25 -> x24, waiting for transfers between devices: 58.1 us -> 45.2 us  [swap(): return lax.ppermute(value, axis, [(n, n ^ turn) for n in range(count)])]
    ppermute x3, starting transfers between devices: 7.53 us -> 12.9 us  [per_device(): lax.ppermute(top, 'prow', [(n, n ^ turn) for n in range(prow_count)])]
    unnamed x30 -> x29, local copies, waits for them, and re-layouts: 12.2 us -> 11.2 us
    ppermute x25 -> x24, starting transfers between devices: 24 us -> 24.2 us  [swap(): return lax.ppermute(value, axis, [(n, n ^ turn) for n in range(count)])]
  transfers between devices with their start and end apart: 29 -> 28, of which waited for: 13 -> 10; matrix products, arithmetic and copies ran while one was open for 6% -> 6% of each run, Pallas kernels for 26% -> 27%
where the time goes in v8:
time: 248 us
  Pallas kernels  133 us (54%)
  waiting for transfers between devices  45.3 us (18%)
  starting transfers between devices  37.1 us (15%)
  local copies, waits for them, and re-layouts  16.3 us (7%)
  between operations  14.3 us (6%)
    pallas_call x1, Pallas kernels, factor(): pl.pallas_call(factor_kernel, out_shape=(jax.ShapeDtypeStruct((K, K), jnp...  66.1 us
    pallas_call x1, Pallas kernels, assemble(): pl.pallas_call(body, grid=(pick_tiles + row_tiles * col_tiles,), out_shap...  47.4 us
    ppermute x24, waiting for transfers between devices, swap(): return lax.ppermute(value, axis, [(n, n ^ turn) for n in range(count)])  45.2 us
    ppermute x24, starting transfers between devices, swap(): return lax.ppermute(value, axis, [(n, n ^ turn) for n in range(count)])  24.2 us
    pallas_call x1, Pallas kernels, solve(): pl.pallas_call(functools.partial(solve_kernel, prow=len(tops)), out_shape...  19.2 us
    ppermute x3, starting transfers between devices, per_device(): lax.ppermute(top, 'prow', [(n, n ^ turn) for n in range(prow_count)])  12.9 us
    unnamed x29, local copies, waits for them, and re-layouts  11.2 us
  transfers between devices with their start and end apart: 28, of which 10 were waited for; matrix products, arithmetic and copies ran while one was open for 6% of the time, Pallas kernels for 27%

profile of v8, /device:TPU:0, one launch (start us, length us, event | category | flops | bytes accessed | tf_op | source)
XLA Modules:
  0.0 247.6 jit_solution(9492078703788348215)
XLA Ops:
  7.2 1.4 copy.19
  8.9 3.1 %collective-permute-start.2 = (bf16[128,16,128]{2,1,0:T(8,128)(2,1)S(1)}, bf16[128,16,128]{2,1,0:T(8,128)(2,1)S(1)}, u32[]{:S(2)}, u32[]{:S(2)}) collective-permute-start(bf16[128,16,128]{2,1,0:T(8,128)(2,1)S(1)} %reshape.177), channel_id=1, source_target_pairs={{0,8},{8,0},{16,24},{24,16},{1,9},{9,1},{17,25},{25,17},{2,10},{10... | collective-permute-start | bytes 1572872 | tf_op jit(solution)/shard_map/ppermute | solution.py:332
  12.0 1.5 collective-permute-start.1
  13.5 1.5 collective-permute-start
  15.0 2.5 collective-permute-start.7
  17.7 6.7 %collective-permute-done.2 = bf16[128,16,128]{2,1,0:T(8,128)(2,1)S(1)} collective-permute-done((bf16[128,16,128]{2,1,0:T(8,128)(2,1)S(1)}, bf16[128,16,128]{2,1,0:T(8,128)(2,1)S(1)}, u32[]{:S(2)}, u32[]{:S(2)}) %collective-permute-start.2) | collective-permute-done | bytes 524320 | tf_op jit(solution)/shard_map/ppermute | solution.py:332
  24.3 1.1 collective-permute-done.1
  25.4 1.2 collective-permute-done
  27.1 1.5 collective-permute-start.3
  29.3 1.5 collective-permute-start.5
  30.9 0.8 constant_dynamic-update-slice_fusion.4
  31.7 0.8 constant_dynamic-update-slice_fusion.3
  32.5 4.9 %collective-permute-done.7 = bf16[128,16,128]{2,1,0:T(8,128)(2,1)S(1)} collective-permute-done((bf16[128,16,128]{2,1,0:T(8,128)(2,1)S(1)}, bf16[128,16,128]{2,1,0:T(8,128)(2,1)S(1)}, u32[]{:S(2)}, u32[]{:S(2)}) %collective-permute-start.7) | collective-permute-done | bytes 524320 | tf_op jit(solution)/shard_map/ppermute | solution.py:332
  37.4 7.3 %collective-permute-done.6 = bf16[64,16,128]{2,1,0:T(8,128)(2,1)S(1)} collective-permute-done((bf16[64,16,128]{2,1,0:T(8,128)(2,1)S(1)}, bf16[64,16,128]{2,1,0:T(8,128)(2,1)S(1)}, u32[]{:S(2)}, u32[]{:S(2)}) %collective-permute-start.6) | collective-permute-done | bytes 262176 | tf_op jit(solution)/shard_map/ppermute | solution.py:332
  44.7 1.5 collective-permute-start.10
  46.2 1.5 collective-permute-start.9
  48.2 1.2 constant_dynamic-update-slice_fusion.2
  52.2 0.8 constant_dynamic-update-slice_fusion.8
  53.9 9.5 %collective-permute-done.12 = bf16[64,16,128]{2,1,0:T(8,128)(2,1)S(1)} collective-permute-done((bf16[64,16,128]{2,1,0:T(8,128)(2,1)S(1)}, bf16[64,16,128]{2,1,0:T(8,128)(2,1)S(1)}, u32[]{:S(2)}, u32[]{:S(2)}) %collective-permute-start.12) | collective-permute-done | bytes 262176 | tf_op jit(solution)/shard_map/ppermute | solution.py:332
  63.8 1.5 collective-permute-start.13
  66.6 1.8 collective-permute-start.15
  69.8 0.9 constant_dynamic-update-slice_fusion.13
  70.7 1.0 constant_dynamic-update-slice_fusion.12
  71.6 7.8 %collective-permute-done.16 = bf16[64,16,128]{2,1,0:T(8,128)(2,1)S(1)} collective-permute-done((bf16[64,16,128]{2,1,0:T(8,128)(2,1)S(1)}, bf16[64,16,128]{2,1,0:T(8,128)(2,1)S(1)}, u32[]{:S(2)}, u32[]{:S(2)}) %collective-permute-start.16) | collective-permute-done | bytes 262176 | tf_op jit(solution)/shard_map/ppermute | solution.py:332
  79.5 1.6 collective-permute-start.18
  81.0 0.9 collective-permute-start.17
  83.5 4.7 %collective-permute-done.18 = bf16[64,16,128]{2,1,0:T(8,128)(2,1)S(1)} collective-permute-done((bf16[64,16,128]{2,1,0:T(8,128)(2,1)S(1)}, bf16[64,16,128]{2,1,0:T(8,128)(2,1)S(1)}, u32[]{:S(2)}, u32[]{:S(2)}) %collective-permute-start.18) | collective-permute-done | bytes 262176 | tf_op jit(solution)/shard_map/ppermute | solution.py:332
  90.8 1.6 collective-permute-done.23.refs_9_
  93.2 47.4 %shard_map.68 = (bf16[4,1024,512]{2,1,0:T(8,128)(2,1)}, bf16[4,1024,512]{2,1,0:T(8,128)(2,1)}, f32[1024,512]{1,0:T(8,128)}, f32[1024,128]{1,0:T(8,128)}, f32[256,512]{1,0:T(8,128)}) custom-call(s32[2560]{0:T(1024)} %reshape.176.slots_ref, bf16[512,512]{1,0:T(8,128)(2,1)} %x_ref.1, bf16[512,512]{1,0:T(8,128)(2,1)} %z_ref.1, ...), custom_call_target="tpu_custom_call" | custom-call | flops 28000000000 | bytes 31457280 | tf_op jit(solution)/shard_map/pallas_call | solution.py:131
  141.3 12.3 %collective-permute-start.26 = (f32[256,512]{1,0:T(8,128)}, f32[256,512]{1,0:T(8,128)S(1)}, u32[]{:S(2)}, u32[]{:S(2)}) collective-permute-start(f32[256,512]{1,0:T(8,128)} %get-tuple-element.55.refs_0_), channel_id=1, source_target_pairs={{0,24},{8,16},{16,8},{24,0},{1,25},{9,17},{17,9},{25,1},{2,26},{10... | collective-permute-start | bytes 1572872 | tf_op jit(solution)/shard_map/ppermute | solution.py:430
  154.2 66.1 %shard_map.69 = (bf16[1024,1024]{1,0:T(8,128)(2,1)}, bf16[1024,1024]{1,0:T(8,128)(2,1)}, f32[1024,128]{1,0:T(8,128)}) custom-call(bf16[4,1024,512]{2,1,0:T(8,128)(2,1)} %get-tuple-element.48.yx_ref, bf16[4,1024,512]{2,1,0:T(8,128)(2,1)} %get-tuple-element.49.yz_ref), custom_call_target="tpu_custom_call" | custom-call | flops 40000000000 | bytes 12582912 | tf_op jit(solution)/shard_map/pallas_call | solution.py:252
  221.5 19.2 %shard_map.70 = (f32[1024,512]{1,0:T(8,128)}, f32[1024,128]{1,0:T(8,128)}) custom-call(s32[2]{0:T(128)} %pad_add_fusion.1.place_ref, bf16[1024,1024]{1,0:T(8,128)(2,1)} %get-tuple-element.50.lh_any, bf16[1024,1024]{1,0:T(8,128)(2,1)} %get-tuple-element.51.ll_any, f32[1024,128]{1,0:T(8,128)} %get-tuple-element.52.d_any, f32[8,1024,128]{2,1,0:T(8,128)} %bitcast.51, ...), custom_call_target="tpu_custom_call" | custom-call | flops 12000000000 | bytes 25165824 | tf_op jit(solution)/shard_map/pallas_call | solution.py:314
  (88 shorter events, 16.3 us)
Async XLA Ops:
  7.2 10.3 %copy-start.7 = (s32[32]{0:T(128)S(1)}, s32[32]{0:T(128)}, u32[]{:S(2)}) copy-start(s32[32]{0:T(128)} %constant.92.clone) | copy-start | bytes 388
  7.2 23.6 %copy-start.2 = (s32[4096]{0:T(1024)S(1)}, s32[4096]{0:T(1024)}, u32[]{:S(2)}) copy-start(s32[4096]{0:T(1024)} %param.8) | copy-start | bytes 49156
  7.2 213.2 %all-gather.3.cloned.1.call-start = ((), (), s32[]{:S(2)}) async-start(), calls=%async_computation | async-start | bytes 4718592 | tf_op jit(solution)/shard_map/all_gather | solution.py:429
  8.9 15.4 %collective-permute-start.2 = (bf16[128,16,128]{2,1,0:T(8,128)(2,1)S(1)}, bf16[128,16,128]{2,1,0:T(8,128)(2,1)S(1)}, u32[]{:S(2)}, u32[]{:S(2)}) collective-permute-start(bf16[128,16,128]{2,1,0:T(8,128)(2,1)S(1)} %reshape.177), channel_id=1, source_target_pairs={{0,8},{8,0},{16,24},{24,16},{1,9},{9,1},{17,25},{25,17},{2,10},{10... | collective-permute-start | bytes 1572872 | tf_op jit(solution)/shard_map/ppermute | solution.py:332
  12.0 13.4 %collective-permute-start.1 = (bf16[128,16,128]{2,1,0:T(8,128)(2,1)S(1)}, bf16[128,16,128]{2,1,0:T(8,128)(2,1)S(1)}, u32[]{:S(2)}, u32[]{:S(2)}) collective-permute-start(bf16[128,16,128]{2,1,0:T(8,128)(2,1)S(1)} %reshape.177), channel_id=1, source_target_pairs={{0,4},{1,5},{2,6},{3,7},{4,0},{5,1},{6,2},{7,3},{8,12},{9,13},{10,... | collective-permute-start | bytes 1572872 | tf_op jit(solution)/shard_map/ppermute | solution.py:332
  13.5 13.1 %collective-permute-start = (bf16[128,16,128]{2,1,0:T(8,128)(2,1)S(1)}, bf16[128,16,128]{2,1,0:T(8,128)(2,1)S(1)}, u32[]{:S(2)}, u32[]{:S(2)}) collective-permute-start(bf16[128,16,128]{2,1,0:T(8,128)(2,1)S(1)} %reshape.177), channel_id=1, source_target_pairs={{0,2},{1,3},{2,0},{3,1},{4,6},{5,7},{6,4},{7,5},{8,10},{9,11},{10,... | collective-permute-start | bytes 1572872 | tf_op jit(solution)/shard_map/ppermute | solution.py:332
  15.0 22.4 %collective-permute-start.7 = (bf16[128,16,128]{2,1,0:T(8,128)(2,1)S(1)}, bf16[128,16,128]{2,1,0:T(8,128)(2,1)S(1)}, u32[]{:S(2)}, u32[]{:S(2)}) collective-permute-start(bf16[128,16,128]{2,1,0:T(8,128)(2,1)S(1)} %reshape.177), channel_id=1, source_target_pairs={{0,24},{8,16},{16,8},{24,0},{1,25},{9,17},{17,9},{25,1},{2,26},{10... | collective-permute-start | bytes 1572872 | tf_op jit(solution)/shard_map/ppermute | solution.py:332
  26.6 18.1 %collective-permute-start.4 = (bf16[128,16,128]{2,1,0:T(8,128)(2,1)S(1)}, bf16[128,16,128]{2,1,0:T(8,128)(2,1)S(1)}, u32[]{:S(2)}, u32[]{:S(2)}) collective-permute-start(bf16[128,16,128]{2,1,0:T(8,128)(2,1)S(1)} %collective-permute-done.2), channel_id=1, source_target_pairs={{0,4},{1,5},{2,6},{3,7},{4,0},{5,1},{6,2},{7,3},{8,12},{9,13},{10,... | collective-permute-start | bytes 1572872 | tf_op jit(solution)/shard_map/ppermute | solution.py:332
  27.1 17.6 %collective-permute-start.3 = (bf16[128,16,128]{2,1,0:T(8,128)(2,1)S(1)}, bf16[128,16,128]{2,1,0:T(8,128)(2,1)S(1)}, u32[]{:S(2)}, u32[]{:S(2)}) collective-permute-start(bf16[128,16,128]{2,1,0:T(8,128)(2,1)S(1)} %collective-permute-done.2), channel_id=1, source_target_pairs={{0,2},{1,3},{2,0},{3,1},{4,6},{5,7},{6,4},{7,5},{8,10},{9,11},{10,... | collective-permute-start | bytes 1572872 | tf_op jit(solution)/shard_map/ppermute | solution.py:332
  28.7 16.0 %collective-permute-start.6 = (bf16[64,16,128]{2,1,0:T(8,128)(2,1)S(1)}, bf16[64,16,128]{2,1,0:T(8,128)(2,1)S(1)}, u32[]{:S(2)}, u32[]{:S(2)}) collective-permute-start(bf16[64,16,128]{2,1,0:T(8,128)(2,1)S(1)} %slice.37), channel_id=1, source_target_pairs={{0,2},{1,3},{2,0},{3,1},{4,6},{5,7},{6,4},{7,5},{8,10},{9,11},{10,... | collective-permute-start | bytes 786440 | tf_op jit(solution)/shard_map/ppermute | solution.py:332
  29.3 15.4 %collective-permute-start.5 = (bf16[64,16,128]{2,1,0:T(8,128)(2,1)S(1)}, bf16[64,16,128]{2,1,0:T(8,128)(2,1)S(1)}, u32[]{:S(2)}, u32[]{:S(2)}) collective-permute-start(bf16[64,16,128]{2,1,0:T(8,128)(2,1)S(1)} %slice.36), channel_id=1, source_target_pairs={{0,4},{1,5},{2,6},{3,7},{4,0},{5,1},{6,2},{7,3},{8,12},{9,13},{10,... | collective-permute-start | bytes 786440 | tf_op jit(solution)/shard_map/ppermute | solution.py:332
  44.7 18.7 %collective-permute-start.10 = (bf16[128,16,128]{2,1,0:T(8,128)(2,1)S(1)}, bf16[128,16,128]{2,1,0:T(8,128)(2,1)S(1)}, u32[]{:S(2)}, u32[]{:S(2)}) collective-permute-start(bf16[128,16,128]{2,1,0:T(8,128)(2,1)S(1)} %collective-permute-done.7), channel_id=1, source_target_pairs={{0,4},{1,5},{2,6},{3,7},{4,0},{5,1},{6,2},{7,3},{8,12},{9,13},{10,... | collective-permute-start | bytes 1572872 | tf_op jit(solution)/shard_map/ppermute | solution.py:332
  46.2 17.2 %collective-permute-start.9 = (bf16[128,16,128]{2,1,0:T(8,128)(2,1)S(1)}, bf16[128,16,128]{2,1,0:T(8,128)(2,1)S(1)}, u32[]{:S(2)}, u32[]{:S(2)}) collective-permute-start(bf16[128,16,128]{2,1,0:T(8,128)(2,1)S(1)} %collective-permute-done.7), channel_id=1, source_target_pairs={{0,2},{1,3},{2,0},{3,1},{4,6},{5,7},{6,4},{7,5},{8,10},{9,11},{10,... | collective-permute-start | bytes 1572872 | tf_op jit(solution)/shard_map/ppermute | solution.py:332
  47.7 15.7 %collective-permute-start.8 = (bf16[128,16,128]{2,1,0:T(8,128)(2,1)S(1)}, bf16[128,16,128]{2,1,0:T(8,128)(2,1)S(1)}, u32[]{:S(2)}, u32[]{:S(2)}) collective-permute-start(bf16[128,16,128]{2,1,0:T(8,128)(2,1)S(1)} %collective-permute-done.7), channel_id=1, source_target_pairs={{0,8},{8,0},{16,24},{24,16},{1,9},{9,1},{17,25},{25,17},{2,10},{10... | collective-permute-start | bytes 1572872 | tf_op jit(solution)/shard_map/ppermute | solution.py:332
  49.4 14.0 %collective-permute-start.12 = (bf16[64,16,128]{2,1,0:T(8,128)(2,1)S(1)}, bf16[64,16,128]{2,1,0:T(8,128)(2,1)S(1)}, u32[]{:S(2)}, u32[]{:S(2)}) collective-permute-start(bf16[64,16,128]{2,1,0:T(8,128)(2,1)S(1)} %slice.39), channel_id=1, source_target_pairs={{0,2},{1,3},{2,0},{3,1},{4,6},{5,7},{6,4},{7,5},{8,10},{9,11},{10,... | collective-permute-start | bytes 786440 | tf_op jit(solution)/shard_map/ppermute | solution.py:332
  50.0 13.4 %collective-permute-start.11 = (bf16[64,16,128]{2,1,0:T(8,128)(2,1)S(1)}, bf16[64,16,128]{2,1,0:T(8,128)(2,1)S(1)}, u32[]{:S(2)}, u32[]{:S(2)}) collective-permute-start(bf16[64,16,128]{2,1,0:T(8,128)(2,1)S(1)} %slice.38), channel_id=1, source_target_pairs={{0,4},{1,5},{2,6},{3,7},{4,0},{5,1},{6,2},{7,3},{8,12},{9,13},{10,... | collective-permute-start | bytes 786440 | tf_op jit(solution)/shard_map/ppermute | solution.py:332
  63.4 16.0 %collective-permute-start.14 = (bf16[128,16,128]{2,1,0:T(8,128)(2,1)S(1)}, bf16[128,16,128]{2,1,0:T(8,128)(2,1)S(1)}, u32[]{:S(2)}, u32[]{:S(2)}) collective-permute-start(bf16[128,16,128]{2,1,0:T(8,128)(2,1)S(1)} %collective-permute-done.8), channel_id=1, source_target_pairs={{0,4},{1,5},{2,6},{3,7},{4,0},{5,1},{6,2},{7,3},{8,12},{9,13},{10,... | collective-permute-start | bytes 1572872 | tf_op jit(solution)/shard_map/ppermute | solution.py:332
  63.8 15.6 %collective-permute-start.13 = (bf16[128,16,128]{2,1,0:T(8,128)(2,1)S(1)}, bf16[128,16,128]{2,1,0:T(8,128)(2,1)S(1)}, u32[]{:S(2)}, u32[]{:S(2)}) collective-permute-start(bf16[128,16,128]{2,1,0:T(8,128)(2,1)S(1)} %collective-permute-done.8), channel_id=1, source_target_pairs={{0,2},{1,3},{2,0},{3,1},{4,6},{5,7},{6,4},{7,5},{8,10},{9,11},{10,... | collective-permute-start | bytes 1572872 | tf_op jit(solution)/shard_map/ppermute | solution.py:332
  66.0 26.4 %collective-permute-start.19 = (bf16[512,16,128]{2,1,0:T(8,128)(2,1)}, bf16[512,16,128]{2,1,0:T(8,128)(2,1)}, u32[]{:S(2)}, u32[]{:S(2)}) collective-permute-start(bf16[512,16,128]{2,1,0:T(8,128)(2,1)} %constant_dynamic-update-slice_fusion.refs_0_), channel_id=1, source_target_pairs={{0,1},{1,0},{2,3},{3,2},{4,5},{5,4},{6,7},{7,6},{8,9},{9,8},{10,11... | collective-permute-start | bytes 6291464 | tf_op jit(solution)/shard_map/ppermute | solution.py:332
  66.0 13.4 %collective-permute-start.16 = (bf16[64,16,128]{2,1,0:T(8,128)(2,1)S(1)}, bf16[64,16,128]{2,1,0:T(8,128)(2,1)S(1)}, u32[]{:S(2)}, u32[]{:S(2)}) collective-permute-start(bf16[64,16,128]{2,1,0:T(8,128)(2,1)S(1)} %slice.41), channel_id=1, source_target_pairs={{0,2},{1,3},{2,0},{3,1},{4,6},{5,7},{6,4},{7,5},{8,10},{9,11},{10,... | collective-permute-start | bytes 786440 | tf_op jit(solution)/shard_map/ppermute | solution.py:332
  66.6 12.8 %collective-permute-start.15 = (bf16[64,16,128]{2,1,0:T(8,128)(2,1)S(1)}, bf16[64,16,128]{2,1,0:T(8,128)(2,1)S(1)}, u32[]{:S(2)}, u32[]{:S(2)}) collective-permute-start(bf16[64,16,128]{2,1,0:T(8,128)(2,1)S(1)} %slice.40), channel_id=1, source_target_pairs={{0,4},{1,5},{2,6},{3,7},{4,0},{5,1},{6,2},{7,3},{8,12},{9,13},{10,... | collective-permute-start | bytes 786440 | tf_op jit(solution)/shard_map/ppermute | solution.py:332
  79.4 13.0 %collective-permute-start.20 = (bf16[512,16,128]{2,1,0:T(8,128)(2,1)}, bf16[512,16,128]{2,1,0:T(8,128)(2,1)}, u32[]{:S(2)}, u32[]{:S(2)}) collective-permute-start(bf16[512,16,128]{2,1,0:T(8,128)(2,1)} %constant_dynamic-update-slice_fusion.5.refs_1_), channel_id=1, source_target_pairs={{0,1},{1,0},{2,3},{3,2},{4,5},{5,4},{6,7},{7,6},{8,9},{9,8},{10,11... | collective-permute-start | bytes 6291464 | tf_op jit(solution)/shard_map/ppermute | solution.py:332
  79.5 8.8 %collective-permute-start.18 = (bf16[64,16,128]{2,1,0:T(8,128)(2,1)S(1)}, bf16[64,16,128]{2,1,0:T(8,128)(2,1)S(1)}, u32[]{:S(2)}, u32[]{:S(2)}) collective-permute-start(bf16[64,16,128]{2,1,0:T(8,128)(2,1)S(1)} %slice.43), channel_id=1, source_target_pairs={{0,2},{1,3},{2,0},{3,1},{4,6},{5,7},{6,4},{7,5},{8,10},{9,11},{10,... | collective-permute-start | bytes 786440 | tf_op jit(solution)/shard_map/ppermute | solution.py:332
  81.0 8.4 %collective-permute-start.17 = (bf16[64,16,128]{2,1,0:T(8,128)(2,1)S(1)}, bf16[64,16,128]{2,1,0:T(8,128)(2,1)S(1)}, u32[]{:S(2)}, u32[]{:S(2)}) collective-permute-start(bf16[64,16,128]{2,1,0:T(8,128)(2,1)S(1)} %slice.42), channel_id=1, source_target_pairs={{0,4},{1,5},{2,6},{3,7},{4,0},{5,1},{6,2},{7,3},{8,12},{9,13},{10,... | collective-permute-start | bytes 786440 | tf_op jit(solution)/shard_map/ppermute | solution.py:332
  83.4 9.1 %collective-permute-start.21 = (bf16[512,16,128]{2,1,0:T(8,128)(2,1)}, bf16[512,16,128]{2,1,0:T(8,128)(2,1)}, u32[]{:S(2)}, u32[]{:S(2)}) collective-permute-start(bf16[512,16,128]{2,1,0:T(8,128)(2,1)} %constant_dynamic-update-slice_fusion.10.refs_2_), channel_id=1, source_target_pairs={{0,1},{1,0},{2,3},{3,2},{4,5},{5,4},{6,7},{7,6},{8,9},{9,8},{10,11... | collective-permute-start | bytes 6291464 | tf_op jit(solution)/shard_map/ppermute | solution.py:332
  83.5 6.0 %copy-start = (bf16[384,16,128]{2,1,0:T(8,128)(2,1)}, bf16[384,16,128]{2,1,0:T(8,128)(2,1)S(1)}, u32[]{:S(2)}) copy-start(bf16[384,16,128]{2,1,0:T(8,128)(2,1)S(1)} %constant_dynamic-update-slice_fusion.15.refs_3_) | copy-start | bytes 4718596
  88.2 4.2 %collective-permute-start.22 = (bf16[384,16,128]{2,1,0:T(8,128)(2,1)S(1)}, bf16[384,16,128]{2,1,0:T(8,128)(2,1)}, u32[]{:S(2)}, u32[]{:S(2)}) collective-permute-start(bf16[384,16,128]{2,1,0:T(8,128)(2,1)S(1)} %constant_dynamic-update-slice_fusion.15.refs_3_), channel_id=1, source_target_pairs={{0,1},{1,0},{2,3},{3,2},{4,5},{5,4},{6,7},{7,6},{8,9},{9,8},{10,11... | collective-permute-start | bytes 4718600 | tf_op jit(solution)/shard_map/ppermute | solution.py:332
  89.5 2.9 %copy-start.1 = (bf16[128,16,128]{2,1,0:T(8,128)(2,1)}, bf16[128,16,128]{2,1,0:T(8,128)(2,1)S(1)}, u32[]{:S(2)}) copy-start(bf16[128,16,128]{2,1,0:T(8,128)(2,1)S(1)} %constant_dynamic-update-slice_fusion.18.refs_4_) | copy-start | bytes 1572868
  89.5 2.9 %collective-permute-start.23 = (bf16[128,16,128]{2,1,0:T(8,128)(2,1)S(1)}, bf16[128,16,128]{2,1,0:T(8,128)(2,1)S(1)}, u32[]{:S(2)}, u32[]{:S(2)}) collective-permute-start(bf16[128,16,128]{2,1,0:T(8,128)(2,1)S(1)} %constant_dynamic-update-slice_fusion.18.refs_4_), channel_id=1, source_target_pairs={{0,1},{1,0},{2,3},{3,2},{4,5},{5,4},{6,7},{7,6},{8,9},{9,8},{10,11... | collective-permute-start | bytes 1572872 | tf_op jit(solution)/shard_map/ppermute | solution.py:332
  141.3 79.0 %collective-permute-start.26 = (f32[256,512]{1,0:T(8,128)}, f32[256,512]{1,0:T(8,128)S(1)}, u32[]{:S(2)}, u32[]{:S(2)}) collective-permute-start(f32[256,512]{1,0:T(8,128)} %get-tuple-element.55.refs_0_), channel_id=1, source_target_pairs={{0,24},{8,16},{16,8},{24,0},{1,25},{9,17},{17,9},{25,1},{2,26},{10... | collective-permute-start | bytes 1572872 | tf_op jit(solution)/shard_map/ppermute | solution.py:430
  153.6 66.7 %collective-permute-start.25 = (f32[256,512]{1,0:T(8,128)}, f32[256,512]{1,0:T(8,128)S(1)}, u32[]{:S(2)}, u32[]{:S(2)}) collective-permute-start(f32[256,512]{1,0:T(8,128)} %get-tuple-element.55.refs_0_), channel_id=1, source_target_pairs={{0,16},{8,24},{16,0},{24,8},{1,17},{9,25},{17,1},{25,9},{2,18},{10... | collective-permute-start | bytes 1572872 | tf_op jit(solution)/shard_map/ppermute | solution.py:430
  153.7 66.7 %collective-permute-start.24 = (f32[256,512]{1,0:T(8,128)}, f32[256,512]{1,0:T(8,128)S(1)}, u32[]{:S(2)}, u32[]{:S(2)}) collective-permute-start(f32[256,512]{1,0:T(8,128)} %get-tuple-element.55.refs_0_), channel_id=1, source_target_pairs={{0,8},{8,0},{16,24},{24,16},{1,9},{9,1},{17,25},{25,17},{2,10},{10... | collective-permute-start | bytes 1572872 | tf_op jit(solution)/shard_map/ppermute | solution.py:430
  (4 other events, 3.7 us)
Sparse Core Ops, SparseCore 0:
  140.8 46.2 all-gather.2

commit v9 on v8

--- a/solution.py
+++ b/solution.py
@@ -164,8 +164,12 @@
         beside(m)
         head_a, head_v = rows_a[m], rows_v[m]
         cols = [spread_lane(head_a, SUB * m + k) for k in range(SUB)]
-        below = [[spread_lane(rows_a[i], SUB * m + k) for k in range(SUB)] for i in range(m + 1, count)]
+        more = m + 1 < count
+        if more:
+            next_a, next_v = rows_a[m + 1], rows_v[m + 1]
+            below = [spread_lane(next_a, SUB * m + k) for k in range(SUB)]
         scale = jnp.zeros((SUB, BLK), jnp.float32)
+        done_a, done_v = [], []
         for j in range(SUB):
             pivot = spread_row(cols[j], j)
             root = lax.rsqrt(pivot)
@@ -174,21 +178,32 @@
             row_a = spread_row(head_a, j) * root
             row_v = spread_row(head_v, j) * root
             lead = [spread_row(cols[k], j) * root if k > j else None for k in range(SUB)]
+            done_a.append(row_a)
+            done_v.append(row_v)
             if j + 1 < SUB:
+                for k in range(j + 1, SUB):
+                    cols[k] = cols[k] - mult * lead[k]
                 head_a = head_a - mult * row_a
                 head_v = head_v - mult * row_v
+            if more:
+                mult_next = below[j] * root
                 for k in range(j + 1, SUB):
-                    cols[k] = cols[k] - mult * lead[k]
-            for n, i in enumerate(range(m + 1, count)):
-                mult_i = below[n][j] * root
-                rows_a[i] = rows_a[i] - mult_i * row_a
-                rows_v[i] = rows_v[i] - mult_i * row_v
-                for k in range(j + 1, SUB):
-                    below[n][k] = below[n][k] - mult_i * lead[k]
-        u = jnp.where(lane_iota >= sub_iota + SUB * m, head_a * scale, 0.0)
-        v = jnp.where(lane_iota <= sub_iota + SUB * m, head_v * scale, 0.0)
-        u_ref[SUB * m:SUB * (m + 1), :] = u
-        v_ref[SUB * m:SUB * (m + 1), :] = v
+                    below[k] = below[k] - mult_next * lead[k]
+                next_a = next_a - mult_next * row_a
+                next_v = next_v - mult_next * row_v
+        u = head_a * scale
+        u_ref[SUB * m:SUB * (m + 1), :] = jnp.where(lane_iota >= sub_iota + SUB * m, u, 0.0)
+        v_ref[SUB * m:SUB * (m + 1), :] = jnp.where(lane_iota <= sub_iota + SUB * m, head_v * scale, 0.0)
+        if more:
+            rows_a[m + 1], rows_v[m + 1] = next_a, next_v
+        if m + 2 < count:
+            turned = u.T
+            for i in range(m + 2, count):
+                mine = turned[SUB * i:SUB * (i + 1), :]
+                for j in range(SUB):
+                    mult_i = spread_lane(mine, j)
+                    rows_a[i] = rows_a[i] - mult_i * done_a[j]
+                    rows_v[i] = rows_v[i] - mult_i * done_v[j]
 
 
 def factor_kernel(yx_ref, yz_ref, lh_ref, ll_ref, d_ref, w_ref, g_ref, u_ref, v_ref):
@@ -336,8 +351,6 @@
     levels = max(level_of.values(), default=0)
     order = [0] + list(range(1, prow_count, 2)) + list(range(2, prow_count, 2))
     items = {0: mine}
-    for turn in range(1, prow_count, 2):
-        items[turn] = swap("prow", prow_count, turn, mine)
     held = {turn: {} for turn in order}
     parts = []
 
@@ -364,9 +377,14 @@
                 for j in range(1, span):
                     if level_of[j] == level:
                         moved[turn, j] = spread(turn, j)
-        if phase + 1 < len(order) and order[phase + 1] in items:
-            moved["z", order[phase + 1]] = [items[order[phase + 1]]]
-        results = iter(lax.optimization_barrier([value for values in moved.values() for value in values]))
+        if phase + 1 < len(order):
+            turn = order[phase + 1]
+            if turn % 2 == 1:
+                moved["z", turn] = [swap("prow", prow_count, turn, mine)]
+            elif turn in items:
+                moved["z", turn] = [items[turn]]
+        mine, *results = lax.optimization_barrier([mine] + [value for values in moved.values() for value in values])
+        results = iter(results)
         for (turn, j), values in moved.items():
             arrived = [next(results) for _ in values]
             if turn == "z":

time: 248 us -> 257 us (1.036)
  Pallas kernels: 133 us -> 142 us
  starting transfers between devices: 37.1 us -> 41.5 us
  waiting for transfers between devices: 45.3 us -> 40.9 us
    pallas_call x1, Pallas kernels: 66.1 us -> 75.4 us  [factor(): pl.pallas_call(factor_kernel, out_shape=(jax.ShapeDtypeStruct((K, K), jnp...]
    ppermute x24, starting transfers between devices: 24.2 us -> 32.2 us  [swap(): return lax.ppermute(value, axis, [(n, n ^ turn) for n in range(count)])]
    ppermute x24, waiting for transfers between devices: 45.2 us -> 40.8 us  [swap(): return lax.ppermute(value, axis, [(n, n ^ turn) for n in range(count)])]
    ppermute x3, starting transfers between devices: 12.9 us -> 9.24 us  [per_device(): lax.ppermute(top, 'prow', [(n, n ^ turn) for n in range(prow_count)])]
  transfers between devices with their start and end apart: 28 -> 28, of which waited for: 10 -> 11; matrix products, arithmetic and copies ran while one was open for 6% -> 6% of each run, Pallas kernels for 27% -> 29%
where the time goes in v9:
time: 257 us
  Pallas kernels  142 us (55%)
  starting transfers between devices  41.5 us (16%)
  waiting for transfers between devices  40.9 us (16%)
  local copies, waits for them, and re-layouts  16.3 us (6%)
  between operations  14.3 us (6%)
    pallas_call x1, Pallas kernels, factor(): pl.pallas_call(factor_kernel, out_shape=(jax.ShapeDtypeStruct((K, K), jnp...  75.4 us
    pallas_call x1, Pallas kernels, assemble(): pl.pallas_call(body, grid=(pick_tiles + row_tiles * col_tiles,), out_shap...  47.4 us
    ppermute x24, waiting for transfers between devices, swap(): return lax.ppermute(value, axis, [(n, n ^ turn) for n in range(count)])  40.8 us
    ppermute x24, starting transfers between devices, swap(): return lax.ppermute(value, axis, [(n, n ^ turn) for n in range(count)])  32.2 us
    pallas_call x1, Pallas kernels, solve(): pl.pallas_call(functools.partial(solve_kernel, prow=len(tops)), out_shape...  19.2 us
    unnamed x29, local copies, waits for them, and re-layouts  11.2 us
    ppermute x3, starting transfers between devices, per_device(): lax.ppermute(top, 'prow', [(n, n ^ turn) for n in range(prow_count)])  9.24 us
  transfers between devices with their start and end apart: 28, of which 11 were waited for; matrix products, arithmetic and copies ran while one was open for 6% of the time, Pallas kernels for 29%

profile of v9, /device:TPU:0, one launch (start us, length us, event | category | flops | bytes accessed | tf_op | source)
XLA Modules:
  0.0 256.9 jit_solution(4756095722839201814)
XLA Ops:
  7.2 1.4 copy.19
  8.9 3.1 %collective-permute-start.2 = (bf16[128,16,128]{2,1,0:T(8,128)(2,1)S(1)}, bf16[128,16,128]{2,1,0:T(8,128)(2,1)S(1)}, u32[]{:S(2)}, u32[]{:S(2)}) collective-permute-start(bf16[128,16,128]{2,1,0:T(8,128)(2,1)S(1)} %reshape.177), channel_id=1, source_target_pairs={{0,8},{8,0},{16,24},{24,16},{1,9},{9,1},{17,25},{25,17},{2,10},{10... | collective-permute-start | bytes 1572872 | tf_op jit(solution)/shard_map/ppermute | solution.py:347
  12.0 1.5 collective-permute-start.1
  13.5 1.5 collective-permute-start
  15.2 8.7 %collective-permute-done.2 = bf16[128,16,128]{2,1,0:T(8,128)(2,1)S(1)} collective-permute-done((bf16[128,16,128]{2,1,0:T(8,128)(2,1)S(1)}, bf16[128,16,128]{2,1,0:T(8,128)(2,1)S(1)}, u32[]{:S(2)}, u32[]{:S(2)}) %collective-permute-start.2) | collective-permute-done | bytes 524320 | tf_op jit(solution)/shard_map/ppermute | solution.py:347
  23.9 1.5 collective-permute-done.1
  25.4 1.2 collective-permute-done
  27.1 1.5 collective-permute-start.3
  28.6 2.5 collective-permute-start.7
  31.7 1.5 collective-permute-start.5
  35.0 9.7 %collective-permute-done.6 = bf16[64,16,128]{2,1,0:T(8,128)(2,1)S(1)} collective-permute-done((bf16[64,16,128]{2,1,0:T(8,128)(2,1)S(1)}, bf16[64,16,128]{2,1,0:T(8,128)(2,1)S(1)}, u32[]{:S(2)}, u32[]{:S(2)}) %collective-permute-start.6) | collective-permute-done | bytes 262176 | tf_op jit(solution)/shard_map/ppermute | solution.py:347
  44.7 1.5 collective-permute-start.10
  46.2 1.5 collective-permute-start.9
  47.7 7.2 %collective-permute-start.8 = (bf16[128,16,128]{2,1,0:T(8,128)(2,1)S(1)}, bf16[128,16,128]{2,1,0:T(8,128)(2,1)S(1)}, u32[]{:S(2)}, u32[]{:S(2)}) collective-permute-start(bf16[128,16,128]{2,1,0:T(8,128)(2,1)S(1)} %collective-permute-done.7), channel_id=1, source_target_pairs={{0,8},{8,0},{16,24},{24,16},{1,9},{9,1},{17,25},{25,17},{2,10},{10... | collective-permute-start | bytes 1572872 | tf_op jit(solution)/shard_map/ppermute | solution.py:347
  54.9 1.2 constant_dynamic-update-slice_fusion.2
  56.1 1.6 collective-permute-start.12
  61.5 1.1 collective-permute-done.12
  62.6 1.5 collective-permute-done.11
  64.1 1.4 collective-permute-done.8
  66.0 1.5 collective-permute-start.13
  68.9 1.4 collective-permute-start.15
  72.6 1.0 constant_dynamic-update-slice_fusion.12
  73.6 9.4 %collective-permute-done.16 = bf16[64,16,128]{2,1,0:T(8,128)(2,1)S(1)} collective-permute-done((bf16[64,16,128]{2,1,0:T(8,128)(2,1)S(1)}, bf16[64,16,128]{2,1,0:T(8,128)(2,1)S(1)}, u32[]{:S(2)}, u32[]{:S(2)}) %collective-permute-start.16) | collective-permute-done | bytes 262176 | tf_op jit(solution)/shard_map/ppermute | solution.py:347
  83.1 1.6 collective-permute-start.18
  84.6 1.4 collective-permute-start.17
  87.7 4.2 %collective-permute-done.18 = bf16[64,16,128]{2,1,0:T(8,128)(2,1)S(1)} collective-permute-done((bf16[64,16,128]{2,1,0:T(8,128)(2,1)S(1)}, bf16[64,16,128]{2,1,0:T(8,128)(2,1)S(1)}, u32[]{:S(2)}, u32[]{:S(2)}) %collective-permute-start.18) | collective-permute-done | bytes 262176 | tf_op jit(solution)/shard_map/ppermute | solution.py:347
  94.4 1.6 collective-permute-done.23.refs_9_
  96.8 47.4 %shard_map.68 = (bf16[4,1024,512]{2,1,0:T(8,128)(2,1)}, bf16[4,1024,512]{2,1,0:T(8,128)(2,1)}, f32[1024,512]{1,0:T(8,128)}, f32[1024,128]{1,0:T(8,128)}, f32[256,512]{1,0:T(8,128)}) custom-call(s32[2560]{0:T(1024)} %reshape.176.slots_ref, bf16[512,512]{1,0:T(8,128)(2,1)} %x_ref.1, bf16[512,512]{1,0:T(8,128)(2,1)} %z_ref.1, ...), custom_call_target="tpu_custom_call" | custom-call | flops 28000000000 | bytes 31457280 | tf_op jit(solution)/shard_map/pallas_call | solution.py:131
  144.9 2.7 %collective-permute-start.26 = (f32[256,512]{1,0:T(8,128)}, f32[256,512]{1,0:T(8,128)S(1)}, u32[]{:S(2)}, u32[]{:S(2)}) collective-permute-start(f32[256,512]{1,0:T(8,128)} %get-tuple-element.57.refs_0_), channel_id=1, source_target_pairs={{0,24},{8,16},{16,8},{24,0},{1,25},{9,17},{17,9},{25,1},{2,26},{10... | collective-permute-start | bytes 1572872 | tf_op jit(solution)/shard_map/ppermute | solution.py:448
  147.6 6.0 %collective-permute-start.25 = (f32[256,512]{1,0:T(8,128)}, f32[256,512]{1,0:T(8,128)S(1)}, u32[]{:S(2)}, u32[]{:S(2)}) collective-permute-start(f32[256,512]{1,0:T(8,128)} %get-tuple-element.57.refs_0_), channel_id=1, source_target_pairs={{0,16},{8,24},{16,0},{24,8},{1,17},{9,25},{17,1},{25,9},{2,18},{10... | collective-permute-start | bytes 1572872 | tf_op jit(solution)/shard_map/ppermute | solution.py:448
  154.2 75.4 %shard_map.69 = (bf16[1024,1024]{1,0:T(8,128)(2,1)}, bf16[1024,1024]{1,0:T(8,128)(2,1)}, f32[1024,128]{1,0:T(8,128)}) custom-call(bf16[4,1024,512]{2,1,0:T(8,128)(2,1)} %get-tuple-element.50.yx_ref, bf16[4,1024,512]{2,1,0:T(8,128)(2,1)} %get-tuple-element.51.yz_ref), custom_call_target="tpu_custom_call" | custom-call | flops 40000000000 | bytes 12582912 | tf_op jit(solution)/shard_map/pallas_call | solution.py:267
  230.8 19.2 %shard_map.70 = (f32[1024,512]{1,0:T(8,128)}, f32[1024,128]{1,0:T(8,128)}) custom-call(s32[2]{0:T(128)} %pad_add_fusion.1.place_ref, bf16[1024,1024]{1,0:T(8,128)(2,1)} %get-tuple-element.52.lh_any, bf16[1024,1024]{1,0:T(8,128)(2,1)} %get-tuple-element.53.ll_any, f32[1024,128]{1,0:T(8,128)} %get-tuple-element.54.d_any, f32[8,1024,128]{2,1,0:T(8,128)} %bitcast.51, ...), custom_call_target="tpu_custom_call" | custom-call | flops 12000000000 | bytes 25165824 | tf_op jit(solution)/shard_map/pallas_call | solution.py:329
  (88 shorter events, 18.7 us)
Async XLA Ops:
  7.2 7.8 %copy-start.7 = (s32[32]{0:T(128)S(1)}, s32[32]{0:T(128)}, u32[]{:S(2)}) copy-start(s32[32]{0:T(128)} %constant.92.clone) | copy-start | bytes 388
  7.2 26.1 %copy-start.2 = (s32[4096]{0:T(1024)S(1)}, s32[4096]{0:T(1024)}, u32[]{:S(2)}) copy-start(s32[4096]{0:T(1024)} %param.8) | copy-start | bytes 49156
  7.2 222.5 %all-gather.3.cloned.1.call-start = ((), (), s32[]{:S(2)}) async-start(), calls=%async_computation | async-start | bytes 4718592 | tf_op jit(solution)/shard_map/all_gather | solution.py:447
  8.9 15.0 %collective-permute-start.2 = (bf16[128,16,128]{2,1,0:T(8,128)(2,1)S(1)}, bf16[128,16,128]{2,1,0:T(8,128)(2,1)S(1)}, u32[]{:S(2)}, u32[]{:S(2)}) collective-permute-start(bf16[128,16,128]{2,1,0:T(8,128)(2,1)S(1)} %reshape.177), channel_id=1, source_target_pairs={{0,8},{8,0},{16,24},{24,16},{1,9},{9,1},{17,25},{25,17},{2,10},{10... | collective-permute-start | bytes 1572872 | tf_op jit(solution)/shard_map/ppermute | solution.py:347
  12.0 13.4 %collective-permute-start.1 = (bf16[128,16,128]{2,1,0:T(8,128)(2,1)S(1)}, bf16[128,16,128]{2,1,0:T(8,128)(2,1)S(1)}, u32[]{:S(2)}, u32[]{:S(2)}) collective-permute-start(bf16[128,16,128]{2,1,0:T(8,128)(2,1)S(1)} %reshape.177), channel_id=1, source_target_pairs={{0,4},{1,5},{2,6},{3,7},{4,0},{5,1},{6,2},{7,3},{8,12},{9,13},{10,... | collective-permute-start | bytes 1572872 | tf_op jit(solution)/shard_map/ppermute | solution.py:347
  13.5 13.1 %collective-permute-start = (bf16[128,16,128]{2,1,0:T(8,128)(2,1)S(1)}, bf16[128,16,128]{2,1,0:T(8,128)(2,1)S(1)}, u32[]{:S(2)}, u32[]{:S(2)}) collective-permute-start(bf16[128,16,128]{2,1,0:T(8,128)(2,1)S(1)} %reshape.177), channel_id=1, source_target_pairs={{0,2},{1,3},{2,0},{3,1},{4,6},{5,7},{6,4},{7,5},{8,10},{9,11},{10,... | collective-permute-start | bytes 1572872 | tf_op jit(solution)/shard_map/ppermute | solution.py:347
  26.6 18.1 %collective-permute-start.4 = (bf16[128,16,128]{2,1,0:T(8,128)(2,1)S(1)}, bf16[128,16,128]{2,1,0:T(8,128)(2,1)S(1)}, u32[]{:S(2)}, u32[]{:S(2)}) collective-permute-start(bf16[128,16,128]{2,1,0:T(8,128)(2,1)S(1)} %collective-permute-done.2), channel_id=1, source_target_pairs={{0,4},{1,5},{2,6},{3,7},{4,0},{5,1},{6,2},{7,3},{8,12},{9,13},{10,... | collective-permute-start | bytes 1572872 | tf_op jit(solution)/shard_map/ppermute | solution.py:347
  27.1 17.6 %collective-permute-start.3 = (bf16[128,16,128]{2,1,0:T(8,128)(2,1)S(1)}, bf16[128,16,128]{2,1,0:T(8,128)(2,1)S(1)}, u32[]{:S(2)}, u32[]{:S(2)}) collective-permute-start(bf16[128,16,128]{2,1,0:T(8,128)(2,1)S(1)} %collective-permute-done.2), channel_id=1, source_target_pairs={{0,2},{1,3},{2,0},{3,1},{4,6},{5,7},{6,4},{7,5},{8,10},{9,11},{10,... | collective-permute-start | bytes 1572872 | tf_op jit(solution)/shard_map/ppermute | solution.py:347
  28.6 16.1 %collective-permute-start.7 = (bf16[128,16,128]{2,1,0:T(8,128)(2,1)S(1)}, bf16[128,16,128]{2,1,0:T(8,128)(2,1)S(1)}, u32[]{:S(2)}, u32[]{:S(2)}) collective-permute-start(bf16[128,16,128]{2,1,0:T(8,128)(2,1)S(1)} %reshape.177), channel_id=1, source_target_pairs={{0,24},{8,16},{16,8},{24,0},{1,25},{9,17},{17,9},{25,1},{2,26},{10... | collective-permute-start | bytes 1572872 | tf_op jit(solution)/shard_map/ppermute | solution.py:347
  31.1 13.6 %collective-permute-start.6 = (bf16[64,16,128]{2,1,0:T(8,128)(2,1)S(1)}, bf16[64,16,128]{2,1,0:T(8,128)(2,1)S(1)}, u32[]{:S(2)}, u32[]{:S(2)}) collective-permute-start(bf16[64,16,128]{2,1,0:T(8,128)(2,1)S(1)} %slice.37), channel_id=1, source_target_pairs={{0,2},{1,3},{2,0},{3,1},{4,6},{5,7},{6,4},{7,5},{8,10},{9,11},{10,... | collective-permute-start | bytes 786440 | tf_op jit(solution)/shard_map/ppermute | solution.py:347
  31.7 13.0 %collective-permute-start.5 = (bf16[64,16,128]{2,1,0:T(8,128)(2,1)S(1)}, bf16[64,16,128]{2,1,0:T(8,128)(2,1)S(1)}, u32[]{:S(2)}, u32[]{:S(2)}) collective-permute-start(bf16[64,16,128]{2,1,0:T(8,128)(2,1)S(1)} %slice.36), channel_id=1, source_target_pairs={{0,4},{1,5},{2,6},{3,7},{4,0},{5,1},{6,2},{7,3},{8,12},{9,13},{10,... | collective-permute-start | bytes 786440 | tf_op jit(solution)/shard_map/ppermute | solution.py:347
  44.7 19.3 %collective-permute-start.10 = (bf16[128,16,128]{2,1,0:T(8,128)(2,1)S(1)}, bf16[128,16,128]{2,1,0:T(8,128)(2,1)S(1)}, u32[]{:S(2)}, u32[]{:S(2)}) collective-permute-start(bf16[128,16,128]{2,1,0:T(8,128)(2,1)S(1)} %collective-permute-done.7), channel_id=1, source_target_pairs={{0,4},{1,5},{2,6},{3,7},{4,0},{5,1},{6,2},{7,3},{8,12},{9,13},{10,... | collective-permute-start | bytes 1572872 | tf_op jit(solution)/shard_map/ppermute | solution.py:347
  46.2 17.8 %collective-permute-start.9 = (bf16[128,16,128]{2,1,0:T(8,128)(2,1)S(1)}, bf16[128,16,128]{2,1,0:T(8,128)(2,1)S(1)}, u32[]{:S(2)}, u32[]{:S(2)}) collective-permute-start(bf16[128,16,128]{2,1,0:T(8,128)(2,1)S(1)} %collective-permute-done.7), channel_id=1, source_target_pairs={{0,2},{1,3},{2,0},{3,1},{4,6},{5,7},{6,4},{7,5},{8,10},{9,11},{10,... | collective-permute-start | bytes 1572872 | tf_op jit(solution)/shard_map/ppermute | solution.py:347
  47.7 17.7 %collective-permute-start.8 = (bf16[128,16,128]{2,1,0:T(8,128)(2,1)S(1)}, bf16[128,16,128]{2,1,0:T(8,128)(2,1)S(1)}, u32[]{:S(2)}, u32[]{:S(2)}) collective-permute-start(bf16[128,16,128]{2,1,0:T(8,128)(2,1)S(1)} %collective-permute-done.7), channel_id=1, source_target_pairs={{0,8},{8,0},{16,24},{24,16},{1,9},{9,1},{17,25},{25,17},{2,10},{10... | collective-permute-start | bytes 1572872 | tf_op jit(solution)/shard_map/ppermute | solution.py:347
  56.1 6.4 %collective-permute-start.12 = (bf16[64,16,128]{2,1,0:T(8,128)(2,1)S(1)}, bf16[64,16,128]{2,1,0:T(8,128)(2,1)S(1)}, u32[]{:S(2)}, u32[]{:S(2)}) collective-permute-start(bf16[64,16,128]{2,1,0:T(8,128)(2,1)S(1)} %slice.39), channel_id=1, source_target_pairs={{0,2},{1,3},{2,0},{3,1},{4,6},{5,7},{6,4},{7,5},{8,10},{9,11},{10,... | collective-permute-start | bytes 786440 | tf_op jit(solution)/shard_map/ppermute | solution.py:347
  57.7 6.4 %collective-permute-start.11 = (bf16[64,16,128]{2,1,0:T(8,128)(2,1)S(1)}, bf16[64,16,128]{2,1,0:T(8,128)(2,1)S(1)}, u32[]{:S(2)}, u32[]{:S(2)}) collective-permute-start(bf16[64,16,128]{2,1,0:T(8,128)(2,1)S(1)} %slice.38), channel_id=1, source_target_pairs={{0,4},{1,5},{2,6},{3,7},{4,0},{5,1},{6,2},{7,3},{8,12},{9,13},{10,... | collective-permute-start | bytes 786440 | tf_op jit(solution)/shard_map/ppermute | solution.py:347
  65.5 17.6 %collective-permute-start.14 = (bf16[128,16,128]{2,1,0:T(8,128)(2,1)S(1)}, bf16[128,16,128]{2,1,0:T(8,128)(2,1)S(1)}, u32[]{:S(2)}, u32[]{:S(2)}) collective-permute-start(bf16[128,16,128]{2,1,0:T(8,128)(2,1)S(1)} %collective-permute-done.8), channel_id=1, source_target_pairs={{0,4},{1,5},{2,6},{3,7},{4,0},{5,1},{6,2},{7,3},{8,12},{9,13},{10,... | collective-permute-start | bytes 1572872 | tf_op jit(solution)/shard_map/ppermute | solution.py:347
  66.0 17.0 %collective-permute-start.13 = (bf16[128,16,128]{2,1,0:T(8,128)(2,1)S(1)}, bf16[128,16,128]{2,1,0:T(8,128)(2,1)S(1)}, u32[]{:S(2)}, u32[]{:S(2)}) collective-permute-start(bf16[128,16,128]{2,1,0:T(8,128)(2,1)S(1)} %collective-permute-done.8), channel_id=1, source_target_pairs={{0,2},{1,3},{2,0},{3,1},{4,6},{5,7},{6,4},{7,5},{8,10},{9,11},{10,... | collective-permute-start | bytes 1572872 | tf_op jit(solution)/shard_map/ppermute | solution.py:347
  68.2 27.8 %collective-permute-start.19 = (bf16[512,16,128]{2,1,0:T(8,128)(2,1)}, bf16[512,16,128]{2,1,0:T(8,128)(2,1)}, u32[]{:S(2)}, u32[]{:S(2)}) collective-permute-start(bf16[512,16,128]{2,1,0:T(8,128)(2,1)} %constant_dynamic-update-slice_fusion.refs_0_), channel_id=1, source_target_pairs={{0,1},{1,0},{2,3},{3,2},{4,5},{5,4},{6,7},{7,6},{8,9},{9,8},{10,11... | collective-permute-start | bytes 6291464 | tf_op jit(solution)/shard_map/ppermute | solution.py:347
  68.3 14.7 %collective-permute-start.16 = (bf16[64,16,128]{2,1,0:T(8,128)(2,1)S(1)}, bf16[64,16,128]{2,1,0:T(8,128)(2,1)S(1)}, u32[]{:S(2)}, u32[]{:S(2)}) collective-permute-start(bf16[64,16,128]{2,1,0:T(8,128)(2,1)S(1)} %slice.41), channel_id=1, source_target_pairs={{0,2},{1,3},{2,0},{3,1},{4,6},{5,7},{6,4},{7,5},{8,10},{9,11},{10,... | collective-permute-start | bytes 786440 | tf_op jit(solution)/shard_map/ppermute | solution.py:347
  68.9 14.1 %collective-permute-start.15 = (bf16[64,16,128]{2,1,0:T(8,128)(2,1)S(1)}, bf16[64,16,128]{2,1,0:T(8,128)(2,1)S(1)}, u32[]{:S(2)}, u32[]{:S(2)}) collective-permute-start(bf16[64,16,128]{2,1,0:T(8,128)(2,1)S(1)} %slice.40), channel_id=1, source_target_pairs={{0,4},{1,5},{2,6},{3,7},{4,0},{5,1},{6,2},{7,3},{8,12},{9,13},{10,... | collective-permute-start | bytes 786440 | tf_op jit(solution)/shard_map/ppermute | solution.py:347
  83.0 13.0 %collective-permute-start.20 = (bf16[512,16,128]{2,1,0:T(8,128)(2,1)}, bf16[512,16,128]{2,1,0:T(8,128)(2,1)}, u32[]{:S(2)}, u32[]{:S(2)}) collective-permute-start(bf16[512,16,128]{2,1,0:T(8,128)(2,1)} %constant_dynamic-update-slice_fusion.5.refs_1_), channel_id=1, source_target_pairs={{0,1},{1,0},{2,3},{3,2},{4,5},{5,4},{6,7},{7,6},{8,9},{9,8},{10,11... | collective-permute-start | bytes 6291464 | tf_op jit(solution)/shard_map/ppermute | solution.py:347
  83.1 8.8 %collective-permute-start.18 = (bf16[64,16,128]{2,1,0:T(8,128)(2,1)S(1)}, bf16[64,16,128]{2,1,0:T(8,128)(2,1)S(1)}, u32[]{:S(2)}, u32[]{:S(2)}) collective-permute-start(bf16[64,16,128]{2,1,0:T(8,128)(2,1)S(1)} %slice.43), channel_id=1, source_target_pairs={{0,2},{1,3},{2,0},{3,1},{4,6},{5,7},{6,4},{7,5},{8,10},{9,11},{10,... | collective-permute-start | bytes 786440 | tf_op jit(solution)/shard_map/ppermute | solution.py:347
  84.6 8.4 %collective-permute-start.17 = (bf16[64,16,128]{2,1,0:T(8,128)(2,1)S(1)}, bf16[64,16,128]{2,1,0:T(8,128)(2,1)S(1)}, u32[]{:S(2)}, u32[]{:S(2)}) collective-permute-start(bf16[64,16,128]{2,1,0:T(8,128)(2,1)S(1)} %slice.42), channel_id=1, source_target_pairs={{0,4},{1,5},{2,6},{3,7},{4,0},{5,1},{6,2},{7,3},{8,12},{9,13},{10,... | collective-permute-start | bytes 786440 | tf_op jit(solution)/shard_map/ppermute | solution.py:347
  87.5 8.5 %collective-permute-start.21 = (bf16[512,16,128]{2,1,0:T(8,128)(2,1)}, bf16[512,16,128]{2,1,0:T(8,128)(2,1)}, u32[]{:S(2)}, u32[]{:S(2)}) collective-permute-start(bf16[512,16,128]{2,1,0:T(8,128)(2,1)} %constant_dynamic-update-slice_fusion.10.refs_2_), channel_id=1, source_target_pairs={{0,1},{1,0},{2,3},{3,2},{4,5},{5,4},{6,7},{7,6},{8,9},{9,8},{10,11... | collective-permute-start | bytes 6291464 | tf_op jit(solution)/shard_map/ppermute | solution.py:347
  87.7 5.5 %copy-start = (bf16[384,16,128]{2,1,0:T(8,128)(2,1)}, bf16[384,16,128]{2,1,0:T(8,128)(2,1)S(1)}, u32[]{:S(2)}) copy-start(bf16[384,16,128]{2,1,0:T(8,128)(2,1)S(1)} %constant_dynamic-update-slice_fusion.15.refs_3_) | copy-start | bytes 4718596
  91.8 4.2 %collective-permute-start.22 = (bf16[384,16,128]{2,1,0:T(8,128)(2,1)S(1)}, bf16[384,16,128]{2,1,0:T(8,128)(2,1)}, u32[]{:S(2)}, u32[]{:S(2)}) collective-permute-start(bf16[384,16,128]{2,1,0:T(8,128)(2,1)S(1)} %constant_dynamic-update-slice_fusion.15.refs_3_), channel_id=1, source_target_pairs={{0,1},{1,0},{2,3},{3,2},{4,5},{5,4},{6,7},{7,6},{8,9},{9,8},{10,11... | collective-permute-start | bytes 4718600 | tf_op jit(solution)/shard_map/ppermute | solution.py:347
  93.1 2.9 %copy-start.1 = (bf16[128,16,128]{2,1,0:T(8,128)(2,1)}, bf16[128,16,128]{2,1,0:T(8,128)(2,1)S(1)}, u32[]{:S(2)}) copy-start(bf16[128,16,128]{2,1,0:T(8,128)(2,1)S(1)} %constant_dynamic-update-slice_fusion.18.refs_4_) | copy-start | bytes 1572868
  93.1 2.9 %collective-permute-start.23 = (bf16[128,16,128]{2,1,0:T(8,128)(2,1)S(1)}, bf16[128,16,128]{2,1,0:T(8,128)(2,1)S(1)}, u32[]{:S(2)}, u32[]{:S(2)}) collective-permute-start(bf16[128,16,128]{2,1,0:T(8,128)(2,1)S(1)} %constant_dynamic-update-slice_fusion.18.refs_4_), channel_id=1, source_target_pairs={{0,1},{1,0},{2,3},{3,2},{4,5},{5,4},{6,7},{7,6},{8,9},{9,8},{10,11... | collective-permute-start | bytes 1572872 | tf_op jit(solution)/shard_map/ppermute | solution.py:347
  144.9 84.7 %collective-permute-start.26 = (f32[256,512]{1,0:T(8,128)}, f32[256,512]{1,0:T(8,128)S(1)}, u32[]{:S(2)}, u32[]{:S(2)}) collective-permute-start(f32[256,512]{1,0:T(8,128)} %get-tuple-element.57.refs_0_), channel_id=1, source_target_pairs={{0,24},{8,16},{16,8},{24,0},{1,25},{9,17},{17,9},{25,1},{2,26},{10... | collective-permute-start | bytes 1572872 | tf_op jit(solution)/shard_map/ppermute | solution.py:448
  147.6 82.0 %collective-permute-start.25 = (f32[256,512]{1,0:T(8,128)}, f32[256,512]{1,0:T(8,128)S(1)}, u32[]{:S(2)}, u32[]{:S(2)}) collective-permute-start(f32[256,512]{1,0:T(8,128)} %get-tuple-element.57.refs_0_), channel_id=1, source_target_pairs={{0,16},{8,24},{16,0},{24,8},{1,17},{9,25},{17,1},{25,9},{2,18},{10... | collective-permute-start | bytes 1572872 | tf_op jit(solution)/shard_map/ppermute | solution.py:448
  153.6 76.0 %collective-permute-start.24 = (f32[256,512]{1,0:T(8,128)}, f32[256,512]{1,0:T(8,128)S(1)}, u32[]{:S(2)}, u32[]{:S(2)}) collective-permute-start(f32[256,512]{1,0:T(8,128)} %get-tuple-element.57.refs_0_), channel_id=1, source_target_pairs={{0,8},{8,0},{16,24},{24,16},{1,9},{9,1},{17,25},{25,17},{2,10},{10... | collective-permute-start | bytes 1572872 | tf_op jit(solution)/shard_map/ppermute | solution.py:448
  (4 other events, 3.7 us)
Sparse Core Ops, SparseCore 0:
  144.4 42.0 all-gather.2

commit v10 on v9

--- a/solution.py
+++ b/solution.py
@@ -17,6 +17,7 @@
 rank_signs = (1.0, 1.0, -1.0, -1.0)
 NT = ((1,), (1,))
 NN = ((1,), (0,))
+TN = ((0,), (0,))
 VMEM = pl.BlockSpec(memory_space=pltpu.VMEM)
 SMEM = pl.BlockSpec(memory_space=pltpu.SMEM)
 
@@ -160,50 +161,70 @@
     def spread_row(x, row):
         return jnp.broadcast_to(x[row:row + 1, :], (SUB, BLK))
 
+    cols = [spread_lane(rows_a[0], k) for k in range(SUB)]
     for m in range(count):
         beside(m)
         head_a, head_v = rows_a[m], rows_v[m]
-        cols = [spread_lane(head_a, SUB * m + k) for k in range(SUB)]
         more = m + 1 < count
+        below, ahead, coming, later = [], [], [], []
+        beyond = m + 2 < count
+        if beyond:
+            later_a, later_v = rows_a[m + 2], rows_v[m + 2]
+            later = [spread_lane(later_a, SUB * m + k) for k in range(SUB)]
         if more:
             next_a, next_v = rows_a[m + 1], rows_v[m + 1]
             below = [spread_lane(next_a, SUB * m + k) for k in range(SUB)]
+            ahead = [spread_lane(head_a, SUB * (m + 1) + k) for k in range(SUB)]
+            coming = [spread_lane(next_a, SUB * (m + 1) + k) for k in range(SUB)]
         scale = jnp.zeros((SUB, BLK), jnp.float32)
-        done_a, done_v = [], []
         for j in range(SUB):
             pivot = spread_row(cols[j], j)
             root = lax.rsqrt(pivot)
             scale = jnp.where(sub_iota == j, root, scale)
             mult = jnp.where(sub_iota > j, cols[j], 0.0) * root
+            lead = [spread_row(cols[k], j) * root if k > j else None for k in range(SUB)]
             row_a = spread_row(head_a, j) * root
             row_v = spread_row(head_v, j) * root
-            lead = [spread_row(cols[k], j) * root if k > j else None for k in range(SUB)]
-            done_a.append(row_a)
-            done_v.append(row_v)
+            row_ahead = [spread_row(value, j) * root for value in ahead]
             if j + 1 < SUB:
                 for k in range(j + 1, SUB):
                     cols[k] = cols[k] - mult * lead[k]
                 head_a = head_a - mult * row_a
                 head_v = head_v - mult * row_v
+                ahead = [value - mult * row for value, row in zip(ahead, row_ahead)]
             if more:
                 mult_next = below[j] * root
                 for k in range(j + 1, SUB):
                     below[k] = below[k] - mult_next * lead[k]
+                coming = [value - mult_next * row for value, row in zip(coming, row_ahead)]
                 next_a = next_a - mult_next * row_a
                 next_v = next_v - mult_next * row_v
-        u = head_a * scale
-        u_ref[SUB * m:SUB * (m + 1), :] = jnp.where(lane_iota >= sub_iota + SUB * m, u, 0.0)
-        v_ref[SUB * m:SUB * (m + 1), :] = jnp.where(lane_iota <= sub_iota + SUB * m, head_v * scale, 0.0)
+            if beyond:
+                mult_later = later[j] * root
+                for k in range(j + 1, SUB):
+                    later[k] = later[k] - mult_later * lead[k]
+                later_a = later_a - mult_later * row_a
+                later_v = later_v - mult_later * row_v
+        u = jnp.where(lane_iota >= sub_iota + SUB * m, head_a * scale, 0.0)
+        v = jnp.where(lane_iota <= sub_iota + SUB * m, head_v * scale, 0.0)
+        u_ref[SUB * m:SUB * (m + 1), :] = u
+        v_ref[SUB * m:SUB * (m + 1), :] = v
         if more:
             rows_a[m + 1], rows_v[m + 1] = next_a, next_v
-        if m + 2 < count:
-            turned = u.T
-            for i in range(m + 2, count):
-                mine = turned[SUB * i:SUB * (i + 1), :]
-                for j in range(SUB):
-                    mult_i = spread_lane(mine, j)
-                    rows_a[i] = rows_a[i] - mult_i * done_a[j]
-                    rows_v[i] = rows_v[i] - mult_i * done_v[j]
+        if beyond:
+            rows_a[m + 2], rows_v[m + 2] = later_a, later_v
+        if m + 3 < count:
+            both = jnp.concatenate([u, v], axis=1)
+            u_hi, both_hi = u.astype(jnp.bfloat16).astype(jnp.float32), both.astype(jnp.bfloat16).astype(jnp.float32)
+            u_lo, both_lo = u - u_hi, both - both_hi
+            left = jnp.concatenate([u_hi, u_hi, u_lo, u_lo], axis=0).astype(jnp.bfloat16)
+            right = jnp.concatenate([both_hi, both_lo, both_hi, both_lo], axis=0).astype(jnp.bfloat16)
+            change = dot_bf16(left, right, TN)
+            for i in range(m + 3, count):
+                at = slice(SUB * i, SUB * (i + 1))
+                rows_a[i] = rows_a[i] - change[at, :BLK]
+                rows_v[i] = rows_v[i] - change[at, BLK:]
+        cols = coming
 
 
 def factor_kernel(yx_ref, yz_ref, lh_ref, ll_ref, d_ref, w_ref, g_ref, u_ref, v_ref):
@@ -349,7 +370,7 @@
     span = pcol_count // 2
     level_of = {j: bin(j).count("1") for j in range(1, span)}
     levels = max(level_of.values(), default=0)
-    order = [0] + list(range(1, prow_count, 2)) + list(range(2, prow_count, 2))
+    order = [0] + [1] * (prow_count > 1) + list(range(2, prow_count, 2)) + list(range(3, prow_count, 2))
     items = {0: mine}
     held = {turn: {} for turn in order}
     parts = []
@@ -369,8 +390,8 @@
         if phase < len(order):
             turn = order[phase]
             held[turn][0] = items[turn]
-            if turn % 2 == 1 and turn > 1:
-                moved["z", turn - 1] = [swap("prow", prow_count, 1, items[turn])]
+            if turn % 2 == 0 and turn > 0:
+                moved["z", turn + 1] = [swap("prow", prow_count, 1, items[turn])]
         for level in range(1, levels + 1):
             if 0 <= phase - level + 1 < len(order):
                 turn = order[phase - level + 1]
@@ -379,7 +400,7 @@
                         moved[turn, j] = spread(turn, j)
         if phase + 1 < len(order):
             turn = order[phase + 1]
-            if turn % 2 == 1:
+            if turn == 1 or turn % 2 == 0:
                 moved["z", turn] = [swap("prow", prow_count, turn, mine)]
             elif turn in items:
                 moved["z", turn] = [items[turn]]

time: 257 us -> 258 us (level)
  waiting for transfers between devices: 40.9 us -> 58.1 us
  starting transfers between devices: 41.5 us -> 28.1 us
  Pallas kernels: 142 us -> 139 us
    ppermute x24, waiting for transfers between devices: 40.8 us -> 58 us  [swap(): return lax.ppermute(value, axis, [(n, n ^ turn) for n in range(count)])]
    ppermute x24, starting transfers between devices: 32.2 us -> 23.7 us  [swap(): return lax.ppermute(value, axis, [(n, n ^ turn) for n in range(count)])]
    ppermute x3, starting transfers between devices: 9.24 us -> 4.39 us  [per_device(): lax.ppermute(top, 'prow', [(n, n ^ turn) for n in range(prow_count)])]
    pallas_call x1, Pallas kernels: 75.4 us -> 72.4 us  [factor(): pl.pallas_call(factor_kernel, out_shape=(jax.ShapeDtypeStruct((K, K), jnp...]
  transfers between devices with their start and end apart: 28 -> 28, of which waited for: 11 -> 9; matrix products, arithmetic and copies ran while one was open for 6% -> 6% of each run, Pallas kernels for 29% -> 28%
where the time goes in v10:
time: 258 us
  Pallas kernels  139 us (54%)
  waiting for transfers between devices  58.1 us (23%)
  starting transfers between devices  28.1 us (11%)
  local copies, waits for them, and re-layouts  16.3 us (6%)
  between operations  14.3 us (6%)
    pallas_call x1, Pallas kernels, factor(): pl.pallas_call(factor_kernel, out_shape=(jax.ShapeDtypeStruct((K, K), jnp...  72.4 us
    ppermute x24, waiting for transfers between devices, swap(): return lax.ppermute(value, axis, [(n, n ^ turn) for n in range(count)])  58 us
    pallas_call x1, Pallas kernels, assemble(): pl.pallas_call(body, grid=(pick_tiles + row_tiles * col_tiles,), out_shap...  47.4 us
    ppermute x24, starting transfers between devices, swap(): return lax.ppermute(value, axis, [(n, n ^ turn) for n in range(count)])  23.7 us
    pallas_call x1, Pallas kernels, solve(): pl.pallas_call(functools.partial(solve_kernel, prow=len(tops)), out_shape...  19.2 us
    unnamed x29, local copies, waits for them, and re-layouts  11.2 us
  transfers between devices with their start and end apart: 28, of which 9 were waited for; matrix products, arithmetic and copies ran while one was open for 6% of the time, Pallas kernels for 28%

profile of v10, /device:TPU:0, one launch (start us, length us, event | category | flops | bytes accessed | tf_op | source)
XLA Modules:
  0.0 257.6 jit_solution(12638498243355156194)
XLA Ops:
  7.2 1.4 copy.19
  8.9 3.1 %collective-permute-start.2 = (bf16[128,16,128]{2,1,0:T(8,128)(2,1)S(1)}, bf16[128,16,128]{2,1,0:T(8,128)(2,1)S(1)}, u32[]{:S(2)}, u32[]{:S(2)}) collective-permute-start(bf16[128,16,128]{2,1,0:T(8,128)(2,1)S(1)} %reshape.177), channel_id=1, source_target_pairs={{0,8},{8,0},{16,24},{24,16},{1,9},{9,1},{17,25},{25,17},{2,10},{10... | collective-permute-start | bytes 1572872 | tf_op jit(solution)/shard_map/ppermute | solution.py:368
  12.0 1.5 collective-permute-start.1
  13.5 1.5 collective-permute-start
  15.2 8.7 %collective-permute-done.2 = bf16[128,16,128]{2,1,0:T(8,128)(2,1)S(1)} collective-permute-done((bf16[128,16,128]{2,1,0:T(8,128)(2,1)S(1)}, bf16[128,16,128]{2,1,0:T(8,128)(2,1)S(1)}, u32[]{:S(2)}, u32[]{:S(2)}) %collective-permute-start.2) | collective-permute-done | bytes 524320 | tf_op jit(solution)/shard_map/ppermute | solution.py:368
  23.9 1.5 collective-permute-done.1
  25.4 1.2 collective-permute-done
  27.1 1.5 collective-permute-start.3
  28.6 2.6 %collective-permute-start.7 = (bf16[128,16,128]{2,1,0:T(8,128)(2,1)S(1)}, bf16[128,16,128]{2,1,0:T(8,128)(2,1)S(1)}, u32[]{:S(2)}, u32[]{:S(2)}) collective-permute-start(bf16[128,16,128]{2,1,0:T(8,128)(2,1)S(1)} %reshape.177), channel_id=1, source_target_pairs={{0,16},{8,24},{16,0},{24,8},{1,17},{9,25},{17,1},{25,9},{2,18},{10... | collective-permute-start | bytes 1572872 | tf_op jit(solution)/shard_map/ppermute | solution.py:368
  31.8 1.5 collective-permute-start.5
  33.5 0.8 constant_dynamic-update-slice_fusion.4
  34.3 0.8 constant_dynamic-update-slice_fusion.3
  35.1 9.6 %collective-permute-done.6 = bf16[64,16,128]{2,1,0:T(8,128)(2,1)S(1)} collective-permute-done((bf16[64,16,128]{2,1,0:T(8,128)(2,1)S(1)}, bf16[64,16,128]{2,1,0:T(8,128)(2,1)S(1)}, u32[]{:S(2)}, u32[]{:S(2)}) %collective-permute-start.6) | collective-permute-done | bytes 262176 | tf_op jit(solution)/shard_map/ppermute | solution.py:368
  44.7 7.7 %collective-permute-done.7 = bf16[128,16,128]{2,1,0:T(8,128)(2,1)S(1)} collective-permute-done((bf16[128,16,128]{2,1,0:T(8,128)(2,1)S(1)}, bf16[128,16,128]{2,1,0:T(8,128)(2,1)S(1)}, u32[]{:S(2)}, u32[]{:S(2)}) %collective-permute-start.7) | collective-permute-done | bytes 524320 | tf_op jit(solution)/shard_map/ppermute | solution.py:368
  52.4 1.3 collective-permute-start.10
  54.3 1.2 constant_dynamic-update-slice_fusion.2
  55.5 1.6 collective-permute-start.12
  59.3 0.8 constant_dynamic-update-slice_fusion.8
  61.0 12.0 %collective-permute-done.12 = bf16[64,16,128]{2,1,0:T(8,128)(2,1)S(1)} collective-permute-done((bf16[64,16,128]{2,1,0:T(8,128)(2,1)S(1)}, bf16[64,16,128]{2,1,0:T(8,128)(2,1)S(1)}, u32[]{:S(2)}, u32[]{:S(2)}) %collective-permute-start.12) | collective-permute-done | bytes 262176 | tf_op jit(solution)/shard_map/ppermute | solution.py:368
  75.0 1.6 collective-permute-start.16
  76.6 1.4 collective-permute-start.15
  79.4 0.9 constant_dynamic-update-slice_fusion.13
  80.2 1.0 constant_dynamic-update-slice_fusion.12
  81.2 10.5 %collective-permute-done.16 = bf16[64,16,128]{2,1,0:T(8,128)(2,1)S(1)} collective-permute-done((bf16[64,16,128]{2,1,0:T(8,128)(2,1)S(1)}, bf16[64,16,128]{2,1,0:T(8,128)(2,1)S(1)}, u32[]{:S(2)}, u32[]{:S(2)}) %collective-permute-start.16) | collective-permute-done | bytes 262176 | tf_op jit(solution)/shard_map/ppermute | solution.py:368
  92.3 1.4 collective-permute-start.17
  95.4 5.2 %collective-permute-done.18 = bf16[64,16,128]{2,1,0:T(8,128)(2,1)S(1)} collective-permute-done((bf16[64,16,128]{2,1,0:T(8,128)(2,1)S(1)}, bf16[64,16,128]{2,1,0:T(8,128)(2,1)S(1)}, u32[]{:S(2)}, u32[]{:S(2)}) %collective-permute-start.18) | collective-permute-done | bytes 262176 | tf_op jit(solution)/shard_map/ppermute | solution.py:368
  103.1 1.6 collective-permute-done.23.refs_9_
  105.5 47.4 %shard_map.68 = (bf16[4,1024,512]{2,1,0:T(8,128)(2,1)}, bf16[4,1024,512]{2,1,0:T(8,128)(2,1)}, f32[1024,512]{1,0:T(8,128)}, f32[1024,128]{1,0:T(8,128)}, f32[256,512]{1,0:T(8,128)}) custom-call(s32[2560]{0:T(1024)} %reshape.176.slots_ref, bf16[512,512]{1,0:T(8,128)(2,1)} %x_ref.1, bf16[512,512]{1,0:T(8,128)(2,1)} %z_ref.1, ...), custom_call_target="tpu_custom_call" | custom-call | flops 28000000000 | bytes 31457280 | tf_op jit(solution)/shard_map/pallas_call | solution.py:132
  153.6 0.8 collective-permute-start.26
  154.5 3.6 %collective-permute-start.24 = (f32[256,512]{1,0:T(8,128)}, f32[256,512]{1,0:T(8,128)S(1)}, u32[]{:S(2)}, u32[]{:S(2)}) collective-permute-start(f32[256,512]{1,0:T(8,128)} %get-tuple-element.57.refs_0_), channel_id=1, source_target_pairs={{0,8},{8,0},{16,24},{24,16},{1,9},{9,1},{17,25},{25,17},{2,10},{10... | collective-permute-start | bytes 1572872 | tf_op jit(solution)/shard_map/ppermute | solution.py:469
  158.0 72.4 %shard_map.69 = (bf16[1024,1024]{1,0:T(8,128)(2,1)}, bf16[1024,1024]{1,0:T(8,128)(2,1)}, f32[1024,128]{1,0:T(8,128)}) custom-call(bf16[4,1024,512]{2,1,0:T(8,128)(2,1)} %get-tuple-element.50.yx_ref, bf16[4,1024,512]{2,1,0:T(8,128)(2,1)} %get-tuple-element.51.yz_ref), custom_call_target="tpu_custom_call" | custom-call | flops 40000000000 | bytes 12582912 | tf_op jit(solution)/shard_map/pallas_call | solution.py:288
  231.5 19.2 %shard_map.70 = (f32[1024,512]{1,0:T(8,128)}, f32[1024,128]{1,0:T(8,128)}) custom-call(s32[2]{0:T(128)} %pad_add_fusion.1.place_ref, bf16[1024,1024]{1,0:T(8,128)(2,1)} %get-tuple-element.52.lh_any, bf16[1024,1024]{1,0:T(8,128)(2,1)} %get-tuple-element.53.ll_any, f32[1024,128]{1,0:T(8,128)} %get-tuple-element.54.d_any, f32[8,1024,128]{2,1,0:T(8,128)} %bitcast.51, ...), custom_call_target="tpu_custom_call" | custom-call | flops 12000000000 | bytes 25165824 | tf_op jit(solution)/shard_map/pallas_call | solution.py:350
  (88 shorter events, 16.0 us)
Async XLA Ops:
  7.2 7.8 %copy-start.7 = (s32[32]{0:T(128)S(1)}, s32[32]{0:T(128)}, u32[]{:S(2)}) copy-start(s32[32]{0:T(128)} %constant.92.clone) | copy-start | bytes 388
  7.2 26.2 %copy-start.2 = (s32[4096]{0:T(1024)S(1)}, s32[4096]{0:T(1024)}, u32[]{:S(2)}) copy-start(s32[4096]{0:T(1024)} %param.8) | copy-start | bytes 49156
  7.2 223.3 %all-gather.3.cloned.1.call-start = ((), (), s32[]{:S(2)}) async-start(), calls=%async_computation | async-start | bytes 4718592 | tf_op jit(solution)/shard_map/all_gather | solution.py:468
  8.9 15.0 %collective-permute-start.2 = (bf16[128,16,128]{2,1,0:T(8,128)(2,1)S(1)}, bf16[128,16,128]{2,1,0:T(8,128)(2,1)S(1)}, u32[]{:S(2)}, u32[]{:S(2)}) collective-permute-start(bf16[128,16,128]{2,1,0:T(8,128)(2,1)S(1)} %reshape.177), channel_id=1, source_target_pairs={{0,8},{8,0},{16,24},{24,16},{1,9},{9,1},{17,25},{25,17},{2,10},{10... | collective-permute-start | bytes 1572872 | tf_op jit(solution)/shard_map/ppermute | solution.py:368
  12.0 13.4 %collective-permute-start.1 = (bf16[128,16,128]{2,1,0:T(8,128)(2,1)S(1)}, bf16[128,16,128]{2,1,0:T(8,128)(2,1)S(1)}, u32[]{:S(2)}, u32[]{:S(2)}) collective-permute-start(bf16[128,16,128]{2,1,0:T(8,128)(2,1)S(1)} %reshape.177), channel_id=1, source_target_pairs={{0,4},{1,5},{2,6},{3,7},{4,0},{5,1},{6,2},{7,3},{8,12},{9,13},{10,... | collective-permute-start | bytes 1572872 | tf_op jit(solution)/shard_map/ppermute | solution.py:368
  13.5 13.1 %collective-permute-start = (bf16[128,16,128]{2,1,0:T(8,128)(2,1)S(1)}, bf16[128,16,128]{2,1,0:T(8,128)(2,1)S(1)}, u32[]{:S(2)}, u32[]{:S(2)}) collective-permute-start(bf16[128,16,128]{2,1,0:T(8,128)(2,1)S(1)} %reshape.177), channel_id=1, source_target_pairs={{0,2},{1,3},{2,0},{3,1},{4,6},{5,7},{6,4},{7,5},{8,10},{9,11},{10,... | collective-permute-start | bytes 1572872 | tf_op jit(solution)/shard_map/ppermute | solution.py:368
  26.6 25.8 %collective-permute-start.4 = (bf16[128,16,128]{2,1,0:T(8,128)(2,1)S(1)}, bf16[128,16,128]{2,1,0:T(8,128)(2,1)S(1)}, u32[]{:S(2)}, u32[]{:S(2)}) collective-permute-start(bf16[128,16,128]{2,1,0:T(8,128)(2,1)S(1)} %collective-permute-done.2), channel_id=1, source_target_pairs={{0,4},{1,5},{2,6},{3,7},{4,0},{5,1},{6,2},{7,3},{8,12},{9,13},{10,... | collective-permute-start | bytes 1572872 | tf_op jit(solution)/shard_map/ppermute | solution.py:368
  27.1 25.3 %collective-permute-start.3 = (bf16[128,16,128]{2,1,0:T(8,128)(2,1)S(1)}, bf16[128,16,128]{2,1,0:T(8,128)(2,1)S(1)}, u32[]{:S(2)}, u32[]{:S(2)}) collective-permute-start(bf16[128,16,128]{2,1,0:T(8,128)(2,1)S(1)} %collective-permute-done.2), channel_id=1, source_target_pairs={{0,2},{1,3},{2,0},{3,1},{4,6},{5,7},{6,4},{7,5},{8,10},{9,11},{10,... | collective-permute-start | bytes 1572872 | tf_op jit(solution)/shard_map/ppermute | solution.py:368
  28.6 23.8 %collective-permute-start.7 = (bf16[128,16,128]{2,1,0:T(8,128)(2,1)S(1)}, bf16[128,16,128]{2,1,0:T(8,128)(2,1)S(1)}, u32[]{:S(2)}, u32[]{:S(2)}) collective-permute-start(bf16[128,16,128]{2,1,0:T(8,128)(2,1)S(1)} %reshape.177), channel_id=1, source_target_pairs={{0,16},{8,24},{16,0},{24,8},{1,17},{9,25},{17,1},{25,9},{2,18},{10... | collective-permute-start | bytes 1572872 | tf_op jit(solution)/shard_map/ppermute | solution.py:368
  31.2 13.5 %collective-permute-start.6 = (bf16[64,16,128]{2,1,0:T(8,128)(2,1)S(1)}, bf16[64,16,128]{2,1,0:T(8,128)(2,1)S(1)}, u32[]{:S(2)}, u32[]{:S(2)}) collective-permute-start(bf16[64,16,128]{2,1,0:T(8,128)(2,1)S(1)} %slice.37), channel_id=1, source_target_pairs={{0,2},{1,3},{2,0},{3,1},{4,6},{5,7},{6,4},{7,5},{8,10},{9,11},{10,... | collective-permute-start | bytes 786440 | tf_op jit(solution)/shard_map/ppermute | solution.py:368
  31.8 12.9 %collective-permute-start.5 = (bf16[64,16,128]{2,1,0:T(8,128)(2,1)S(1)}, bf16[64,16,128]{2,1,0:T(8,128)(2,1)S(1)}, u32[]{:S(2)}, u32[]{:S(2)}) collective-permute-start(bf16[64,16,128]{2,1,0:T(8,128)(2,1)S(1)} %slice.36), channel_id=1, source_target_pairs={{0,4},{1,5},{2,6},{3,7},{4,0},{5,1},{6,2},{7,3},{8,12},{9,13},{10,... | collective-permute-start | bytes 786440 | tf_op jit(solution)/shard_map/ppermute | solution.py:368
  52.4 20.5 %collective-permute-start.10 = (bf16[128,16,128]{2,1,0:T(8,128)(2,1)S(1)}, bf16[128,16,128]{2,1,0:T(8,128)(2,1)S(1)}, u32[]{:S(2)}, u32[]{:S(2)}) collective-permute-start(bf16[128,16,128]{2,1,0:T(8,128)(2,1)S(1)} %collective-permute-done.7), channel_id=1, source_target_pairs={{0,4},{1,5},{2,6},{3,7},{4,0},{5,1},{6,2},{7,3},{8,12},{9,13},{10,... | collective-permute-start | bytes 1572872 | tf_op jit(solution)/shard_map/ppermute | solution.py:368
  53.8 19.2 %collective-permute-start.9 = (bf16[128,16,128]{2,1,0:T(8,128)(2,1)S(1)}, bf16[128,16,128]{2,1,0:T(8,128)(2,1)S(1)}, u32[]{:S(2)}, u32[]{:S(2)}) collective-permute-start(bf16[128,16,128]{2,1,0:T(8,128)(2,1)S(1)} %collective-permute-done.7), channel_id=1, source_target_pairs={{0,2},{1,3},{2,0},{3,1},{4,6},{5,7},{6,4},{7,5},{8,10},{9,11},{10,... | collective-permute-start | bytes 1572872 | tf_op jit(solution)/shard_map/ppermute | solution.py:368
  54.3 18.7 %collective-permute-start.8 = (bf16[128,16,128]{2,1,0:T(8,128)(2,1)S(1)}, bf16[128,16,128]{2,1,0:T(8,128)(2,1)S(1)}, u32[]{:S(2)}, u32[]{:S(2)}) collective-permute-start(bf16[128,16,128]{2,1,0:T(8,128)(2,1)S(1)} %collective-permute-done.7), channel_id=1, source_target_pairs={{0,8},{8,0},{16,24},{24,16},{1,9},{9,1},{17,25},{25,17},{2,10},{10... | collective-permute-start | bytes 1572872 | tf_op jit(solution)/shard_map/ppermute | solution.py:368
  55.5 17.4 %collective-permute-start.12 = (bf16[64,16,128]{2,1,0:T(8,128)(2,1)S(1)}, bf16[64,16,128]{2,1,0:T(8,128)(2,1)S(1)}, u32[]{:S(2)}, u32[]{:S(2)}) collective-permute-start(bf16[64,16,128]{2,1,0:T(8,128)(2,1)S(1)} %slice.39), channel_id=1, source_target_pairs={{0,2},{1,3},{2,0},{3,1},{4,6},{5,7},{6,4},{7,5},{8,10},{9,11},{10,... | collective-permute-start | bytes 786440 | tf_op jit(solution)/shard_map/ppermute | solution.py:368
  57.1 15.9 %collective-permute-start.11 = (bf16[64,16,128]{2,1,0:T(8,128)(2,1)S(1)}, bf16[64,16,128]{2,1,0:T(8,128)(2,1)S(1)}, u32[]{:S(2)}, u32[]{:S(2)}) collective-permute-start(bf16[64,16,128]{2,1,0:T(8,128)(2,1)S(1)} %slice.38), channel_id=1, source_target_pairs={{0,4},{1,5},{2,6},{3,7},{4,0},{5,1},{6,2},{7,3},{8,12},{9,13},{10,... | collective-permute-start | bytes 786440 | tf_op jit(solution)/shard_map/ppermute | solution.py:368
  73.0 18.7 %collective-permute-start.14 = (bf16[128,16,128]{2,1,0:T(8,128)(2,1)S(1)}, bf16[128,16,128]{2,1,0:T(8,128)(2,1)S(1)}, u32[]{:S(2)}, u32[]{:S(2)}) collective-permute-start(bf16[128,16,128]{2,1,0:T(8,128)(2,1)S(1)} %collective-permute-done.8), channel_id=1, source_target_pairs={{0,4},{1,5},{2,6},{3,7},{4,0},{5,1},{6,2},{7,3},{8,12},{9,13},{10,... | collective-permute-start | bytes 1572872 | tf_op jit(solution)/shard_map/ppermute | solution.py:368
  73.7 18.0 %collective-permute-start.13 = (bf16[128,16,128]{2,1,0:T(8,128)(2,1)S(1)}, bf16[128,16,128]{2,1,0:T(8,128)(2,1)S(1)}, u32[]{:S(2)}, u32[]{:S(2)}) collective-permute-start(bf16[128,16,128]{2,1,0:T(8,128)(2,1)S(1)} %collective-permute-done.8), channel_id=1, source_target_pairs={{0,2},{1,3},{2,0},{3,1},{4,6},{5,7},{6,4},{7,5},{8,10},{9,11},{10,... | collective-permute-start | bytes 1572872 | tf_op jit(solution)/shard_map/ppermute | solution.py:368
  74.9 29.7 %collective-permute-start.19 = (bf16[512,16,128]{2,1,0:T(8,128)(2,1)}, bf16[512,16,128]{2,1,0:T(8,128)(2,1)}, u32[]{:S(2)}, u32[]{:S(2)}) collective-permute-start(bf16[512,16,128]{2,1,0:T(8,128)(2,1)} %constant_dynamic-update-slice_fusion.refs_0_), channel_id=1, source_target_pairs={{0,1},{1,0},{2,3},{3,2},{4,5},{5,4},{6,7},{7,6},{8,9},{9,8},{10,11... | collective-permute-start | bytes 6291464 | tf_op jit(solution)/shard_map/ppermute | solution.py:368
  75.0 16.7 %collective-permute-start.16 = (bf16[64,16,128]{2,1,0:T(8,128)(2,1)S(1)}, bf16[64,16,128]{2,1,0:T(8,128)(2,1)S(1)}, u32[]{:S(2)}, u32[]{:S(2)}) collective-permute-start(bf16[64,16,128]{2,1,0:T(8,128)(2,1)S(1)} %slice.41), channel_id=1, source_target_pairs={{0,2},{1,3},{2,0},{3,1},{4,6},{5,7},{6,4},{7,5},{8,10},{9,11},{10,... | collective-permute-start | bytes 786440 | tf_op jit(solution)/shard_map/ppermute | solution.py:368
  76.6 15.1 %collective-permute-start.15 = (bf16[64,16,128]{2,1,0:T(8,128)(2,1)S(1)}, bf16[64,16,128]{2,1,0:T(8,128)(2,1)S(1)}, u32[]{:S(2)}, u32[]{:S(2)}) collective-permute-start(bf16[64,16,128]{2,1,0:T(8,128)(2,1)S(1)} %slice.40), channel_id=1, source_target_pairs={{0,4},{1,5},{2,6},{3,7},{4,0},{5,1},{6,2},{7,3},{8,12},{9,13},{10,... | collective-permute-start | bytes 786440 | tf_op jit(solution)/shard_map/ppermute | solution.py:368
  91.7 13.0 %collective-permute-start.20 = (bf16[512,16,128]{2,1,0:T(8,128)(2,1)}, bf16[512,16,128]{2,1,0:T(8,128)(2,1)}, u32[]{:S(2)}, u32[]{:S(2)}) collective-permute-start(bf16[512,16,128]{2,1,0:T(8,128)(2,1)} %constant_dynamic-update-slice_fusion.5.refs_1_), channel_id=1, source_target_pairs={{0,1},{1,0},{2,3},{3,2},{4,5},{5,4},{6,7},{7,6},{8,9},{9,8},{10,11... | collective-permute-start | bytes 6291464 | tf_op jit(solution)/shard_map/ppermute | solution.py:368
  91.7 8.8 %collective-permute-start.18 = (bf16[64,16,128]{2,1,0:T(8,128)(2,1)S(1)}, bf16[64,16,128]{2,1,0:T(8,128)(2,1)S(1)}, u32[]{:S(2)}, u32[]{:S(2)}) collective-permute-start(bf16[64,16,128]{2,1,0:T(8,128)(2,1)S(1)} %slice.43), channel_id=1, source_target_pairs={{0,2},{1,3},{2,0},{3,1},{4,6},{5,7},{6,4},{7,5},{8,10},{9,11},{10,... | collective-permute-start | bytes 786440 | tf_op jit(solution)/shard_map/ppermute | solution.py:368
  92.3 8.9 %collective-permute-start.17 = (bf16[64,16,128]{2,1,0:T(8,128)(2,1)S(1)}, bf16[64,16,128]{2,1,0:T(8,128)(2,1)S(1)}, u32[]{:S(2)}, u32[]{:S(2)}) collective-permute-start(bf16[64,16,128]{2,1,0:T(8,128)(2,1)S(1)} %slice.42), channel_id=1, source_target_pairs={{0,4},{1,5},{2,6},{3,7},{4,0},{5,1},{6,2},{7,3},{8,12},{9,13},{10,... | collective-permute-start | bytes 786440 | tf_op jit(solution)/shard_map/ppermute | solution.py:368
  95.2 9.5 %collective-permute-start.21 = (bf16[512,16,128]{2,1,0:T(8,128)(2,1)}, bf16[512,16,128]{2,1,0:T(8,128)(2,1)}, u32[]{:S(2)}, u32[]{:S(2)}) collective-permute-start(bf16[512,16,128]{2,1,0:T(8,128)(2,1)} %constant_dynamic-update-slice_fusion.10.refs_2_), channel_id=1, source_target_pairs={{0,1},{1,0},{2,3},{3,2},{4,5},{5,4},{6,7},{7,6},{8,9},{9,8},{10,11... | collective-permute-start | bytes 6291464 | tf_op jit(solution)/shard_map/ppermute | solution.py:368
  95.3 5.9 %copy-start = (bf16[384,16,128]{2,1,0:T(8,128)(2,1)}, bf16[384,16,128]{2,1,0:T(8,128)(2,1)S(1)}, u32[]{:S(2)}) copy-start(bf16[384,16,128]{2,1,0:T(8,128)(2,1)S(1)} %constant_dynamic-update-slice_fusion.15.refs_3_) | copy-start | bytes 4718596
  100.5 4.2 %collective-permute-start.22 = (bf16[384,16,128]{2,1,0:T(8,128)(2,1)S(1)}, bf16[384,16,128]{2,1,0:T(8,128)(2,1)}, u32[]{:S(2)}, u32[]{:S(2)}) collective-permute-start(bf16[384,16,128]{2,1,0:T(8,128)(2,1)S(1)} %constant_dynamic-update-slice_fusion.15.refs_3_), channel_id=1, source_target_pairs={{0,1},{1,0},{2,3},{3,2},{4,5},{5,4},{6,7},{7,6},{8,9},{9,8},{10,11... | collective-permute-start | bytes 4718600 | tf_op jit(solution)/shard_map/ppermute | solution.py:368
  101.3 3.4 %copy-start.1 = (bf16[128,16,128]{2,1,0:T(8,128)(2,1)}, bf16[128,16,128]{2,1,0:T(8,128)(2,1)S(1)}, u32[]{:S(2)}) copy-start(bf16[128,16,128]{2,1,0:T(8,128)(2,1)S(1)} %constant_dynamic-update-slice_fusion.18.refs_4_) | copy-start | bytes 1572868
  101.3 3.4 %collective-permute-start.23 = (bf16[128,16,128]{2,1,0:T(8,128)(2,1)S(1)}, bf16[128,16,128]{2,1,0:T(8,128)(2,1)S(1)}, u32[]{:S(2)}, u32[]{:S(2)}) collective-permute-start(bf16[128,16,128]{2,1,0:T(8,128)(2,1)S(1)} %constant_dynamic-update-slice_fusion.18.refs_4_), channel_id=1, source_target_pairs={{0,1},{1,0},{2,3},{3,2},{4,5},{5,4},{6,7},{7,6},{8,9},{9,8},{10,11... | collective-permute-start | bytes 1572872 | tf_op jit(solution)/shard_map/ppermute | solution.py:368
  153.6 76.8 %collective-permute-start.26 = (f32[256,512]{1,0:T(8,128)}, f32[256,512]{1,0:T(8,128)S(1)}, u32[]{:S(2)}, u32[]{:S(2)}) collective-permute-start(f32[256,512]{1,0:T(8,128)} %get-tuple-element.57.refs_0_), channel_id=1, source_target_pairs={{0,24},{8,16},{16,8},{24,0},{1,25},{9,17},{17,9},{25,1},{2,26},{10... | collective-permute-start | bytes 1572872 | tf_op jit(solution)/shard_map/ppermute | solution.py:469
  154.4 75.9 %collective-permute-start.25 = (f32[256,512]{1,0:T(8,128)}, f32[256,512]{1,0:T(8,128)S(1)}, u32[]{:S(2)}, u32[]{:S(2)}) collective-permute-start(f32[256,512]{1,0:T(8,128)} %get-tuple-element.57.refs_0_), channel_id=1, source_target_pairs={{0,16},{8,24},{16,0},{24,8},{1,17},{9,25},{17,1},{25,9},{2,18},{10... | collective-permute-start | bytes 1572872 | tf_op jit(solution)/shard_map/ppermute | solution.py:469
  154.5 76.0 %collective-permute-start.24 = (f32[256,512]{1,0:T(8,128)}, f32[256,512]{1,0:T(8,128)S(1)}, u32[]{:S(2)}, u32[]{:S(2)}) collective-permute-start(f32[256,512]{1,0:T(8,128)} %get-tuple-element.57.refs_0_), channel_id=1, source_target_pairs={{0,8},{8,0},{16,24},{24,16},{1,9},{9,1},{17,25},{25,17},{2,10},{10... | collective-permute-start | bytes 1572872 | tf_op jit(solution)/shard_map/ppermute | solution.py:469
  (4 other events, 3.7 us)
Sparse Core Ops, SparseCore 0:
  153.1 33.8 all-gather.2

commit v11 on v8

--- a/solution.py
+++ b/solution.py
@@ -35,7 +35,7 @@
     return dot_bf16(a[0], b[0], dims) + (dot_bf16(a[0], b[1], dims) + dot_bf16(a[1], b[0], dims))
 
 
-def assemble_kernel(slots_ref, x_ref, z_ref, *refs, sources, lead_tiles, pick_tiles, col_tiles, rows):
+def assemble_kernel(place_ref, slots_ref, x_ref, z_ref, *refs, sources, lead_tiles, pick_tiles, col_tiles, rows, prow, pcol):
     source_refs, refs = refs[:sources], refs[sources:]
     lead_x_ref, lead_z_ref, schur_ref, front_ref, top_ref, every_ref, picked_ref, yx_ref, yz_ref, sem_ref = refs
     step = pl.program_id(0)
@@ -68,14 +68,35 @@
         images_x = dot_bf16(mine, x_ref[...], NN).astype(jnp.bfloat16).reshape(RANK, tile, width)
         images_z = dot_bf16(mine, z_ref[...], NN).astype(jnp.bfloat16).reshape(RANK, tile, width)
 
+        def keep(block, s):
+            at = pl.ds(pl.multiple_of(block * NB, NB), NB)
+            yx_ref[:, at, :] = images_x[:, s * NB:(s + 1) * NB, :]
+            yz_ref[:, at, :] = images_z[:, s * NB:(s + 1) * NB, :]
+
         @pl.when(step < lead_tiles)
         def _():
             lead_x_ref[...], lead_z_ref[...] = images_x, images_z
+            for s in range(tile // NB):
+                block = step * (tile // NB) + s
+
+                @pl.when(block % prow == place_ref[0])
+                def _():
+                    keep(block // prow, s)
+
+                @pl.when(block % pcol == place_ref[1])
+                def _():
+                    keep(rows // NB + block // pcol, s)
 
         @pl.when(step >= lead_tiles)
         def _():
-            at = pl.ds(pl.multiple_of((step - lead_tiles) * tile, tile), tile)
-            yx_ref[:, at, :], yz_ref[:, at, :] = images_x, images_z
+            lead = K // NB
+            row_rest, col_rest = rows // NB - lead // prow, (yx_ref.shape[1] - rows) // NB - lead // pcol
+            for s in range(tile // NB):
+                block = (step - lead_tiles) * (tile // NB) + s
+
+                @pl.when(block < row_rest + col_rest)
+                def _():
+                    keep(jnp.where(block < row_rest, lead // prow + block, rows // NB + lead // pcol + block - row_rest), s)
 
     @pl.when(step >= pick_tiles)
     def _():
@@ -114,7 +135,7 @@
     return total + term if rank_signs[q] * rank_signs[r] > 0 else total - term
 
 
-def assemble(slots, sources, x_factor, z_factor, rows, cols, lead_rows, lead_cols):
+def assemble(place, slots, sources, x_factor, z_factor, rows, cols, lead_rows, lead_cols):
     _, parts, lanes = sources[0].shape
     slots_held = sum(source.shape[0] for source in sources)
     width = x_factor.shape[0]
@@ -127,7 +148,7 @@
     after = lambda s: jnp.maximum(s - pick_tiles, 0)
     bf16 = jnp.bfloat16
     any_space = pl.BlockSpec(memory_space=pl.ANY)
-    body = functools.partial(assemble_kernel, sources=len(sources), lead_tiles=lead_tiles, pick_tiles=pick_tiles, col_tiles=col_tiles, rows=rows)
+    body = functools.partial(assemble_kernel, sources=len(sources), lead_tiles=lead_tiles, pick_tiles=pick_tiles, col_tiles=col_tiles, rows=rows, prow=K // lead_rows, pcol=K // lead_cols)
     return pl.pallas_call(
         body,
         grid=(pick_tiles + row_tiles * col_tiles,),
@@ -135,7 +156,7 @@
             jax.ShapeDtypeStruct((rows, cols), jnp.float32),
             jax.ShapeDtypeStruct((rows, lead_cols), jnp.float32),
             jax.ShapeDtypeStruct((lead_rows, cols), jnp.float32)),
-        in_specs=[SMEM, whole, whole] + [any_space] * len(sources),
+        in_specs=[SMEM, SMEM, whole, whole] + [any_space] * len(sources),
         out_specs=(lead, lead,
                    pl.BlockSpec((high, wide), lambda s: (after(s) // col_tiles, after(s) % col_tiles)),
                    pl.BlockSpec((high, lead_cols), lambda s: (after(s) // col_tiles, 0)),
@@ -144,7 +165,7 @@
         + [pltpu.VMEM((RANK, rows + cols, width), bf16)] * 2 + [pltpu.SemaphoreType.DMA((len(sources),))],
         compiler_params=pltpu.CompilerParams(vmem_limit_bytes=58 * MIB),
         cost_estimate=pl.CostEstimate(flops=28 * 10**9, bytes_accessed=30 * MIB, transcendentals=0),
-    )(slots, x_factor, z_factor, *sources)
+    )(place, slots, x_factor, z_factor, *sources)
 
 
 def factor_block(block, u_ref, v_ref, beside):
@@ -225,21 +246,13 @@
             @pl.when(b == k)
             def _():
                 first = (k + 1) * BLK
-                inv = split(v_ref[...])
-
-                def panel(t, c):
-                    rows = pl.ds(pl.multiple_of(first + t * BLK, BLK), BLK)
-                    lh_ref[rows, k * BLK:first], ll_ref[rows, k * BLK:first] = split(dot3(split(w_ref[rows, k * BLK:first]), inv, NT))
-                    return c
-                lax.fori_loop(0, steps - 1 - k, panel, 0)
-                right = (lh_ref[first:, k * BLK:first], ll_ref[first:, k * BLK:first])
-
-                def update(t, c):
-                    rows = pl.ds(pl.multiple_of(first + t * BLK, BLK), BLK)
-                    left = (lh_ref[rows, k * BLK:first], ll_ref[rows, k * BLK:first])
-                    w_ref[rows, first:] = w_ref[rows, first:] - dot3(left, right, NT)
-                    return c
-                lax.fori_loop(0, steps - 1 - k, update, 0)
+                column = slice(k * BLK, first)
+                lh_ref[first:, column], ll_ref[first:, column] = split(dot3(split(w_ref[first:, column]), split(v_ref[...]), NT))
+                for top in range(first, order, tile):
+                    bottom = min(top + tile, order)
+                    left = (lh_ref[top:bottom, column], ll_ref[top:bottom, column])
+                    right = (lh_ref[first:bottom, column], ll_ref[first:bottom, column])
+                    w_ref[top:bottom, first:bottom] = w_ref[top:bottom, first:bottom] - dot3(left, right, NT)
                 if k % 2 == 1:
                     w_ref[first:, first:first + tile] = w_ref[first:, first:first + tile] + g_ref[first:, :]
         return carry
@@ -336,8 +349,6 @@
     levels = max(level_of.values(), default=0)
     order = [0] + list(range(1, prow_count, 2)) + list(range(2, prow_count, 2))
     items = {0: mine}
-    for turn in range(1, prow_count, 2):
-        items[turn] = swap("prow", prow_count, turn, mine)
     held = {turn: {} for turn in order}
     parts = []
 
@@ -364,9 +375,14 @@
                 for j in range(1, span):
                     if level_of[j] == level:
                         moved[turn, j] = spread(turn, j)
-        if phase + 1 < len(order) and order[phase + 1] in items:
-            moved["z", order[phase + 1]] = [items[order[phase + 1]]]
-        results = iter(lax.optimization_barrier([value for values in moved.values() for value in values]))
+        if phase + 1 < len(order):
+            turn = order[phase + 1]
+            if turn % 2 == 1:
+                moved["z", turn] = [swap("prow", prow_count, turn, mine)]
+            elif turn in items:
+                moved["z", turn] = [items[turn]]
+        mine, *results = lax.optimization_barrier([mine] + [value for values in moved.values() for value in values])
+        results = iter(results)
         for (turn, j), values in moved.items():
             arrived = [next(results) for _ in values]
             if turn == "z":
@@ -422,14 +438,16 @@
     found = places_of(placement, order, prow_id, pcol_id, pcol_count)
     by_row = lax.dynamic_index_in_dim(found.reshape(local_rows // NB, prow_count, NB), prow_id, 1, keepdims=False)
     by_col = lax.dynamic_index_in_dim(found.reshape(local_cols // NB, pcol_count, NB), pcol_id, 1, keepdims=False)
-    places = jnp.concatenate([found[:K // NB], by_row, by_col]).reshape(-1)
     lead_rows, lead_cols = K // prow_count, K // pcol_count
+    places = jnp.concatenate([found[:K // NB], by_row[lead_rows // NB:], by_col[lead_cols // NB:]])
+    places = jnp.pad(places, ((0, -places.shape[0] % (256 // NB)), (0, 0))).reshape(-1)
+    place = jnp.stack([prow_id, pcol_id]).astype(jnp.int32)
     lead_x, lead_z, schur_local, front, top = assemble(
-        places.astype(jnp.int32), sources, x_factor, zinv_factor, local_rows, local_cols, lead_rows, lead_cols)
+        place, places.astype(jnp.int32), sources, x_factor, zinv_factor, local_rows, local_cols, lead_rows, lead_cols)
     pieces = lax.all_gather(front, "pcol", axis=0, tiled=False)
     tops = [top] + [lax.ppermute(top, "prow", [(n, n ^ turn) for n in range(prow_count)]) for turn in range(1, prow_count)]
     high, low, inverses = factor(lead_x, lead_z)
-    return solve(jnp.stack([prow_id, pcol_id]).astype(jnp.int32), high, low, inverses, pieces, schur_local, tops)
+    return solve(place, high, low, inverses, pieces, schur_local, tops)
 
 
 def solution(mesh):

time: 248 us -> 237 us (0.956)
  Pallas kernels: 133 us -> 123 us
  waiting for transfers between devices: 45.3 us -> 40.3 us
  starting transfers between devices: 37.1 us -> 41.6 us
    pallas_call x1, Pallas kernels: 66.1 us -> 57.1 us  [factor(): pl.pallas_call(factor_kernel, out_shape=(jax.ShapeDtypeStruct((K, K), jnp...]
    ppermute x24, starting transfers between devices: 24.2 us -> 32.2 us  [swap(): return lax.ppermute(value, axis, [(n, n ^ turn) for n in range(count)])]
    ppermute x24, waiting for transfers between devices: 45.2 us -> 40.2 us  [swap(): return lax.ppermute(value, axis, [(n, n ^ turn) for n in range(count)])]
    ppermute x3, starting transfers between devices: 12.9 us -> 9.3 us  [per_device(): lax.ppermute(top, 'prow', [(n, n ^ turn) for n in range(prow_count)])]
    unnamed x29 -> x32, local copies, waits for them, and re-layouts: 11.2 us -> 11.5 us
  transfers between devices with their start and end apart: 28 -> 28, of which waited for: 10 -> 11; matrix products, arithmetic and copies ran while one was open for 6% -> 6% of each run, Pallas kernels for 27% -> 24%
where the time goes in v11:
time: 237 us
  Pallas kernels  123 us (52%)
  starting transfers between devices  41.6 us (18%)
  waiting for transfers between devices  40.3 us (17%)
  local copies, waits for them, and re-layouts  16.3 us (7%)
  between operations  14.3 us (6%)
    pallas_call x1, Pallas kernels, factor(): pl.pallas_call(factor_kernel, out_shape=(jax.ShapeDtypeStruct((K, K), jnp...  57.1 us
    pallas_call x1, Pallas kernels, assemble(): pl.pallas_call(body, grid=(pick_tiles + row_tiles * col_tiles,), out_shap...  46.3 us
    ppermute x24, waiting for transfers between devices, swap(): return lax.ppermute(value, axis, [(n, n ^ turn) for n in range(count)])  40.2 us
    ppermute x24, starting transfers between devices, swap(): return lax.ppermute(value, axis, [(n, n ^ turn) for n in range(count)])  32.2 us
    pallas_call x1, Pallas kernels, solve(): pl.pallas_call(functools.partial(solve_kernel, prow=len(tops)), out_shape...  19.2 us
    unnamed x32, local copies, waits for them, and re-layouts  11.5 us
    ppermute x3, starting transfers between devices, per_device(): lax.ppermute(top, 'prow', [(n, n ^ turn) for n in range(prow_count)])  9.3 us
  transfers between devices with their start and end apart: 28, of which 11 were waited for; matrix products, arithmetic and copies ran while one was open for 6% of the time, Pallas kernels for 24%

profile of v11, /device:TPU:0, one launch (start us, length us, event | category | flops | bytes accessed | tf_op | source)
XLA Modules:
  0.0 236.8 jit_solution(1617643081465351077)
XLA Ops:
  7.2 1.4 copy.21
  8.9 3.1 %collective-permute-start.2 = (bf16[128,16,128]{2,1,0:T(8,128)(2,1)S(1)}, bf16[128,16,128]{2,1,0:T(8,128)(2,1)S(1)}, u32[]{:S(2)}, u32[]{:S(2)}) collective-permute-start(bf16[128,16,128]{2,1,0:T(8,128)(2,1)S(1)} %reshape.179), channel_id=1, source_target_pairs={{0,8},{8,0},{16,24},{24,16},{1,9},{9,1},{17,25},{25,17},{2,10},{10... | collective-permute-start | bytes 1572872 | tf_op jit(solution)/shard_map/ppermute | solution.py:345
  12.0 1.5 collective-permute-start.1
  13.5 1.5 collective-permute-start
  15.2 8.7 %collective-permute-done.2 = bf16[128,16,128]{2,1,0:T(8,128)(2,1)S(1)} collective-permute-done((bf16[128,16,128]{2,1,0:T(8,128)(2,1)S(1)}, bf16[128,16,128]{2,1,0:T(8,128)(2,1)S(1)}, u32[]{:S(2)}, u32[]{:S(2)}) %collective-permute-start.2) | collective-permute-done | bytes 524320 | tf_op jit(solution)/shard_map/ppermute | solution.py:345
  23.9 1.5 collective-permute-done.1
  25.4 1.2 collective-permute-done
  27.1 1.5 collective-permute-start.3
  28.6 2.5 %collective-permute-start.7 = (bf16[128,16,128]{2,1,0:T(8,128)(2,1)S(1)}, bf16[128,16,128]{2,1,0:T(8,128)(2,1)S(1)}, u32[]{:S(2)}, u32[]{:S(2)}) collective-permute-start(bf16[128,16,128]{2,1,0:T(8,128)(2,1)S(1)} %reshape.179), channel_id=1, source_target_pairs={{0,24},{8,16},{16,8},{24,0},{1,25},{9,17},{17,9},{25,1},{2,26},{10... | collective-permute-start | bytes 1572872 | tf_op jit(solution)/shard_map/ppermute | solution.py:345
  31.7 1.5 collective-permute-start.5
  35.0 9.7 %collective-permute-done.6 = bf16[64,16,128]{2,1,0:T(8,128)(2,1)S(1)} collective-permute-done((bf16[64,16,128]{2,1,0:T(8,128)(2,1)S(1)}, bf16[64,16,128]{2,1,0:T(8,128)(2,1)S(1)}, u32[]{:S(2)}, u32[]{:S(2)}) %collective-permute-start.6) | collective-permute-done | bytes 262176 | tf_op jit(solution)/shard_map/ppermute | solution.py:345
  44.7 1.5 collective-permute-start.10
  46.2 1.5 collective-permute-start.9
  47.7 7.2 %collective-permute-start.8 = (bf16[128,16,128]{2,1,0:T(8,128)(2,1)S(1)}, bf16[128,16,128]{2,1,0:T(8,128)(2,1)S(1)}, u32[]{:S(2)}, u32[]{:S(2)}) collective-permute-start(bf16[128,16,128]{2,1,0:T(8,128)(2,1)S(1)} %collective-permute-done.7), channel_id=1, source_target_pairs={{0,8},{8,0},{16,24},{24,16},{1,9},{9,1},{17,25},{25,17},{2,10},{10... | collective-permute-start | bytes 1572872 | tf_op jit(solution)/shard_map/ppermute | solution.py:345
  54.9 1.2 constant_dynamic-update-slice_fusion.2
  56.1 1.6 collective-permute-start.12
  61.5 1.1 collective-permute-done.12
  62.6 1.5 collective-permute-done.11
  64.1 1.4 collective-permute-done.8
  66.0 1.5 collective-permute-start.13
  68.9 1.4 collective-permute-start.15
  72.6 1.0 constant_dynamic-update-slice_fusion.12
  73.6 9.4 %collective-permute-done.16 = bf16[64,16,128]{2,1,0:T(8,128)(2,1)S(1)} collective-permute-done((bf16[64,16,128]{2,1,0:T(8,128)(2,1)S(1)}, bf16[64,16,128]{2,1,0:T(8,128)(2,1)S(1)}, u32[]{:S(2)}, u32[]{:S(2)}) %collective-permute-start.16) | collective-permute-done | bytes 262176 | tf_op jit(solution)/shard_map/ppermute | solution.py:345
  83.1 1.6 collective-permute-start.18
  84.6 1.4 collective-permute-start.17
  87.7 4.2 %collective-permute-done.18 = bf16[64,16,128]{2,1,0:T(8,128)(2,1)S(1)} collective-permute-done((bf16[64,16,128]{2,1,0:T(8,128)(2,1)S(1)}, bf16[64,16,128]{2,1,0:T(8,128)(2,1)S(1)}, u32[]{:S(2)}, u32[]{:S(2)}) %collective-permute-start.18) | collective-permute-done | bytes 262176 | tf_op jit(solution)/shard_map/ppermute | solution.py:345
  95.1 1.0 collective-permute-done.23.refs_9_
  96.8 46.3 %shard_map.68 = (bf16[4,1024,512]{2,1,0:T(8,128)(2,1)}, bf16[4,1024,512]{2,1,0:T(8,128)(2,1)}, f32[1024,512]{1,0:T(8,128)}, f32[1024,128]{1,0:T(8,128)}, f32[256,512]{1,0:T(8,128)}) custom-call(s32[2]{0:T(128)} %pad_add_fusion.1.place_ref, s32[2304]{0:T(1024)} %reshape.178.slots_ref, bf16[512,512]{1,0:T(8,128)(2,1)} %x_ref.1, bf16[512,512]{1,0:T(8,128)(2,1)} %z_ref.1, ...), custom_call_target="tpu_custom_call" | custom-call | flops 28000000000 | bytes 31457280 | tf_op jit(solution)/shard_map/pallas_call | solution.py:152
  143.1 2.7 %collective-permute-start.26 = (f32[256,512]{1,0:T(8,128)}, f32[256,512]{1,0:T(8,128)S(1)}, u32[]{:S(2)}, u32[]{:S(2)}) collective-permute-start(f32[256,512]{1,0:T(8,128)} %get-tuple-element.57.refs_0_), channel_id=1, source_target_pairs={{0,24},{8,16},{16,8},{24,0},{1,25},{9,17},{17,9},{25,1},{2,26},{10... | collective-permute-start | bytes 1572872 | tf_op jit(solution)/shard_map/ppermute | solution.py:448
  145.9 6.1 %collective-permute-start.25 = (f32[256,512]{1,0:T(8,128)}, f32[256,512]{1,0:T(8,128)S(1)}, u32[]{:S(2)}, u32[]{:S(2)}) collective-permute-start(f32[256,512]{1,0:T(8,128)} %get-tuple-element.57.refs_0_), channel_id=1, source_target_pairs={{0,16},{8,24},{16,0},{24,8},{1,17},{9,25},{17,1},{25,9},{2,18},{10... | collective-permute-start | bytes 1572872 | tf_op jit(solution)/shard_map/ppermute | solution.py:448
  152.5 57.1 %shard_map.69 = (bf16[1024,1024]{1,0:T(8,128)(2,1)}, bf16[1024,1024]{1,0:T(8,128)(2,1)}, f32[1024,128]{1,0:T(8,128)}) custom-call(bf16[4,1024,512]{2,1,0:T(8,128)(2,1)} %get-tuple-element.50.yx_ref, bf16[4,1024,512]{2,1,0:T(8,128)(2,1)} %get-tuple-element.51.yz_ref), custom_call_target="tpu_custom_call" | custom-call | flops 40000000000 | bytes 12582912 | tf_op jit(solution)/shard_map/pallas_call | solution.py:265
  210.7 19.2 %shard_map.70 = (f32[1024,512]{1,0:T(8,128)}, f32[1024,128]{1,0:T(8,128)}) custom-call(s32[2]{0:T(128)} %pad_add_fusion.1.place_ref, bf16[1024,1024]{1,0:T(8,128)(2,1)} %get-tuple-element.52.lh_any, bf16[1024,1024]{1,0:T(8,128)(2,1)} %get-tuple-element.53.ll_any, f32[1024,128]{1,0:T(8,128)} %get-tuple-element.54.d_any, f32[8,1024,128]{2,1,0:T(8,128)} %bitcast.51, ...), custom_call_target="tpu_custom_call" | custom-call | flops 12000000000 | bytes 25165824 | tf_op jit(solution)/shard_map/pallas_call | solution.py:327
  (89 shorter events, 18.6 us)
Async XLA Ops:
  7.2 7.8 %copy-start.7 = (s32[32]{0:T(128)S(1)}, s32[32]{0:T(128)}, u32[]{:S(2)}) copy-start(s32[32]{0:T(128)} %constant.92.clone) | copy-start | bytes 388
  7.2 26.1 %copy-start.2 = (s32[4096]{0:T(1024)S(1)}, s32[4096]{0:T(1024)}, u32[]{:S(2)}) copy-start(s32[4096]{0:T(1024)} %param.8) | copy-start | bytes 49156
  7.2 202.4 %all-gather.3.cloned.1.call-start = ((), (), s32[]{:S(2)}) async-start(), calls=%async_computation | async-start | bytes 4718592 | tf_op jit(solution)/shard_map/all_gather | solution.py:447
  8.9 15.0 %collective-permute-start.2 = (bf16[128,16,128]{2,1,0:T(8,128)(2,1)S(1)}, bf16[128,16,128]{2,1,0:T(8,128)(2,1)S(1)}, u32[]{:S(2)}, u32[]{:S(2)}) collective-permute-start(bf16[128,16,128]{2,1,0:T(8,128)(2,1)S(1)} %reshape.179), channel_id=1, source_target_pairs={{0,8},{8,0},{16,24},{24,16},{1,9},{9,1},{17,25},{25,17},{2,10},{10... | collective-permute-start | bytes 1572872 | tf_op jit(solution)/shard_map/ppermute | solution.py:345
  12.0 13.4 %collective-permute-start.1 = (bf16[128,16,128]{2,1,0:T(8,128)(2,1)S(1)}, bf16[128,16,128]{2,1,0:T(8,128)(2,1)S(1)}, u32[]{:S(2)}, u32[]{:S(2)}) collective-permute-start(bf16[128,16,128]{2,1,0:T(8,128)(2,1)S(1)} %reshape.179), channel_id=1, source_target_pairs={{0,4},{1,5},{2,6},{3,7},{4,0},{5,1},{6,2},{7,3},{8,12},{9,13},{10,... | collective-permute-start | bytes 1572872 | tf_op jit(solution)/shard_map/ppermute | solution.py:345
  13.5 13.1 %collective-permute-start = (bf16[128,16,128]{2,1,0:T(8,128)(2,1)S(1)}, bf16[128,16,128]{2,1,0:T(8,128)(2,1)S(1)}, u32[]{:S(2)}, u32[]{:S(2)}) collective-permute-start(bf16[128,16,128]{2,1,0:T(8,128)(2,1)S(1)} %reshape.179), channel_id=1, source_target_pairs={{0,2},{1,3},{2,0},{3,1},{4,6},{5,7},{6,4},{7,5},{8,10},{9,11},{10,... | collective-permute-start | bytes 1572872 | tf_op jit(solution)/shard_map/ppermute | solution.py:345
  26.6 18.1 %collective-permute-start.4 = (bf16[128,16,128]{2,1,0:T(8,128)(2,1)S(1)}, bf16[128,16,128]{2,1,0:T(8,128)(2,1)S(1)}, u32[]{:S(2)}, u32[]{:S(2)}) collective-permute-start(bf16[128,16,128]{2,1,0:T(8,128)(2,1)S(1)} %collective-permute-done.2), channel_id=1, source_target_pairs={{0,4},{1,5},{2,6},{3,7},{4,0},{5,1},{6,2},{7,3},{8,12},{9,13},{10,... | collective-permute-start | bytes 1572872 | tf_op jit(solution)/shard_map/ppermute | solution.py:345
  27.1 17.6 %collective-permute-start.3 = (bf16[128,16,128]{2,1,0:T(8,128)(2,1)S(1)}, bf16[128,16,128]{2,1,0:T(8,128)(2,1)S(1)}, u32[]{:S(2)}, u32[]{:S(2)}) collective-permute-start(bf16[128,16,128]{2,1,0:T(8,128)(2,1)S(1)} %collective-permute-done.2), channel_id=1, source_target_pairs={{0,2},{1,3},{2,0},{3,1},{4,6},{5,7},{6,4},{7,5},{8,10},{9,11},{10,... | collective-permute-start | bytes 1572872 | tf_op jit(solution)/shard_map/ppermute | solution.py:345
  28.6 16.1 %collective-permute-start.7 = (bf16[128,16,128]{2,1,0:T(8,128)(2,1)S(1)}, bf16[128,16,128]{2,1,0:T(8,128)(2,1)S(1)}, u32[]{:S(2)}, u32[]{:S(2)}) collective-permute-start(bf16[128,16,128]{2,1,0:T(8,128)(2,1)S(1)} %reshape.179), channel_id=1, source_target_pairs={{0,24},{8,16},{16,8},{24,0},{1,25},{9,17},{17,9},{25,1},{2,26},{10... | collective-permute-start | bytes 1572872 | tf_op jit(solution)/shard_map/ppermute | solution.py:345
  31.1 13.6 %collective-permute-start.6 = (bf16[64,16,128]{2,1,0:T(8,128)(2,1)S(1)}, bf16[64,16,128]{2,1,0:T(8,128)(2,1)S(1)}, u32[]{:S(2)}, u32[]{:S(2)}) collective-permute-start(bf16[64,16,128]{2,1,0:T(8,128)(2,1)S(1)} %slice.53), channel_id=1, source_target_pairs={{0,2},{1,3},{2,0},{3,1},{4,6},{5,7},{6,4},{7,5},{8,10},{9,11},{10,... | collective-permute-start | bytes 786440 | tf_op jit(solution)/shard_map/ppermute | solution.py:345
  31.7 13.0 %collective-permute-start.5 = (bf16[64,16,128]{2,1,0:T(8,128)(2,1)S(1)}, bf16[64,16,128]{2,1,0:T(8,128)(2,1)S(1)}, u32[]{:S(2)}, u32[]{:S(2)}) collective-permute-start(bf16[64,16,128]{2,1,0:T(8,128)(2,1)S(1)} %slice.52), channel_id=1, source_target_pairs={{0,4},{1,5},{2,6},{3,7},{4,0},{5,1},{6,2},{7,3},{8,12},{9,13},{10,... | collective-permute-start | bytes 786440 | tf_op jit(solution)/shard_map/ppermute | solution.py:345
  44.7 19.3 %collective-permute-start.10 = (bf16[128,16,128]{2,1,0:T(8,128)(2,1)S(1)}, bf16[128,16,128]{2,1,0:T(8,128)(2,1)S(1)}, u32[]{:S(2)}, u32[]{:S(2)}) collective-permute-start(bf16[128,16,128]{2,1,0:T(8,128)(2,1)S(1)} %collective-permute-done.7), channel_id=1, source_target_pairs={{0,4},{1,5},{2,6},{3,7},{4,0},{5,1},{6,2},{7,3},{8,12},{9,13},{10,... | collective-permute-start | bytes 1572872 | tf_op jit(solution)/shard_map/ppermute | solution.py:345
  46.2 17.8 %collective-permute-start.9 = (bf16[128,16,128]{2,1,0:T(8,128)(2,1)S(1)}, bf16[128,16,128]{2,1,0:T(8,128)(2,1)S(1)}, u32[]{:S(2)}, u32[]{:S(2)}) collective-permute-start(bf16[128,16,128]{2,1,0:T(8,128)(2,1)S(1)} %collective-permute-done.7), channel_id=1, source_target_pairs={{0,2},{1,3},{2,0},{3,1},{4,6},{5,7},{6,4},{7,5},{8,10},{9,11},{10,... | collective-permute-start | bytes 1572872 | tf_op jit(solution)/shard_map/ppermute | solution.py:345
  47.7 17.7 %collective-permute-start.8 = (bf16[128,16,128]{2,1,0:T(8,128)(2,1)S(1)}, bf16[128,16,128]{2,1,0:T(8,128)(2,1)S(1)}, u32[]{:S(2)}, u32[]{:S(2)}) collective-permute-start(bf16[128,16,128]{2,1,0:T(8,128)(2,1)S(1)} %collective-permute-done.7), channel_id=1, source_target_pairs={{0,8},{8,0},{16,24},{24,16},{1,9},{9,1},{17,25},{25,17},{2,10},{10... | collective-permute-start | bytes 1572872 | tf_op jit(solution)/shard_map/ppermute | solution.py:345
  56.1 6.4 %collective-permute-start.12 = (bf16[64,16,128]{2,1,0:T(8,128)(2,1)S(1)}, bf16[64,16,128]{2,1,0:T(8,128)(2,1)S(1)}, u32[]{:S(2)}, u32[]{:S(2)}) collective-permute-start(bf16[64,16,128]{2,1,0:T(8,128)(2,1)S(1)} %slice.55), channel_id=1, source_target_pairs={{0,2},{1,3},{2,0},{3,1},{4,6},{5,7},{6,4},{7,5},{8,10},{9,11},{10,... | collective-permute-start | bytes 786440 | tf_op jit(solution)/shard_map/ppermute | solution.py:345
  57.7 6.4 %collective-permute-start.11 = (bf16[64,16,128]{2,1,0:T(8,128)(2,1)S(1)}, bf16[64,16,128]{2,1,0:T(8,128)(2,1)S(1)}, u32[]{:S(2)}, u32[]{:S(2)}) collective-permute-start(bf16[64,16,128]{2,1,0:T(8,128)(2,1)S(1)} %slice.54), channel_id=1, source_target_pairs={{0,4},{1,5},{2,6},{3,7},{4,0},{5,1},{6,2},{7,3},{8,12},{9,13},{10,... | collective-permute-start | bytes 786440 | tf_op jit(solution)/shard_map/ppermute | solution.py:345
  65.5 17.6 %collective-permute-start.14 = (bf16[128,16,128]{2,1,0:T(8,128)(2,1)S(1)}, bf16[128,16,128]{2,1,0:T(8,128)(2,1)S(1)}, u32[]{:S(2)}, u32[]{:S(2)}) collective-permute-start(bf16[128,16,128]{2,1,0:T(8,128)(2,1)S(1)} %collective-permute-done.8), channel_id=1, source_target_pairs={{0,4},{1,5},{2,6},{3,7},{4,0},{5,1},{6,2},{7,3},{8,12},{9,13},{10,... | collective-permute-start | bytes 1572872 | tf_op jit(solution)/shard_map/ppermute | solution.py:345
  66.0 17.0 %collective-permute-start.13 = (bf16[128,16,128]{2,1,0:T(8,128)(2,1)S(1)}, bf16[128,16,128]{2,1,0:T(8,128)(2,1)S(1)}, u32[]{:S(2)}, u32[]{:S(2)}) collective-permute-start(bf16[128,16,128]{2,1,0:T(8,128)(2,1)S(1)} %collective-permute-done.8), channel_id=1, source_target_pairs={{0,2},{1,3},{2,0},{3,1},{4,6},{5,7},{6,4},{7,5},{8,10},{9,11},{10,... | collective-permute-start | bytes 1572872 | tf_op jit(solution)/shard_map/ppermute | solution.py:345
  68.2 27.8 %collective-permute-start.19 = (bf16[512,16,128]{2,1,0:T(8,128)(2,1)}, bf16[512,16,128]{2,1,0:T(8,128)(2,1)}, u32[]{:S(2)}, u32[]{:S(2)}) collective-permute-start(bf16[512,16,128]{2,1,0:T(8,128)(2,1)} %constant_dynamic-update-slice_fusion.refs_0_), channel_id=1, source_target_pairs={{0,1},{1,0},{2,3},{3,2},{4,5},{5,4},{6,7},{7,6},{8,9},{9,8},{10,11... | collective-permute-start | bytes 6291464 | tf_op jit(solution)/shard_map/ppermute | solution.py:345
  68.3 14.7 %collective-permute-start.16 = (bf16[64,16,128]{2,1,0:T(8,128)(2,1)S(1)}, bf16[64,16,128]{2,1,0:T(8,128)(2,1)S(1)}, u32[]{:S(2)}, u32[]{:S(2)}) collective-permute-start(bf16[64,16,128]{2,1,0:T(8,128)(2,1)S(1)} %slice.57), channel_id=1, source_target_pairs={{0,2},{1,3},{2,0},{3,1},{4,6},{5,7},{6,4},{7,5},{8,10},{9,11},{10,... | collective-permute-start | bytes 786440 | tf_op jit(solution)/shard_map/ppermute | solution.py:345
  68.9 14.1 %collective-permute-start.15 = (bf16[64,16,128]{2,1,0:T(8,128)(2,1)S(1)}, bf16[64,16,128]{2,1,0:T(8,128)(2,1)S(1)}, u32[]{:S(2)}, u32[]{:S(2)}) collective-permute-start(bf16[64,16,128]{2,1,0:T(8,128)(2,1)S(1)} %slice.56), channel_id=1, source_target_pairs={{0,4},{1,5},{2,6},{3,7},{4,0},{5,1},{6,2},{7,3},{8,12},{9,13},{10,... | collective-permute-start | bytes 786440 | tf_op jit(solution)/shard_map/ppermute | solution.py:345
  83.0 13.0 %collective-permute-start.20 = (bf16[512,16,128]{2,1,0:T(8,128)(2,1)}, bf16[512,16,128]{2,1,0:T(8,128)(2,1)}, u32[]{:S(2)}, u32[]{:S(2)}) collective-permute-start(bf16[512,16,128]{2,1,0:T(8,128)(2,1)} %constant_dynamic-update-slice_fusion.5.refs_1_), channel_id=1, source_target_pairs={{0,1},{1,0},{2,3},{3,2},{4,5},{5,4},{6,7},{7,6},{8,9},{9,8},{10,11... | collective-permute-start | bytes 6291464 | tf_op jit(solution)/shard_map/ppermute | solution.py:345
  83.1 8.8 %collective-permute-start.18 = (bf16[64,16,128]{2,1,0:T(8,128)(2,1)S(1)}, bf16[64,16,128]{2,1,0:T(8,128)(2,1)S(1)}, u32[]{:S(2)}, u32[]{:S(2)}) collective-permute-start(bf16[64,16,128]{2,1,0:T(8,128)(2,1)S(1)} %slice.59), channel_id=1, source_target_pairs={{0,2},{1,3},{2,0},{3,1},{4,6},{5,7},{6,4},{7,5},{8,10},{9,11},{10,... | collective-permute-start | bytes 786440 | tf_op jit(solution)/shard_map/ppermute | solution.py:345
  84.6 8.4 %collective-permute-start.17 = (bf16[64,16,128]{2,1,0:T(8,128)(2,1)S(1)}, bf16[64,16,128]{2,1,0:T(8,128)(2,1)S(1)}, u32[]{:S(2)}, u32[]{:S(2)}) collective-permute-start(bf16[64,16,128]{2,1,0:T(8,128)(2,1)S(1)} %slice.58), channel_id=1, source_target_pairs={{0,4},{1,5},{2,6},{3,7},{4,0},{5,1},{6,2},{7,3},{8,12},{9,13},{10,... | collective-permute-start | bytes 786440 | tf_op jit(solution)/shard_map/ppermute | solution.py:345
  87.5 8.5 %collective-permute-start.21 = (bf16[512,16,128]{2,1,0:T(8,128)(2,1)}, bf16[512,16,128]{2,1,0:T(8,128)(2,1)}, u32[]{:S(2)}, u32[]{:S(2)}) collective-permute-start(bf16[512,16,128]{2,1,0:T(8,128)(2,1)} %constant_dynamic-update-slice_fusion.10.refs_2_), channel_id=1, source_target_pairs={{0,1},{1,0},{2,3},{3,2},{4,5},{5,4},{6,7},{7,6},{8,9},{9,8},{10,11... | collective-permute-start | bytes 6291464 | tf_op jit(solution)/shard_map/ppermute | solution.py:345
  87.7 5.5 %copy-start = (bf16[384,16,128]{2,1,0:T(8,128)(2,1)}, bf16[384,16,128]{2,1,0:T(8,128)(2,1)S(1)}, u32[]{:S(2)}) copy-start(bf16[384,16,128]{2,1,0:T(8,128)(2,1)S(1)} %constant_dynamic-update-slice_fusion.15.refs_3_) | copy-start | bytes 4718596
  91.8 4.2 %collective-permute-start.22 = (bf16[384,16,128]{2,1,0:T(8,128)(2,1)S(1)}, bf16[384,16,128]{2,1,0:T(8,128)(2,1)}, u32[]{:S(2)}, u32[]{:S(2)}) collective-permute-start(bf16[384,16,128]{2,1,0:T(8,128)(2,1)S(1)} %constant_dynamic-update-slice_fusion.15.refs_3_), channel_id=1, source_target_pairs={{0,1},{1,0},{2,3},{3,2},{4,5},{5,4},{6,7},{7,6},{8,9},{9,8},{10,11... | collective-permute-start | bytes 4718600 | tf_op jit(solution)/shard_map/ppermute | solution.py:345
  93.1 2.9 %copy-start.1 = (bf16[128,16,128]{2,1,0:T(8,128)(2,1)}, bf16[128,16,128]{2,1,0:T(8,128)(2,1)S(1)}, u32[]{:S(2)}) copy-start(bf16[128,16,128]{2,1,0:T(8,128)(2,1)S(1)} %constant_dynamic-update-slice_fusion.18.refs_4_) | copy-start | bytes 1572868
  93.1 2.9 %collective-permute-start.23 = (bf16[128,16,128]{2,1,0:T(8,128)(2,1)S(1)}, bf16[128,16,128]{2,1,0:T(8,128)(2,1)S(1)}, u32[]{:S(2)}, u32[]{:S(2)}) collective-permute-start(bf16[128,16,128]{2,1,0:T(8,128)(2,1)S(1)} %constant_dynamic-update-slice_fusion.18.refs_4_), channel_id=1, source_target_pairs={{0,1},{1,0},{2,3},{3,2},{4,5},{5,4},{6,7},{7,6},{8,9},{9,8},{10,11... | collective-permute-start | bytes 1572872 | tf_op jit(solution)/shard_map/ppermute | solution.py:345
  143.1 66.4 %collective-permute-start.26 = (f32[256,512]{1,0:T(8,128)}, f32[256,512]{1,0:T(8,128)S(1)}, u32[]{:S(2)}, u32[]{:S(2)}) collective-permute-start(f32[256,512]{1,0:T(8,128)} %get-tuple-element.57.refs_0_), channel_id=1, source_target_pairs={{0,24},{8,16},{16,8},{24,0},{1,25},{9,17},{17,9},{25,1},{2,26},{10... | collective-permute-start | bytes 1572872 | tf_op jit(solution)/shard_map/ppermute | solution.py:448
  145.9 63.7 %collective-permute-start.25 = (f32[256,512]{1,0:T(8,128)}, f32[256,512]{1,0:T(8,128)S(1)}, u32[]{:S(2)}, u32[]{:S(2)}) collective-permute-start(f32[256,512]{1,0:T(8,128)} %get-tuple-element.57.refs_0_), channel_id=1, source_target_pairs={{0,16},{8,24},{16,0},{24,8},{1,17},{9,25},{17,1},{25,9},{2,18},{10... | collective-permute-start | bytes 1572872 | tf_op jit(solution)/shard_map/ppermute | solution.py:448
  152.0 57.6 %collective-permute-start.24 = (f32[256,512]{1,0:T(8,128)}, f32[256,512]{1,0:T(8,128)S(1)}, u32[]{:S(2)}, u32[]{:S(2)}) collective-permute-start(f32[256,512]{1,0:T(8,128)} %get-tuple-element.57.refs_0_), channel_id=1, source_target_pairs={{0,8},{8,0},{16,24},{24,16},{1,9},{9,1},{17,25},{25,17},{2,10},{10... | collective-permute-start | bytes 1572872 | tf_op jit(solution)/shard_map/ppermute | solution.py:448
  (4 other events, 3.7 us)
Sparse Core Ops, SparseCore 0:
  143.3 42.0 all-gather.2

commit v12 on v11

--- a/solution.py
+++ b/solution.py
@@ -35,9 +35,9 @@
     return dot_bf16(a[0], b[0], dims) + (dot_bf16(a[0], b[1], dims) + dot_bf16(a[1], b[0], dims))
 
 
-def assemble_kernel(place_ref, slots_ref, x_ref, z_ref, *refs, sources, lead_tiles, pick_tiles, col_tiles, rows, prow, pcol):
+def assemble_kernel(place_ref, slots_ref, x_ref, z_ref, *refs, sources, lead_tiles, pick_tiles, row_tiles, rows, prow, pcol):
     source_refs, refs = refs[:sources], refs[sources:]
-    lead_x_ref, lead_z_ref, schur_ref, front_ref, top_ref, every_ref, picked_ref, yx_ref, yz_ref, sem_ref = refs
+    lead_x_ref, lead_z_ref, early_ref, front_ref, top_ref, rest_x, rest_z, every_ref, picked_ref, yx_ref, yz_ref, sem_ref = refs
     step = pl.program_id(0)
     tile, parts, lanes = picked_ref.shape
     width = x_ref.shape[0]
@@ -98,21 +98,36 @@
                 def _():
                     keep(jnp.where(block < row_rest, lead // prow + block, rows // NB + lead // pcol + block - row_rest), s)
 
-    @pl.when(step >= pick_tiles)
+    skipped, wide = top_ref.shape[0], early_ref.shape[1]
+    kept, beyond = rows - skipped, rows + wide
+    hand_over = []
+    for n, (mine, out) in enumerate(((yx_ref, rest_x), (yz_ref, rest_z))):
+        count = mine.shape[1] - beyond
+        hand_over.append(pltpu.make_async_copy(mine.at[:, pl.ds(skipped, kept), :], out.at[:, pl.ds(0, kept), :], sem_ref.at[sources + 2 * n]))
+        hand_over.append(pltpu.make_async_copy(mine.at[:, pl.ds(beyond, count), :], out.at[:, pl.ds(kept, count), :], sem_ref.at[sources + 2 * n + 1]))
+
+    @pl.when(step == pick_tiles)
     def _():
-        high, wide = schur_ref.shape
-        i, j = (step - pick_tiles) // col_tiles, (step - pick_tiles) % col_tiles
+        for copy in hand_over:
+            copy.start()
+
+    @pl.when((step >= pick_tiles) & (step < pick_tiles + row_tiles))
+    def _():
+        high = early_ref.shape[0]
+        i = step - pick_tiles
         left = pl.ds(pl.multiple_of(i * high, high), high)
-        right = pl.ds(pl.multiple_of(rows + j * wide, wide), wide)
-        schur_ref[...] = gram_tile(yx_ref, yz_ref, left, right)
-
-        @pl.when(j == 0)
-        def _():
-            front_ref[...] = schur_ref[:, :front_ref.shape[1]]
+        early_ref[...] = gram_tile(yx_ref, yz_ref, left, pl.ds(rows, wide))
+        front_ref[...] = early_ref[:, :front_ref.shape[1]]
 
         @pl.when(i == 0)
         def _():
-            top_ref[...] = schur_ref[:top_ref.shape[0], :]
+            top_ref[:, :wide] = early_ref[:skipped, :]
+
+    @pl.when(step == pick_tiles + row_tiles)
+    def _():
+        top_ref[:, wide:] = gram_tile(yx_ref, yz_ref, pl.ds(0, skipped), pl.ds(beyond, top_ref.shape[1] - wide))
+        for copy in hand_over:
+            copy.wait()
 
 
 def gram_tile(yx_ref, yz_ref, left, right):
@@ -140,29 +155,30 @@
     slots_held = sum(source.shape[0] for source in sources)
     width = x_factor.shape[0]
     tile = 256
-    high, wide = min(512, rows), min(256, cols)
+    high, wide = min(512, rows), cols // 2
     lead_tiles, pick_tiles = K // tile, slots.shape[0] // tile
-    row_tiles, col_tiles = rows // high, cols // wide
+    row_tiles = rows // high
     whole = pl.BlockSpec((width, width), lambda s: (0, 0), pipeline_mode=pl.Buffered(1))
     lead = pl.BlockSpec((RANK, tile, width), lambda s: (0, jnp.minimum(s, lead_tiles - 1), 0))
-    after = lambda s: jnp.maximum(s - pick_tiles, 0)
+    tile_of = lambda s: (jnp.clip(s - pick_tiles, 0, row_tiles - 1), 0)
+    handed = jax.ShapeDtypeStruct((RANK, rows - lead_rows + cols - wide, width), jnp.bfloat16)
     bf16 = jnp.bfloat16
     any_space = pl.BlockSpec(memory_space=pl.ANY)
-    body = functools.partial(assemble_kernel, sources=len(sources), lead_tiles=lead_tiles, pick_tiles=pick_tiles, col_tiles=col_tiles, rows=rows, prow=K // lead_rows, pcol=K // lead_cols)
+    body = functools.partial(assemble_kernel, sources=len(sources), lead_tiles=lead_tiles, pick_tiles=pick_tiles, row_tiles=row_tiles, rows=rows, prow=K // lead_rows, pcol=K // lead_cols)
     return pl.pallas_call(
         body,
-        grid=(pick_tiles + row_tiles * col_tiles,),
+        grid=(pick_tiles + row_tiles + 1,),
         out_shape=(jax.ShapeDtypeStruct((RANK, K, width), bf16),) * 2 + (
-            jax.ShapeDtypeStruct((rows, cols), jnp.float32),
+            jax.ShapeDtypeStruct((rows, wide), jnp.float32),
             jax.ShapeDtypeStruct((rows, lead_cols), jnp.float32),
-            jax.ShapeDtypeStruct((lead_rows, cols), jnp.float32)),
+            jax.ShapeDtypeStruct((lead_rows, cols), jnp.float32), handed, handed),
         in_specs=[SMEM, SMEM, whole, whole] + [any_space] * len(sources),
         out_specs=(lead, lead,
-                   pl.BlockSpec((high, wide), lambda s: (after(s) // col_tiles, after(s) % col_tiles)),
-                   pl.BlockSpec((high, lead_cols), lambda s: (after(s) // col_tiles, 0)),
-                   pl.BlockSpec((lead_rows, wide), lambda s: (0, jnp.minimum(after(s), col_tiles - 1)))),
+                   pl.BlockSpec((high, wide), tile_of),
+                   pl.BlockSpec((high, lead_cols), tile_of),
+                   pl.BlockSpec((lead_rows, cols), lambda s: (0, 0)), any_space, any_space),
         scratch_shapes=[pltpu.VMEM((slots_held, parts, lanes), bf16), pltpu.VMEM((tile, parts, lanes), bf16)]
-        + [pltpu.VMEM((RANK, rows + cols, width), bf16)] * 2 + [pltpu.SemaphoreType.DMA((len(sources),))],
+        + [pltpu.VMEM((RANK, rows + cols, width), bf16)] * 2 + [pltpu.SemaphoreType.DMA((len(sources) + 4,))],
         compiler_params=pltpu.CompilerParams(vmem_limit_bytes=58 * MIB),
         cost_estimate=pl.CostEstimate(flops=28 * 10**9, bytes_accessed=30 * MIB, transcendentals=0),
     )(place, slots, x_factor, z_factor, *sources)
@@ -212,11 +228,14 @@
         v_ref[SUB * m:SUB * (m + 1), :] = v
 
 
-def factor_kernel(yx_ref, yz_ref, lh_ref, ll_ref, d_ref, w_ref, g_ref, u_ref, v_ref):
+def factor_kernel(yx_ref, yz_ref, rest_x_any, rest_z_any, lh_ref, ll_ref, d_ref, rest_ref, w_ref, g_ref, u_ref, v_ref, rest_x, rest_z, sem_ref):
     order = lh_ref.shape[0]
     steps = order // BLK
     tile = 2 * BLK
-    window = 3 * BLK
+    rest_rows, rest_cols = rest_ref.shape
+    fetched = [pltpu.make_async_copy(here, there, sem_ref.at[n]) for n, (here, there) in enumerate(((rest_x_any, rest_x), (rest_z_any, rest_z)))]
+    for copy in fetched:
+        copy.start()
     lh_ref[...] = jnp.zeros_like(lh_ref)
     ll_ref[...] = jnp.zeros_like(ll_ref)
     w_ref[:, tile:] = jnp.zeros((order, order - tile), jnp.float32)
@@ -227,17 +246,23 @@
         return carry
     lax.fori_loop(0, order // (2 * tile), rows_of, 0)
 
-    def step(b, carry):
+    def step(b, window, share):
         at = pl.ds(pl.multiple_of(b * BLK, BLK), BLK)
         after = jnp.minimum(b // 2 + 1, order // tile - 1)
-        top = pl.multiple_of(jnp.minimum(after * tile + (b % 2) * window, order - window), BLK)
-        left = pl.ds(top, window)
+        left = pl.ds(pl.multiple_of(jnp.minimum(after * tile + (b % 2) * window, order - window), BLK), window)
         right = pl.ds(pl.multiple_of(after * tile, tile), tile)
+        if share > 0:
+            part = pl.ds(pl.multiple_of((b - 2) * share, share), share)
+
+        def pair(x_ref, z_ref, lhs, rhs, q, r):
+            return dot_bf16(x_ref[r, lhs, :], x_ref[q, rhs, :], NT) * dot_bf16(z_ref[r, lhs, :], z_ref[q, rhs, :], NT)
 
         def beside(m):
             q, r = m // RANK, m % RANK
-            term = dot_bf16(yx_ref[r, left, :], yx_ref[q, right, :], NT) * dot_bf16(yz_ref[r, left, :], yz_ref[q, right, :], NT)
-            g_ref[left, :] = signed(g_ref[left, :] if m > 0 else None, term, q, r)
+            g_ref[left, :] = signed(g_ref[left, :] if m > 0 else None, pair(yx_ref, yz_ref, left, right, q, r), q, r)
+            if share > 0:
+                term = pair(rest_x, rest_z, part, pl.ds(rest_rows, rest_cols), q, r)
+                rest_ref[part, :] = signed(rest_ref[part, :] if m > 0 else None, term, q, r)
 
         factor_block(w_ref[at, at], u_ref, v_ref, beside)
         lh_ref[at, at], ll_ref[at, at] = split(u_ref[...].T)
@@ -255,32 +280,49 @@
                     w_ref[top:bottom, first:bottom] = w_ref[top:bottom, first:bottom] - dot3(left, right, NT)
                 if k % 2 == 1:
                     w_ref[first:, first:first + tile] = w_ref[first:, first:first + tile] + g_ref[first:, :]
+
+    def first_step(b, carry):
+        step(b, 3 * BLK, 0)
         return carry
-    lax.fori_loop(0, steps, step, 0)
-
-
-def factor(yx, yz):
+
+    def later_step(b, carry):
+        step(b, 2 * BLK, rest_rows // (steps - 2))
+        return carry
+
+    lax.fori_loop(0, 2, first_step, 0)
+    for copy in fetched:
+        copy.wait()
+    lax.fori_loop(2, steps, later_step, 0)
+
+
+def factor(yx, yz, rest_x, rest_z, rest_rows):
     tile = 2 * BLK
     f32 = jnp.float32
+    any_space = pl.BlockSpec(memory_space=pl.ANY)
+    rest_cols = rest_x.shape[1] - rest_rows
     return pl.pallas_call(
         factor_kernel,
-        out_shape=(jax.ShapeDtypeStruct((K, K), jnp.bfloat16),) * 2 + (jax.ShapeDtypeStruct((K, BLK), f32),),
-        in_specs=[VMEM] * 2,
-        out_specs=(VMEM,) * 3,
-        scratch_shapes=[pltpu.VMEM((K, K), f32), pltpu.VMEM((K, tile), f32), pltpu.VMEM((BLK, BLK), f32), pltpu.VMEM((BLK, BLK), f32)],
+        out_shape=(jax.ShapeDtypeStruct((K, K), jnp.bfloat16),) * 2 + (jax.ShapeDtypeStruct((K, BLK), f32), jax.ShapeDtypeStruct((rest_rows, rest_cols), f32)),
+        in_specs=[VMEM] * 2 + [any_space] * 2,
+        out_specs=(VMEM,) * 4,
+        scratch_shapes=[pltpu.VMEM((K, K), f32), pltpu.VMEM((K, tile), f32), pltpu.VMEM((BLK, BLK), f32), pltpu.VMEM((BLK, BLK), f32)]
+        + [pltpu.VMEM(rest_x.shape, jnp.bfloat16)] * 2 + [pltpu.SemaphoreType.DMA((2,))],
         compiler_params=pltpu.CompilerParams(vmem_limit_bytes=58 * MIB),
         cost_estimate=pl.CostEstimate(flops=40 * 10**9, bytes_accessed=12 * MIB, transcendentals=0),
-    )(yx, yz)
-
-
-def solve_kernel(place_ref, lh_any, ll_any, d_any, pieces_any, schur_any, *refs, prow):
+    )(yx, yz, rest_x, rest_z)
+
+
+def solve_kernel(place_ref, lh_any, ll_any, d_any, pieces_any, early_any, last_any, *refs, prow):
     top_refs, refs = refs[:prow], refs[prow:]
     rest_ref, panel_ref, lh, ll, d_ref, pieces_ref, tops_ref, schur_ref, xh, xl, zh, zl, sem_ref = refs
     pcol = pieces_ref.shape[0]
     row, column = place_ref[0], place_ref[1]
     pairs = [(d_any, d_ref), (lh_any, lh), (ll_any, ll)]
     pairs += [(ref, tops_ref.at[turn ^ row]) for turn, ref in enumerate(top_refs)]
-    pairs += [(pieces_any, pieces_ref), (schur_any, schur_ref)]
+    skipped, halfway = tops_ref.shape[1], early_any.shape[1]
+    left, right = pl.ds(0, halfway), pl.ds(halfway, schur_ref.shape[1] - halfway)
+    pairs += [(pieces_any, pieces_ref), (early_any, schur_ref.at[:, left]), (top_refs[0].at[:, right], schur_ref.at[pl.ds(0, skipped), right]),
+              (last_any, schur_ref.at[pl.ds(skipped, schur_ref.shape[0] - skipped), right])]
     copies = [pltpu.make_async_copy(here, there, sem_ref.at[n]) for n, (here, there) in enumerate(pairs)]
     for copy in copies:
         copy.start()
@@ -296,7 +338,7 @@
         inverses.append(split(jnp.concatenate([
             jnp.concatenate([d_ref[upper, :], jnp.zeros((BLK, BLK), jnp.float32)], axis=1),
             jnp.concatenate([corner, d_ref[lower, :]], axis=1)], axis=0)))
-    for copy in copies[3:-1]:
+    for copy in copies[3:-3]:
         copy.wait()
     for b in range(K // wide):
         at, done = slice(b * wide, (b + 1) * wide), slice(0, b * wide)
@@ -315,26 +357,27 @@
             @pl.when(column == block % pcol)
             def _():
                 panel_ref[:, block // pcol * NB:(block // pcol + 1) * NB] = value[:, place * NB:(place + 1) * NB]
-    copies[-1].wait()
+    for copy in copies[-3:]:
+        copy.wait()
     rest_ref[...] = schur_ref[...] - dot3((xh[...], xl[...]), (zh[...], zl[...]), NN)
 
 
-def solve(place, high, low, inverses, pieces, schur, tops):
-    rows, cols = schur.shape
+def solve(place, high, low, inverses, pieces, early, last, tops):
+    rows, cols = early.shape[0], tops[0].shape[1]
     lead = K // pieces.shape[0]
     bf16, f32 = jnp.bfloat16, jnp.float32
     any_space = pl.BlockSpec(memory_space=pl.ANY)
     return pl.pallas_call(
         functools.partial(solve_kernel, prow=len(tops)),
         out_shape=(jax.ShapeDtypeStruct((rows, cols), f32), jax.ShapeDtypeStruct((rows, lead), f32)),
-        in_specs=[SMEM] + [any_space] * (5 + len(tops)),
+        in_specs=[SMEM] + [any_space] * (6 + len(tops)),
         out_specs=(VMEM, VMEM),
         scratch_shapes=[pltpu.VMEM((K, K), bf16)] * 2 + [pltpu.VMEM((K, BLK), f32), pltpu.VMEM(pieces.shape, f32)]
-        + [pltpu.VMEM((len(tops),) + tops[0].shape, f32), pltpu.VMEM(schur.shape, f32)]
-        + [pltpu.VMEM((rows, K), bf16)] * 2 + [pltpu.VMEM((K, cols), bf16)] * 2 + [pltpu.SemaphoreType.DMA((len(tops) + 5,))],
+        + [pltpu.VMEM((len(tops),) + tops[0].shape, f32), pltpu.VMEM((rows, cols), f32)]
+        + [pltpu.VMEM((rows, K), bf16)] * 2 + [pltpu.VMEM((K, cols), bf16)] * 2 + [pltpu.SemaphoreType.DMA((len(tops) + 7,))],
         compiler_params=pltpu.CompilerParams(vmem_limit_bytes=58 * MIB),
         cost_estimate=pl.CostEstimate(flops=12 * 10**9, bytes_accessed=24 * MIB, transcendentals=0),
-    )(place, high, low, inverses, pieces, schur, *tops)
+    )(place, high, low, inverses, pieces, early, last, *tops)
 
 
 def gather_factors(mine, prow_count, pcol_count):
@@ -442,12 +485,12 @@
     places = jnp.concatenate([found[:K // NB], by_row[lead_rows // NB:], by_col[lead_cols // NB:]])
     places = jnp.pad(places, ((0, -places.shape[0] % (256 // NB)), (0, 0))).reshape(-1)
     place = jnp.stack([prow_id, pcol_id]).astype(jnp.int32)
-    lead_x, lead_z, schur_local, front, top = assemble(
+    lead_x, lead_z, early, front, top, rest_x, rest_z = assemble(
         place, places.astype(jnp.int32), sources, x_factor, zinv_factor, local_rows, local_cols, lead_rows, lead_cols)
     pieces = lax.all_gather(front, "pcol", axis=0, tiled=False)
     tops = [top] + [lax.ppermute(top, "prow", [(n, n ^ turn) for n in range(prow_count)]) for turn in range(1, prow_count)]
-    high, low, inverses = factor(lead_x, lead_z)
-    return solve(place, high, low, inverses, pieces, schur_local, tops)
+    high, low, inverses, last = factor(lead_x, lead_z, rest_x, rest_z, local_rows - lead_rows)
+    return solve(place, high, low, inverses, pieces, early, last, tops)
 
 
 def solution(mesh):

time: 237 us -> 243 us (1.025); the launches traced: 237 us -> 239 us
    pallas_call x1, Pallas kernels: 57.1 us -> 66.1 us  [factor(): pl.pallas_call(factor_kernel, out_shape=(jax.ShapeDtypeStruct((K, K), jnp...]
    pallas_call x1, Pallas kernels: 46.3 us -> 39.3 us  [assemble(): pl.pallas_call(body, grid=(pick_tiles + row_tiles + 1,), out_shape=(jax.S...]
  transfers between devices with their start and end apart: 28 -> 28, of which waited for: 11 -> 11; matrix products, arithmetic and copies ran while one was open for 6% -> 6% of each run, Pallas kernels for 24% -> 28%
where the time goes in v12:
time: 243 us; the launch traced here: 239 us
  Pallas kernels  125 us (51%)
  starting transfers between devices  41.6 us (17%)
  waiting for transfers between devices  40.1 us (17%)
  local copies, waits for them, and re-layouts  16.4 us (7%)
  between operations  14.6 us (6%)
    pallas_call x1, Pallas kernels, factor(): pl.pallas_call(factor_kernel, out_shape=(jax.ShapeDtypeStruct((K, K), jnp...  66.1 us
    ppermute x24, waiting for transfers between devices, swap(): return lax.ppermute(value, axis, [(n, n ^ turn) for n in range(count)])  40.1 us
    pallas_call x1, Pallas kernels, assemble(): pl.pallas_call(body, grid=(pick_tiles + row_tiles + 1,), out_shape=(jax.S...  39.3 us
    ppermute x24, starting transfers between devices, swap(): return lax.ppermute(value, axis, [(n, n ^ turn) for n in range(count)])  32.2 us
    pallas_call x1, Pallas kernels, solve(): pl.pallas_call(functools.partial(solve_kernel, prow=len(tops)), out_shape...  19.2 us
    unnamed x32, local copies, waits for them, and re-layouts  11.6 us
    ppermute x3, starting transfers between devices, per_device(): lax.ppermute(top, 'prow', [(n, n ^ turn) for n in range(prow_count)])  9.3 us
  transfers between devices with their start and end apart: 28, of which 11 were waited for; matrix products, arithmetic and copies ran while one was open for 6% of the time, Pallas kernels for 28%

profile of v12, /device:TPU:0, one launch (start us, length us, event | category | flops | bytes accessed | tf_op | source)
XLA Modules:
  0.0 238.9 jit_solution(16039387299108791316)
XLA Ops:
  7.2 1.4 copy.21
  8.9 3.1 %collective-permute-start.2 = (bf16[128,16,128]{2,1,0:T(8,128)(2,1)S(1)}, bf16[128,16,128]{2,1,0:T(8,128)(2,1)S(1)}, u32[]{:S(2)}, u32[]{:S(2)}) collective-permute-start(bf16[128,16,128]{2,1,0:T(8,128)(2,1)S(1)} %reshape.179), channel_id=1, source_target_pairs={{0,8},{8,0},{16,24},{24,16},{1,9},{9,1},{17,25},{25,17},{2,10},{10... | collective-permute-start | bytes 1572872 | tf_op jit(solution)/shard_map/ppermute | solution.py:388
  12.0 1.5 collective-permute-start.1
  13.5 1.5 collective-permute-start
  15.2 8.7 %collective-permute-done.2 = bf16[128,16,128]{2,1,0:T(8,128)(2,1)S(1)} collective-permute-done((bf16[128,16,128]{2,1,0:T(8,128)(2,1)S(1)}, bf16[128,16,128]{2,1,0:T(8,128)(2,1)S(1)}, u32[]{:S(2)}, u32[]{:S(2)}) %collective-permute-start.2) | collective-permute-done | bytes 524320 | tf_op jit(solution)/shard_map/ppermute | solution.py:388
  23.9 1.5 collective-permute-done.1
  25.4 1.2 collective-permute-done
  27.1 1.5 collective-permute-start.3
  28.6 2.5 %collective-permute-start.7 = (bf16[128,16,128]{2,1,0:T(8,128)(2,1)S(1)}, bf16[128,16,128]{2,1,0:T(8,128)(2,1)S(1)}, u32[]{:S(2)}, u32[]{:S(2)}) collective-permute-start(bf16[128,16,128]{2,1,0:T(8,128)(2,1)S(1)} %reshape.179), channel_id=1, source_target_pairs={{0,24},{8,16},{16,8},{24,0},{1,25},{9,17},{17,9},{25,1},{2,26},{10... | collective-permute-start | bytes 1572872 | tf_op jit(solution)/shard_map/ppermute | solution.py:388
  31.7 1.5 collective-permute-start.5
  35.0 9.7 %collective-permute-done.6 = bf16[64,16,128]{2,1,0:T(8,128)(2,1)S(1)} collective-permute-done((bf16[64,16,128]{2,1,0:T(8,128)(2,1)S(1)}, bf16[64,16,128]{2,1,0:T(8,128)(2,1)S(1)}, u32[]{:S(2)}, u32[]{:S(2)}) %collective-permute-start.6) | collective-permute-done | bytes 262176 | tf_op jit(solution)/shard_map/ppermute | solution.py:388
  44.7 1.5 collective-permute-start.10
  46.2 1.5 collective-permute-start.9
  47.7 7.2 %collective-permute-start.8 = (bf16[128,16,128]{2,1,0:T(8,128)(2,1)S(1)}, bf16[128,16,128]{2,1,0:T(8,128)(2,1)S(1)}, u32[]{:S(2)}, u32[]{:S(2)}) collective-permute-start(bf16[128,16,128]{2,1,0:T(8,128)(2,1)S(1)} %collective-permute-done.7), channel_id=1, source_target_pairs={{0,8},{8,0},{16,24},{24,16},{1,9},{9,1},{17,25},{25,17},{2,10},{10... | collective-permute-start | bytes 1572872 | tf_op jit(solution)/shard_map/ppermute | solution.py:388
  54.9 1.2 constant_dynamic-update-slice_fusion.2
  56.2 1.6 collective-permute-start.12
  61.5 1.1 collective-permute-done.12
  62.6 1.5 collective-permute-done.11
  64.1 1.4 collective-permute-done.8
  66.0 1.5 collective-permute-start.13
  68.9 1.4 collective-permute-start.15
  72.6 1.0 constant_dynamic-update-slice_fusion.12
  73.6 9.4 %collective-permute-done.16 = bf16[64,16,128]{2,1,0:T(8,128)(2,1)S(1)} collective-permute-done((bf16[64,16,128]{2,1,0:T(8,128)(2,1)S(1)}, bf16[64,16,128]{2,1,0:T(8,128)(2,1)S(1)}, u32[]{:S(2)}, u32[]{:S(2)}) %collective-permute-start.16) | collective-permute-done | bytes 262176 | tf_op jit(solution)/shard_map/ppermute | solution.py:388
  83.1 1.6 collective-permute-start.18
  84.6 1.4 collective-permute-start.17
  87.7 4.1 %collective-permute-done.18 = bf16[64,16,128]{2,1,0:T(8,128)(2,1)S(1)} collective-permute-done((bf16[64,16,128]{2,1,0:T(8,128)(2,1)S(1)}, bf16[64,16,128]{2,1,0:T(8,128)(2,1)S(1)}, u32[]{:S(2)}, u32[]{:S(2)}) %collective-permute-start.18) | collective-permute-done | bytes 262176 | tf_op jit(solution)/shard_map/ppermute | solution.py:388
  95.1 0.9 collective-permute-done.23.refs_9_
  96.8 39.3 %shard_map.68 = (bf16[4,1024,512]{2,1,0:T(8,128)(2,1)}, bf16[4,1024,512]{2,1,0:T(8,128)(2,1)}, f32[1024,256]{1,0:T(8,128)}, f32[1024,128]{1,0:T(8,128)}, f32[256...) custom-call(s32[2]{0:T(128)} %pad_add_fusion.1.place_ref, s32[2304]{0:T(1024)} %reshape.178.slots_ref, ...), custom_call_target="tpu_custom_call" | custom-call | flops 28000000000 | bytes 31457280 | tf_op jit(solution)/shard_map/pallas_call | solution.py:168
  136.1 2.7 %collective-permute-start.26 = (f32[256,512]{1,0:T(8,128)}, f32[256,512]{1,0:T(8,128)S(1)}, u32[]{:S(2)}, u32[]{:S(2)}) collective-permute-start(f32[256,512]{1,0:T(8,128)} %get-tuple-element.63.refs_0_), channel_id=1, source_target_pairs={{0,24},{8,16},{16,8},{24,0},{1,25},{9,17},{17,9},{25,1},{2,26},{10... | collective-permute-start | bytes 1572872 | tf_op jit(solution)/shard_map/ppermute | solution.py:491
  138.9 6.1 %collective-permute-start.25 = (f32[256,512]{1,0:T(8,128)}, f32[256,512]{1,0:T(8,128)S(1)}, u32[]{:S(2)}, u32[]{:S(2)}) collective-permute-start(f32[256,512]{1,0:T(8,128)} %get-tuple-element.63.refs_0_), channel_id=1, source_target_pairs={{0,16},{8,24},{16,0},{24,8},{1,17},{9,25},{17,1},{25,9},{2,18},{10... | collective-permute-start | bytes 1572872 | tf_op jit(solution)/shard_map/ppermute | solution.py:491
  145.4 66.1 %shard_map.69 = (bf16[1024,1024]{1,0:T(8,128)(2,1)}, bf16[1024,1024]{1,0:T(8,128)(2,1)}, f32[1024,128]{1,0:T(8,128)}, f32[768,256]{1,0:T(8,128)}) custom-call(bf16[4,1024,512]{2,1,0:T(8,128)(2,1)} %get-tuple-element.53.yx_ref, bf16[4,1024,512]{2,1,0:T(8,128)(2,1)} %get-tuple-element.54.yz_ref, bf16[4,1024,512]{2,1,0:T(8,128)(2,1)} %get-tuple-element.55.rest_x_any, ...), custom_call_target="tpu_custom_call" | custom-call | flops 40000000000 | bytes 12582912 | tf_op jit(solution)/shard_map/pallas_call | solution.py:303
  212.7 19.2 %shard_map.70 = (f32[1024,512]{1,0:T(8,128)}, f32[1024,128]{1,0:T(8,128)}) custom-call(s32[2]{0:T(128)} %pad_add_fusion.1.place_ref, bf16[1024,1024]{1,0:T(8,128)(2,1)} %get-tuple-element.57.lh_any, bf16[1024,1024]{1,0:T(8,128)(2,1)} %get-tuple-element.58.ll_any, f32[1024,128]{1,0:T(8,128)} %get-tuple-element.59.d_any, f32[8,1024,128]{2,1,0:T(8,128)} %bitcast.51, ...), custom_call_target="tpu_custom_call" | custom-call | flops 12000000000 | bytes 25165824 | tf_op jit(solution)/shard_map/pallas_call | solution.py:370
  (89 shorter events, 18.6 us)
Async XLA Ops:
  7.2 7.8 %copy-start.7 = (s32[32]{0:T(128)S(1)}, s32[32]{0:T(128)}, u32[]{:S(2)}) copy-start(s32[32]{0:T(128)} %constant.92.clone) | copy-start | bytes 388
  7.2 26.1 %copy-start.2 = (s32[4096]{0:T(1024)S(1)}, s32[4096]{0:T(1024)}, u32[]{:S(2)}) copy-start(s32[4096]{0:T(1024)} %param.8) | copy-start | bytes 49156
  7.2 204.4 %all-gather.3.cloned.1.call-start = ((), (), s32[]{:S(2)}) async-start(), calls=%async_computation | async-start | bytes 4718592 | tf_op jit(solution)/shard_map/all_gather | solution.py:490
  8.9 15.0 %collective-permute-start.2 = (bf16[128,16,128]{2,1,0:T(8,128)(2,1)S(1)}, bf16[128,16,128]{2,1,0:T(8,128)(2,1)S(1)}, u32[]{:S(2)}, u32[]{:S(2)}) collective-permute-start(bf16[128,16,128]{2,1,0:T(8,128)(2,1)S(1)} %reshape.179), channel_id=1, source_target_pairs={{0,8},{8,0},{16,24},{24,16},{1,9},{9,1},{17,25},{25,17},{2,10},{10... | collective-permute-start | bytes 1572872 | tf_op jit(solution)/shard_map/ppermute | solution.py:388
  12.0 13.4 %collective-permute-start.1 = (bf16[128,16,128]{2,1,0:T(8,128)(2,1)S(1)}, bf16[128,16,128]{2,1,0:T(8,128)(2,1)S(1)}, u32[]{:S(2)}, u32[]{:S(2)}) collective-permute-start(bf16[128,16,128]{2,1,0:T(8,128)(2,1)S(1)} %reshape.179), channel_id=1, source_target_pairs={{0,4},{1,5},{2,6},{3,7},{4,0},{5,1},{6,2},{7,3},{8,12},{9,13},{10,... | collective-permute-start | bytes 1572872 | tf_op jit(solution)/shard_map/ppermute | solution.py:388
  13.5 13.1 %collective-permute-start = (bf16[128,16,128]{2,1,0:T(8,128)(2,1)S(1)}, bf16[128,16,128]{2,1,0:T(8,128)(2,1)S(1)}, u32[]{:S(2)}, u32[]{:S(2)}) collective-permute-start(bf16[128,16,128]{2,1,0:T(8,128)(2,1)S(1)} %reshape.179), channel_id=1, source_target_pairs={{0,2},{1,3},{2,0},{3,1},{4,6},{5,7},{6,4},{7,5},{8,10},{9,11},{10,... | collective-permute-start | bytes 1572872 | tf_op jit(solution)/shard_map/ppermute | solution.py:388
  26.6 18.1 %collective-permute-start.4 = (bf16[128,16,128]{2,1,0:T(8,128)(2,1)S(1)}, bf16[128,16,128]{2,1,0:T(8,128)(2,1)S(1)}, u32[]{:S(2)}, u32[]{:S(2)}) collective-permute-start(bf16[128,16,128]{2,1,0:T(8,128)(2,1)S(1)} %collective-permute-done.2), channel_id=1, source_target_pairs={{0,4},{1,5},{2,6},{3,7},{4,0},{5,1},{6,2},{7,3},{8,12},{9,13},{10,... | collective-permute-start | bytes 1572872 | tf_op jit(solution)/shard_map/ppermute | solution.py:388
  27.1 17.6 %collective-permute-start.3 = (bf16[128,16,128]{2,1,0:T(8,128)(2,1)S(1)}, bf16[128,16,128]{2,1,0:T(8,128)(2,1)S(1)}, u32[]{:S(2)}, u32[]{:S(2)}) collective-permute-start(bf16[128,16,128]{2,1,0:T(8,128)(2,1)S(1)} %collective-permute-done.2), channel_id=1, source_target_pairs={{0,2},{1,3},{2,0},{3,1},{4,6},{5,7},{6,4},{7,5},{8,10},{9,11},{10,... | collective-permute-start | bytes 1572872 | tf_op jit(solution)/shard_map/ppermute | solution.py:388
  28.6 16.1 %collective-permute-start.7 = (bf16[128,16,128]{2,1,0:T(8,128)(2,1)S(1)}, bf16[128,16,128]{2,1,0:T(8,128)(2,1)S(1)}, u32[]{:S(2)}, u32[]{:S(2)}) collective-permute-start(bf16[128,16,128]{2,1,0:T(8,128)(2,1)S(1)} %reshape.179), channel_id=1, source_target_pairs={{0,24},{8,16},{16,8},{24,0},{1,25},{9,17},{17,9},{25,1},{2,26},{10... | collective-permute-start | bytes 1572872 | tf_op jit(solution)/shard_map/ppermute | solution.py:388
  31.1 13.6 %collective-permute-start.6 = (bf16[64,16,128]{2,1,0:T(8,128)(2,1)S(1)}, bf16[64,16,128]{2,1,0:T(8,128)(2,1)S(1)}, u32[]{:S(2)}, u32[]{:S(2)}) collective-permute-start(bf16[64,16,128]{2,1,0:T(8,128)(2,1)S(1)} %slice.53), channel_id=1, source_target_pairs={{0,2},{1,3},{2,0},{3,1},{4,6},{5,7},{6,4},{7,5},{8,10},{9,11},{10,... | collective-permute-start | bytes 786440 | tf_op jit(solution)/shard_map/ppermute | solution.py:388
  31.7 13.0 %collective-permute-start.5 = (bf16[64,16,128]{2,1,0:T(8,128)(2,1)S(1)}, bf16[64,16,128]{2,1,0:T(8,128)(2,1)S(1)}, u32[]{:S(2)}, u32[]{:S(2)}) collective-permute-start(bf16[64,16,128]{2,1,0:T(8,128)(2,1)S(1)} %slice.52), channel_id=1, source_target_pairs={{0,4},{1,5},{2,6},{3,7},{4,0},{5,1},{6,2},{7,3},{8,12},{9,13},{10,... | collective-permute-start | bytes 786440 | tf_op jit(solution)/shard_map/ppermute | solution.py:388
  44.7 19.4 %collective-permute-start.10 = (bf16[128,16,128]{2,1,0:T(8,128)(2,1)S(1)}, bf16[128,16,128]{2,1,0:T(8,128)(2,1)S(1)}, u32[]{:S(2)}, u32[]{:S(2)}) collective-permute-start(bf16[128,16,128]{2,1,0:T(8,128)(2,1)S(1)} %collective-permute-done.7), channel_id=1, source_target_pairs={{0,4},{1,5},{2,6},{3,7},{4,0},{5,1},{6,2},{7,3},{8,12},{9,13},{10,... | collective-permute-start | bytes 1572872 | tf_op jit(solution)/shard_map/ppermute | solution.py:388
  46.2 17.9 %collective-permute-start.9 = (bf16[128,16,128]{2,1,0:T(8,128)(2,1)S(1)}, bf16[128,16,128]{2,1,0:T(8,128)(2,1)S(1)}, u32[]{:S(2)}, u32[]{:S(2)}) collective-permute-start(bf16[128,16,128]{2,1,0:T(8,128)(2,1)S(1)} %collective-permute-done.7), channel_id=1, source_target_pairs={{0,2},{1,3},{2,0},{3,1},{4,6},{5,7},{6,4},{7,5},{8,10},{9,11},{10,... | collective-permute-start | bytes 1572872 | tf_op jit(solution)/shard_map/ppermute | solution.py:388
  47.7 17.7 %collective-permute-start.8 = (bf16[128,16,128]{2,1,0:T(8,128)(2,1)S(1)}, bf16[128,16,128]{2,1,0:T(8,128)(2,1)S(1)}, u32[]{:S(2)}, u32[]{:S(2)}) collective-permute-start(bf16[128,16,128]{2,1,0:T(8,128)(2,1)S(1)} %collective-permute-done.7), channel_id=1, source_target_pairs={{0,8},{8,0},{16,24},{24,16},{1,9},{9,1},{17,25},{25,17},{2,10},{10... | collective-permute-start | bytes 1572872 | tf_op jit(solution)/shard_map/ppermute | solution.py:388
  56.2 6.4 %collective-permute-start.12 = (bf16[64,16,128]{2,1,0:T(8,128)(2,1)S(1)}, bf16[64,16,128]{2,1,0:T(8,128)(2,1)S(1)}, u32[]{:S(2)}, u32[]{:S(2)}) collective-permute-start(bf16[64,16,128]{2,1,0:T(8,128)(2,1)S(1)} %slice.55), channel_id=1, source_target_pairs={{0,2},{1,3},{2,0},{3,1},{4,6},{5,7},{6,4},{7,5},{8,10},{9,11},{10,... | collective-permute-start | bytes 786440 | tf_op jit(solution)/shard_map/ppermute | solution.py:388
  57.7 6.4 %collective-permute-start.11 = (bf16[64,16,128]{2,1,0:T(8,128)(2,1)S(1)}, bf16[64,16,128]{2,1,0:T(8,128)(2,1)S(1)}, u32[]{:S(2)}, u32[]{:S(2)}) collective-permute-start(bf16[64,16,128]{2,1,0:T(8,128)(2,1)S(1)} %slice.54), channel_id=1, source_target_pairs={{0,4},{1,5},{2,6},{3,7},{4,0},{5,1},{6,2},{7,3},{8,12},{9,13},{10,... | collective-permute-start | bytes 786440 | tf_op jit(solution)/shard_map/ppermute | solution.py:388
  65.5 17.6 %collective-permute-start.14 = (bf16[128,16,128]{2,1,0:T(8,128)(2,1)S(1)}, bf16[128,16,128]{2,1,0:T(8,128)(2,1)S(1)}, u32[]{:S(2)}, u32[]{:S(2)}) collective-permute-start(bf16[128,16,128]{2,1,0:T(8,128)(2,1)S(1)} %collective-permute-done.8), channel_id=1, source_target_pairs={{0,4},{1,5},{2,6},{3,7},{4,0},{5,1},{6,2},{7,3},{8,12},{9,13},{10,... | collective-permute-start | bytes 1572872 | tf_op jit(solution)/shard_map/ppermute | solution.py:388
  66.0 17.0 %collective-permute-start.13 = (bf16[128,16,128]{2,1,0:T(8,128)(2,1)S(1)}, bf16[128,16,128]{2,1,0:T(8,128)(2,1)S(1)}, u32[]{:S(2)}, u32[]{:S(2)}) collective-permute-start(bf16[128,16,128]{2,1,0:T(8,128)(2,1)S(1)} %collective-permute-done.8), channel_id=1, source_target_pairs={{0,2},{1,3},{2,0},{3,1},{4,6},{5,7},{6,4},{7,5},{8,10},{9,11},{10,... | collective-permute-start | bytes 1572872 | tf_op jit(solution)/shard_map/ppermute | solution.py:388
  68.2 27.8 %collective-permute-start.19 = (bf16[512,16,128]{2,1,0:T(8,128)(2,1)}, bf16[512,16,128]{2,1,0:T(8,128)(2,1)}, u32[]{:S(2)}, u32[]{:S(2)}) collective-permute-start(bf16[512,16,128]{2,1,0:T(8,128)(2,1)} %constant_dynamic-update-slice_fusion.refs_0_), channel_id=1, source_target_pairs={{0,1},{1,0},{2,3},{3,2},{4,5},{5,4},{6,7},{7,6},{8,9},{9,8},{10,11... | collective-permute-start | bytes 6291464 | tf_op jit(solution)/shard_map/ppermute | solution.py:388
  68.3 14.7 %collective-permute-start.16 = (bf16[64,16,128]{2,1,0:T(8,128)(2,1)S(1)}, bf16[64,16,128]{2,1,0:T(8,128)(2,1)S(1)}, u32[]{:S(2)}, u32[]{:S(2)}) collective-permute-start(bf16[64,16,128]{2,1,0:T(8,128)(2,1)S(1)} %slice.57), channel_id=1, source_target_pairs={{0,2},{1,3},{2,0},{3,1},{4,6},{5,7},{6,4},{7,5},{8,10},{9,11},{10,... | collective-permute-start | bytes 786440 | tf_op jit(solution)/shard_map/ppermute | solution.py:388
  68.9 14.1 %collective-permute-start.15 = (bf16[64,16,128]{2,1,0:T(8,128)(2,1)S(1)}, bf16[64,16,128]{2,1,0:T(8,128)(2,1)S(1)}, u32[]{:S(2)}, u32[]{:S(2)}) collective-permute-start(bf16[64,16,128]{2,1,0:T(8,128)(2,1)S(1)} %slice.56), channel_id=1, source_target_pairs={{0,4},{1,5},{2,6},{3,7},{4,0},{5,1},{6,2},{7,3},{8,12},{9,13},{10,... | collective-permute-start | bytes 786440 | tf_op jit(solution)/shard_map/ppermute | solution.py:388
  83.0 13.0 %collective-permute-start.20 = (bf16[512,16,128]{2,1,0:T(8,128)(2,1)}, bf16[512,16,128]{2,1,0:T(8,128)(2,1)}, u32[]{:S(2)}, u32[]{:S(2)}) collective-permute-start(bf16[512,16,128]{2,1,0:T(8,128)(2,1)} %constant_dynamic-update-slice_fusion.5.refs_1_), channel_id=1, source_target_pairs={{0,1},{1,0},{2,3},{3,2},{4,5},{5,4},{6,7},{7,6},{8,9},{9,8},{10,11... | collective-permute-start | bytes 6291464 | tf_op jit(solution)/shard_map/ppermute | solution.py:388
  83.1 8.8 %collective-permute-start.18 = (bf16[64,16,128]{2,1,0:T(8,128)(2,1)S(1)}, bf16[64,16,128]{2,1,0:T(8,128)(2,1)S(1)}, u32[]{:S(2)}, u32[]{:S(2)}) collective-permute-start(bf16[64,16,128]{2,1,0:T(8,128)(2,1)S(1)} %slice.59), channel_id=1, source_target_pairs={{0,2},{1,3},{2,0},{3,1},{4,6},{5,7},{6,4},{7,5},{8,10},{9,11},{10,... | collective-permute-start | bytes 786440 | tf_op jit(solution)/shard_map/ppermute | solution.py:388
  84.6 8.4 %collective-permute-start.17 = (bf16[64,16,128]{2,1,0:T(8,128)(2,1)S(1)}, bf16[64,16,128]{2,1,0:T(8,128)(2,1)S(1)}, u32[]{:S(2)}, u32[]{:S(2)}) collective-permute-start(bf16[64,16,128]{2,1,0:T(8,128)(2,1)S(1)} %slice.58), channel_id=1, source_target_pairs={{0,4},{1,5},{2,6},{3,7},{4,0},{5,1},{6,2},{7,3},{8,12},{9,13},{10,... | collective-permute-start | bytes 786440 | tf_op jit(solution)/shard_map/ppermute | solution.py:388
  87.5 8.5 %collective-permute-start.21 = (bf16[512,16,128]{2,1,0:T(8,128)(2,1)}, bf16[512,16,128]{2,1,0:T(8,128)(2,1)}, u32[]{:S(2)}, u32[]{:S(2)}) collective-permute-start(bf16[512,16,128]{2,1,0:T(8,128)(2,1)} %constant_dynamic-update-slice_fusion.10.refs_2_), channel_id=1, source_target_pairs={{0,1},{1,0},{2,3},{3,2},{4,5},{5,4},{6,7},{7,6},{8,9},{9,8},{10,11... | collective-permute-start | bytes 6291464 | tf_op jit(solution)/shard_map/ppermute | solution.py:388
  87.7 5.4 %copy-start = (bf16[384,16,128]{2,1,0:T(8,128)(2,1)}, bf16[384,16,128]{2,1,0:T(8,128)(2,1)S(1)}, u32[]{:S(2)}) copy-start(bf16[384,16,128]{2,1,0:T(8,128)(2,1)S(1)} %constant_dynamic-update-slice_fusion.15.refs_3_) | copy-start | bytes 4718596
  91.8 4.2 %collective-permute-start.22 = (bf16[384,16,128]{2,1,0:T(8,128)(2,1)S(1)}, bf16[384,16,128]{2,1,0:T(8,128)(2,1)}, u32[]{:S(2)}, u32[]{:S(2)}) collective-permute-start(bf16[384,16,128]{2,1,0:T(8,128)(2,1)S(1)} %constant_dynamic-update-slice_fusion.15.refs_3_), channel_id=1, source_target_pairs={{0,1},{1,0},{2,3},{3,2},{4,5},{5,4},{6,7},{7,6},{8,9},{9,8},{10,11... | collective-permute-start | bytes 4718600 | tf_op jit(solution)/shard_map/ppermute | solution.py:388
  93.1 2.9 %copy-start.1 = (bf16[128,16,128]{2,1,0:T(8,128)(2,1)}, bf16[128,16,128]{2,1,0:T(8,128)(2,1)S(1)}, u32[]{:S(2)}) copy-start(bf16[128,16,128]{2,1,0:T(8,128)(2,1)S(1)} %constant_dynamic-update-slice_fusion.18.refs_4_) | copy-start | bytes 1572868
  93.1 2.9 %collective-permute-start.23 = (bf16[128,16,128]{2,1,0:T(8,128)(2,1)S(1)}, bf16[128,16,128]{2,1,0:T(8,128)(2,1)S(1)}, u32[]{:S(2)}, u32[]{:S(2)}) collective-permute-start(bf16[128,16,128]{2,1,0:T(8,128)(2,1)S(1)} %constant_dynamic-update-slice_fusion.18.refs_4_), channel_id=1, source_target_pairs={{0,1},{1,0},{2,3},{3,2},{4,5},{5,4},{6,7},{7,6},{8,9},{9,8},{10,11... | collective-permute-start | bytes 1572872 | tf_op jit(solution)/shard_map/ppermute | solution.py:388
  136.1 75.4 %collective-permute-start.26 = (f32[256,512]{1,0:T(8,128)}, f32[256,512]{1,0:T(8,128)S(1)}, u32[]{:S(2)}, u32[]{:S(2)}) collective-permute-start(f32[256,512]{1,0:T(8,128)} %get-tuple-element.63.refs_0_), channel_id=1, source_target_pairs={{0,24},{8,16},{16,8},{24,0},{1,25},{9,17},{17,9},{25,1},{2,26},{10... | collective-permute-start | bytes 1572872 | tf_op jit(solution)/shard_map/ppermute | solution.py:491
  138.9 72.7 %collective-permute-start.25 = (f32[256,512]{1,0:T(8,128)}, f32[256,512]{1,0:T(8,128)S(1)}, u32[]{:S(2)}, u32[]{:S(2)}) collective-permute-start(f32[256,512]{1,0:T(8,128)} %get-tuple-element.63.refs_0_), channel_id=1, source_target_pairs={{0,16},{8,24},{16,0},{24,8},{1,17},{9,25},{17,1},{25,9},{2,18},{10... | collective-permute-start | bytes 1572872 | tf_op jit(solution)/shard_map/ppermute | solution.py:491
  144.9 66.6 %collective-permute-start.24 = (f32[256,512]{1,0:T(8,128)}, f32[256,512]{1,0:T(8,128)S(1)}, u32[]{:S(2)}, u32[]{:S(2)}) collective-permute-start(f32[256,512]{1,0:T(8,128)} %get-tuple-element.63.refs_0_), channel_id=1, source_target_pairs={{0,8},{8,0},{16,24},{24,16},{1,9},{9,1},{17,25},{25,17},{2,10},{10... | collective-permute-start | bytes 1572872 | tf_op jit(solution)/shard_map/ppermute | solution.py:491
  (4 other events, 3.7 us)
Sparse Core Ops, SparseCore 0:
  136.2 42.0 all-gather.2

commit v13 on v11

--- a/solution.py
+++ b/solution.py
@@ -216,7 +216,6 @@
     order = lh_ref.shape[0]
     steps = order // BLK
     tile = 2 * BLK
-    window = 3 * BLK
     lh_ref[...] = jnp.zeros_like(lh_ref)
     ll_ref[...] = jnp.zeros_like(ll_ref)
     w_ref[:, tile:] = jnp.zeros((order, order - tile), jnp.float32)
@@ -227,22 +226,21 @@
         return carry
     lax.fori_loop(0, order // (2 * tile), rows_of, 0)
 
-    def step(b, carry):
+    def step(b, ahead, window):
         at = pl.ds(pl.multiple_of(b * BLK, BLK), BLK)
-        after = jnp.minimum(b // 2 + 1, order // tile - 1)
-        top = pl.multiple_of(jnp.minimum(after * tile + (b % 2) * window, order - window), BLK)
-        left = pl.ds(top, window)
-        right = pl.ds(pl.multiple_of(after * tile, tile), tile)
+        left = pl.ds(pl.multiple_of(ahead * tile + (b % 2) * window, BLK), window)
+        right = slice(ahead * tile, (ahead + 1) * tile)
 
         def beside(m):
-            q, r = m // RANK, m % RANK
-            term = dot_bf16(yx_ref[r, left, :], yx_ref[q, right, :], NT) * dot_bf16(yz_ref[r, left, :], yz_ref[q, right, :], NT)
-            g_ref[left, :] = signed(g_ref[left, :] if m > 0 else None, term, q, r)
+            if window > 0:
+                q, r = m // RANK, m % RANK
+                term = dot_bf16(yx_ref[r, left, :], yx_ref[q, right, :], NT) * dot_bf16(yz_ref[r, left, :], yz_ref[q, right, :], NT)
+                g_ref[left, :] = signed(g_ref[left, :] if m > 0 else None, term, q, r)
 
         factor_block(w_ref[at, at], u_ref, v_ref, beside)
         lh_ref[at, at], ll_ref[at, at] = split(u_ref[...].T)
         d_ref[at, :] = v_ref[...]
-        for k in range(steps - 1):
+        for k in range(2 * ahead - 2, min(2 * ahead, steps - 1)):
             @pl.when(b == k)
             def _():
                 first = (k + 1) * BLK
@@ -255,8 +253,12 @@
                     w_ref[top:bottom, first:bottom] = w_ref[top:bottom, first:bottom] - dot3(left, right, NT)
                 if k % 2 == 1:
                     w_ref[first:, first:first + tile] = w_ref[first:, first:first + tile] + g_ref[first:, :]
-        return carry
-    lax.fori_loop(0, steps, step, 0)
+
+    for ahead in range(1, order // tile + 1):
+        def two_steps(b, carry, ahead=ahead):
+            step(b, ahead, (order - ahead * tile) // 2)
+            return carry
+        lax.fori_loop(2 * ahead - 2, 2 * ahead, two_steps, 0)
 
 
 def factor(yx, yz):
@@ -337,12 +339,15 @@
     )(place, high, low, inverses, pieces, schur, *tops)
 
 
-def gather_factors(mine, prow_count, pcol_count):
+def gather_factors(mine, prow_count, pcol_count, prow_id):
     own = mine.shape[0]
     half = own // 2
 
-    def swap(axis, count, turn, value):
-        return lax.ppermute(value, axis, [(n, n ^ turn) for n in range(count)])
+    def swap(axis, count, turn, value, chosen=lambda n: True):
+        return lax.ppermute(value, axis, [(n, n ^ turn) for n in range(count) if chosen(n)])
+
+    def close(n):
+        return abs(n - (n ^ 3)) == 1
 
     span = pcol_count // 2
     level_of = {j: bin(j).count("1") for j in range(1, span)}
@@ -350,6 +355,9 @@
     order = [0] + list(range(1, prow_count, 2)) + list(range(2, prow_count, 2))
     items = {0: mine}
     held = {turn: {} for turn in order}
+    split_turn = 3 if prow_count == 4 else None
+    if split_turn:
+        middle = swap("prow", prow_count, split_turn, mine, close)
     parts = []
 
     def spread(turn, j):
@@ -378,14 +386,23 @@
         if phase + 1 < len(order):
             turn = order[phase + 1]
             if turn % 2 == 1:
-                moved["z", turn] = [swap("prow", prow_count, turn, mine)]
+                if turn == split_turn:
+                    moved["z", turn] = [swap("prow", prow_count, turn, mine, lambda n: not close(n))]
+                else:
+                    moved["z", turn] = [swap("prow", prow_count, turn, mine)]
             elif turn in items:
                 moved["z", turn] = [items[turn]]
+        if phase == 0 and split_turn:
+            moved["middle", split_turn] = [middle]
         mine, *results = lax.optimization_barrier([mine] + [value for values in moved.values() for value in values])
         results = iter(results)
         for (turn, j), values in moved.items():
             arrived = [next(results) for _ in values]
-            if turn == "z":
+            if turn == "middle":
+                middle = arrived[0]
+            elif turn == "z" and j == split_turn:
+                items[j] = jnp.where(close(prow_id), middle, arrived[0])
+            elif turn == "z":
                 items[j] = arrived[0]
             else:
                 held[turn][j] = arrived[0] if len(arrived) == 1 else jnp.concatenate(arrived)
@@ -434,7 +451,7 @@
     count = prow_count * pcol_count
     lanes = BLK
     mine = factors.transpose(1, 0, 2).reshape(own, RANK * width // lanes, lanes)
-    sources, order = gather_factors(mine, prow_count, pcol_count)
+    sources, order = gather_factors(mine, prow_count, pcol_count, prow_id)
     found = places_of(placement, order, prow_id, pcol_id, pcol_count)
     by_row = lax.dynamic_index_in_dim(found.reshape(local_rows // NB, prow_count, NB), prow_id, 1, keepdims=False)
     by_col = lax.dynamic_index_in_dim(found.reshape(local_cols // NB, pcol_count, NB), pcol_id, 1, keepdims=False)

time: 237 us -> 238 us (level); the launches traced: 237 us -> 234 us
  starting transfers between devices: 41.6 us -> 32.1 us
  local copies, waits for them, and re-layouts: 16.3 us -> 19 us
    ppermute x3, starting transfers between devices: 9.3 us -> 4.45 us  [per_device(): lax.ppermute(top, 'prow', [(n, n ^ turn) for n in range(prow_count)])]
    ppermute x24 -> x25, starting transfers between devices: 32.2 us -> 27.7 us  [swap(): lax.ppermute(value, axis, [(n, n ^ turn) for n in range(count) if chosen(...]
    unnamed x32 -> x31, local copies, waits for them, and re-layouts: 11.5 us -> 12.8 us
    ppermute x24 -> x25, waiting for transfers between devices: 40.2 us -> 41.4 us  [swap(): lax.ppermute(value, axis, [(n, n ^ turn) for n in range(count) if chosen(...]
  transfers between devices with their start and end apart: 28 -> 29, of which waited for: 11 -> 9; matrix products, arithmetic and copies ran while one was open for 6% -> 7% of each run, Pallas kernels for 24% -> 24%
where the time goes in v13:
time: 238 us; the launch traced here: 234 us
  Pallas kernels  123 us (52%)
  waiting for transfers between devices  41.4 us (17%)
  starting transfers between devices  32.1 us (13%)
  local copies, waits for them, and re-layouts  19 us (8%)
  between operations  14.6 us (6%)
  other arithmetic  3.21 us (1%)
    pallas_call x1, Pallas kernels, factor(): pl.pallas_call(factor_kernel, out_shape=(jax.ShapeDtypeStruct((K, K), jnp...  57.2 us
    pallas_call x1, Pallas kernels, assemble(): pl.pallas_call(body, grid=(pick_tiles + row_tiles * col_tiles,), out_shap...  46.5 us
    ppermute x25, waiting for transfers between devices, swap(): lax.ppermute(value, axis, [(n, n ^ turn) for n in range(count) if chosen(...  41.4 us
    ppermute x25, starting transfers between devices, swap(): lax.ppermute(value, axis, [(n, n ^ turn) for n in range(count) if chosen(...  27.7 us
    pallas_call x1, Pallas kernels, solve(): pl.pallas_call(functools.partial(solve_kernel, prow=len(tops)), out_shape...  19.1 us
    unnamed x31, local copies, waits for them, and re-layouts  12.8 us
  transfers between devices with their start and end apart: 29, of which 9 were waited for; matrix products, arithmetic and copies ran while one was open for 7% of the time, Pallas kernels for 24%

profile of v13, /device:TPU:0, one launch (start us, length us, event | category | flops | bytes accessed | tf_op | source)
XLA Modules:
  0.0 233.6 jit_solution(1307387946233056468)
XLA Ops:
  7.2 1.5 copy.21
  9.6 5.9 %collective-permute-start.2 = (bf16[128,16,128]{2,1,0:T(8,128)(2,1)S(1)}, bf16[128,16,128]{2,1,0:T(8,128)(2,1)}, u32[]{:S(2)}, u32[]{:S(2)}) collective-permute-start(bf16[128,16,128]{2,1,0:T(8,128)(2,1)S(1)} %reshape.179), channel_id=1, source_target_pairs={{0,8},{8,0},{16,24},{24,16},{1,9},{9,1},{17,25},{25,17},{2,10},{10... | collective-permute-start | bytes 1572872 | tf_op jit(solution)/shard_map/ppermute | solution.py:347
  15.5 1.5 collective-permute-start.1
  17.0 1.5 collective-permute-start
  18.7 8.5 %collective-permute-done.2 = bf16[128,16,128]{2,1,0:T(8,128)(2,1)} collective-permute-done((bf16[128,16,128]{2,1,0:T(8,128)(2,1)S(1)}, bf16[128,16,128]{2,1,0:T(8,128)(2,1)}, u32[]{:S(2)}, u32[]{:S(2)}) %collective-permute-start.2) | collective-permute-done | bytes 524320 | tf_op jit(solution)/shard_map/ppermute | solution.py:347
  27.2 1.4 collective-permute-done.1
  28.6 1.2 collective-permute-done
  30.3 1.5 collective-permute-start.4
  31.8 3.2 %collective-permute-start.8 = (bf16[128,16,128]{2,1,0:T(8,128)(2,1)S(1)}, bf16[128,16,128]{2,1,0:T(8,128)(2,1)}, u32[]{:S(2)}, u32[]{:S(2)}) collective-permute-start(bf16[128,16,128]{2,1,0:T(8,128)(2,1)S(1)} %reshape.179), channel_id=1, source_target_pairs={{0,24},{24,0},{1,25},{25,1},{2,26},{26,2},{3,27},{27,3},{4,28},{28... | collective-permute-start | bytes 1572872 | tf_op jit(solution)/shard_map/ppermute | solution.py:347
  37.1 1.5 collective-permute-start.6
  39.5 8.4 %collective-permute-done.7 = bf16[64,16,128]{2,1,0:T(8,128)(2,1)S(1)} collective-permute-done((bf16[64,16,128]{2,1,0:T(8,128)(2,1)}, bf16[64,16,128]{2,1,0:T(8,128)(2,1)S(1)}, u32[]{:S(2)}, u32[]{:S(2)}) %collective-permute-start.7) | collective-permute-done | bytes 262176 | tf_op jit(solution)/shard_map/ppermute | solution.py:347
  48.0 2.0 constant_dynamic-update-slice_fusion.14
  49.9 1.4 collective-permute-start.11
  51.3 1.5 collective-permute-start.10
  53.6 2.2 constant_dynamic-update-slice_fusion.2
  57.1 1.7 constant_dynamic-update-slice_fusion.1
  58.8 0.9 constant_dynamic-update-slice_fusion.8
  60.5 7.7 %collective-permute-done.13 = bf16[64,16,128]{2,1,0:T(8,128)(2,1)S(1)} collective-permute-done((bf16[64,16,128]{2,1,0:T(8,128)(2,1)S(1)}, bf16[64,16,128]{2,1,0:T(8,128)(2,1)S(1)}, u32[]{:S(2)}, u32[]{:S(2)}) %collective-permute-start.13) | collective-permute-done | bytes 262176 | tf_op jit(solution)/shard_map/ppermute | solution.py:347
  68.9 1.5 collective-permute-start.14
  71.8 1.4 collective-permute-start.16
  74.6 0.9 constant_dynamic-update-slice_fusion.13
  75.5 1.0 constant_dynamic-update-slice_fusion.12
  76.5 7.8 %collective-permute-done.17 = bf16[64,16,128]{2,1,0:T(8,128)(2,1)S(1)} collective-permute-done((bf16[64,16,128]{2,1,0:T(8,128)(2,1)S(1)}, bf16[64,16,128]{2,1,0:T(8,128)(2,1)S(1)}, u32[]{:S(2)}, u32[]{:S(2)}) %collective-permute-start.17) | collective-permute-done | bytes 262176 | tf_op jit(solution)/shard_map/ppermute | solution.py:347
  84.4 1.6 collective-permute-start.19
  85.9 0.8 collective-permute-start.18
  88.3 4.8 %collective-permute-done.19 = bf16[64,16,128]{2,1,0:T(8,128)(2,1)S(1)} collective-permute-done((bf16[64,16,128]{2,1,0:T(8,128)(2,1)S(1)}, bf16[64,16,128]{2,1,0:T(8,128)(2,1)S(1)}, u32[]{:S(2)}, u32[]{:S(2)}) %collective-permute-start.19) | collective-permute-done | bytes 262176 | tf_op jit(solution)/shard_map/ppermute | solution.py:347
  96.4 0.9 collective-permute-done.24.refs_9_
  98.1 46.5 %shard_map.68 = (bf16[4,1024,512]{2,1,0:T(8,128)(2,1)}, bf16[4,1024,512]{2,1,0:T(8,128)(2,1)}, f32[1024,512]{1,0:T(8,128)}, f32[1024,128]{1,0:T(8,128)}, f32[256,512]{1,0:T(8,128)}) custom-call(s32[2]{0:T(128)} %pad_add_fusion.1.place_ref, s32[2304]{0:T(1024)} %reshape.178.slots_ref, bf16[512,512]{1,0:T(8,128)(2,1)} %x_ref.1, bf16[512,512]{1,0:T(8,128)(2,1)} %z_ref.1, ...), custom_call_target="tpu_custom_call" | custom-call | flops 28000000000 | bytes 31457280 | tf_op jit(solution)/shard_map/pallas_call | solution.py:152
  144.6 1.4 collective-permute-start.27
  146.3 2.8 %collective-permute-start.25 = (f32[256,512]{1,0:T(8,128)}, f32[256,512]{1,0:T(8,128)S(1)}, u32[]{:S(2)}, u32[]{:S(2)}) collective-permute-start(f32[256,512]{1,0:T(8,128)} %get-tuple-element.59.refs_0_), channel_id=1, source_target_pairs={{0,8},{8,0},{16,24},{24,16},{1,9},{9,1},{17,25},{25,17},{2,10},{10... | collective-permute-start | bytes 1572872 | tf_op jit(solution)/shard_map/ppermute | solution.py:465
  149.1 57.2 %shard_map.69 = (bf16[1024,1024]{1,0:T(8,128)(2,1)}, bf16[1024,1024]{1,0:T(8,128)(2,1)}, f32[1024,128]{1,0:T(8,128)}) custom-call(bf16[4,1024,512]{2,1,0:T(8,128)(2,1)} %get-tuple-element.52.yx_ref, bf16[4,1024,512]{2,1,0:T(8,128)(2,1)} %get-tuple-element.53.yz_ref), custom_call_target="tpu_custom_call" | custom-call | flops 40000000000 | bytes 12582912 | tf_op jit(solution)/shard_map/pallas_call | solution.py:267
  207.4 19.1 %shard_map.70 = (f32[1024,512]{1,0:T(8,128)}, f32[1024,128]{1,0:T(8,128)}) custom-call(s32[2]{0:T(128)} %pad_add_fusion.1.place_ref, bf16[1024,1024]{1,0:T(8,128)(2,1)} %get-tuple-element.54.lh_any, bf16[1024,1024]{1,0:T(8,128)(2,1)} %get-tuple-element.55.ll_any, f32[1024,128]{1,0:T(8,128)} %get-tuple-element.56.d_any, f32[8,1024,128]{2,1,0:T(8,128)} %bitcast.51, ...), custom_call_target="tpu_custom_call" | custom-call | flops 12000000000 | bytes 25165824 | tf_op jit(solution)/shard_map/pallas_call | solution.py:329
  (91 shorter events, 18.0 us)
Async XLA Ops:
  7.2 11.3 %copy-start.7 = (s32[32]{0:T(128)S(1)}, s32[32]{0:T(128)}, u32[]{:S(2)}) copy-start(s32[32]{0:T(128)} %constant.94.clone) | copy-start | bytes 388
  7.2 199.1 %all-gather.3.cloned.1.call-start = ((), (), s32[]{:S(2)}) async-start(), calls=%async_computation | async-start | bytes 4718592 | tf_op jit(solution)/shard_map/all_gather | solution.py:464
  7.2 32.2 %copy-start.2 = (s32[4096]{0:T(1024)S(1)}, s32[4096]{0:T(1024)}, u32[]{:S(2)}) copy-start(s32[4096]{0:T(1024)} %param.8) | copy-start | bytes 49156
  8.9 9.8 %collective-permute-start.3 = (bf16[128,16,128]{2,1,0:T(8,128)(2,1)S(1)}, bf16[128,16,128]{2,1,0:T(8,128)(2,1)S(1)}, u32[]{:S(2)}, u32[]{:S(2)}) collective-permute-start(bf16[128,16,128]{2,1,0:T(8,128)(2,1)S(1)} %reshape.179), channel_id=1, source_target_pairs={{8,16},{16,8},{9,17},{17,9},{10,18},{18,10},{11,19},{19,11},{12,20... | collective-permute-start | bytes 1572872 | tf_op jit(solution)/shard_map/ppermute | solution.py:347
  9.6 17.6 %collective-permute-start.2 = (bf16[128,16,128]{2,1,0:T(8,128)(2,1)S(1)}, bf16[128,16,128]{2,1,0:T(8,128)(2,1)}, u32[]{:S(2)}, u32[]{:S(2)}) collective-permute-start(bf16[128,16,128]{2,1,0:T(8,128)(2,1)S(1)} %reshape.179), channel_id=1, source_target_pairs={{0,8},{8,0},{16,24},{24,16},{1,9},{9,1},{17,25},{25,17},{2,10},{10... | collective-permute-start | bytes 1572872 | tf_op jit(solution)/shard_map/ppermute | solution.py:347
  15.5 13.1 %collective-permute-start.1 = (bf16[128,16,128]{2,1,0:T(8,128)(2,1)S(1)}, bf16[128,16,128]{2,1,0:T(8,128)(2,1)S(1)}, u32[]{:S(2)}, u32[]{:S(2)}) collective-permute-start(bf16[128,16,128]{2,1,0:T(8,128)(2,1)S(1)} %reshape.179), channel_id=1, source_target_pairs={{0,4},{1,5},{2,6},{3,7},{4,0},{5,1},{6,2},{7,3},{8,12},{9,13},{10,... | collective-permute-start | bytes 1572872 | tf_op jit(solution)/shard_map/ppermute | solution.py:347
  17.0 12.8 %collective-permute-start = (bf16[128,16,128]{2,1,0:T(8,128)(2,1)S(1)}, bf16[128,16,128]{2,1,0:T(8,128)(2,1)S(1)}, u32[]{:S(2)}, u32[]{:S(2)}) collective-permute-start(bf16[128,16,128]{2,1,0:T(8,128)(2,1)S(1)} %reshape.179), channel_id=1, source_target_pairs={{0,2},{1,3},{2,0},{3,1},{4,6},{5,7},{6,4},{7,5},{8,10},{9,11},{10,... | collective-permute-start | bytes 1572872 | tf_op jit(solution)/shard_map/ppermute | solution.py:347
  29.8 18.1 %collective-permute-start.5 = (bf16[128,16,128]{2,1,0:T(8,128)(2,1)}, bf16[128,16,128]{2,1,0:T(8,128)(2,1)S(1)}, u32[]{:S(2)}, u32[]{:S(2)}) collective-permute-start(bf16[128,16,128]{2,1,0:T(8,128)(2,1)} %collective-permute-done.2), channel_id=1, source_target_pairs={{0,4},{1,5},{2,6},{3,7},{4,0},{5,1},{6,2},{7,3},{8,12},{9,13},{10,... | collective-permute-start | bytes 1572872 | tf_op jit(solution)/shard_map/ppermute | solution.py:347
  30.3 17.6 %collective-permute-start.4 = (bf16[128,16,128]{2,1,0:T(8,128)(2,1)}, bf16[128,16,128]{2,1,0:T(8,128)(2,1)S(1)}, u32[]{:S(2)}, u32[]{:S(2)}) collective-permute-start(bf16[128,16,128]{2,1,0:T(8,128)(2,1)} %collective-permute-done.2), channel_id=1, source_target_pairs={{0,2},{1,3},{2,0},{3,1},{4,6},{5,7},{6,4},{7,5},{8,10},{9,11},{10,... | collective-permute-start | bytes 1572872 | tf_op jit(solution)/shard_map/ppermute | solution.py:347
  31.8 16.1 %collective-permute-start.8 = (bf16[128,16,128]{2,1,0:T(8,128)(2,1)S(1)}, bf16[128,16,128]{2,1,0:T(8,128)(2,1)}, u32[]{:S(2)}, u32[]{:S(2)}) collective-permute-start(bf16[128,16,128]{2,1,0:T(8,128)(2,1)S(1)} %reshape.179), channel_id=1, source_target_pairs={{0,24},{24,0},{1,25},{25,1},{2,26},{26,2},{3,27},{27,3},{4,28},{28... | collective-permute-start | bytes 1572872 | tf_op jit(solution)/shard_map/ppermute | solution.py:347
  36.5 11.4 %collective-permute-start.7 = (bf16[64,16,128]{2,1,0:T(8,128)(2,1)}, bf16[64,16,128]{2,1,0:T(8,128)(2,1)S(1)}, u32[]{:S(2)}, u32[]{:S(2)}) collective-permute-start(bf16[64,16,128]{2,1,0:T(8,128)(2,1)} %slice.53), channel_id=1, source_target_pairs={{0,2},{1,3},{2,0},{3,1},{4,6},{5,7},{6,4},{7,5},{8,10},{9,11},{10,... | collective-permute-start | bytes 786440 | tf_op jit(solution)/shard_map/ppermute | solution.py:347
  37.1 10.9 %collective-permute-start.6 = (bf16[64,16,128]{2,1,0:T(8,128)(2,1)}, bf16[64,16,128]{2,1,0:T(8,128)(2,1)}, u32[]{:S(2)}, u32[]{:S(2)}) collective-permute-start(bf16[64,16,128]{2,1,0:T(8,128)(2,1)} %slice.52), channel_id=1, source_target_pairs={{0,4},{1,5},{2,6},{3,7},{4,0},{5,1},{6,2},{7,3},{8,12},{9,13},{10,... | collective-permute-start | bytes 786440 | tf_op jit(solution)/shard_map/ppermute | solution.py:347
  49.9 18.3 %collective-permute-start.11 = (bf16[128,16,128]{2,1,0:T(8,128)(2,1)S(1)}, bf16[128,16,128]{2,1,0:T(8,128)(2,1)S(1)}, u32[]{:S(2)}, u32[]{:S(2)}) collective-permute-start(bf16[128,16,128]{2,1,0:T(8,128)(2,1)S(1)} %get-tuple-element.61), channel_id=1, source_target_pairs={{0,4},{1,5},{2,6},{3,7},{4,0},{5,1},{6,2},{7,3},{8,12},{9,13},{10,... | collective-permute-start | bytes 1572872 | tf_op jit(solution)/shard_map/ppermute | solution.py:347
  51.3 16.9 %collective-permute-start.10 = (bf16[128,16,128]{2,1,0:T(8,128)(2,1)S(1)}, bf16[128,16,128]{2,1,0:T(8,128)(2,1)S(1)}, u32[]{:S(2)}, u32[]{:S(2)}) collective-permute-start(bf16[128,16,128]{2,1,0:T(8,128)(2,1)S(1)} %get-tuple-element.61), channel_id=1, source_target_pairs={{0,2},{1,3},{2,0},{3,1},{4,6},{5,7},{6,4},{7,5},{8,10},{9,11},{10,... | collective-permute-start | bytes 1572872 | tf_op jit(solution)/shard_map/ppermute | solution.py:347
  52.8 15.4 %collective-permute-start.9 = (bf16[128,16,128]{2,1,0:T(8,128)(2,1)S(1)}, bf16[128,16,128]{2,1,0:T(8,128)(2,1)S(1)}, u32[]{:S(2)}, u32[]{:S(2)}) collective-permute-start(bf16[128,16,128]{2,1,0:T(8,128)(2,1)S(1)} %get-tuple-element.61), channel_id=1, source_target_pairs={{0,8},{8,0},{16,24},{24,16},{1,9},{9,1},{17,25},{25,17},{2,10},{10... | collective-permute-start | bytes 1572872 | tf_op jit(solution)/shard_map/ppermute | solution.py:347
  55.9 12.3 %collective-permute-start.13 = (bf16[64,16,128]{2,1,0:T(8,128)(2,1)S(1)}, bf16[64,16,128]{2,1,0:T(8,128)(2,1)S(1)}, u32[]{:S(2)}, u32[]{:S(2)}) collective-permute-start(bf16[64,16,128]{2,1,0:T(8,128)(2,1)S(1)} %slice.55), channel_id=1, source_target_pairs={{0,2},{1,3},{2,0},{3,1},{4,6},{5,7},{6,4},{7,5},{8,10},{9,11},{10,... | collective-permute-start | bytes 786440 | tf_op jit(solution)/shard_map/ppermute | solution.py:347
  56.5 11.7 %collective-permute-start.12 = (bf16[64,16,128]{2,1,0:T(8,128)(2,1)S(1)}, bf16[64,16,128]{2,1,0:T(8,128)(2,1)S(1)}, u32[]{:S(2)}, u32[]{:S(2)}) collective-permute-start(bf16[64,16,128]{2,1,0:T(8,128)(2,1)S(1)} %slice.54), channel_id=1, source_target_pairs={{0,4},{1,5},{2,6},{3,7},{4,0},{5,1},{6,2},{7,3},{8,12},{9,13},{10,... | collective-permute-start | bytes 786440 | tf_op jit(solution)/shard_map/ppermute | solution.py:347
  68.2 16.1 %collective-permute-start.15 = (bf16[128,16,128]{2,1,0:T(8,128)(2,1)S(1)}, bf16[128,16,128]{2,1,0:T(8,128)(2,1)S(1)}, u32[]{:S(2)}, u32[]{:S(2)}) collective-permute-start(bf16[128,16,128]{2,1,0:T(8,128)(2,1)S(1)} %collective-permute-done.9), channel_id=1, source_target_pairs={{0,4},{1,5},{2,6},{3,7},{4,0},{5,1},{6,2},{7,3},{8,12},{9,13},{10,... | collective-permute-start | bytes 1572872 | tf_op jit(solution)/shard_map/ppermute | solution.py:347
  68.9 15.4 %collective-permute-start.14 = (bf16[128,16,128]{2,1,0:T(8,128)(2,1)S(1)}, bf16[128,16,128]{2,1,0:T(8,128)(2,1)S(1)}, u32[]{:S(2)}, u32[]{:S(2)}) collective-permute-start(bf16[128,16,128]{2,1,0:T(8,128)(2,1)S(1)} %collective-permute-done.9), channel_id=1, source_target_pairs={{0,2},{1,3},{2,0},{3,1},{4,6},{5,7},{6,4},{7,5},{8,10},{9,11},{10,... | collective-permute-start | bytes 1572872 | tf_op jit(solution)/shard_map/ppermute | solution.py:347
  71.1 26.2 %collective-permute-start.20 = (bf16[512,16,128]{2,1,0:T(8,128)(2,1)}, bf16[512,16,128]{2,1,0:T(8,128)(2,1)}, u32[]{:S(2)}, u32[]{:S(2)}) collective-permute-start(bf16[512,16,128]{2,1,0:T(8,128)(2,1)} %constant_dynamic-update-slice_fusion.refs_0_), channel_id=1, source_target_pairs={{0,1},{1,0},{2,3},{3,2},{4,5},{5,4},{6,7},{7,6},{8,9},{9,8},{10,11... | collective-permute-start | bytes 6291464 | tf_op jit(solution)/shard_map/ppermute | solution.py:347
  71.2 13.1 %collective-permute-start.17 = (bf16[64,16,128]{2,1,0:T(8,128)(2,1)S(1)}, bf16[64,16,128]{2,1,0:T(8,128)(2,1)S(1)}, u32[]{:S(2)}, u32[]{:S(2)}) collective-permute-start(bf16[64,16,128]{2,1,0:T(8,128)(2,1)S(1)} %slice.57), channel_id=1, source_target_pairs={{0,2},{1,3},{2,0},{3,1},{4,6},{5,7},{6,4},{7,5},{8,10},{9,11},{10,... | collective-permute-start | bytes 786440 | tf_op jit(solution)/shard_map/ppermute | solution.py:347
  71.8 12.5 %collective-permute-start.16 = (bf16[64,16,128]{2,1,0:T(8,128)(2,1)S(1)}, bf16[64,16,128]{2,1,0:T(8,128)(2,1)S(1)}, u32[]{:S(2)}, u32[]{:S(2)}) collective-permute-start(bf16[64,16,128]{2,1,0:T(8,128)(2,1)S(1)} %slice.56), channel_id=1, source_target_pairs={{0,4},{1,5},{2,6},{3,7},{4,0},{5,1},{6,2},{7,3},{8,12},{9,13},{10,... | collective-permute-start | bytes 786440 | tf_op jit(solution)/shard_map/ppermute | solution.py:347
  84.3 13.0 %collective-permute-start.21 = (bf16[512,16,128]{2,1,0:T(8,128)(2,1)}, bf16[512,16,128]{2,1,0:T(8,128)(2,1)}, u32[]{:S(2)}, u32[]{:S(2)}) collective-permute-start(bf16[512,16,128]{2,1,0:T(8,128)(2,1)} %constant_dynamic-update-slice_fusion.5.refs_1_), channel_id=1, source_target_pairs={{0,1},{1,0},{2,3},{3,2},{4,5},{5,4},{6,7},{7,6},{8,9},{9,8},{10,11... | collective-permute-start | bytes 6291464 | tf_op jit(solution)/shard_map/ppermute | solution.py:347
  84.4 8.8 %collective-permute-start.19 = (bf16[64,16,128]{2,1,0:T(8,128)(2,1)S(1)}, bf16[64,16,128]{2,1,0:T(8,128)(2,1)S(1)}, u32[]{:S(2)}, u32[]{:S(2)}) collective-permute-start(bf16[64,16,128]{2,1,0:T(8,128)(2,1)S(1)} %slice.59), channel_id=1, source_target_pairs={{0,2},{1,3},{2,0},{3,1},{4,6},{5,7},{6,4},{7,5},{8,10},{9,11},{10,... | collective-permute-start | bytes 786440 | tf_op jit(solution)/shard_map/ppermute | solution.py:347
  85.9 8.4 %collective-permute-start.18 = (bf16[64,16,128]{2,1,0:T(8,128)(2,1)S(1)}, bf16[64,16,128]{2,1,0:T(8,128)(2,1)S(1)}, u32[]{:S(2)}, u32[]{:S(2)}) collective-permute-start(bf16[64,16,128]{2,1,0:T(8,128)(2,1)S(1)} %slice.58), channel_id=1, source_target_pairs={{0,4},{1,5},{2,6},{3,7},{4,0},{5,1},{6,2},{7,3},{8,12},{9,13},{10,... | collective-permute-start | bytes 786440 | tf_op jit(solution)/shard_map/ppermute | solution.py:347
  88.2 9.2 %collective-permute-start.22 = (bf16[512,16,128]{2,1,0:T(8,128)(2,1)}, bf16[512,16,128]{2,1,0:T(8,128)(2,1)}, u32[]{:S(2)}, u32[]{:S(2)}) collective-permute-start(bf16[512,16,128]{2,1,0:T(8,128)(2,1)} %constant_dynamic-update-slice_fusion.10.refs_2_), channel_id=1, source_target_pairs={{0,1},{1,0},{2,3},{3,2},{4,5},{5,4},{6,7},{7,6},{8,9},{9,8},{10,11... | collective-permute-start | bytes 6291464 | tf_op jit(solution)/shard_map/ppermute | solution.py:347
  88.3 6.1 %copy-start = (bf16[384,16,128]{2,1,0:T(8,128)(2,1)}, bf16[384,16,128]{2,1,0:T(8,128)(2,1)S(1)}, u32[]{:S(2)}) copy-start(bf16[384,16,128]{2,1,0:T(8,128)(2,1)S(1)} %constant_dynamic-update-slice_fusion.15.refs_3_) | copy-start | bytes 4718596
  93.1 4.2 %collective-permute-start.23 = (bf16[384,16,128]{2,1,0:T(8,128)(2,1)S(1)}, bf16[384,16,128]{2,1,0:T(8,128)(2,1)}, u32[]{:S(2)}, u32[]{:S(2)}) collective-permute-start(bf16[384,16,128]{2,1,0:T(8,128)(2,1)S(1)} %constant_dynamic-update-slice_fusion.15.refs_3_), channel_id=1, source_target_pairs={{0,1},{1,0},{2,3},{3,2},{4,5},{5,4},{6,7},{7,6},{8,9},{9,8},{10,11... | collective-permute-start | bytes 4718600 | tf_op jit(solution)/shard_map/ppermute | solution.py:347
  94.4 2.9 %collective-permute-start.24 = (bf16[128,16,128]{2,1,0:T(8,128)(2,1)S(1)}, bf16[128,16,128]{2,1,0:T(8,128)(2,1)S(1)}, u32[]{:S(2)}, u32[]{:S(2)}) collective-permute-start(bf16[128,16,128]{2,1,0:T(8,128)(2,1)S(1)} %constant_dynamic-update-slice_fusion.18.refs_4_), channel_id=1, source_target_pairs={{0,1},{1,0},{2,3},{3,2},{4,5},{5,4},{6,7},{7,6},{8,9},{9,8},{10,11... | collective-permute-start | bytes 1572872 | tf_op jit(solution)/shard_map/ppermute | solution.py:347
  144.6 61.6 %collective-permute-start.27 = (f32[256,512]{1,0:T(8,128)}, f32[256,512]{1,0:T(8,128)S(1)}, u32[]{:S(2)}, u32[]{:S(2)}) collective-permute-start(f32[256,512]{1,0:T(8,128)} %get-tuple-element.59.refs_0_), channel_id=1, source_target_pairs={{0,24},{8,16},{16,8},{24,0},{1,25},{9,17},{17,9},{25,1},{2,26},{10... | collective-permute-start | bytes 1572872 | tf_op jit(solution)/shard_map/ppermute | solution.py:465
  146.1 60.2 %collective-permute-start.26 = (f32[256,512]{1,0:T(8,128)}, f32[256,512]{1,0:T(8,128)S(1)}, u32[]{:S(2)}, u32[]{:S(2)}) collective-permute-start(f32[256,512]{1,0:T(8,128)} %get-tuple-element.59.refs_0_), channel_id=1, source_target_pairs={{0,16},{8,24},{16,0},{24,8},{1,17},{9,25},{17,1},{25,9},{2,18},{10... | collective-permute-start | bytes 1572872 | tf_op jit(solution)/shard_map/ppermute | solution.py:465
  146.3 60.0 %collective-permute-start.25 = (f32[256,512]{1,0:T(8,128)}, f32[256,512]{1,0:T(8,128)S(1)}, u32[]{:S(2)}, u32[]{:S(2)}) collective-permute-start(f32[256,512]{1,0:T(8,128)} %get-tuple-element.59.refs_0_), channel_id=1, source_target_pairs={{0,8},{8,0},{16,24},{24,16},{1,9},{9,1},{17,25},{25,17},{2,10},{10... | collective-permute-start | bytes 1572872 | tf_op jit(solution)/shard_map/ppermute | solution.py:465
  (5 other events, 6.7 us)
Sparse Core Ops, SparseCore 0:
  144.8 35.0 all-gather.2

commit v14 on v13

--- a/solution.py
+++ b/solution.py
@@ -216,31 +216,33 @@
     order = lh_ref.shape[0]
     steps = order // BLK
     tile = 2 * BLK
+    window = 3 * BLK
     lh_ref[...] = jnp.zeros_like(lh_ref)
     ll_ref[...] = jnp.zeros_like(ll_ref)
     w_ref[:, tile:] = jnp.zeros((order, order - tile), jnp.float32)
 
     def rows_of(i, carry):
-        left = pl.ds(pl.multiple_of(i * 2 * tile, 2 * tile), 2 * tile)
+        left = pl.ds(pl.multiple_of(i * tile, tile), tile)
         w_ref[left, :tile] = gram_tile(yx_ref, yz_ref, left, pl.ds(0, tile))
         return carry
-    lax.fori_loop(0, order // (2 * tile), rows_of, 0)
-
-    def step(b, ahead, window):
+    lax.fori_loop(0, order // tile, rows_of, 0)
+
+    def step(b, carry):
         at = pl.ds(pl.multiple_of(b * BLK, BLK), BLK)
-        left = pl.ds(pl.multiple_of(ahead * tile + (b % 2) * window, BLK), window)
-        right = slice(ahead * tile, (ahead + 1) * tile)
+        after = jnp.minimum(b // 2 + 1, order // tile - 1)
+        top = pl.multiple_of(jnp.minimum(after * tile + (b % 2) * window, order - window), BLK)
+        left = pl.ds(top, window)
+        right = pl.ds(pl.multiple_of(after * tile, tile), tile)
 
         def beside(m):
-            if window > 0:
-                q, r = m // RANK, m % RANK
-                term = dot_bf16(yx_ref[r, left, :], yx_ref[q, right, :], NT) * dot_bf16(yz_ref[r, left, :], yz_ref[q, right, :], NT)
-                g_ref[left, :] = signed(g_ref[left, :] if m > 0 else None, term, q, r)
+            q, r = m // RANK, m % RANK
+            term = dot_bf16(yx_ref[r, left, :], yx_ref[q, right, :], NT) * dot_bf16(yz_ref[r, left, :], yz_ref[q, right, :], NT)
+            g_ref[left, :] = signed(g_ref[left, :] if m > 0 else None, term, q, r)
 
         factor_block(w_ref[at, at], u_ref, v_ref, beside)
         lh_ref[at, at], ll_ref[at, at] = split(u_ref[...].T)
         d_ref[at, :] = v_ref[...]
-        for k in range(2 * ahead - 2, min(2 * ahead, steps - 1)):
+        for k in range(steps - 1):
             @pl.when(b == k)
             def _():
                 first = (k + 1) * BLK
@@ -253,12 +255,8 @@
                     w_ref[top:bottom, first:bottom] = w_ref[top:bottom, first:bottom] - dot3(left, right, NT)
                 if k % 2 == 1:
                     w_ref[first:, first:first + tile] = w_ref[first:, first:first + tile] + g_ref[first:, :]
-
-    for ahead in range(1, order // tile + 1):
-        def two_steps(b, carry, ahead=ahead):
-            step(b, ahead, (order - ahead * tile) // 2)
-            return carry
-        lax.fori_loop(2 * ahead - 2, 2 * ahead, two_steps, 0)
+        return carry
+    lax.fori_loop(0, steps, step, 0)
 
 
 def factor(yx, yz):

time: 238 us -> 234 us (0.983); the launches traced: 234 us -> 234 us
  transfers between devices with their start and end apart: 29 -> 29, of which waited for: 9 -> 9; matrix products, arithmetic and copies ran while one was open for 7% -> 7% of each run, Pallas kernels for 24% -> 25%
where the time goes in v14:
time: 234 us
  Pallas kernels  123 us (53%)
  waiting for transfers between devices  41.4 us (18%)
  starting transfers between devices  32.1 us (14%)
  local copies, waits for them, and re-layouts  19 us (8%)
  between operations  14.4 us (6%)
  other arithmetic  3.21 us (1%)
    pallas_call x1, Pallas kernels, factor(): pl.pallas_call(factor_kernel, out_shape=(jax.ShapeDtypeStruct((K, K), jnp...  57.7 us
    pallas_call x1, Pallas kernels, assemble(): pl.pallas_call(body, grid=(pick_tiles + row_tiles * col_tiles,), out_shap...  46.2 us
    ppermute x25, waiting for transfers between devices, swap(): lax.ppermute(value, axis, [(n, n ^ turn) for n in range(count) if chosen(...  41.4 us
    ppermute x25, starting transfers between devices, swap(): lax.ppermute(value, axis, [(n, n ^ turn) for n in range(count) if chosen(...  27.7 us
    pallas_call x1, Pallas kernels, solve(): pl.pallas_call(functools.partial(solve_kernel, prow=len(tops)), out_shape...  19.2 us
    unnamed x31, local copies, waits for them, and re-layouts  12.8 us
  transfers between devices with their start and end apart: 29, of which 9 were waited for; matrix products, arithmetic and copies ran while one was open for 7% of the time, Pallas kernels for 25%

profile of v14, /device:TPU:0, one launch (start us, length us, event | category | flops | bytes accessed | tf_op | source)
XLA Modules:
  0.0 233.8 jit_solution(14078168626980513205)
XLA Ops:
  7.2 1.5 copy.21
  9.6 5.9 %collective-permute-start.2 = (bf16[128,16,128]{2,1,0:T(8,128)(2,1)S(1)}, bf16[128,16,128]{2,1,0:T(8,128)(2,1)}, u32[]{:S(2)}, u32[]{:S(2)}) collective-permute-start(bf16[128,16,128]{2,1,0:T(8,128)(2,1)S(1)} %reshape.179), channel_id=1, source_target_pairs={{0,8},{8,0},{16,24},{24,16},{1,9},{9,1},{17,25},{25,17},{2,10},{10... | collective-permute-start | bytes 1572872 | tf_op jit(solution)/shard_map/ppermute | solution.py:345
  15.5 1.5 collective-permute-start.1
  17.0 1.5 collective-permute-start
  18.7 8.5 %collective-permute-done.2 = bf16[128,16,128]{2,1,0:T(8,128)(2,1)} collective-permute-done((bf16[128,16,128]{2,1,0:T(8,128)(2,1)S(1)}, bf16[128,16,128]{2,1,0:T(8,128)(2,1)}, u32[]{:S(2)}, u32[]{:S(2)}) %collective-permute-start.2) | collective-permute-done | bytes 524320 | tf_op jit(solution)/shard_map/ppermute | solution.py:345
  27.2 1.4 collective-permute-done.1
  28.6 1.2 collective-permute-done
  30.3 1.5 collective-permute-start.4
  31.8 3.2 %collective-permute-start.8 = (bf16[128,16,128]{2,1,0:T(8,128)(2,1)S(1)}, bf16[128,16,128]{2,1,0:T(8,128)(2,1)}, u32[]{:S(2)}, u32[]{:S(2)}) collective-permute-start(bf16[128,16,128]{2,1,0:T(8,128)(2,1)S(1)} %reshape.179), channel_id=1, source_target_pairs={{0,24},{24,0},{1,25},{25,1},{2,26},{26,2},{3,27},{27,3},{4,28},{28... | collective-permute-start | bytes 1572872 | tf_op jit(solution)/shard_map/ppermute | solution.py:345
  37.1 1.5 collective-permute-start.6
  39.5 8.4 %collective-permute-done.7 = bf16[64,16,128]{2,1,0:T(8,128)(2,1)S(1)} collective-permute-done((bf16[64,16,128]{2,1,0:T(8,128)(2,1)}, bf16[64,16,128]{2,1,0:T(8,128)(2,1)S(1)}, u32[]{:S(2)}, u32[]{:S(2)}) %collective-permute-start.7) | collective-permute-done | bytes 262176 | tf_op jit(solution)/shard_map/ppermute | solution.py:345
  48.0 2.0 constant_dynamic-update-slice_fusion.14
  49.9 1.4 collective-permute-start.11
  51.3 1.5 collective-permute-start.10
  53.6 2.2 constant_dynamic-update-slice_fusion.2
  57.1 1.7 constant_dynamic-update-slice_fusion.1
  58.8 0.9 constant_dynamic-update-slice_fusion.8
  60.5 7.7 %collective-permute-done.13 = bf16[64,16,128]{2,1,0:T(8,128)(2,1)S(1)} collective-permute-done((bf16[64,16,128]{2,1,0:T(8,128)(2,1)S(1)}, bf16[64,16,128]{2,1,0:T(8,128)(2,1)S(1)}, u32[]{:S(2)}, u32[]{:S(2)}) %collective-permute-start.13) | collective-permute-done | bytes 262176 | tf_op jit(solution)/shard_map/ppermute | solution.py:345
  68.9 1.5 collective-permute-start.14
  71.8 1.4 collective-permute-start.16
  74.6 0.9 constant_dynamic-update-slice_fusion.13
  75.5 1.0 constant_dynamic-update-slice_fusion.12
  76.5 7.8 %collective-permute-done.17 = bf16[64,16,128]{2,1,0:T(8,128)(2,1)S(1)} collective-permute-done((bf16[64,16,128]{2,1,0:T(8,128)(2,1)S(1)}, bf16[64,16,128]{2,1,0:T(8,128)(2,1)S(1)}, u32[]{:S(2)}, u32[]{:S(2)}) %collective-permute-start.17) | collective-permute-done | bytes 262176 | tf_op jit(solution)/shard_map/ppermute | solution.py:345
  84.4 1.6 collective-permute-start.19
  85.9 0.8 collective-permute-start.18
  88.3 4.8 %collective-permute-done.19 = bf16[64,16,128]{2,1,0:T(8,128)(2,1)S(1)} collective-permute-done((bf16[64,16,128]{2,1,0:T(8,128)(2,1)S(1)}, bf16[64,16,128]{2,1,0:T(8,128)(2,1)S(1)}, u32[]{:S(2)}, u32[]{:S(2)}) %collective-permute-start.19) | collective-permute-done | bytes 262176 | tf_op jit(solution)/shard_map/ppermute | solution.py:345
  96.4 0.9 collective-permute-done.24.refs_9_
  98.1 46.2 %shard_map.68 = (bf16[4,1024,512]{2,1,0:T(8,128)(2,1)}, bf16[4,1024,512]{2,1,0:T(8,128)(2,1)}, f32[1024,512]{1,0:T(8,128)}, f32[1024,128]{1,0:T(8,128)}, f32[256,512]{1,0:T(8,128)}) custom-call(s32[2]{0:T(128)} %pad_add_fusion.1.place_ref, s32[2304]{0:T(1024)} %reshape.178.slots_ref, bf16[512,512]{1,0:T(8,128)(2,1)} %x_ref.1, bf16[512,512]{1,0:T(8,128)(2,1)} %z_ref.1, ...), custom_call_target="tpu_custom_call" | custom-call | flops 28000000000 | bytes 31457280 | tf_op jit(solution)/shard_map/pallas_call | solution.py:152
  144.4 1.4 collective-permute-start.27
  146.0 2.8 %collective-permute-start.25 = (f32[256,512]{1,0:T(8,128)}, f32[256,512]{1,0:T(8,128)S(1)}, u32[]{:S(2)}, u32[]{:S(2)}) collective-permute-start(f32[256,512]{1,0:T(8,128)} %get-tuple-element.59.refs_0_), channel_id=1, source_target_pairs={{0,8},{8,0},{16,24},{24,16},{1,9},{9,1},{17,25},{25,17},{2,10},{10... | collective-permute-start | bytes 1572872 | tf_op jit(solution)/shard_map/ppermute | solution.py:463
  148.9 57.7 %shard_map.69 = (bf16[1024,1024]{1,0:T(8,128)(2,1)}, bf16[1024,1024]{1,0:T(8,128)(2,1)}, f32[1024,128]{1,0:T(8,128)}) custom-call(bf16[4,1024,512]{2,1,0:T(8,128)(2,1)} %get-tuple-element.52.yx_ref, bf16[4,1024,512]{2,1,0:T(8,128)(2,1)} %get-tuple-element.53.yz_ref), custom_call_target="tpu_custom_call" | custom-call | flops 40000000000 | bytes 12582912 | tf_op jit(solution)/shard_map/pallas_call | solution.py:265
  207.7 19.2 %shard_map.70 = (f32[1024,512]{1,0:T(8,128)}, f32[1024,128]{1,0:T(8,128)}) custom-call(s32[2]{0:T(128)} %pad_add_fusion.1.place_ref, bf16[1024,1024]{1,0:T(8,128)(2,1)} %get-tuple-element.54.lh_any, bf16[1024,1024]{1,0:T(8,128)(2,1)} %get-tuple-element.55.ll_any, f32[1024,128]{1,0:T(8,128)} %get-tuple-element.56.d_any, f32[8,1024,128]{2,1,0:T(8,128)} %bitcast.51, ...), custom_call_target="tpu_custom_call" | custom-call | flops 12000000000 | bytes 25165824 | tf_op jit(solution)/shard_map/pallas_call | solution.py:327
  (91 shorter events, 18.0 us)
Async XLA Ops:
  7.2 11.3 %copy-start.7 = (s32[32]{0:T(128)S(1)}, s32[32]{0:T(128)}, u32[]{:S(2)}) copy-start(s32[32]{0:T(128)} %constant.94.clone) | copy-start | bytes 388
  7.2 199.4 %all-gather.3.cloned.1.call-start = ((), (), s32[]{:S(2)}) async-start(), calls=%async_computation | async-start | bytes 4718592 | tf_op jit(solution)/shard_map/all_gather | solution.py:462
  7.2 32.2 %copy-start.2 = (s32[4096]{0:T(1024)S(1)}, s32[4096]{0:T(1024)}, u32[]{:S(2)}) copy-start(s32[4096]{0:T(1024)} %param.8) | copy-start | bytes 49156
  8.9 9.8 %collective-permute-start.3 = (bf16[128,16,128]{2,1,0:T(8,128)(2,1)S(1)}, bf16[128,16,128]{2,1,0:T(8,128)(2,1)S(1)}, u32[]{:S(2)}, u32[]{:S(2)}) collective-permute-start(bf16[128,16,128]{2,1,0:T(8,128)(2,1)S(1)} %reshape.179), channel_id=1, source_target_pairs={{8,16},{16,8},{9,17},{17,9},{10,18},{18,10},{11,19},{19,11},{12,20... | collective-permute-start | bytes 1572872 | tf_op jit(solution)/shard_map/ppermute | solution.py:345
  9.6 17.6 %collective-permute-start.2 = (bf16[128,16,128]{2,1,0:T(8,128)(2,1)S(1)}, bf16[128,16,128]{2,1,0:T(8,128)(2,1)}, u32[]{:S(2)}, u32[]{:S(2)}) collective-permute-start(bf16[128,16,128]{2,1,0:T(8,128)(2,1)S(1)} %reshape.179), channel_id=1, source_target_pairs={{0,8},{8,0},{16,24},{24,16},{1,9},{9,1},{17,25},{25,17},{2,10},{10... | collective-permute-start | bytes 1572872 | tf_op jit(solution)/shard_map/ppermute | solution.py:345
  15.5 13.1 %collective-permute-start.1 = (bf16[128,16,128]{2,1,0:T(8,128)(2,1)S(1)}, bf16[128,16,128]{2,1,0:T(8,128)(2,1)S(1)}, u32[]{:S(2)}, u32[]{:S(2)}) collective-permute-start(bf16[128,16,128]{2,1,0:T(8,128)(2,1)S(1)} %reshape.179), channel_id=1, source_target_pairs={{0,4},{1,5},{2,6},{3,7},{4,0},{5,1},{6,2},{7,3},{8,12},{9,13},{10,... | collective-permute-start | bytes 1572872 | tf_op jit(solution)/shard_map/ppermute | solution.py:345
  17.0 12.8 %collective-permute-start = (bf16[128,16,128]{2,1,0:T(8,128)(2,1)S(1)}, bf16[128,16,128]{2,1,0:T(8,128)(2,1)S(1)}, u32[]{:S(2)}, u32[]{:S(2)}) collective-permute-start(bf16[128,16,128]{2,1,0:T(8,128)(2,1)S(1)} %reshape.179), channel_id=1, source_target_pairs={{0,2},{1,3},{2,0},{3,1},{4,6},{5,7},{6,4},{7,5},{8,10},{9,11},{10,... | collective-permute-start | bytes 1572872 | tf_op jit(solution)/shard_map/ppermute | solution.py:345
  29.8 18.1 %collective-permute-start.5 = (bf16[128,16,128]{2,1,0:T(8,128)(2,1)}, bf16[128,16,128]{2,1,0:T(8,128)(2,1)S(1)}, u32[]{:S(2)}, u32[]{:S(2)}) collective-permute-start(bf16[128,16,128]{2,1,0:T(8,128)(2,1)} %collective-permute-done.2), channel_id=1, source_target_pairs={{0,4},{1,5},{2,6},{3,7},{4,0},{5,1},{6,2},{7,3},{8,12},{9,13},{10,... | collective-permute-start | bytes 1572872 | tf_op jit(solution)/shard_map/ppermute | solution.py:345
  30.3 17.6 %collective-permute-start.4 = (bf16[128,16,128]{2,1,0:T(8,128)(2,1)}, bf16[128,16,128]{2,1,0:T(8,128)(2,1)S(1)}, u32[]{:S(2)}, u32[]{:S(2)}) collective-permute-start(bf16[128,16,128]{2,1,0:T(8,128)(2,1)} %collective-permute-done.2), channel_id=1, source_target_pairs={{0,2},{1,3},{2,0},{3,1},{4,6},{5,7},{6,4},{7,5},{8,10},{9,11},{10,... | collective-permute-start | bytes 1572872 | tf_op jit(solution)/shard_map/ppermute | solution.py:345
  31.8 16.1 %collective-permute-start.8 = (bf16[128,16,128]{2,1,0:T(8,128)(2,1)S(1)}, bf16[128,16,128]{2,1,0:T(8,128)(2,1)}, u32[]{:S(2)}, u32[]{:S(2)}) collective-permute-start(bf16[128,16,128]{2,1,0:T(8,128)(2,1)S(1)} %reshape.179), channel_id=1, source_target_pairs={{0,24},{24,0},{1,25},{25,1},{2,26},{26,2},{3,27},{27,3},{4,28},{28... | collective-permute-start | bytes 1572872 | tf_op jit(solution)/shard_map/ppermute | solution.py:345
  36.5 11.4 %collective-permute-start.7 = (bf16[64,16,128]{2,1,0:T(8,128)(2,1)}, bf16[64,16,128]{2,1,0:T(8,128)(2,1)S(1)}, u32[]{:S(2)}, u32[]{:S(2)}) collective-permute-start(bf16[64,16,128]{2,1,0:T(8,128)(2,1)} %slice.53), channel_id=1, source_target_pairs={{0,2},{1,3},{2,0},{3,1},{4,6},{5,7},{6,4},{7,5},{8,10},{9,11},{10,... | collective-permute-start | bytes 786440 | tf_op jit(solution)/shard_map/ppermute | solution.py:345
  37.1 10.9 %collective-permute-start.6 = (bf16[64,16,128]{2,1,0:T(8,128)(2,1)}, bf16[64,16,128]{2,1,0:T(8,128)(2,1)}, u32[]{:S(2)}, u32[]{:S(2)}) collective-permute-start(bf16[64,16,128]{2,1,0:T(8,128)(2,1)} %slice.52), channel_id=1, source_target_pairs={{0,4},{1,5},{2,6},{3,7},{4,0},{5,1},{6,2},{7,3},{8,12},{9,13},{10,... | collective-permute-start | bytes 786440 | tf_op jit(solution)/shard_map/ppermute | solution.py:345
  49.9 18.3 %collective-permute-start.11 = (bf16[128,16,128]{2,1,0:T(8,128)(2,1)S(1)}, bf16[128,16,128]{2,1,0:T(8,128)(2,1)S(1)}, u32[]{:S(2)}, u32[]{:S(2)}) collective-permute-start(bf16[128,16,128]{2,1,0:T(8,128)(2,1)S(1)} %get-tuple-element.61), channel_id=1, source_target_pairs={{0,4},{1,5},{2,6},{3,7},{4,0},{5,1},{6,2},{7,3},{8,12},{9,13},{10,... | collective-permute-start | bytes 1572872 | tf_op jit(solution)/shard_map/ppermute | solution.py:345
  51.3 16.9 %collective-permute-start.10 = (bf16[128,16,128]{2,1,0:T(8,128)(2,1)S(1)}, bf16[128,16,128]{2,1,0:T(8,128)(2,1)S(1)}, u32[]{:S(2)}, u32[]{:S(2)}) collective-permute-start(bf16[128,16,128]{2,1,0:T(8,128)(2,1)S(1)} %get-tuple-element.61), channel_id=1, source_target_pairs={{0,2},{1,3},{2,0},{3,1},{4,6},{5,7},{6,4},{7,5},{8,10},{9,11},{10,... | collective-permute-start | bytes 1572872 | tf_op jit(solution)/shard_map/ppermute | solution.py:345
  52.8 15.4 %collective-permute-start.9 = (bf16[128,16,128]{2,1,0:T(8,128)(2,1)S(1)}, bf16[128,16,128]{2,1,0:T(8,128)(2,1)S(1)}, u32[]{:S(2)}, u32[]{:S(2)}) collective-permute-start(bf16[128,16,128]{2,1,0:T(8,128)(2,1)S(1)} %get-tuple-element.61), channel_id=1, source_target_pairs={{0,8},{8,0},{16,24},{24,16},{1,9},{9,1},{17,25},{25,17},{2,10},{10... | collective-permute-start | bytes 1572872 | tf_op jit(solution)/shard_map/ppermute | solution.py:345
  55.9 12.3 %collective-permute-start.13 = (bf16[64,16,128]{2,1,0:T(8,128)(2,1)S(1)}, bf16[64,16,128]{2,1,0:T(8,128)(2,1)S(1)}, u32[]{:S(2)}, u32[]{:S(2)}) collective-permute-start(bf16[64,16,128]{2,1,0:T(8,128)(2,1)S(1)} %slice.55), channel_id=1, source_target_pairs={{0,2},{1,3},{2,0},{3,1},{4,6},{5,7},{6,4},{7,5},{8,10},{9,11},{10,... | collective-permute-start | bytes 786440 | tf_op jit(solution)/shard_map/ppermute | solution.py:345
  56.5 11.7 %collective-permute-start.12 = (bf16[64,16,128]{2,1,0:T(8,128)(2,1)S(1)}, bf16[64,16,128]{2,1,0:T(8,128)(2,1)S(1)}, u32[]{:S(2)}, u32[]{:S(2)}) collective-permute-start(bf16[64,16,128]{2,1,0:T(8,128)(2,1)S(1)} %slice.54), channel_id=1, source_target_pairs={{0,4},{1,5},{2,6},{3,7},{4,0},{5,1},{6,2},{7,3},{8,12},{9,13},{10,... | collective-permute-start | bytes 786440 | tf_op jit(solution)/shard_map/ppermute | solution.py:345
  68.2 16.1 %collective-permute-start.15 = (bf16[128,16,128]{2,1,0:T(8,128)(2,1)S(1)}, bf16[128,16,128]{2,1,0:T(8,128)(2,1)S(1)}, u32[]{:S(2)}, u32[]{:S(2)}) collective-permute-start(bf16[128,16,128]{2,1,0:T(8,128)(2,1)S(1)} %collective-permute-done.9), channel_id=1, source_target_pairs={{0,4},{1,5},{2,6},{3,7},{4,0},{5,1},{6,2},{7,3},{8,12},{9,13},{10,... | collective-permute-start | bytes 1572872 | tf_op jit(solution)/shard_map/ppermute | solution.py:345
  68.9 15.4 %collective-permute-start.14 = (bf16[128,16,128]{2,1,0:T(8,128)(2,1)S(1)}, bf16[128,16,128]{2,1,0:T(8,128)(2,1)S(1)}, u32[]{:S(2)}, u32[]{:S(2)}) collective-permute-start(bf16[128,16,128]{2,1,0:T(8,128)(2,1)S(1)} %collective-permute-done.9), channel_id=1, source_target_pairs={{0,2},{1,3},{2,0},{3,1},{4,6},{5,7},{6,4},{7,5},{8,10},{9,11},{10,... | collective-permute-start | bytes 1572872 | tf_op jit(solution)/shard_map/ppermute | solution.py:345
  71.1 26.2 %collective-permute-start.20 = (bf16[512,16,128]{2,1,0:T(8,128)(2,1)}, bf16[512,16,128]{2,1,0:T(8,128)(2,1)}, u32[]{:S(2)}, u32[]{:S(2)}) collective-permute-start(bf16[512,16,128]{2,1,0:T(8,128)(2,1)} %constant_dynamic-update-slice_fusion.refs_0_), channel_id=1, source_target_pairs={{0,1},{1,0},{2,3},{3,2},{4,5},{5,4},{6,7},{7,6},{8,9},{9,8},{10,11... | collective-permute-start | bytes 6291464 | tf_op jit(solution)/shard_map/ppermute | solution.py:345
  71.2 13.1 %collective-permute-start.17 = (bf16[64,16,128]{2,1,0:T(8,128)(2,1)S(1)}, bf16[64,16,128]{2,1,0:T(8,128)(2,1)S(1)}, u32[]{:S(2)}, u32[]{:S(2)}) collective-permute-start(bf16[64,16,128]{2,1,0:T(8,128)(2,1)S(1)} %slice.57), channel_id=1, source_target_pairs={{0,2},{1,3},{2,0},{3,1},{4,6},{5,7},{6,4},{7,5},{8,10},{9,11},{10,... | collective-permute-start | bytes 786440 | tf_op jit(solution)/shard_map/ppermute | solution.py:345
  71.8 12.5 %collective-permute-start.16 = (bf16[64,16,128]{2,1,0:T(8,128)(2,1)S(1)}, bf16[64,16,128]{2,1,0:T(8,128)(2,1)S(1)}, u32[]{:S(2)}, u32[]{:S(2)}) collective-permute-start(bf16[64,16,128]{2,1,0:T(8,128)(2,1)S(1)} %slice.56), channel_id=1, source_target_pairs={{0,4},{1,5},{2,6},{3,7},{4,0},{5,1},{6,2},{7,3},{8,12},{9,13},{10,... | collective-permute-start | bytes 786440 | tf_op jit(solution)/shard_map/ppermute | solution.py:345
  84.3 13.0 %collective-permute-start.21 = (bf16[512,16,128]{2,1,0:T(8,128)(2,1)}, bf16[512,16,128]{2,1,0:T(8,128)(2,1)}, u32[]{:S(2)}, u32[]{:S(2)}) collective-permute-start(bf16[512,16,128]{2,1,0:T(8,128)(2,1)} %constant_dynamic-update-slice_fusion.5.refs_1_), channel_id=1, source_target_pairs={{0,1},{1,0},{2,3},{3,2},{4,5},{5,4},{6,7},{7,6},{8,9},{9,8},{10,11... | collective-permute-start | bytes 6291464 | tf_op jit(solution)/shard_map/ppermute | solution.py:345
  84.4 8.8 %collective-permute-start.19 = (bf16[64,16,128]{2,1,0:T(8,128)(2,1)S(1)}, bf16[64,16,128]{2,1,0:T(8,128)(2,1)S(1)}, u32[]{:S(2)}, u32[]{:S(2)}) collective-permute-start(bf16[64,16,128]{2,1,0:T(8,128)(2,1)S(1)} %slice.59), channel_id=1, source_target_pairs={{0,2},{1,3},{2,0},{3,1},{4,6},{5,7},{6,4},{7,5},{8,10},{9,11},{10,... | collective-permute-start | bytes 786440 | tf_op jit(solution)/shard_map/ppermute | solution.py:345
  85.9 8.4 %collective-permute-start.18 = (bf16[64,16,128]{2,1,0:T(8,128)(2,1)S(1)}, bf16[64,16,128]{2,1,0:T(8,128)(2,1)S(1)}, u32[]{:S(2)}, u32[]{:S(2)}) collective-permute-start(bf16[64,16,128]{2,1,0:T(8,128)(2,1)S(1)} %slice.58), channel_id=1, source_target_pairs={{0,4},{1,5},{2,6},{3,7},{4,0},{5,1},{6,2},{7,3},{8,12},{9,13},{10,... | collective-permute-start | bytes 786440 | tf_op jit(solution)/shard_map/ppermute | solution.py:345
  88.2 9.2 %collective-permute-start.22 = (bf16[512,16,128]{2,1,0:T(8,128)(2,1)}, bf16[512,16,128]{2,1,0:T(8,128)(2,1)}, u32[]{:S(2)}, u32[]{:S(2)}) collective-permute-start(bf16[512,16,128]{2,1,0:T(8,128)(2,1)} %constant_dynamic-update-slice_fusion.10.refs_2_), channel_id=1, source_target_pairs={{0,1},{1,0},{2,3},{3,2},{4,5},{5,4},{6,7},{7,6},{8,9},{9,8},{10,11... | collective-permute-start | bytes 6291464 | tf_op jit(solution)/shard_map/ppermute | solution.py:345
  88.3 6.1 %copy-start = (bf16[384,16,128]{2,1,0:T(8,128)(2,1)}, bf16[384,16,128]{2,1,0:T(8,128)(2,1)S(1)}, u32[]{:S(2)}) copy-start(bf16[384,16,128]{2,1,0:T(8,128)(2,1)S(1)} %constant_dynamic-update-slice_fusion.15.refs_3_) | copy-start | bytes 4718596
  93.1 4.2 %collective-permute-start.23 = (bf16[384,16,128]{2,1,0:T(8,128)(2,1)S(1)}, bf16[384,16,128]{2,1,0:T(8,128)(2,1)}, u32[]{:S(2)}, u32[]{:S(2)}) collective-permute-start(bf16[384,16,128]{2,1,0:T(8,128)(2,1)S(1)} %constant_dynamic-update-slice_fusion.15.refs_3_), channel_id=1, source_target_pairs={{0,1},{1,0},{2,3},{3,2},{4,5},{5,4},{6,7},{7,6},{8,9},{9,8},{10,11... | collective-permute-start | bytes 4718600 | tf_op jit(solution)/shard_map/ppermute | solution.py:345
  94.4 2.9 %collective-permute-start.24 = (bf16[128,16,128]{2,1,0:T(8,128)(2,1)S(1)}, bf16[128,16,128]{2,1,0:T(8,128)(2,1)S(1)}, u32[]{:S(2)}, u32[]{:S(2)}) collective-permute-start(bf16[128,16,128]{2,1,0:T(8,128)(2,1)S(1)} %constant_dynamic-update-slice_fusion.18.refs_4_), channel_id=1, source_target_pairs={{0,1},{1,0},{2,3},{3,2},{4,5},{5,4},{6,7},{7,6},{8,9},{9,8},{10,11... | collective-permute-start | bytes 1572872 | tf_op jit(solution)/shard_map/ppermute | solution.py:345
  144.4 62.1 %collective-permute-start.27 = (f32[256,512]{1,0:T(8,128)}, f32[256,512]{1,0:T(8,128)S(1)}, u32[]{:S(2)}, u32[]{:S(2)}) collective-permute-start(f32[256,512]{1,0:T(8,128)} %get-tuple-element.59.refs_0_), channel_id=1, source_target_pairs={{0,24},{8,16},{16,8},{24,0},{1,25},{9,17},{17,9},{25,1},{2,26},{10... | collective-permute-start | bytes 1572872 | tf_op jit(solution)/shard_map/ppermute | solution.py:463
  145.8 60.7 %collective-permute-start.26 = (f32[256,512]{1,0:T(8,128)}, f32[256,512]{1,0:T(8,128)S(1)}, u32[]{:S(2)}, u32[]{:S(2)}) collective-permute-start(f32[256,512]{1,0:T(8,128)} %get-tuple-element.59.refs_0_), channel_id=1, source_target_pairs={{0,16},{8,24},{16,0},{24,8},{1,17},{9,25},{17,1},{25,9},{2,18},{10... | collective-permute-start | bytes 1572872 | tf_op jit(solution)/shard_map/ppermute | solution.py:463
  146.0 60.5 %collective-permute-start.25 = (f32[256,512]{1,0:T(8,128)}, f32[256,512]{1,0:T(8,128)S(1)}, u32[]{:S(2)}, u32[]{:S(2)}) collective-permute-start(f32[256,512]{1,0:T(8,128)} %get-tuple-element.59.refs_0_), channel_id=1, source_target_pairs={{0,8},{8,0},{16,24},{24,16},{1,9},{9,1},{17,25},{25,17},{2,10},{10... | collective-permute-start | bytes 1572872 | tf_op jit(solution)/shard_map/ppermute | solution.py:463
  (5 other events, 6.7 us)
Sparse Core Ops, SparseCore 0:
  144.5 35.0 all-gather.2

commit v15 on v14

--- a/solution.py
+++ b/solution.py
@@ -185,7 +185,8 @@
         beside(m)
         head_a, head_v = rows_a[m], rows_v[m]
         cols = [spread_lane(head_a, SUB * m + k) for k in range(SUB)]
-        below = [[spread_lane(rows_a[i], SUB * m + k) for k in range(SUB)] for i in range(m + 1, count)]
+        below = [[spread_lane(rows_a[i], SUB * m + k) for k in range(SUB if i == m + 1 else SUB // 2)] + [None] * (0 if i == m + 1 else SUB // 2)
+                 for i in range(m + 1, count)]
         scale = jnp.zeros((SUB, BLK), jnp.float32)
         for j in range(SUB):
             pivot = spread_row(cols[j], j)
@@ -204,7 +205,9 @@
                 mult_i = below[n][j] * root
                 rows_a[i] = rows_a[i] - mult_i * row_a
                 rows_v[i] = rows_v[i] - mult_i * row_v
-                for k in range(j + 1, SUB):
+                if n > 0 and j + 1 == SUB // 2:
+                    below[n][j + 1:] = [spread_lane(rows_a[i], SUB * m + k) for k in range(j + 1, SUB)]
+                for k in range(j + 1, SUB if n == 0 else max(SUB // 2, j // (SUB // 2) * SUB)):
                     below[n][k] = below[n][k] - mult_i * lead[k]
         u = jnp.where(lane_iota >= sub_iota + SUB * m, head_a * scale, 0.0)
         v = jnp.where(lane_iota <= sub_iota + SUB * m, head_v * scale, 0.0)

time: 234 us -> 241 us (1.030)
  Pallas kernels: 123 us -> 130 us
    pallas_call x1, Pallas kernels: 57.7 us -> 64.1 us  [factor(): pl.pallas_call(factor_kernel, out_shape=(jax.ShapeDtypeStruct((K, K), jnp...]
  transfers between devices with their start and end apart: 29 -> 29, of which waited for: 9 -> 9; matrix products, arithmetic and copies ran while one was open for 7% -> 7% of each run, Pallas kernels for 25% -> 27%
where the time goes in v15:
time: 241 us; the launch traced here: 240 us
  Pallas kernels  130 us (54%)
  waiting for transfers between devices  41.4 us (17%)
  starting transfers between devices  32.1 us (13%)
  local copies, waits for them, and re-layouts  19 us (8%)
  between operations  14.4 us (6%)
  other arithmetic  3.21 us (1%)
    pallas_call x1, Pallas kernels, factor(): pl.pallas_call(factor_kernel, out_shape=(jax.ShapeDtypeStruct((K, K), jnp...  64.1 us
    pallas_call x1, Pallas kernels, assemble(): pl.pallas_call(body, grid=(pick_tiles + row_tiles * col_tiles,), out_shap...  46.2 us
    ppermute x25, waiting for transfers between devices, swap(): lax.ppermute(value, axis, [(n, n ^ turn) for n in range(count) if chosen(...  41.4 us
    ppermute x25, starting transfers between devices, swap(): lax.ppermute(value, axis, [(n, n ^ turn) for n in range(count) if chosen(...  27.7 us
    pallas_call x1, Pallas kernels, solve(): pl.pallas_call(functools.partial(solve_kernel, prow=len(tops)), out_shape...  19.2 us
    unnamed x31, local copies, waits for them, and re-layouts  12.8 us
  transfers between devices with their start and end apart: 29, of which 9 were waited for; matrix products, arithmetic and copies ran while one was open for 7% of the time, Pallas kernels for 27%

profile of v15, /device:TPU:0, one launch (start us, length us, event | category | flops | bytes accessed | tf_op | source)
XLA Modules:
  0.0 240.2 jit_solution(17409384547758335096)
XLA Ops:
  7.2 1.5 copy.21
  9.6 5.9 %collective-permute-start.2 = (bf16[128,16,128]{2,1,0:T(8,128)(2,1)S(1)}, bf16[128,16,128]{2,1,0:T(8,128)(2,1)}, u32[]{:S(2)}, u32[]{:S(2)}) collective-permute-start(bf16[128,16,128]{2,1,0:T(8,128)(2,1)S(1)} %reshape.179), channel_id=1, source_target_pairs={{0,8},{8,0},{16,24},{24,16},{1,9},{9,1},{17,25},{25,17},{2,10},{10... | collective-permute-start | bytes 1572872 | tf_op jit(solution)/shard_map/ppermute | solution.py:348
  15.5 1.5 collective-permute-start.1
  17.0 1.5 collective-permute-start
  18.7 8.5 %collective-permute-done.2 = bf16[128,16,128]{2,1,0:T(8,128)(2,1)} collective-permute-done((bf16[128,16,128]{2,1,0:T(8,128)(2,1)S(1)}, bf16[128,16,128]{2,1,0:T(8,128)(2,1)}, u32[]{:S(2)}, u32[]{:S(2)}) %collective-permute-start.2) | collective-permute-done | bytes 524320 | tf_op jit(solution)/shard_map/ppermute | solution.py:348
  27.2 1.4 collective-permute-done.1
  28.6 1.2 collective-permute-done
  30.3 1.5 collective-permute-start.4
  31.8 3.2 %collective-permute-start.8 = (bf16[128,16,128]{2,1,0:T(8,128)(2,1)S(1)}, bf16[128,16,128]{2,1,0:T(8,128)(2,1)}, u32[]{:S(2)}, u32[]{:S(2)}) collective-permute-start(bf16[128,16,128]{2,1,0:T(8,128)(2,1)S(1)} %reshape.179), channel_id=1, source_target_pairs={{0,24},{24,0},{1,25},{25,1},{2,26},{26,2},{3,27},{27,3},{4,28},{28... | collective-permute-start | bytes 1572872 | tf_op jit(solution)/shard_map/ppermute | solution.py:348
  37.1 1.5 collective-permute-start.6
  39.5 8.4 %collective-permute-done.7 = bf16[64,16,128]{2,1,0:T(8,128)(2,1)S(1)} collective-permute-done((bf16[64,16,128]{2,1,0:T(8,128)(2,1)}, bf16[64,16,128]{2,1,0:T(8,128)(2,1)S(1)}, u32[]{:S(2)}, u32[]{:S(2)}) %collective-permute-start.7) | collective-permute-done | bytes 262176 | tf_op jit(solution)/shard_map/ppermute | solution.py:348
  48.0 2.0 constant_dynamic-update-slice_fusion.14
  49.9 1.4 collective-permute-start.11
  51.3 1.5 collective-permute-start.10
  53.6 2.2 constant_dynamic-update-slice_fusion.2
  57.1 1.7 constant_dynamic-update-slice_fusion.1
  58.8 0.9 constant_dynamic-update-slice_fusion.8
  60.5 7.7 %collective-permute-done.13 = bf16[64,16,128]{2,1,0:T(8,128)(2,1)S(1)} collective-permute-done((bf16[64,16,128]{2,1,0:T(8,128)(2,1)S(1)}, bf16[64,16,128]{2,1,0:T(8,128)(2,1)S(1)}, u32[]{:S(2)}, u32[]{:S(2)}) %collective-permute-start.13) | collective-permute-done | bytes 262176 | tf_op jit(solution)/shard_map/ppermute | solution.py:348
  68.9 1.5 collective-permute-start.14
  71.8 1.4 collective-permute-start.16
  74.6 0.9 constant_dynamic-update-slice_fusion.13
  75.5 1.0 constant_dynamic-update-slice_fusion.12
  76.5 7.8 %collective-permute-done.17 = bf16[64,16,128]{2,1,0:T(8,128)(2,1)S(1)} collective-permute-done((bf16[64,16,128]{2,1,0:T(8,128)(2,1)S(1)}, bf16[64,16,128]{2,1,0:T(8,128)(2,1)S(1)}, u32[]{:S(2)}, u32[]{:S(2)}) %collective-permute-start.17) | collective-permute-done | bytes 262176 | tf_op jit(solution)/shard_map/ppermute | solution.py:348
  84.4 1.6 collective-permute-start.19
  85.9 0.8 collective-permute-start.18
  88.3 4.8 %collective-permute-done.19 = bf16[64,16,128]{2,1,0:T(8,128)(2,1)S(1)} collective-permute-done((bf16[64,16,128]{2,1,0:T(8,128)(2,1)S(1)}, bf16[64,16,128]{2,1,0:T(8,128)(2,1)S(1)}, u32[]{:S(2)}, u32[]{:S(2)}) %collective-permute-start.19) | collective-permute-done | bytes 262176 | tf_op jit(solution)/shard_map/ppermute | solution.py:348
  96.4 0.9 collective-permute-done.24.refs_9_
  98.1 46.2 %shard_map.68 = (bf16[4,1024,512]{2,1,0:T(8,128)(2,1)}, bf16[4,1024,512]{2,1,0:T(8,128)(2,1)}, f32[1024,512]{1,0:T(8,128)}, f32[1024,128]{1,0:T(8,128)}, f32[256,512]{1,0:T(8,128)}) custom-call(s32[2]{0:T(128)} %pad_add_fusion.1.place_ref, s32[2304]{0:T(1024)} %reshape.178.slots_ref, bf16[512,512]{1,0:T(8,128)(2,1)} %x_ref.1, bf16[512,512]{1,0:T(8,128)(2,1)} %z_ref.1, ...), custom_call_target="tpu_custom_call" | custom-call | flops 28000000000 | bytes 31457280 | tf_op jit(solution)/shard_map/pallas_call | solution.py:152
  144.4 1.4 collective-permute-start.27
  146.0 2.8 %collective-permute-start.25 = (f32[256,512]{1,0:T(8,128)}, f32[256,512]{1,0:T(8,128)S(1)}, u32[]{:S(2)}, u32[]{:S(2)}) collective-permute-start(f32[256,512]{1,0:T(8,128)} %get-tuple-element.59.refs_0_), channel_id=1, source_target_pairs={{0,8},{8,0},{16,24},{24,16},{1,9},{9,1},{17,25},{25,17},{2,10},{10... | collective-permute-start | bytes 1572872 | tf_op jit(solution)/shard_map/ppermute | solution.py:466
  148.9 64.1 %shard_map.69 = (bf16[1024,1024]{1,0:T(8,128)(2,1)}, bf16[1024,1024]{1,0:T(8,128)(2,1)}, f32[1024,128]{1,0:T(8,128)}) custom-call(bf16[4,1024,512]{2,1,0:T(8,128)(2,1)} %get-tuple-element.52.yx_ref, bf16[4,1024,512]{2,1,0:T(8,128)(2,1)} %get-tuple-element.53.yz_ref), custom_call_target="tpu_custom_call" | custom-call | flops 40000000000 | bytes 12582912 | tf_op jit(solution)/shard_map/pallas_call | solution.py:268
  214.1 19.2 %shard_map.70 = (f32[1024,512]{1,0:T(8,128)}, f32[1024,128]{1,0:T(8,128)}) custom-call(s32[2]{0:T(128)} %pad_add_fusion.1.place_ref, bf16[1024,1024]{1,0:T(8,128)(2,1)} %get-tuple-element.54.lh_any, bf16[1024,1024]{1,0:T(8,128)(2,1)} %get-tuple-element.55.ll_any, f32[1024,128]{1,0:T(8,128)} %get-tuple-element.56.d_any, f32[8,1024,128]{2,1,0:T(8,128)} %bitcast.51, ...), custom_call_target="tpu_custom_call" | custom-call | flops 12000000000 | bytes 25165824 | tf_op jit(solution)/shard_map/pallas_call | solution.py:330
  (91 shorter events, 18.0 us)
Async XLA Ops:
  7.2 11.3 %copy-start.7 = (s32[32]{0:T(128)S(1)}, s32[32]{0:T(128)}, u32[]{:S(2)}) copy-start(s32[32]{0:T(128)} %constant.94.clone) | copy-start | bytes 388
  7.2 205.8 %all-gather.3.cloned.1.call-start = ((), (), s32[]{:S(2)}) async-start(), calls=%async_computation | async-start | bytes 4718592 | tf_op jit(solution)/shard_map/all_gather | solution.py:465
  7.2 32.2 %copy-start.2 = (s32[4096]{0:T(1024)S(1)}, s32[4096]{0:T(1024)}, u32[]{:S(2)}) copy-start(s32[4096]{0:T(1024)} %param.8) | copy-start | bytes 49156
  8.9 9.8 %collective-permute-start.3 = (bf16[128,16,128]{2,1,0:T(8,128)(2,1)S(1)}, bf16[128,16,128]{2,1,0:T(8,128)(2,1)S(1)}, u32[]{:S(2)}, u32[]{:S(2)}) collective-permute-start(bf16[128,16,128]{2,1,0:T(8,128)(2,1)S(1)} %reshape.179), channel_id=1, source_target_pairs={{8,16},{16,8},{9,17},{17,9},{10,18},{18,10},{11,19},{19,11},{12,20... | collective-permute-start | bytes 1572872 | tf_op jit(solution)/shard_map/ppermute | solution.py:348
  9.6 17.6 %collective-permute-start.2 = (bf16[128,16,128]{2,1,0:T(8,128)(2,1)S(1)}, bf16[128,16,128]{2,1,0:T(8,128)(2,1)}, u32[]{:S(2)}, u32[]{:S(2)}) collective-permute-start(bf16[128,16,128]{2,1,0:T(8,128)(2,1)S(1)} %reshape.179), channel_id=1, source_target_pairs={{0,8},{8,0},{16,24},{24,16},{1,9},{9,1},{17,25},{25,17},{2,10},{10... | collective-permute-start | bytes 1572872 | tf_op jit(solution)/shard_map/ppermute | solution.py:348
  15.5 13.1 %collective-permute-start.1 = (bf16[128,16,128]{2,1,0:T(8,128)(2,1)S(1)}, bf16[128,16,128]{2,1,0:T(8,128)(2,1)S(1)}, u32[]{:S(2)}, u32[]{:S(2)}) collective-permute-start(bf16[128,16,128]{2,1,0:T(8,128)(2,1)S(1)} %reshape.179), channel_id=1, source_target_pairs={{0,4},{1,5},{2,6},{3,7},{4,0},{5,1},{6,2},{7,3},{8,12},{9,13},{10,... | collective-permute-start | bytes 1572872 | tf_op jit(solution)/shard_map/ppermute | solution.py:348
  17.0 12.8 %collective-permute-start = (bf16[128,16,128]{2,1,0:T(8,128)(2,1)S(1)}, bf16[128,16,128]{2,1,0:T(8,128)(2,1)S(1)}, u32[]{:S(2)}, u32[]{:S(2)}) collective-permute-start(bf16[128,16,128]{2,1,0:T(8,128)(2,1)S(1)} %reshape.179), channel_id=1, source_target_pairs={{0,2},{1,3},{2,0},{3,1},{4,6},{5,7},{6,4},{7,5},{8,10},{9,11},{10,... | collective-permute-start | bytes 1572872 | tf_op jit(solution)/shard_map/ppermute | solution.py:348
  29.8 18.1 %collective-permute-start.5 = (bf16[128,16,128]{2,1,0:T(8,128)(2,1)}, bf16[128,16,128]{2,1,0:T(8,128)(2,1)S(1)}, u32[]{:S(2)}, u32[]{:S(2)}) collective-permute-start(bf16[128,16,128]{2,1,0:T(8,128)(2,1)} %collective-permute-done.2), channel_id=1, source_target_pairs={{0,4},{1,5},{2,6},{3,7},{4,0},{5,1},{6,2},{7,3},{8,12},{9,13},{10,... | collective-permute-start | bytes 1572872 | tf_op jit(solution)/shard_map/ppermute | solution.py:348
  30.3 17.6 %collective-permute-start.4 = (bf16[128,16,128]{2,1,0:T(8,128)(2,1)}, bf16[128,16,128]{2,1,0:T(8,128)(2,1)S(1)}, u32[]{:S(2)}, u32[]{:S(2)}) collective-permute-start(bf16[128,16,128]{2,1,0:T(8,128)(2,1)} %collective-permute-done.2), channel_id=1, source_target_pairs={{0,2},{1,3},{2,0},{3,1},{4,6},{5,7},{6,4},{7,5},{8,10},{9,11},{10,... | collective-permute-start | bytes 1572872 | tf_op jit(solution)/shard_map/ppermute | solution.py:348
  31.8 16.1 %collective-permute-start.8 = (bf16[128,16,128]{2,1,0:T(8,128)(2,1)S(1)}, bf16[128,16,128]{2,1,0:T(8,128)(2,1)}, u32[]{:S(2)}, u32[]{:S(2)}) collective-permute-start(bf16[128,16,128]{2,1,0:T(8,128)(2,1)S(1)} %reshape.179), channel_id=1, source_target_pairs={{0,24},{24,0},{1,25},{25,1},{2,26},{26,2},{3,27},{27,3},{4,28},{28... | collective-permute-start | bytes 1572872 | tf_op jit(solution)/shard_map/ppermute | solution.py:348
  36.5 11.4 %collective-permute-start.7 = (bf16[64,16,128]{2,1,0:T(8,128)(2,1)}, bf16[64,16,128]{2,1,0:T(8,128)(2,1)S(1)}, u32[]{:S(2)}, u32[]{:S(2)}) collective-permute-start(bf16[64,16,128]{2,1,0:T(8,128)(2,1)} %slice.53), channel_id=1, source_target_pairs={{0,2},{1,3},{2,0},{3,1},{4,6},{5,7},{6,4},{7,5},{8,10},{9,11},{10,... | collective-permute-start | bytes 786440 | tf_op jit(solution)/shard_map/ppermute | solution.py:348
  37.1 10.9 %collective-permute-start.6 = (bf16[64,16,128]{2,1,0:T(8,128)(2,1)}, bf16[64,16,128]{2,1,0:T(8,128)(2,1)}, u32[]{:S(2)}, u32[]{:S(2)}) collective-permute-start(bf16[64,16,128]{2,1,0:T(8,128)(2,1)} %slice.52), channel_id=1, source_target_pairs={{0,4},{1,5},{2,6},{3,7},{4,0},{5,1},{6,2},{7,3},{8,12},{9,13},{10,... | collective-permute-start | bytes 786440 | tf_op jit(solution)/shard_map/ppermute | solution.py:348
  49.9 18.3 %collective-permute-start.11 = (bf16[128,16,128]{2,1,0:T(8,128)(2,1)S(1)}, bf16[128,16,128]{2,1,0:T(8,128)(2,1)S(1)}, u32[]{:S(2)}, u32[]{:S(2)}) collective-permute-start(bf16[128,16,128]{2,1,0:T(8,128)(2,1)S(1)} %get-tuple-element.61), channel_id=1, source_target_pairs={{0,4},{1,5},{2,6},{3,7},{4,0},{5,1},{6,2},{7,3},{8,12},{9,13},{10,... | collective-permute-start | bytes 1572872 | tf_op jit(solution)/shard_map/ppermute | solution.py:348
  51.3 16.9 %collective-permute-start.10 = (bf16[128,16,128]{2,1,0:T(8,128)(2,1)S(1)}, bf16[128,16,128]{2,1,0:T(8,128)(2,1)S(1)}, u32[]{:S(2)}, u32[]{:S(2)}) collective-permute-start(bf16[128,16,128]{2,1,0:T(8,128)(2,1)S(1)} %get-tuple-element.61), channel_id=1, source_target_pairs={{0,2},{1,3},{2,0},{3,1},{4,6},{5,7},{6,4},{7,5},{8,10},{9,11},{10,... | collective-permute-start | bytes 1572872 | tf_op jit(solution)/shard_map/ppermute | solution.py:348
  52.8 15.4 %collective-permute-start.9 = (bf16[128,16,128]{2,1,0:T(8,128)(2,1)S(1)}, bf16[128,16,128]{2,1,0:T(8,128)(2,1)S(1)}, u32[]{:S(2)}, u32[]{:S(2)}) collective-permute-start(bf16[128,16,128]{2,1,0:T(8,128)(2,1)S(1)} %get-tuple-element.61), channel_id=1, source_target_pairs={{0,8},{8,0},{16,24},{24,16},{1,9},{9,1},{17,25},{25,17},{2,10},{10... | collective-permute-start | bytes 1572872 | tf_op jit(solution)/shard_map/ppermute | solution.py:348
  55.9 12.3 %collective-permute-start.13 = (bf16[64,16,128]{2,1,0:T(8,128)(2,1)S(1)}, bf16[64,16,128]{2,1,0:T(8,128)(2,1)S(1)}, u32[]{:S(2)}, u32[]{:S(2)}) collective-permute-start(bf16[64,16,128]{2,1,0:T(8,128)(2,1)S(1)} %slice.55), channel_id=1, source_target_pairs={{0,2},{1,3},{2,0},{3,1},{4,6},{5,7},{6,4},{7,5},{8,10},{9,11},{10,... | collective-permute-start | bytes 786440 | tf_op jit(solution)/shard_map/ppermute | solution.py:348
  56.5 11.7 %collective-permute-start.12 = (bf16[64,16,128]{2,1,0:T(8,128)(2,1)S(1)}, bf16[64,16,128]{2,1,0:T(8,128)(2,1)S(1)}, u32[]{:S(2)}, u32[]{:S(2)}) collective-permute-start(bf16[64,16,128]{2,1,0:T(8,128)(2,1)S(1)} %slice.54), channel_id=1, source_target_pairs={{0,4},{1,5},{2,6},{3,7},{4,0},{5,1},{6,2},{7,3},{8,12},{9,13},{10,... | collective-permute-start | bytes 786440 | tf_op jit(solution)/shard_map/ppermute | solution.py:348
  68.2 16.1 %collective-permute-start.15 = (bf16[128,16,128]{2,1,0:T(8,128)(2,1)S(1)}, bf16[128,16,128]{2,1,0:T(8,128)(2,1)S(1)}, u32[]{:S(2)}, u32[]{:S(2)}) collective-permute-start(bf16[128,16,128]{2,1,0:T(8,128)(2,1)S(1)} %collective-permute-done.9), channel_id=1, source_target_pairs={{0,4},{1,5},{2,6},{3,7},{4,0},{5,1},{6,2},{7,3},{8,12},{9,13},{10,... | collective-permute-start | bytes 1572872 | tf_op jit(solution)/shard_map/ppermute | solution.py:348
  68.9 15.4 %collective-permute-start.14 = (bf16[128,16,128]{2,1,0:T(8,128)(2,1)S(1)}, bf16[128,16,128]{2,1,0:T(8,128)(2,1)S(1)}, u32[]{:S(2)}, u32[]{:S(2)}) collective-permute-start(bf16[128,16,128]{2,1,0:T(8,128)(2,1)S(1)} %collective-permute-done.9), channel_id=1, source_target_pairs={{0,2},{1,3},{2,0},{3,1},{4,6},{5,7},{6,4},{7,5},{8,10},{9,11},{10,... | collective-permute-start | bytes 1572872 | tf_op jit(solution)/shard_map/ppermute | solution.py:348
  71.1 26.2 %collective-permute-start.20 = (bf16[512,16,128]{2,1,0:T(8,128)(2,1)}, bf16[512,16,128]{2,1,0:T(8,128)(2,1)}, u32[]{:S(2)}, u32[]{:S(2)}) collective-permute-start(bf16[512,16,128]{2,1,0:T(8,128)(2,1)} %constant_dynamic-update-slice_fusion.refs_0_), channel_id=1, source_target_pairs={{0,1},{1,0},{2,3},{3,2},{4,5},{5,4},{6,7},{7,6},{8,9},{9,8},{10,11... | collective-permute-start | bytes 6291464 | tf_op jit(solution)/shard_map/ppermute | solution.py:348
  71.2 13.1 %collective-permute-start.17 = (bf16[64,16,128]{2,1,0:T(8,128)(2,1)S(1)}, bf16[64,16,128]{2,1,0:T(8,128)(2,1)S(1)}, u32[]{:S(2)}, u32[]{:S(2)}) collective-permute-start(bf16[64,16,128]{2,1,0:T(8,128)(2,1)S(1)} %slice.57), channel_id=1, source_target_pairs={{0,2},{1,3},{2,0},{3,1},{4,6},{5,7},{6,4},{7,5},{8,10},{9,11},{10,... | collective-permute-start | bytes 786440 | tf_op jit(solution)/shard_map/ppermute | solution.py:348
  71.8 12.5 %collective-permute-start.16 = (bf16[64,16,128]{2,1,0:T(8,128)(2,1)S(1)}, bf16[64,16,128]{2,1,0:T(8,128)(2,1)S(1)}, u32[]{:S(2)}, u32[]{:S(2)}) collective-permute-start(bf16[64,16,128]{2,1,0:T(8,128)(2,1)S(1)} %slice.56), channel_id=1, source_target_pairs={{0,4},{1,5},{2,6},{3,7},{4,0},{5,1},{6,2},{7,3},{8,12},{9,13},{10,... | collective-permute-start | bytes 786440 | tf_op jit(solution)/shard_map/ppermute | solution.py:348
  84.3 13.0 %collective-permute-start.21 = (bf16[512,16,128]{2,1,0:T(8,128)(2,1)}, bf16[512,16,128]{2,1,0:T(8,128)(2,1)}, u32[]{:S(2)}, u32[]{:S(2)}) collective-permute-start(bf16[512,16,128]{2,1,0:T(8,128)(2,1)} %constant_dynamic-update-slice_fusion.5.refs_1_), channel_id=1, source_target_pairs={{0,1},{1,0},{2,3},{3,2},{4,5},{5,4},{6,7},{7,6},{8,9},{9,8},{10,11... | collective-permute-start | bytes 6291464 | tf_op jit(solution)/shard_map/ppermute | solution.py:348
  84.4 8.8 %collective-permute-start.19 = (bf16[64,16,128]{2,1,0:T(8,128)(2,1)S(1)}, bf16[64,16,128]{2,1,0:T(8,128)(2,1)S(1)}, u32[]{:S(2)}, u32[]{:S(2)}) collective-permute-start(bf16[64,16,128]{2,1,0:T(8,128)(2,1)S(1)} %slice.59), channel_id=1, source_target_pairs={{0,2},{1,3},{2,0},{3,1},{4,6},{5,7},{6,4},{7,5},{8,10},{9,11},{10,... | collective-permute-start | bytes 786440 | tf_op jit(solution)/shard_map/ppermute | solution.py:348
  85.9 8.4 %collective-permute-start.18 = (bf16[64,16,128]{2,1,0:T(8,128)(2,1)S(1)}, bf16[64,16,128]{2,1,0:T(8,128)(2,1)S(1)}, u32[]{:S(2)}, u32[]{:S(2)}) collective-permute-start(bf16[64,16,128]{2,1,0:T(8,128)(2,1)S(1)} %slice.58), channel_id=1, source_target_pairs={{0,4},{1,5},{2,6},{3,7},{4,0},{5,1},{6,2},{7,3},{8,12},{9,13},{10,... | collective-permute-start | bytes 786440 | tf_op jit(solution)/shard_map/ppermute | solution.py:348
  88.2 9.2 %collective-permute-start.22 = (bf16[512,16,128]{2,1,0:T(8,128)(2,1)}, bf16[512,16,128]{2,1,0:T(8,128)(2,1)}, u32[]{:S(2)}, u32[]{:S(2)}) collective-permute-start(bf16[512,16,128]{2,1,0:T(8,128)(2,1)} %constant_dynamic-update-slice_fusion.10.refs_2_), channel_id=1, source_target_pairs={{0,1},{1,0},{2,3},{3,2},{4,5},{5,4},{6,7},{7,6},{8,9},{9,8},{10,11... | collective-permute-start | bytes 6291464 | tf_op jit(solution)/shard_map/ppermute | solution.py:348
  88.3 6.1 %copy-start = (bf16[384,16,128]{2,1,0:T(8,128)(2,1)}, bf16[384,16,128]{2,1,0:T(8,128)(2,1)S(1)}, u32[]{:S(2)}) copy-start(bf16[384,16,128]{2,1,0:T(8,128)(2,1)S(1)} %constant_dynamic-update-slice_fusion.15.refs_3_) | copy-start | bytes 4718596
  93.1 4.2 %collective-permute-start.23 = (bf16[384,16,128]{2,1,0:T(8,128)(2,1)S(1)}, bf16[384,16,128]{2,1,0:T(8,128)(2,1)}, u32[]{:S(2)}, u32[]{:S(2)}) collective-permute-start(bf16[384,16,128]{2,1,0:T(8,128)(2,1)S(1)} %constant_dynamic-update-slice_fusion.15.refs_3_), channel_id=1, source_target_pairs={{0,1},{1,0},{2,3},{3,2},{4,5},{5,4},{6,7},{7,6},{8,9},{9,8},{10,11... | collective-permute-start | bytes 4718600 | tf_op jit(solution)/shard_map/ppermute | solution.py:348
  94.4 2.9 %collective-permute-start.24 = (bf16[128,16,128]{2,1,0:T(8,128)(2,1)S(1)}, bf16[128,16,128]{2,1,0:T(8,128)(2,1)S(1)}, u32[]{:S(2)}, u32[]{:S(2)}) collective-permute-start(bf16[128,16,128]{2,1,0:T(8,128)(2,1)S(1)} %constant_dynamic-update-slice_fusion.18.refs_4_), channel_id=1, source_target_pairs={{0,1},{1,0},{2,3},{3,2},{4,5},{5,4},{6,7},{7,6},{8,9},{9,8},{10,11... | collective-permute-start | bytes 1572872 | tf_op jit(solution)/shard_map/ppermute | solution.py:348
  144.4 68.5 %collective-permute-start.27 = (f32[256,512]{1,0:T(8,128)}, f32[256,512]{1,0:T(8,128)S(1)}, u32[]{:S(2)}, u32[]{:S(2)}) collective-permute-start(f32[256,512]{1,0:T(8,128)} %get-tuple-element.59.refs_0_), channel_id=1, source_target_pairs={{0,24},{8,16},{16,8},{24,0},{1,25},{9,17},{17,9},{25,1},{2,26},{10... | collective-permute-start | bytes 1572872 | tf_op jit(solution)/shard_map/ppermute | solution.py:466
  145.8 67.1 %collective-permute-start.26 = (f32[256,512]{1,0:T(8,128)}, f32[256,512]{1,0:T(8,128)S(1)}, u32[]{:S(2)}, u32[]{:S(2)}) collective-permute-start(f32[256,512]{1,0:T(8,128)} %get-tuple-element.59.refs_0_), channel_id=1, source_target_pairs={{0,16},{8,24},{16,0},{24,8},{1,17},{9,25},{17,1},{25,9},{2,18},{10... | collective-permute-start | bytes 1572872 | tf_op jit(solution)/shard_map/ppermute | solution.py:466
  146.0 66.9 %collective-permute-start.25 = (f32[256,512]{1,0:T(8,128)}, f32[256,512]{1,0:T(8,128)S(1)}, u32[]{:S(2)}, u32[]{:S(2)}) collective-permute-start(f32[256,512]{1,0:T(8,128)} %get-tuple-element.59.refs_0_), channel_id=1, source_target_pairs={{0,8},{8,0},{16,24},{24,16},{1,9},{9,1},{17,25},{25,17},{2,10},{10... | collective-permute-start | bytes 1572872 | tf_op jit(solution)/shard_map/ppermute | solution.py:466
  (5 other events, 6.7 us)
Sparse Core Ops, SparseCore 0:
  144.5 35.0 all-gather.2
